TPU v7x, 32 devices: a whole 2x2x4 slice. The times are simulated.
32 devices in a mesh: row: 8 (over y, x, core), col: 4 (over z).
Axes of the slice: x: 2, y: 2, z: 4, core: 2. Of those that a mesh axis runs over, the one named last changes fastest.
Arguments:
- fine_blocks: bfloat16 [8, 4, 64, 128, 128], P('row', 'col'), may hold values from -0.5 to 0.5
- fine_rows: int32 [8, 4, 64], P('row', 'col'), may hold values from 0 to 7
- fine_cols: int32 [8, 4, 64], P('row', 'col'), may hold values from 0 to 39
- fine_counts: int32 [8, 4], P('row', 'col'), may hold values from 8 to 64, as said below
- prolong_blocks: bfloat16 [8, 4, 12, 128, 128], P('row', 'col'), may hold values from -1.5 to 1.5
- prolong_codes: int32 [8, 4, 12], P('row', 'col'), may hold values from 0 to 15, as said below
- prolong_counts: int32 [8, 4], P('row', 'col'), may hold values from 6 to 12, as said below
- second_blocks: bfloat16 [8, 4, 2, 128, 128], P('row', 'col'), may hold values from -0.25 to 0.25
- second_aggs: int32 [8, 4, 2], P('row', 'col'), may hold values from 0 to 1
Outputs:
- coarse_one: bfloat16 [8, 4, 2, 5, 2, 128, 128], P('row', 'col')
- coarse_two: float32 [8, 2, 3, 2, 128, 128], P('row')
Inputs may be any that keep to these rules, and one draw needn't show every extreme that they name: Slots from fine_counts[r, c] to 63 are padding and are ignored; in every draw some device has all 64 slots live. `fine_cols`: a source outside the grid of devices contributes nothing. `prolong_codes`: the live slots of one device name distinct blocks. Slots from prolong_counts[r, c] to 11 are padding and are ignored; in every draw some device has all 12 slots live.
All inputs are finite; a program needn't handle non-finite values.
Results may differ from a plain program's by a relative error of at most 0.0057.
Values may be sent and summed in bfloat16 or wider, within the bound.
No kernel may reach another device: no remote copies, remote signals or barrier semaphores. Data moves between devices by JAX's collectives and lax.ppermute only.
A program may use at most 64 MiB of HBM per device.

v0:
```python
import jax
import jax.numpy as jnp
from jax import lax
from jax.sharding import PartitionSpec as P

BS = 128
FB = 8
CB = 2
NA = 64
NP = 12
G2 = 2


def padded_2(cells, sides, width):
    for axis, dim in sides:
        count = lax.axis_size(axis)
        ends = count - 1
        head = lax.slice_in_dim(cells, 0, width, axis=dim)
        tail = lax.slice_in_dim(cells, cells.shape[dim] - width, cells.shape[dim], axis=dim)
        cells = jnp.concatenate(
            [
                lax.ppermute(tail, axis, [(i, (i + 1) % count) for i in range(ends)]),
                cells,
                lax.ppermute(head, axis, [((i + 1) % count, i) for i in range(ends)]),
            ],
            axis=dim,
        )
    return cells


def source_stack(padded):
    return jnp.stack([padded[1, 1], padded[1, 0], padded[1, 2], padded[0, 1], padded[2, 1]], axis=0)


def half_product(coarse, sources):
    inside = jnp.einsum(
        "Jsjxy,sjayz->Jaxz", coarse[:, 0:3], sources[0:3], preferred_element_type=jnp.float32
    )
    before = jnp.einsum(
        "Jjxy,jayz->Jaxz", coarse[:, 3], sources[3], preferred_element_type=jnp.float32
    )
    beyond = jnp.einsum(
        "Jjxy,jayz->Jaxz", coarse[:, 4], sources[4], preferred_element_type=jnp.float32
    )
    return jnp.stack([inside, before, beyond], axis=1).astype(jnp.bfloat16)


def per_device(
    fine_blocks,
    fine_rows,
    fine_cols,
    fine_counts,
    prolong_blocks,
    prolong_codes,
    prolong_counts,
    second_blocks,
    second_aggs,
):
    blocks = fine_blocks[0, 0]
    columns = fine_cols[0, 0]
    live_prolong = jnp.arange(NP) < prolong_counts[0, 0]
    placing = (
        (prolong_codes[0, 0][:, None] == jnp.arange(FB * CB)[None, :]) & live_prolong[:, None]
    ).astype(jnp.bfloat16)
    dense_p = jnp.einsum(
        "kq,kxy->qxy", placing, prolong_blocks[0, 0], preferred_element_type=jnp.float32
    ).astype(jnp.bfloat16)
    member = (second_aggs[0, 0][:, None] == jnp.arange(G2)[None, :]).astype(jnp.bfloat16)
    lifted = second_blocks[0, 0][:, None] * member[:, :, None, None]
    padded = padded_2(dense_p.reshape(1, 1, FB * CB, BS, BS), (("row", 0), ("col", 1)), 1)
    rim_lifted = padded_2(lifted.reshape(1, 1, CB, G2, BS, BS), (("row", 0), ("col", 1)), 1)
    near_p = source_stack(padded).reshape(5 * FB, CB, BS, BS)
    fetched = near_p[columns]
    products = jnp.einsum("kxy,kjyz->kjxz", blocks, fetched, preferred_element_type=jnp.float32)
    live_fine = jnp.arange(NA) < fine_counts[0, 0]
    target = fine_rows[0, 0] * 5 + columns // FB
    placing_rows = ((target[:, None] == jnp.arange(5 * FB)[None, :]) & live_fine[:, None]).astype(
        jnp.float32
    )
    summed = jnp.einsum("kt,kjxz->tjxz", placing_rows, products, precision=lax.Precision.HIGHEST)
    fine_product = summed.astype(jnp.bfloat16).reshape(FB, 5, CB, BS, BS)
    own_p = dense_p.reshape(FB, CB, BS, BS)
    coarse_one = jnp.einsum(
        "iJxy,isjxz->Jsjyz", own_p, fine_product, preferred_element_type=jnp.float32
    ).astype(jnp.bfloat16)
    half_prod = half_product(coarse_one, source_stack(rim_lifted))
    own_term = jnp.einsum(
        "Jaxy,Jgbxz->agbyz", lifted, half_prod, preferred_element_type=jnp.float32
    )
    coarse_two = lax.psum(own_term, "col")
    return (coarse_one[None, None], coarse_two[None])


def solution(mesh):
    in_specs = (
        P("row", "col", None, None, None),
        P("row", "col", None),
        P("row", "col", None),
        P("row", "col"),
        P("row", "col", None, None, None),
        P("row", "col", None),
        P("row", "col"),
        P("row", "col", None, None, None),
        P("row", "col", None),
    )
    out_specs = (
        P("row", "col", None, None, None, None, None),
        P("row", None, None, None, None, None),
    )
    return jax.shard_map(
        per_device, mesh=mesh, in_specs=in_specs, out_specs=out_specs, check_vma=False
    )
```

profile of v0, /device:TPU:0, one launch (start us, length us, event | category | flops | bytes accessed | tf_op | source)
XLA Modules:
  0.0 172.8 jit_solution(17156931065392653950)
XLA Ops:
  7.2 0.0 copy-start
  7.2 0.0 all-reduce.2.cloned.1.call-start
  8.0 0.0 copy-start.6
  8.0 0.0 copy-start.7
  8.0 2.3 %bitcast_dynamic-update-slice_fusion.2 = (bf16[5,16,128,128]{3,1,2,0:T(8,128)(2,1)}, bf16[16,128,128]{2,0,1:T(8,128)(2,1)}) fusion(bf16[12,128,128]{2,1,0:T(8,128)(2,1)} %bitcast.181, s32[12]{0:T(128)} %bitcast.184, pred[12]{0:T(512)(128)(4,1)S(1)} %iota_compare_fusion.2), kind=kOutput, calls=%fused_computation.29 | convolution fusion | flops 6553983 | bytes 1441852 | tf_op jit(solution)/shard_map/kq,kxy->qxy/dot_general | solution.py:65
  10.4 2.4 %collective-permute-start = (bf16[1,1,16,128,128]{4,2,3,1,0:T(8,128)(2,1)}, bf16[1,1,16,128,128]{4,2,3,1,0:T(8,128)(2,1)S(1)}, u32[]{:S(2)}, u32[]{:S(2)}) collective-permute-start(bf16[1,1,16,128,128]{4,2,3,1,0:T(8,128)(2,1)} %bitcast.10), channel_id=1, source_target_pairs={{0,4},{4,8},{8,12},{12,16},{16,20},{20,24},{24,28},{1,5},{5,9},{9,... | collective-permute-start | bytes 1572872 | tf_op jit(solution)/shard_map/ppermute | solution.py:22
  12.8 1.3 collective-permute-start.1
  14.1 1.0 copy.27
  15.0 0.0 copy-start.1
  15.0 0.8 compare_convert_fusion
  15.8 0.0 collective-permute-done
  15.9 3.0 %collective-permute-done.1 = bf16[1,1,16,128,128]{4,2,3,1,0:T(8,128)(2,1)S(1)} collective-permute-done((bf16[1,1,16,128,128]{4,2,3,1,0:T(8,128)(2,1)}, bf16[1,1,16,128,128]{4,2,3,1,0:T(8,128)(2,1)S(1)}, u32[]{:S(2)}, u32[]{:S(2)}) %collective-permute-start.1) | collective-permute-done | bytes 524320 | tf_op jit(solution)/shard_map/ppermute | solution.py:24
  18.9 1.2 pad_maximum_fusion
  20.1 3.6 %collective-permute-start.2 = (bf16[3,1,16,128,128]{4,2,3,1,0:T(8,128)(2,1)S(1)}, bf16[3,1,16,128,128]{4,2,3,1,0:T(8,128)(2,1)S(1)}, u32[]{:S(2)}, u32[]{:S(2)}) collective-permute-start(bf16[3,1,16,128,128]{4,2,3,1,0:T(8,128)(2,1)S(1)} %pad_maximum_fusion), channel_id=1, source_target_pairs={{0,1},{1,2},{2,3},{4,5},{5,6},{6,7},{8,9},{9,10},{10,11},{12,13},{... | collective-permute-start | bytes 4718600 | tf_op jit(solution)/shard_map/ppermute | solution.py:22
  23.7 0.1 broadcast_multiply_fusion
  23.7 12.0 %collective-permute-start.4 = (bf16[1,1,2,2,128,128]{4,5,2,3,1,0:T(8,128)(2,1)S(1)}, bf16[1,1,2,2,128,128]{4,5,2,3,1,0:T(8,128)(2,1)S(1)}, u32[]{:S(2)}, u32[]{:S(2)}) collective-permute-start(bf16[1,1,2,2,128,128]{4,5,2,3,1,0:T(8,128)(2,1)S(1)} %broadcast_multiply_fusion), channel_id=1, source_target_pairs={{0,4},{4,8},{8,12},{12,16},{16,20},{20,24},{24,28},{1,5},{5,9},{9,... | collective-permute-start | bytes 393224 | tf_op jit(solution)/shard_map/ppermute | solution.py:22
  35.7 1.3 collective-permute-start.5
  37.0 1.3 collective-permute-start.3
  38.3 0.7 broadcast_multiply_fusion.1
  39.7 0.0 copy-done.6
  39.7 0.0 copy-done.7
  39.8 0.0 collective-permute-done.4
  39.8 0.0 collective-permute-done.5
  39.8 1.3 collective-permute-start.7
  41.1 5.2 %collective-permute-start.6 = (bf16[3,1,2,2,128,128]{4,5,2,3,1,0:T(8,128)(2,1)S(1)}, bf16[3,1,2,2,128,128]{4,5,2,3,1,0:T(8,128)(2,1)S(1)}, u32[]{:S(2)}, u32[]{:S(2)}) collective-permute-start(bf16[3,1,2,2,128,128]{4,5,2,3,1,0:T(8,128)(2,1)S(1)} %pad_maximum_fusion.1), channel_id=1, source_target_pairs={{0,1},{1,2},{2,3},{4,5},{5,6},{6,7},{8,9},{9,10},{10,11},{12,13},{... | collective-permute-start | bytes 1179656 | tf_op jit(solution)/shard_map/ppermute | solution.py:22
  46.4 38.1 %collective-permute-done.7 = bf16[3,1,2,2,128,128]{4,5,2,3,1,0:T(8,128)(2,1)S(1)} collective-permute-done((bf16[3,1,2,2,128,128]{4,5,2,3,1,0:T(8,128)(2,1)S(1)}, bf16[3,1,2,2,128,128]{4,5,2,3,1,0:T(8,128)(2,1)S(1)}, u32[]{:S(2)}, u32[]{:S(2)}) %collective-permute-start.7) | collective-permute-done | bytes 393248 | tf_op jit(solution)/shard_map/ppermute | solution.py:24
  84.5 0.7 slice_bitcast_fusion.7
  85.1 0.0 collective-permute-done.6
  85.1 0.7 slice_bitcast_fusion.8
  85.8 0.0 collective-permute-done.2
  85.8 0.0 copy-done.1
  85.8 0.1 fusion.22
  85.9 0.0 collective-permute-done.3
  85.9 0.1 fusion.21
  86.0 0.1 bitcast_dynamic-update-slice_fusion.1
  86.1 0.1 bitcast_dynamic-update-slice_fusion
  86.1 2.2 %copy.23 = bf16[5,16,128,128]{3,2,1,0:T(8,128)(2,1)} copy(bf16[5,16,128,128]{3,1,2,0:T(8,128)(2,1)S(1)} %bitcast_dynamic-update-slice_fusion) | data formatting | bytes 5242880 | tf_op jit(solution)/shard_map/stack | solution.py:32
  88.3 4.8 %gather_fusion = bf16[64,2,128,128]{3,2,1,0:T(8,128)(2,1)} fusion(bf16[40,2,128,128]{3,2,1,0:T(8,128)(2,1)} %bitcast.175, s32[1024]{0:T(1024)S(1)} %pad_clamp_fusion), kind=kCustom, calls=%fused_computation | custom fusion | bytes 8388864 | tf_op jit(solution)/shard_map/gather | solution.py:73
  93.1 0.0 copy-done
  93.1 6.7 %fusion.4 = f32[64,2,128,128]{3,2,1,0:T(8,128)} fusion(bf16[64,2,128,128]{3,2,1,0:T(8,128)(2,1)} %gather_fusion, bf16[1,1,64,128,128]{4,3,2,1,0:T(8,128)(2,1)S(1)} %copy-done), kind=kOutput, calls=%fused_computation.5 | convolution fusion | flops 536870912 | bytes 14680064 | tf_op jit(solution)/shard_map/kxy,kjyz->kjxz/dot_general | solution.py:74
  99.8 8.7 %copy.36 = f32[64,2,128,128]{2,0,3,1:T(8,128)} copy(f32[64,2,128,128]{3,2,1,0:T(8,128)} %fusion.4) | data formatting | bytes 16777216 | tf_op jit(solution)/shard_map/kxy,kjyz->kjxz/dot_general | solution.py:74
  108.6 7.4 %fusion.6 = bf16[40,2,128,128]{3,0,2,1:T(8,128)(2,1)S(1)} fusion(f32[64,2,128,128]{2,0,3,1:T(8,128)} %copy.36, s32[64]{0:T(128)S(1)} %bitcast_add_fusion, pred[64]{0:T(512)(128)(4,1)S(1)} %iota_compare_fusion.3), kind=kOutput, calls=%fused_computation.7 | convolution fusion | flops 1007948800 | bytes 11010368 | tf_op jit(solution)/shard_map/kt,kjxz->tjxz/dot_general | solution.py:80
  115.9 0.7 copy.24
  116.6 0.0 copy-start.2
  116.6 0.0 copy-start.3
  116.6 0.0 copy-start.4
  116.6 2.0 %fusion.12 = bf16[5,2,128,2,128]{4,2,3,1,0:T(8,128)(2,1)S(1)} fusion(bf16[8,5,2,128,128,1]{4,3,2,1,0,5:T(8,128)(2,1)S(1)} %bitcast.176, bf16[8,2,128,128,1,1]{3,1,0,2,5,4:T(2,128)(2,1)} %bitcast.25), kind=kOutput, calls=%fused_computation.10 | convolution fusion | flops 671416320 | bytes 3801088 | tf_op jit(solution)/shard_map/iJxy,isjxz->Jsjyz/dot_general | solution.py:83
  118.6 0.0 copy-start.5
  118.6 0.0 copy-done.2
  118.6 0.0 copy-done.3
  118.6 0.0 copy-done.4
  118.7 0.3 fusion.18
  118.9 0.2 fusion.19
  119.1 0.2 fusion.20
  119.3 0.1 copy-done.5
  119.5 1.2 convolution_bitcast_fusion
  120.7 0.0 all-reduce.2.cloned.1.call-update
  120.7 1.1 copy.33
  121.8 41.9 %all-reduce.2.cloned.1.call-done = f32[1,2,3,2,128,128]{4,5,1,3,2,0:T(8,128)} async-done(((f32[1,2,3,2,128,128]{4,5,1,3,2,0:T(8,128)}), f32[1,2,3,2,128,128]{4,5,1,3,2,0:T(8,128)}) %all-reduce.2.cloned.1.call-update) | async-done | bytes 786448 | tf_op jit(solution)/shard_map/psum | solution.py:90
  163.7 2.3 %copy.34 = f32[1,2,3,2,128,128]{5,4,3,2,1,0:T(8,128)} copy(f32[1,2,3,2,128,128]{4,5,1,3,2,0:T(8,128)} %all-reduce.2.cloned.1.call-done) | data formatting | bytes 1572864
  (6 shorter events, 0.1 us)
Async XLA Ops:
  7.2 86.0 %copy-start = (bf16[1,1,64,128,128]{4,3,2,1,0:T(8,128)(2,1)S(1)}, bf16[1,1,64,128,128]{4,3,2,1,0:T(8,128)(2,1)}, u32[]{:S(2)}) copy-start(bf16[1,1,64,128,128]{4,3,2,1,0:T(8,128)(2,1)} %param.9) | copy-start | bytes 6291460
  7.2 156.5 %all-reduce.2.cloned.1.call-start = ((), (), s32[]{:S(2)}) async-start(), calls=%async_computation | async-start | bytes 1572864 | tf_op jit(solution)/shard_map/psum | solution.py:90
  8.0 31.7 %copy-start.6 = (s32[1,1,64]{2,1,0:T(1,128)S(1)}, s32[1,1,64]{2,1,0:T(1,128)}, u32[]{:S(2)}) copy-start(s32[1,1,64]{2,1,0:T(1,128)} %param.10) | copy-start | bytes 772
  8.0 31.7 %copy-start.7 = (s32[1,1,64]{2,1,0:T(1,128)S(1)}, s32[1,1,64]{2,1,0:T(1,128)}, u32[]{:S(2)}) copy-start(s32[1,1,64]{2,1,0:T(1,128)} %param.11) | copy-start | bytes 772
  10.4 5.5 %collective-permute-start = (bf16[1,1,16,128,128]{4,2,3,1,0:T(8,128)(2,1)}, bf16[1,1,16,128,128]{4,2,3,1,0:T(8,128)(2,1)S(1)}, u32[]{:S(2)}, u32[]{:S(2)}) collective-permute-start(bf16[1,1,16,128,128]{4,2,3,1,0:T(8,128)(2,1)} %bitcast.10), channel_id=1, source_target_pairs={{0,4},{4,8},{8,12},{12,16},{16,20},{20,24},{24,28},{1,5},{5,9},{9,... | collective-permute-start | bytes 1572872 | tf_op jit(solution)/shard_map/ppermute | solution.py:22
  12.8 6.1 %collective-permute-start.1 = (bf16[1,1,16,128,128]{4,2,3,1,0:T(8,128)(2,1)}, bf16[1,1,16,128,128]{4,2,3,1,0:T(8,128)(2,1)S(1)}, u32[]{:S(2)}, u32[]{:S(2)}) collective-permute-start(bf16[1,1,16,128,128]{4,2,3,1,0:T(8,128)(2,1)} %bitcast.10), channel_id=1, source_target_pairs={{4,0},{8,4},{12,8},{16,12},{20,16},{24,20},{28,24},{5,1},{9,5},{13... | collective-permute-start | bytes 1572872 | tf_op jit(solution)/shard_map/ppermute | solution.py:24
  15.0 70.8 %copy-start.1 = (bf16[5,16,128,128]{3,1,2,0:T(8,128)(2,1)S(1)}, bf16[5,16,128,128]{3,1,2,0:T(8,128)(2,1)}, u32[]{:S(2)}) copy-start(bf16[5,16,128,128]{3,1,2,0:T(8,128)(2,1)} %get-tuple-element.6) | copy-start | bytes 7864324
  20.1 65.7 %collective-permute-start.2 = (bf16[3,1,16,128,128]{4,2,3,1,0:T(8,128)(2,1)S(1)}, bf16[3,1,16,128,128]{4,2,3,1,0:T(8,128)(2,1)S(1)}, u32[]{:S(2)}, u32[]{:S(2)}) collective-permute-start(bf16[3,1,16,128,128]{4,2,3,1,0:T(8,128)(2,1)S(1)} %pad_maximum_fusion), channel_id=1, source_target_pairs={{0,1},{1,2},{2,3},{4,5},{5,6},{6,7},{8,9},{9,10},{10,11},{12,13},{... | collective-permute-start | bytes 4718600 | tf_op jit(solution)/shard_map/ppermute | solution.py:22
  23.7 16.0 %collective-permute-start.4 = (bf16[1,1,2,2,128,128]{4,5,2,3,1,0:T(8,128)(2,1)S(1)}, bf16[1,1,2,2,128,128]{4,5,2,3,1,0:T(8,128)(2,1)S(1)}, u32[]{:S(2)}, u32[]{:S(2)}) collective-permute-start(bf16[1,1,2,2,128,128]{4,5,2,3,1,0:T(8,128)(2,1)S(1)} %broadcast_multiply_fusion), channel_id=1, source_target_pairs={{0,4},{4,8},{8,12},{12,16},{16,20},{20,24},{24,28},{1,5},{5,9},{9,... | collective-permute-start | bytes 393224 | tf_op jit(solution)/shard_map/ppermute | solution.py:22
  35.7 4.0 %collective-permute-start.5 = (bf16[1,1,2,2,128,128]{4,5,2,3,1,0:T(8,128)(2,1)S(1)}, bf16[1,1,2,2,128,128]{4,5,2,3,1,0:T(8,128)(2,1)S(1)}, u32[]{:S(2)}, u32[]{:S(2)}) collective-permute-start(bf16[1,1,2,2,128,128]{4,5,2,3,1,0:T(8,128)(2,1)S(1)} %broadcast_multiply_fusion), channel_id=1, source_target_pairs={{4,0},{8,4},{12,8},{16,12},{20,16},{24,20},{28,24},{5,1},{9,5},{13... | collective-permute-start | bytes 393224 | tf_op jit(solution)/shard_map/ppermute | solution.py:24
  37.0 48.8 %collective-permute-start.3 = (bf16[3,1,16,128,128]{4,2,3,1,0:T(8,128)(2,1)S(1)}, bf16[3,1,16,128,128]{4,2,3,1,0:T(8,128)(2,1)S(1)}, u32[]{:S(2)}, u32[]{:S(2)}) collective-permute-start(bf16[3,1,16,128,128]{4,2,3,1,0:T(8,128)(2,1)S(1)} %pad_maximum_fusion), channel_id=1, source_target_pairs={{1,0},{2,1},{3,2},{5,4},{6,5},{7,6},{9,8},{10,9},{11,10},{13,12},{... | collective-permute-start | bytes 4718600 | tf_op jit(solution)/shard_map/ppermute | solution.py:24
  39.8 44.6 %collective-permute-start.7 = (bf16[3,1,2,2,128,128]{4,5,2,3,1,0:T(8,128)(2,1)S(1)}, bf16[3,1,2,2,128,128]{4,5,2,3,1,0:T(8,128)(2,1)S(1)}, u32[]{:S(2)}, u32[]{:S(2)}) collective-permute-start(bf16[3,1,2,2,128,128]{4,5,2,3,1,0:T(8,128)(2,1)S(1)} %pad_maximum_fusion.1), channel_id=1, source_target_pairs={{1,0},{2,1},{3,2},{5,4},{6,5},{7,6},{9,8},{10,9},{11,10},{13,12},{... | collective-permute-start | bytes 1179656 | tf_op jit(solution)/shard_map/ppermute | solution.py:24
  41.1 44.0 %collective-permute-start.6 = (bf16[3,1,2,2,128,128]{4,5,2,3,1,0:T(8,128)(2,1)S(1)}, bf16[3,1,2,2,128,128]{4,5,2,3,1,0:T(8,128)(2,1)S(1)}, u32[]{:S(2)}, u32[]{:S(2)}) collective-permute-start(bf16[3,1,2,2,128,128]{4,5,2,3,1,0:T(8,128)(2,1)S(1)} %pad_maximum_fusion.1), channel_id=1, source_target_pairs={{0,1},{1,2},{2,3},{4,5},{5,6},{6,7},{8,9},{9,10},{10,11},{12,13},{... | collective-permute-start | bytes 1179656 | tf_op jit(solution)/shard_map/ppermute | solution.py:22
  116.6 2.0 %copy-start.2 = (bf16[1,2,2,128,128]{3,4,0,1,2:T(8,128)(2,1)S(1)}, bf16[1,2,2,128,128]{3,4,0,1,2:T(8,128)(2,1)}, u32[]{:S(2)}) copy-start(bf16[1,2,2,128,128]{3,4,0,1,2:T(8,128)(2,1)} %broadcast_multiply_fusion.1) | copy-start | bytes 393220
  116.6 2.0 %copy-start.3 = (bf16[1,2,2,128,128]{3,4,0,1,2:T(8,128)(2,1)S(1)}, bf16[1,2,2,128,128]{3,4,0,1,2:T(8,128)(2,1)}, u32[]{:S(2)}) copy-start(bf16[1,2,2,128,128]{3,4,0,1,2:T(8,128)(2,1)} %slice_bitcast_fusion.7) | copy-start | bytes 393220
  116.6 2.0 %copy-start.4 = (bf16[1,2,2,128,128]{3,4,0,1,2:T(8,128)(2,1)S(1)}, bf16[1,2,2,128,128]{3,4,0,1,2:T(8,128)(2,1)}, u32[]{:S(2)}) copy-start(bf16[1,2,2,128,128]{3,4,0,1,2:T(8,128)(2,1)} %slice_bitcast_fusion.8) | copy-start | bytes 393220
  118.6 0.8 copy-start.5
Sparse Core Ops, SparseCore 0:
  120.8 42.8 all-reduce.1
where the time goes:
time: 174 us; the launch traced here: 173 us
  waiting for transfers between devices  83.1 us (48%)
  starting transfers between devices  28.4 us (16%)
  local copies, waits for them, and re-layouts  22.5 us (13%)
  matrix products  20.3 us (12%)
  between operations  15.8 us (9%)
  other arithmetic  2.91 us (2%)
    psum x1, waiting for transfers between devices, per_device(): coarse_two = lax.psum(own_term, 'col')  41.9 us
    ppermute x4, waiting for transfers between devices, padded_2(): lax.ppermute(head, axis, [((i + 1) % count, i) for i in range(ends)])  41.1 us
    ppermute x4, starting transfers between devices, padded_2(): lax.ppermute(tail, axis, [(i, (i + 1) % count) for i in range(ends)])  23.1 us
    dot_general x1, local copies, waits for them, and re-layouts, per_device(): jnp.einsum('kxy,kjyz->kjxz', blocks, fetched, preferred_element_type=jnp....  8.72 us
    dot_general x1, matrix products, per_device(): jnp.einsum('kt,kjxz->tjxz', placing_rows, products, precision=lax.Precisi...  7.37 us
    dot_general x1, matrix products, per_device(): jnp.einsum('kxy,kjyz->kjxz', blocks, fetched, preferred_element_type=jnp....  6.71 us
    ppermute x4, starting transfers between devices, padded_2(): lax.ppermute(head, axis, [((i + 1) % count, i) for i in range(ends)])  5.17 us
    gather x1, local copies, waits for them, and re-layouts, per_device(): fetched = near_p[columns]  4.79 us
  transfers between devices with their start and end apart: 9, of which 3 were waited for; matrix products, arithmetic and copies ran while one was open for 3% of the time, Pallas kernels for 0%

commit v1 on v0

v1 whole, which is shorter than its diff:
```python
import functools
import math

import jax
import jax.numpy as jnp
from jax import lax
from jax.experimental import pallas as pl
from jax.experimental.pallas import tpu as pltpu
from jax.sharding import PartitionSpec as P

FB = 8
CB = 2
G2 = 2
NS = 5
PB = FB * CB
UNROLL = 4
META = 16
F32 = jnp.float32
BF16 = jnp.bfloat16

VMEM = pl.BlockSpec(memory_space=pltpu.VMEM)
SMEM = pl.BlockSpec(memory_space=pltpu.SMEM)
ANY = pl.BlockSpec(memory_space=pl.ANY)


def pack_kernel(codes, count, aggs, blocks, second, out, tile, sems):
    n_p, n_s = blocks.shape[0], second.shape[0]
    first = pltpu.make_async_copy(blocks, out.at[0:n_p], sems.at[0])
    first.start()
    after = pltpu.make_async_copy(second, out.at[n_p : n_p + n_s], sems.at[1])
    after.start()
    slots = codes.shape[0]
    lane = lax.broadcasted_iota(jnp.int32, tile.shape, 1)
    word = jnp.zeros(tile.shape, jnp.int32)
    for k in range(slots):
        word = jnp.where(lane == k, jnp.where(k < count[0], codes[k], PB), word)
    for j in range(CB):
        word = jnp.where(lane == slots + j, aggs[j], word)
    tile[...] = word.astype(F32).astype(BF16)
    last = pltpu.make_async_copy(tile, out.at[n_p + n_s : n_p + n_s + META], sems.at[2])
    last.start()
    first.wait()
    after.wait()
    last.wait()


def main_kernel(
    slots, size, cols_n, rows, cols, count, fine, own, left, right, up, down,
    c_one, *rest,
):
    sends = rest[:cols_n]
    dense, turned, acc, lift, terms, words, codes, sem = rest[cols_n:]
    near = (own, left, right, up, down)
    tail = (slots + CB) * size
    for s in range(NS):
        word = near[s][tail : tail + META, :].astype(F32).astype(jnp.int32)
        words[s : s + 1, :] = word[0:1, :]
    fetch = pltpu.make_async_copy(words, codes, sem)
    fetch.start()
    zero = jnp.zeros((size, size), BF16)
    for s in range(NS):
        for q in range(PB):
            dense[s * (PB + 1) + q] = zero
    acc[...] = jnp.zeros_like(acc)
    fetch.wait()
    for s in range(NS):
        for k in range(slots):
            dense[s * (PB + 1) + codes[s, k]] = near[s][k * size : (k + 1) * size, :]
        for j in range(CB):
            block = near[s][(slots + j) * size : (slots + j + 1) * size, :]
            for a in range(G2):
                lift[s, j * size : (j + 1) * size, a * size : (a + 1) * size] = jnp.where(
                    codes[s, slots + j] == a, block, zero
                )
    for i in range(FB):
        for j in range(CB):
            turned[j * size : (j + 1) * size, i * size : (i + 1) * size] = dense[i * CB + j].T

    def step(t, carry):
        products, targets = [], []
        for u in range(UNROLL):
            k = t * UNROLL + u
            live = k < count[0]
            at = jnp.where(live, cols[k], 0)
            s = at // FB
            base = s * (PB + 1) + (at - s * FB) * CB
            wide = jnp.concatenate([dense[base + j] for j in range(CB)], axis=1)
            products.append(jnp.dot(fine[k], wide, preferred_element_type=F32))
            targets.append(jnp.where(live, s * FB + rows[k], NS * FB))
        for u in range(UNROLL):
            acc[targets[u]] += products[u]
        return carry

    lax.fori_loop(0, (count[0] + UNROLL - 1) // UNROLL, step, 0)

    halves = [None, None, None]
    for s in range(NS):
        product = acc[s * FB : (s + 1) * FB].reshape(FB * size, CB * size).astype(BF16)
        coarse = jnp.dot(turned[...], product, preferred_element_type=F32).astype(BF16)
        for i in range(CB):
            for j in range(CB):
                c_one[i, s, j] = coarse[i * size : (i + 1) * size, j * size : (j + 1) * size]
        part = jnp.dot(coarse, lift[s], preferred_element_type=F32)
        g = 0 if s < 3 else s - 2
        halves[g] = part if halves[g] is None else halves[g] + part
    lift_t = lift[0].T
    for g in range(3):
        terms[g * G2 * size : (g + 1) * G2 * size, :] = jnp.dot(
            lift_t, halves[g].astype(BF16), preferred_element_type=F32
        )
    chunk = terms.shape[0] // cols_n
    me = lax.axis_index("col")
    for d in range(cols_n):
        to = lax.rem(me + d, cols_n)
        part = terms[pl.ds(pl.multiple_of(to * chunk, chunk), chunk), :]
        sends[d][...] = part.astype(BF16)


def sum_kernel(*refs):
    total = refs[0][...].astype(F32)
    for ref in refs[1:-1]:
        total = total + ref[...].astype(F32)
    refs[-1][...] = total.astype(BF16)


def spread_kernel(size, cols_n, *refs):
    out = refs[-1]
    chunk = refs[0].shape[0]
    unit = math.gcd(chunk, size)
    per = size // unit
    me = lax.axis_index("col")
    for d in range(cols_n):
        owner = lax.rem(me - d + cols_n, cols_n)
        for t in range(chunk // unit):
            at = owner * (chunk // unit) + t
            g = at // (G2 * per)
            a = lax.rem(at // per, G2)
            h = pl.multiple_of(lax.rem(at, per) * unit, unit)
            for b in range(G2):
                out[a, g, b, pl.ds(h, unit), :] = refs[d][
                    t * unit : (t + 1) * unit, b * size : (b + 1) * size
                ].astype(F32)


def shift(x, axis, step, wrap):
    n = lax.axis_size(axis)
    pairs = [(i, (i + step) % n) for i in range(n) if wrap or 0 <= i + step < n]
    return lax.ppermute(x, axis, pairs)


def per_device(
    fine_blocks, fine_rows, fine_cols, fine_counts, prolong_blocks, prolong_codes,
    prolong_counts, second_blocks, second_aggs,
):
    slots, size = prolong_blocks.shape[2], prolong_blocks.shape[3]
    cols_n = lax.axis_size("col")
    packed_rows = (slots + CB) * size + META
    packed = pl.pallas_call(
        pack_kernel,
        out_shape=jax.ShapeDtypeStruct((packed_rows, size), BF16),
        in_specs=[SMEM, SMEM, SMEM, ANY, ANY],
        out_specs=ANY,
        scratch_shapes=[pltpu.VMEM((META, size), BF16), pltpu.SemaphoreType.DMA((3,))],
        name="pack",
    )(
        prolong_codes[0, 0],
        prolong_counts[0],
        second_aggs[0, 0],
        prolong_blocks.reshape(slots * size, size),
        second_blocks.reshape(CB * size, size),
    )
    left = shift(packed, "col", 1, False)
    right = shift(packed, "col", -1, False)
    up = shift(packed, "row", 1, False)
    down = shift(packed, "row", -1, False)

    chunk = 3 * G2 * size // cols_n
    piece = jax.ShapeDtypeStruct((chunk, G2 * size), BF16)
    c_one, *sends = pl.pallas_call(
        functools.partial(main_kernel, slots, size, cols_n),
        out_shape=[jax.ShapeDtypeStruct((CB, NS, CB, size, size), BF16)] + [piece] * cols_n,
        in_specs=[SMEM] * 3 + [VMEM] * 6,
        out_specs=[VMEM] * (1 + cols_n),
        scratch_shapes=[
            pltpu.VMEM((NS * (PB + 1), size, size), BF16),
            pltpu.VMEM((CB * size, FB * size), BF16),
            pltpu.VMEM((NS * FB + 1, size, CB * size), F32),
            pltpu.VMEM((NS, CB * size, G2 * size), BF16),
            pltpu.VMEM((3 * G2 * size, G2 * size), F32),
            pltpu.VMEM((8, size), jnp.int32),
            pltpu.SMEM((8, size), jnp.int32),
            pltpu.SemaphoreType.DMA,
        ],
        compiler_params=pltpu.CompilerParams(vmem_limit_bytes=40 * 1024 * 1024),
        name="products",
    )(
        fine_rows[0, 0], fine_cols[0, 0], fine_counts[0], fine_blocks[0, 0],
        packed, left, right, up, down,
    )
    parts = [sends[0]] + [shift(sends[d], "col", d, True) for d in range(1, cols_n)]
    total = pl.pallas_call(
        sum_kernel, out_shape=piece, in_specs=[VMEM] * cols_n, out_specs=VMEM, name="total"
    )(*parts)
    gathered = [total] + [shift(total, "col", d, True) for d in range(1, cols_n)]
    c_two = pl.pallas_call(
        functools.partial(spread_kernel, size, cols_n),
        out_shape=jax.ShapeDtypeStruct((G2, 3, G2, size, size), F32),
        in_specs=[VMEM] * cols_n,
        out_specs=VMEM,
        name="spread",
    )(*gathered)
    return (c_one[None, None], c_two[None])


def solution(mesh):
    in_specs = (
        P("row", "col", None, None, None),
        P("row", "col", None),
        P("row", "col", None),
        P("row", "col"),
        P("row", "col", None, None, None),
        P("row", "col", None),
        P("row", "col"),
        P("row", "col", None, None, None),
        P("row", "col", None),
    )
    out_specs = (
        P("row", "col", None, None, None, None, None),
        P("row", None, None, None, None, None),
    )
    return jax.shard_map(
        per_device, mesh=mesh, in_specs=in_specs, out_specs=out_specs, check_vma=False
    )
```

time: 174 us -> 81.9 us (0.47)
  waiting for transfers between devices: 83.1 us -> 24.4 us
  Pallas kernels: 0 us -> 25 us
  matrix products: 20.3 us -> 0 us
  local copies, waits for them, and re-layouts: 22.5 us -> 6.45 us
  between operations: 15.8 us -> 2.02 us
  starting transfers between devices: 28.4 us -> 22.8 us
  other arithmetic: 2.91 us -> 0 us
    psum x1 -> x0, waiting for transfers between devices: 41.9 us -> none  [per_device(): coarse_two = lax.psum(own_term, 'col')]
    pallas_call x0 -> x4, Pallas kernels: none -> 25 us  [the longest x1 15.7 us: per_device(): pl.pallas_call(pack_kernel, out_shape=jax.ShapeDtypeStruct((packed_rows,...]
    dot_general x8 -> x0, matrix products: 20.3 us -> none  [the longest x1 7.37 us: per_device(): jnp.einsum('kt,kjxz->tjxz', placing_rows, products, precision=lax.Precisi...]
    ppermute x8 -> x10, waiting for transfers between devices: 41.1 us -> 24.4 us  [shift(): return lax.ppermute(x, axis, pairs)]
    dot_general x1 -> x0, local copies, waits for them, and re-layouts: 8.72 us -> none  [per_device(): jnp.einsum('kxy,kjyz->kjxz', blocks, fetched, preferred_element_type=jnp....]
    ppermute x8 -> x10, starting transfers between devices: 28.3 us -> 22.8 us  [shift(): return lax.ppermute(x, axis, pairs)]
    gather x1 -> x0, local copies, waits for them, and re-layouts: 4.79 us -> none  [per_device(): fetched = near_p[columns]]
    another operation x4 -> x0, local copies, waits for them, and re-layouts: 3.59 us -> none  [source_stack(): jnp.stack([padded[1, 1], padded[1, 0], padded[1, 2], padded[0, 1], padded...]
  transfers between devices with their start and end apart: 9 -> 10, of which waited for: 3 -> 7; matrix products, arithmetic and copies ran while one was open for 3% -> 0% of each run, Pallas kernels for 0% -> 0%
where the time goes in v1:
time: 81.9 us; the launch traced here: 80.7 us
  Pallas kernels  25 us (31%)
  waiting for transfers between devices  24.4 us (30%)
  starting transfers between devices  22.8 us (28%)
  local copies, waits for them, and re-layouts  6.45 us (8%)
  between operations  2.02 us (2%)
    ppermute x10, waiting for transfers between devices, shift(): return lax.ppermute(x, axis, pairs)  24.4 us
    ppermute x10, starting transfers between devices, shift(): return lax.ppermute(x, axis, pairs)  22.8 us
    pallas_call x1, Pallas kernels, per_device(): pl.pallas_call(pack_kernel, out_shape=jax.ShapeDtypeStruct((packed_rows,...  15.7 us
    unnamed x22, local copies, waits for them, and re-layouts  6.45 us
    pallas_call x1, Pallas kernels, per_device(): pl.pallas_call(functools.partial(main_kernel, slots, size, cols_n), out_s...  5.52 us
    pallas_call x1, Pallas kernels, per_device(): pl.pallas_call(functools.partial(spread_kernel, size, cols_n), out_shape=...  2.09 us
    pallas_call x1, Pallas kernels, per_device(): pl.pallas_call(sum_kernel, out_shape=piece, in_specs=[VMEM] * cols_n, out...  1.73 us
  transfers between devices with their start and end apart: 10, of which 7 were waited for; matrix products, arithmetic and copies ran while one was open for 0% of the time, Pallas kernels for 0%

profile of v1, /device:TPU:0, one launch (start us, length us, event | category | flops | bytes accessed | tf_op | source)
XLA Modules:
  0.0 80.7 jit_solution(25633249423744923)
XLA Ops:
  1.3 15.7 %pack.1.own = bf16[1808,128]{1,0:T(8,128)(2,1)} custom-call(s32[12]{0:T(128)} %bitcast.19, s32[1]{0:T(128)} %bitcast.12.count, s32[2]{0:T(128)} %bitcast.20, bf16[1536,128]{1,0:T(8,128)(2,1)} %bitcast.17, bf16[256,128]{1,0:T(8,128)(2,1)} %bitcast.18), custom_call_target="tpu_custom_call" | custom-call | tf_op jit(solution)/shard_map/pack/pallas_call | solution.py:158
  17.0 1.3 %collective-permute-start.3 = (bf16[1808,128]{1,0:T(8,128)(2,1)}, bf16[1808,128]{1,0:T(8,128)(2,1)S(1)}, u32[]{:S(2)}, u32[]{:S(2)}) collective-permute-start(bf16[1808,128]{1,0:T(8,128)(2,1)} %pack.1.own), channel_id=1, source_target_pairs={{4,0},{8,4},{12,8},{16,12},{20,16},{24,20},{28,24},{5,1},{9,5},{13... | collective-permute-start | bytes 1388552 | tf_op jit(solution)/shard_map/ppermute | solution.py:148
  18.3 3.1 %collective-permute-start.2 = (bf16[1808,128]{1,0:T(8,128)(2,1)}, bf16[1808,128]{1,0:T(8,128)(2,1)S(1)}, u32[]{:S(2)}, u32[]{:S(2)}) collective-permute-start(bf16[1808,128]{1,0:T(8,128)(2,1)} %pack.1.own), channel_id=1, source_target_pairs={{0,4},{4,8},{8,12},{12,16},{16,20},{20,24},{24,28},{1,5},{5,9},{9,... | collective-permute-start | bytes 1388552 | tf_op jit(solution)/shard_map/ppermute | solution.py:148
  21.3 1.3 %collective-permute-start.1 = (bf16[1808,128]{1,0:T(8,128)(2,1)}, bf16[1808,128]{1,0:T(8,128)(2,1)S(1)}, u32[]{:S(2)}, u32[]{:S(2)}) collective-permute-start(bf16[1808,128]{1,0:T(8,128)(2,1)} %pack.1.own), channel_id=1, source_target_pairs={{1,0},{2,1},{3,2},{5,4},{6,5},{7,6},{9,8},{10,9},{11,10},{13,12},{... | collective-permute-start | bytes 1388552 | tf_op jit(solution)/shard_map/ppermute | solution.py:148
  22.6 5.6 %collective-permute-start = (bf16[1808,128]{1,0:T(8,128)(2,1)}, bf16[1808,128]{1,0:T(8,128)(2,1)S(1)}, u32[]{:S(2)}, u32[]{:S(2)}) collective-permute-start(bf16[1808,128]{1,0:T(8,128)(2,1)} %pack.1.own), channel_id=1, source_target_pairs={{0,1},{1,2},{2,3},{4,5},{5,6},{6,7},{8,9},{9,10},{10,11},{12,13},{... | collective-permute-start | bytes 1388552 | tf_op jit(solution)/shard_map/ppermute | solution.py:148
  28.9 0.0 collective-permute-done.3.down
  28.9 0.0 collective-permute-done.2.up
  28.9 8.5 %collective-permute-done.1.right = bf16[1808,128]{1,0:T(8,128)(2,1)S(1)} collective-permute-done((bf16[1808,128]{1,0:T(8,128)(2,1)}, bf16[1808,128]{1,0:T(8,128)(2,1)S(1)}, u32[]{:S(2)}, u32[]{:S(2)}) %collective-permute-start.1) | collective-permute-done | bytes 462880 | tf_op jit(solution)/shard_map/ppermute | solution.py:148
  37.5 1.8 %collective-permute-done.left = bf16[1808,128]{1,0:T(8,128)(2,1)S(1)} collective-permute-done((bf16[1808,128]{1,0:T(8,128)(2,1)}, bf16[1808,128]{1,0:T(8,128)(2,1)S(1)}, u32[]{:S(2)}, u32[]{:S(2)}) %collective-permute-start) | collective-permute-done | bytes 462880 | tf_op jit(solution)/shard_map/ppermute | solution.py:148
  39.2 0.0 copy-start
  39.2 1.6 %copy-done = bf16[1,1,64,128,128]{4,3,2,1,0:T(8,128)(2,1)S(1)} copy-done((bf16[1,1,64,128,128]{4,3,2,1,0:T(8,128)(2,1)S(1)}, bf16[1,1,64,128,128]{4,3,2,1,0:T(8,128)(2,1)}, u32[]{:S(2)}) %copy-start) | copy-done | bytes 2097176
  40.8 0.0 copy-start.1
  40.8 1.0 %copy-done.1 = bf16[1808,128]{1,0:T(8,128)(2,1)S(1)} copy-done((bf16[1808,128]{1,0:T(8,128)(2,1)S(1)}, bf16[1808,128]{1,0:T(8,128)(2,1)}, u32[]{:S(2)}) %copy-start.1) | copy-done | bytes 462872
  41.8 0.0 copy-start.3
  41.8 0.7 copy-done.3
  42.5 0.0 copy-start.4
  42.5 0.7 copy-done.4
  43.2 5.5 %products.1 = (bf16[2,5,2,128,128]{4,3,2,1,0:T(8,128)(2,1)}, bf16[192,256]{1,0:T(8,128)(2,1)S(1)}, bf16[192,256]{1,0:T(8,128)(2,1)S(1)}, bf16[192,256]{1,0:T(8,128)(2,1)S(1)}, bf16[192,256]{1,0:T(8,128)(2,1)S(1)}) custom-call(s32[64]{0:T(128)S(1)} %bitcast.14, s32[64]{0:T(128)S(1)} %bitcast.15, s32[1]{0:T(128)} %bitcast.11.count, ...), custom_call_target="tpu_custom_call" | custom-call | tf_op jit(solution)/shard_map/products/pallas_call | solution.py:179
  48.7 0.0 copy-start.2
  48.7 0.6 copy-done.2
  49.3 2.6 %collective-permute-start.4 = (bf16[192,256]{1,0:T(8,128)(2,1)S(1)}, bf16[192,256]{1,0:T(8,128)(2,1)S(1)}, u32[]{:S(2)}, u32[]{:S(2)}) collective-permute-start(bf16[192,256]{1,0:T(8,128)(2,1)S(1)} %get-tuple-element.9), channel_id=1, source_target_pairs={{0,1},{1,2},{2,3},{3,0},{4,5},{5,6},{6,7},{7,4},{8,9},{9,10},{10,1... | collective-permute-start | bytes 294920 | tf_op jit(solution)/shard_map/ppermute | solution.py:148
  51.9 5.8 %collective-permute-start.5 = (bf16[192,256]{1,0:T(8,128)(2,1)S(1)}, bf16[192,256]{1,0:T(8,128)(2,1)S(1)}, u32[]{:S(2)}, u32[]{:S(2)}) collective-permute-start(bf16[192,256]{1,0:T(8,128)(2,1)S(1)} %get-tuple-element.10), channel_id=1, source_target_pairs={{0,2},{1,3},{2,0},{3,1},{4,6},{5,7},{6,4},{7,5},{8,10},{9,11},{10,... | collective-permute-start | bytes 294920 | tf_op jit(solution)/shard_map/ppermute | solution.py:148
  57.7 0.0 collective-permute-start.6
  57.7 2.6 %collective-permute-done.4.refs_1_ = bf16[192,256]{1,0:T(8,128)(2,1)S(1)} collective-permute-done((bf16[192,256]{1,0:T(8,128)(2,1)S(1)}, bf16[192,256]{1,0:T(8,128)(2,1)S(1)}, u32[]{:S(2)}, u32[]{:S(2)}) %collective-permute-start.4) | collective-permute-done | bytes 98336 | tf_op jit(solution)/shard_map/ppermute | solution.py:148
  60.4 0.0 copy-start.8
  60.4 2.9 %collective-permute-done.5.refs_2_ = bf16[192,256]{1,0:T(8,128)(2,1)S(1)} collective-permute-done((bf16[192,256]{1,0:T(8,128)(2,1)S(1)}, bf16[192,256]{1,0:T(8,128)(2,1)S(1)}, u32[]{:S(2)}, u32[]{:S(2)}) %collective-permute-start.5) | collective-permute-done | bytes 98336 | tf_op jit(solution)/shard_map/ppermute | solution.py:148
  63.3 0.0 copy-start.9
  63.3 0.1 collective-permute-done.6.refs_3_
  63.4 0.0 copy-start.10
  63.4 0.0 copy-done.8
  63.4 0.5 copy-done.9
  63.9 0.1 copy-done.10
  64.0 1.7 %total.1.refs_0_ = bf16[192,256]{1,0:T(8,128)(2,1)} custom-call(bf16[192,256]{1,0:T(8,128)(2,1)} %copy-done.2, bf16[192,256]{1,0:T(8,128)(2,1)} %copy-done.8, bf16[192,256]{1,0:T(8,128)(2,1)} %copy-done.9, bf16[192,256]{1,0:T(8,128)(2,1)} %copy-done.10), custom_call_target="tpu_custom_call" | custom-call | tf_op jit(solution)/shard_map/total/pallas_call | solution.py:201
  65.8 2.0 %collective-permute-start.9 = (bf16[192,256]{1,0:T(8,128)(2,1)}, bf16[192,256]{1,0:T(8,128)(2,1)S(1)}, u32[]{:S(2)}, u32[]{:S(2)}) collective-permute-start(bf16[192,256]{1,0:T(8,128)(2,1)} %total.1.refs_0_), channel_id=1, source_target_pairs={{0,3},{1,0},{2,1},{3,2},{4,7},{5,4},{6,5},{7,6},{8,11},{9,8},{10,9... | collective-permute-start | bytes 294920 | tf_op jit(solution)/shard_map/ppermute | solution.py:148
  67.8 1.1 %collective-permute-start.8 = (bf16[192,256]{1,0:T(8,128)(2,1)}, bf16[192,256]{1,0:T(8,128)(2,1)S(1)}, u32[]{:S(2)}, u32[]{:S(2)}) collective-permute-start(bf16[192,256]{1,0:T(8,128)(2,1)} %total.1.refs_0_), channel_id=1, source_target_pairs={{0,2},{1,3},{2,0},{3,1},{4,6},{5,7},{6,4},{7,5},{8,10},{9,11},{10,... | collective-permute-start | bytes 294920 | tf_op jit(solution)/shard_map/ppermute | solution.py:148
  68.9 0.0 collective-permute-start.7
  68.9 2.4 %collective-permute-done.9.refs_3_ = bf16[192,256]{1,0:T(8,128)(2,1)S(1)} collective-permute-done((bf16[192,256]{1,0:T(8,128)(2,1)}, bf16[192,256]{1,0:T(8,128)(2,1)S(1)}, u32[]{:S(2)}, u32[]{:S(2)}) %collective-permute-start.9) | collective-permute-done | bytes 98336 | tf_op jit(solution)/shard_map/ppermute | solution.py:148
  71.3 0.0 copy-start.5
  71.3 6.0 %collective-permute-done.8.refs_2_ = bf16[192,256]{1,0:T(8,128)(2,1)S(1)} collective-permute-done((bf16[192,256]{1,0:T(8,128)(2,1)}, bf16[192,256]{1,0:T(8,128)(2,1)S(1)}, u32[]{:S(2)}, u32[]{:S(2)}) %collective-permute-start.8) | collective-permute-done | bytes 98336 | tf_op jit(solution)/shard_map/ppermute | solution.py:148
  77.3 0.0 copy-start.6
  77.3 0.0 collective-permute-done.7.refs_1_
  77.3 0.0 copy-done.5
  77.3 0.6 copy-done.6
  78.0 0.0 copy-start.7
  78.0 0.6 copy-done.7
  78.6 2.1 %spread.1 = f32[2,3,2,128,128]{4,3,2,1,0:T(8,128)} custom-call(bf16[192,256]{1,0:T(8,128)(2,1)} %total.1.refs_0_, bf16[192,256]{1,0:T(8,128)(2,1)} %copy-done.7, bf16[192,256]{1,0:T(8,128)(2,1)} %copy-done.6, bf16[192,256]{1,0:T(8,128)(2,1)} %copy-done.5), custom_call_target="tpu_custom_call" | custom-call | tf_op jit(solution)/shard_map/spread/pallas_call | solution.py:205
Async XLA Ops:
  17.0 11.9 %collective-permute-start.3 = (bf16[1808,128]{1,0:T(8,128)(2,1)}, bf16[1808,128]{1,0:T(8,128)(2,1)S(1)}, u32[]{:S(2)}, u32[]{:S(2)}) collective-permute-start(bf16[1808,128]{1,0:T(8,128)(2,1)} %pack.1.own), channel_id=1, source_target_pairs={{4,0},{8,4},{12,8},{16,12},{20,16},{24,20},{28,24},{5,1},{9,5},{13... | collective-permute-start | bytes 1388552 | tf_op jit(solution)/shard_map/ppermute | solution.py:148
  18.3 10.6 %collective-permute-start.2 = (bf16[1808,128]{1,0:T(8,128)(2,1)}, bf16[1808,128]{1,0:T(8,128)(2,1)S(1)}, u32[]{:S(2)}, u32[]{:S(2)}) collective-permute-start(bf16[1808,128]{1,0:T(8,128)(2,1)} %pack.1.own), channel_id=1, source_target_pairs={{0,4},{4,8},{8,12},{12,16},{16,20},{20,24},{24,28},{1,5},{5,9},{9,... | collective-permute-start | bytes 1388552 | tf_op jit(solution)/shard_map/ppermute | solution.py:148
  21.3 16.1 %collective-permute-start.1 = (bf16[1808,128]{1,0:T(8,128)(2,1)}, bf16[1808,128]{1,0:T(8,128)(2,1)S(1)}, u32[]{:S(2)}, u32[]{:S(2)}) collective-permute-start(bf16[1808,128]{1,0:T(8,128)(2,1)} %pack.1.own), channel_id=1, source_target_pairs={{1,0},{2,1},{3,2},{5,4},{6,5},{7,6},{9,8},{10,9},{11,10},{13,12},{... | collective-permute-start | bytes 1388552 | tf_op jit(solution)/shard_map/ppermute | solution.py:148
  22.6 16.6 %collective-permute-start = (bf16[1808,128]{1,0:T(8,128)(2,1)}, bf16[1808,128]{1,0:T(8,128)(2,1)S(1)}, u32[]{:S(2)}, u32[]{:S(2)}) collective-permute-start(bf16[1808,128]{1,0:T(8,128)(2,1)} %pack.1.own), channel_id=1, source_target_pairs={{0,1},{1,2},{2,3},{4,5},{5,6},{6,7},{8,9},{9,10},{10,11},{12,13},{... | collective-permute-start | bytes 1388552 | tf_op jit(solution)/shard_map/ppermute | solution.py:148
  39.2 1.6 %copy-start = (bf16[1,1,64,128,128]{4,3,2,1,0:T(8,128)(2,1)S(1)}, bf16[1,1,64,128,128]{4,3,2,1,0:T(8,128)(2,1)}, u32[]{:S(2)}) copy-start(bf16[1,1,64,128,128]{4,3,2,1,0:T(8,128)(2,1)} %param.9) | copy-start | bytes 6291460
  40.8 1.0 %copy-start.1 = (bf16[1808,128]{1,0:T(8,128)(2,1)S(1)}, bf16[1808,128]{1,0:T(8,128)(2,1)}, u32[]{:S(2)}) copy-start(bf16[1808,128]{1,0:T(8,128)(2,1)} %pack.1.own) | copy-start | bytes 1388548
  41.8 0.7 copy-start.3
  42.5 0.7 copy-start.4
  48.7 0.6 copy-start.2
  49.3 11.0 %collective-permute-start.4 = (bf16[192,256]{1,0:T(8,128)(2,1)S(1)}, bf16[192,256]{1,0:T(8,128)(2,1)S(1)}, u32[]{:S(2)}, u32[]{:S(2)}) collective-permute-start(bf16[192,256]{1,0:T(8,128)(2,1)S(1)} %get-tuple-element.9), channel_id=1, source_target_pairs={{0,1},{1,2},{2,3},{3,0},{4,5},{5,6},{6,7},{7,4},{8,9},{9,10},{10,1... | collective-permute-start | bytes 294920 | tf_op jit(solution)/shard_map/ppermute | solution.py:148
  51.9 11.4 %collective-permute-start.5 = (bf16[192,256]{1,0:T(8,128)(2,1)S(1)}, bf16[192,256]{1,0:T(8,128)(2,1)S(1)}, u32[]{:S(2)}, u32[]{:S(2)}) collective-permute-start(bf16[192,256]{1,0:T(8,128)(2,1)S(1)} %get-tuple-element.10), channel_id=1, source_target_pairs={{0,2},{1,3},{2,0},{3,1},{4,6},{5,7},{6,4},{7,5},{8,10},{9,11},{10,... | collective-permute-start | bytes 294920 | tf_op jit(solution)/shard_map/ppermute | solution.py:148
  57.7 5.7 %collective-permute-start.6 = (bf16[192,256]{1,0:T(8,128)(2,1)S(1)}, bf16[192,256]{1,0:T(8,128)(2,1)S(1)}, u32[]{:S(2)}, u32[]{:S(2)}) collective-permute-start(bf16[192,256]{1,0:T(8,128)(2,1)S(1)} %get-tuple-element.11), channel_id=1, source_target_pairs={{0,3},{1,0},{2,1},{3,2},{4,7},{5,4},{6,5},{7,6},{8,11},{9,8},{10,9... | collective-permute-start | bytes 294920 | tf_op jit(solution)/shard_map/ppermute | solution.py:148
  60.4 3.0 %copy-start.8 = (bf16[192,256]{1,0:T(8,128)(2,1)}, bf16[192,256]{1,0:T(8,128)(2,1)S(1)}, u32[]{:S(2)}) copy-start(bf16[192,256]{1,0:T(8,128)(2,1)S(1)} %collective-permute-done.4.refs_1_) | copy-start | bytes 294916
  63.3 0.6 copy-start.9
  63.4 0.6 copy-start.10
  65.8 5.6 %collective-permute-start.9 = (bf16[192,256]{1,0:T(8,128)(2,1)}, bf16[192,256]{1,0:T(8,128)(2,1)S(1)}, u32[]{:S(2)}, u32[]{:S(2)}) collective-permute-start(bf16[192,256]{1,0:T(8,128)(2,1)} %total.1.refs_0_), channel_id=1, source_target_pairs={{0,3},{1,0},{2,1},{3,2},{4,7},{5,4},{6,5},{7,6},{8,11},{9,8},{10,9... | collective-permute-start | bytes 294920 | tf_op jit(solution)/shard_map/ppermute | solution.py:148
  67.8 9.5 %collective-permute-start.8 = (bf16[192,256]{1,0:T(8,128)(2,1)}, bf16[192,256]{1,0:T(8,128)(2,1)S(1)}, u32[]{:S(2)}, u32[]{:S(2)}) collective-permute-start(bf16[192,256]{1,0:T(8,128)(2,1)} %total.1.refs_0_), channel_id=1, source_target_pairs={{0,2},{1,3},{2,0},{3,1},{4,6},{5,7},{6,4},{7,5},{8,10},{9,11},{10,... | collective-permute-start | bytes 294920 | tf_op jit(solution)/shard_map/ppermute | solution.py:148
  68.9 8.4 %collective-permute-start.7 = (bf16[192,256]{1,0:T(8,128)(2,1)}, bf16[192,256]{1,0:T(8,128)(2,1)S(1)}, u32[]{:S(2)}, u32[]{:S(2)}) collective-permute-start(bf16[192,256]{1,0:T(8,128)(2,1)} %total.1.refs_0_), channel_id=1, source_target_pairs={{0,1},{1,2},{2,3},{3,0},{4,5},{5,6},{6,7},{7,4},{8,9},{9,10},{10,1... | collective-permute-start | bytes 294920 | tf_op jit(solution)/shard_map/ppermute | solution.py:148
  71.3 6.0 %copy-start.5 = (bf16[192,256]{1,0:T(8,128)(2,1)}, bf16[192,256]{1,0:T(8,128)(2,1)S(1)}, u32[]{:S(2)}) copy-start(bf16[192,256]{1,0:T(8,128)(2,1)S(1)} %collective-permute-done.9.refs_3_) | copy-start | bytes 294916
  77.3 0.6 copy-start.6
  78.0 0.6 copy-start.7

commit v2 on v1

v2 whole, which is shorter than its diff:
```python
import functools
import math

import jax
import jax.numpy as jnp
from jax import lax
from jax.experimental import pallas as pl
from jax.experimental.pallas import tpu as pltpu
from jax.sharding import PartitionSpec as P

FB = 8
CB = 2
G2 = 2
NS = 5
PB = FB * CB
UNROLL = 4
META = 16
F32 = jnp.float32
BF16 = jnp.bfloat16

VMEM = pl.BlockSpec(memory_space=pltpu.VMEM)
SMEM = pl.BlockSpec(memory_space=pltpu.SMEM)
SMALL = pltpu.CompilerParams(vmem_limit_bytes=4 * 1024 * 1024)
LARGE = pltpu.CompilerParams(vmem_limit_bytes=20 * 1024 * 1024)


def pack_kernel(codes, count, aggs, blocks, second, out):
    n_p, n_s = blocks.shape[0], second.shape[0]
    slots = codes.shape[0]
    out[0:n_p, :] = blocks[...]
    out[n_p : n_p + n_s, :] = second[...]
    lane = lax.broadcasted_iota(jnp.int32, (META, out.shape[1]), 1)
    word = jnp.zeros(lane.shape, jnp.int32)
    for k in range(slots):
        word = jnp.where(lane == k, jnp.where(k < count[0], codes[k], PB), word)
    for j in range(CB):
        word = jnp.where(lane == slots + j, aggs[j], word)
    out[n_p + n_s : n_p + n_s + META, :] = word.astype(F32).astype(BF16)


def slot_products(s, size, table, rows, cols, order, begin, end, fine, near, acc, base):
    def step(t, carry):
        products, targets = [], []
        for u in range(UNROLL):
            at = begin + t * UNROLL + u
            live = at < end
            k = order[jnp.minimum(at, end - 1)]
            m = cols[k] - s * FB
            parts = []
            for j in range(CB):
                slot = table[s, m * CB + j]
                first = pl.multiple_of(jnp.maximum(slot, 0) * size, size)
                block = near[pl.ds(first, size), :]
                parts.append(jnp.where(slot >= 0, block, jnp.zeros_like(block)))
            wide = jnp.concatenate(parts, axis=1)
            products.append(jnp.dot(fine[k], wide, preferred_element_type=F32))
            targets.append(jnp.where(live, base + rows[k], acc.shape[0] - 1))
        for u in range(UNROLL):
            acc[targets[u]] += products[u]
        return carry

    lax.fori_loop(0, (end - begin + UNROLL - 1) // UNROLL, step, 0)


def fill_table(s, slots, table, code_of):
    for q in range(PB + 1):
        table[s, q] = -1
    for k in range(slots):
        table[s, code_of(k)] = k


def lift_of(near, slots, size, agg_of):
    lines = []
    for j in range(CB):
        block = near[(slots + j) * size : (slots + j + 1) * size, :]
        lines.append(
            jnp.concatenate(
                [jnp.where(agg_of(j) == a, block, jnp.zeros_like(block)) for a in range(G2)],
                axis=1,
            )
        )
    return jnp.concatenate(lines, axis=0)


def coarse_of(turned, acc, base, size):
    product = acc[base : base + FB].reshape(FB * size, CB * size).astype(BF16)
    return jnp.dot(turned, product, preferred_element_type=F32).astype(BF16)


def own_kernel(
    slots, size, rows, cols, count, codes, p_count, aggs, fine, own,
    turned, coarse, half, lift_t, order, bounds, acc, table, fill,
):
    total = order.shape[0]
    for s in range(NS):
        fill[s] = 0

    def tally(k, carry):
        s = cols[k] // FB
        fill[s] += 1
        return carry

    lax.fori_loop(0, count[0], tally, 0)
    at = jnp.int32(0)
    for s in range(NS):
        n = fill[s]
        bounds[s] = at
        fill[s] = at
        at = at + n
    bounds[NS] = at

    def place(k, carry):
        s = cols[k] // FB
        order[fill[s]] = k
        fill[s] += 1
        return carry

    lax.fori_loop(0, count[0], place, 0)
    fill_table(0, slots, table, lambda k: jnp.where(k < p_count[0], codes[k], PB))
    for i in range(FB):
        for j in range(CB):
            slot = table[0, i * CB + j]
            block = own[pl.ds(pl.multiple_of(jnp.maximum(slot, 0) * size, size), size), :]
            block = jnp.where(slot >= 0, block, jnp.zeros_like(block))
            turned[j * size : (j + 1) * size, i * size : (i + 1) * size] = block.T
    acc[...] = jnp.zeros_like(acc)
    slot_products(0, size, table, rows, cols, order, 0, bounds[1], fine, own, acc, 0)
    coarse[...] = coarse_of(turned[...], acc, 0, size)
    lift = lift_of(own, slots, size, lambda j: aggs[j])
    half[...] = jnp.dot(coarse[...], lift, preferred_element_type=F32)
    lift_t[...] = lift.T


def near_kernel(
    slots, size, cols_n, rows, cols, order, bounds, fine, turned, coarse0, half0, lift_t,
    left, right, up, down, c_one, *rest,
):
    sends = rest[:cols_n]
    acc, terms, words, codes, table, sem = rest[cols_n:]
    near = (None, left, right, up, down)
    tail = (slots + CB) * size
    for s in range(1, NS):
        word = near[s][tail : tail + META, :].astype(F32).astype(jnp.int32)
        words[s : s + 1, :] = word[0:1, :]
    fetch = pltpu.make_async_copy(words, codes, sem)
    fetch.start()
    acc[...] = jnp.zeros_like(acc)
    fetch.wait()
    halves = [half0[...], None, None]
    for s in range(NS):
        if s == 0:
            coarse = coarse0[...]
        else:
            fill_table(s, slots, table, lambda k: codes[s, k])
            base = (s - 1) * FB
            slot_products(
                s, size, table, rows, cols, order, bounds[s], bounds[s + 1], fine, near[s], acc, base
            )
            coarse = coarse_of(turned[...], acc, base, size)
            lift = lift_of(near[s], slots, size, lambda j: codes[s, slots + j])
            part = jnp.dot(coarse, lift, preferred_element_type=F32)
            g = 0 if s < 3 else s - 2
            halves[g] = part if halves[g] is None else halves[g] + part
        for i in range(CB):
            for j in range(CB):
                c_one[i, s, j] = coarse[i * size : (i + 1) * size, j * size : (j + 1) * size]
    for g in range(3):
        terms[g * G2 * size : (g + 1) * G2 * size, :] = jnp.dot(
            lift_t[...], halves[g].astype(BF16), preferred_element_type=F32
        )
    chunk = terms.shape[0] // cols_n
    me = lax.axis_index("col")
    for d in range(cols_n):
        to = lax.rem(me + d, cols_n)
        part = terms[pl.ds(pl.multiple_of(to * chunk, chunk), chunk), :]
        sends[d][...] = part.astype(BF16)


def sum_kernel(*refs):
    total = refs[0][...].astype(F32)
    for ref in refs[1:-1]:
        total = total + ref[...].astype(F32)
    refs[-1][...] = total.astype(BF16)


def spread_kernel(size, cols_n, *refs):
    out = refs[-1]
    chunk = refs[0].shape[0]
    unit = math.gcd(chunk, size)
    per = size // unit
    me = lax.axis_index("col")
    for d in range(cols_n):
        owner = lax.rem(me - d + cols_n, cols_n)
        for t in range(chunk // unit):
            at = owner * (chunk // unit) + t
            g = at // (G2 * per)
            a = lax.rem(at // per, G2)
            h = pl.multiple_of(lax.rem(at, per) * unit, unit)
            for b in range(G2):
                out[a, g, b, pl.ds(h, unit), :] = refs[d][
                    t * unit : (t + 1) * unit, b * size : (b + 1) * size
                ].astype(F32)


def shift(x, axis, step, wrap):
    n = lax.axis_size(axis)
    pairs = [(i, (i + step) % n) for i in range(n) if wrap or 0 <= i + step < n]
    return lax.ppermute(x, axis, pairs)


def per_device(
    fine_blocks, fine_rows, fine_cols, fine_counts, prolong_blocks, prolong_codes,
    prolong_counts, second_blocks, second_aggs,
):
    slots, size = prolong_blocks.shape[2], prolong_blocks.shape[3]
    cols_n = lax.axis_size("col")
    packed_rows = (slots + CB) * size + META
    grid_slots = fine_blocks.shape[2]
    wide = CB * size
    packed = pl.pallas_call(
        pack_kernel,
        out_shape=jax.ShapeDtypeStruct((packed_rows, size), BF16),
        in_specs=[SMEM] * 3 + [VMEM] * 2,
        out_specs=VMEM,
        compiler_params=SMALL,
        name="pack",
    )(
        prolong_codes[0, 0],
        prolong_counts[0],
        second_aggs[0, 0],
        prolong_blocks.reshape(slots * size, size),
        second_blocks.reshape(CB * size, size),
    )
    up = shift(packed, "row", 1, False)
    down = shift(packed, "row", -1, False)
    left = shift(packed, "col", 1, False)
    right = shift(packed, "col", -1, False)

    turned, coarse0, half0, lift_t, order, bounds = pl.pallas_call(
        functools.partial(own_kernel, slots, size),
        out_shape=[
            jax.ShapeDtypeStruct((wide, FB * size), BF16),
            jax.ShapeDtypeStruct((wide, wide), BF16),
            jax.ShapeDtypeStruct((wide, G2 * size), F32),
            jax.ShapeDtypeStruct((G2 * size, wide), BF16),
            jax.ShapeDtypeStruct((grid_slots,), jnp.int32),
            jax.ShapeDtypeStruct((8,), jnp.int32),
        ],
        in_specs=[SMEM] * 6 + [VMEM] * 2,
        out_specs=[VMEM] * 4 + [SMEM] * 2,
        scratch_shapes=[
            pltpu.VMEM((FB + 1, size, wide), F32),
            pltpu.SMEM((NS, PB + 1), jnp.int32),
            pltpu.SMEM((8,), jnp.int32),
        ],
        compiler_params=LARGE,
        cost_estimate=pl.CostEstimate(flops=10**9, bytes_accessed=4 * 10**6, transcendentals=0),
        name="own_source",
    )(
        fine_rows[0, 0], fine_cols[0, 0], fine_counts[0],
        prolong_codes[0, 0], prolong_counts[0], second_aggs[0, 0],
        fine_blocks[0, 0], packed,
    )

    chunk = 3 * G2 * size // cols_n
    piece = jax.ShapeDtypeStruct((chunk, G2 * size), BF16)
    c_one, *sends = pl.pallas_call(
        functools.partial(near_kernel, slots, size, cols_n),
        out_shape=[jax.ShapeDtypeStruct((CB, NS, CB, size, size), BF16)] + [piece] * cols_n,
        in_specs=[SMEM] * 4 + [VMEM] * 9,
        out_specs=[VMEM] * (1 + cols_n),
        scratch_shapes=[
            pltpu.VMEM(((NS - 1) * FB + 1, size, wide), F32),
            pltpu.VMEM((3 * G2 * size, G2 * size), F32),
            pltpu.VMEM((8, size), jnp.int32),
            pltpu.SMEM((8, size), jnp.int32),
            pltpu.SMEM((NS, PB + 1), jnp.int32),
            pltpu.SemaphoreType.DMA,
        ],
        compiler_params=LARGE,
        name="near_sources",
    )(
        fine_rows[0, 0], fine_cols[0, 0], order, bounds, fine_blocks[0, 0],
        turned, coarse0, half0, lift_t, left, right, up, down,
    )
    parts = [sends[0]] + [shift(sends[d], "col", d, True) for d in range(1, cols_n)]
    total = pl.pallas_call(
        sum_kernel, out_shape=piece, in_specs=[VMEM] * cols_n, out_specs=VMEM,
        compiler_params=SMALL, name="total"
    )(*parts)
    gathered = [total] + [shift(total, "col", d, True) for d in range(1, cols_n)]
    c_two = pl.pallas_call(
        functools.partial(spread_kernel, size, cols_n),
        out_shape=jax.ShapeDtypeStruct((G2, 3, G2, size, size), F32),
        in_specs=[VMEM] * cols_n,
        out_specs=VMEM,
        compiler_params=SMALL,
        name="spread",
    )(*gathered)
    return (c_one[None, None], c_two[None])


def solution(mesh):
    in_specs = (
        P("row", "col", None, None, None),
        P("row", "col", None),
        P("row", "col", None),
        P("row", "col"),
        P("row", "col", None, None, None),
        P("row", "col", None),
        P("row", "col"),
        P("row", "col", None, None, None),
        P("row", "col", None),
    )
    out_specs = (
        P("row", "col", None, None, None, None, None),
        P("row", None, None, None, None, None),
    )
    return jax.shard_map(
        per_device, mesh=mesh, in_specs=in_specs, out_specs=out_specs, check_vma=False
    )
```

time: 81.9 us -> 58.5 us (0.71)
  Pallas kernels: 25 us -> 10.1 us
  waiting for transfers between devices: 24.4 us -> 14.3 us
  starting transfers between devices: 22.8 us -> 24.2 us
  local copies, waits for them, and re-layouts: 6.45 us -> 7.35 us
    pallas_call x1, Pallas kernels: 15.7 us -> 0.57 us  [per_device(): pl.pallas_call(pack_kernel, out_shape=jax.ShapeDtypeStruct((packed_rows,...]
    ppermute x10, waiting for transfers between devices: 24.4 us -> 14.3 us  [shift(): return lax.ppermute(x, axis, pairs)]
    pallas_call x1 -> x2, Pallas kernels: 5.52 us -> 8.42 us  [the longest x1 5.93 us: per_device(): pl.pallas_call(functools.partial(near_kernel, slots, size, cols_n), out_s...]
    pallas_call x1, Pallas kernels: 1.73 us -> 0.05 us  [per_device(): pl.pallas_call(sum_kernel, out_shape=piece, in_specs=[VMEM] * cols_n, out...]
    ppermute x10, starting transfers between devices: 22.8 us -> 24.2 us  [shift(): return lax.ppermute(x, axis, pairs)]
    pallas_call x1, Pallas kernels: 2.09 us -> 1.06 us  [per_device(): pl.pallas_call(functools.partial(spread_kernel, size, cols_n), out_shape=...]
    unnamed x22 -> x20, local copies, waits for them, and re-layouts: 6.45 us -> 7.35 us
  transfers between devices with their start and end apart: 10 -> 10, of which waited for: 7 -> 5; matrix products, arithmetic and copies ran while one was open for 0% -> 0% of each run, Pallas kernels for 0% -> 4%
where the time goes in v2:
time: 58.5 us; the launch traced here: 58 us
  starting transfers between devices  24.2 us (41%)
  waiting for transfers between devices  14.3 us (24%)
  Pallas kernels  10.1 us (17%)
  local copies, waits for them, and re-layouts  7.35 us (13%)
  between operations  2.03 us (3%)
    ppermute x10, starting transfers between devices, shift(): return lax.ppermute(x, axis, pairs)  24.2 us
    ppermute x10, waiting for transfers between devices, shift(): return lax.ppermute(x, axis, pairs)  14.3 us
    unnamed x20, local copies, waits for them, and re-layouts  7.35 us
    pallas_call x1, Pallas kernels, per_device(): pl.pallas_call(functools.partial(near_kernel, slots, size, cols_n), out_s...  5.93 us
    pallas_call x1, Pallas kernels, per_device(): pl.pallas_call(functools.partial(own_kernel, slots, size), out_shape=[jax...  2.49 us
  transfers between devices with their start and end apart: 10, of which 5 were waited for; matrix products, arithmetic and copies ran while one was open for 0% of the time, Pallas kernels for 4%

profile of v2, /device:TPU:0, one launch (start us, length us, event | category | flops | bytes accessed | tf_op | source)
XLA Modules:
  0.0 58.0 jit_solution(14392664605391002048)
XLA Ops:
  1.3 0.0 copy-start.2
  1.3 1.0 %copy-done.2 = bf16[1,1,12,128,128]{4,3,2,1,0:T(8,128)(2,1)S(1)} copy-done((bf16[1,1,12,128,128]{4,3,2,1,0:T(8,128)(2,1)S(1)}, bf16[1,1,12,128,128]{4,3,2,1,0:T(8,128)(2,1)}, u32[]{:S(2)}) %copy-start.2) | copy-done | bytes 393240
  2.3 0.0 copy-start.3
  2.3 0.8 %copy-done.3 = bf16[1,1,2,128,128]{4,3,2,1,0:T(8,128)(2,1)S(1)} copy-done((bf16[1,1,2,128,128]{4,3,2,1,0:T(8,128)(2,1)S(1)}, bf16[1,1,2,128,128]{4,3,2,1,0:T(8,128)(2,1)}, u32[]{:S(2)}) %copy-start.3) | copy-done | bytes 65560
  3.1 0.0 copy-start.4
  3.1 0.7 %copy-done.4 = s32[1,1,12]{2,1,0:T(1,128)S(1)} copy-done((s32[1,1,12]{2,1,0:T(1,128)S(1)}, s32[1,1,12]{2,1,0:T(1,128)}, u32[]{:S(2)}) %copy-start.4) | copy-done | bytes 72
  3.8 0.0 copy-start.6
  3.8 0.7 %copy-done.6 = s32[1,1,2]{2,1,0:T(1,128)S(1)} copy-done((s32[1,1,2]{2,1,0:T(1,128)S(1)}, s32[1,1,2]{2,1,0:T(1,128)}, u32[]{:S(2)}) %copy-start.6) | copy-done | bytes 32
  4.4 0.6 pack.1.own
  5.0 1.3 %collective-permute-start.3 = (bf16[1808,128]{1,0:T(8,128)(2,1)S(1)}, bf16[1808,128]{1,0:T(8,128)(2,1)S(1)}, u32[]{:S(2)}, u32[]{:S(2)}) collective-permute-start(bf16[1808,128]{1,0:T(8,128)(2,1)S(1)} %pack.1.own), channel_id=1, source_target_pairs={{4,0},{8,4},{12,8},{16,12},{20,16},{24,20},{28,24},{5,1},{9,5},{13... | collective-permute-start | bytes 1388552 | tf_op jit(solution)/shard_map/ppermute | solution.py:208
  6.3 3.1 %collective-permute-start.2 = (bf16[1808,128]{1,0:T(8,128)(2,1)S(1)}, bf16[1808,128]{1,0:T(8,128)(2,1)S(1)}, u32[]{:S(2)}, u32[]{:S(2)}) collective-permute-start(bf16[1808,128]{1,0:T(8,128)(2,1)S(1)} %pack.1.own), channel_id=1, source_target_pairs={{0,4},{4,8},{8,12},{12,16},{16,20},{20,24},{24,28},{1,5},{5,9},{9,... | collective-permute-start | bytes 1388552 | tf_op jit(solution)/shard_map/ppermute | solution.py:208
  9.4 1.3 %collective-permute-start.1 = (bf16[1808,128]{1,0:T(8,128)(2,1)S(1)}, bf16[1808,128]{1,0:T(8,128)(2,1)S(1)}, u32[]{:S(2)}, u32[]{:S(2)}) collective-permute-start(bf16[1808,128]{1,0:T(8,128)(2,1)S(1)} %pack.1.own), channel_id=1, source_target_pairs={{1,0},{2,1},{3,2},{5,4},{6,5},{7,6},{9,8},{10,9},{11,10},{13,12},{... | collective-permute-start | bytes 1388552 | tf_op jit(solution)/shard_map/ppermute | solution.py:208
  10.7 5.6 %collective-permute-start = (bf16[1808,128]{1,0:T(8,128)(2,1)S(1)}, bf16[1808,128]{1,0:T(8,128)(2,1)S(1)}, u32[]{:S(2)}, u32[]{:S(2)}) collective-permute-start(bf16[1808,128]{1,0:T(8,128)(2,1)S(1)} %pack.1.own), channel_id=1, source_target_pairs={{0,1},{1,2},{2,3},{4,5},{5,6},{6,7},{8,9},{9,10},{10,11},{12,13},{... | collective-permute-start | bytes 1388552 | tf_op jit(solution)/shard_map/ppermute | solution.py:208
  16.9 0.0 copy-start
  16.9 1.6 %copy-done = bf16[1,1,64,128,128]{4,3,2,1,0:T(8,128)(2,1)S(1)} copy-done((bf16[1,1,64,128,128]{4,3,2,1,0:T(8,128)(2,1)S(1)}, bf16[1,1,64,128,128]{4,3,2,1,0:T(8,128)(2,1)}, u32[]{:S(2)}) %copy-start) | copy-done | bytes 2097176
  18.5 0.0 copy-start.5
  18.5 0.7 %copy-done.5 = s32[1,1,12]{2,1,0:T(1,128)S(1)} copy-done((s32[1,1,12]{2,1,0:T(1,128)S(1)}, s32[1,1,12]{2,1,0:T(1,128)}, u32[]{:S(2)}) %copy-start.5) | copy-done | bytes 72
  19.2 0.0 copy-start.7
  19.2 0.7 %copy-done.7 = s32[1,1,2]{2,1,0:T(1,128)S(1)} copy-done((s32[1,1,2]{2,1,0:T(1,128)S(1)}, s32[1,1,2]{2,1,0:T(1,128)}, u32[]{:S(2)}) %copy-start.7) | copy-done | bytes 32
  19.8 0.0 copy-start.8
  19.8 0.7 %copy-done.8 = s32[1,1,64]{2,1,0:T(1,128)S(1)} copy-done((s32[1,1,64]{2,1,0:T(1,128)S(1)}, s32[1,1,64]{2,1,0:T(1,128)}, u32[]{:S(2)}) %copy-start.8) | copy-done | bytes 280
  20.5 0.0 copy-start.9
  20.5 0.7 %copy-done.9 = s32[1,1,64]{2,1,0:T(1,128)S(1)} copy-done((s32[1,1,64]{2,1,0:T(1,128)S(1)}, s32[1,1,64]{2,1,0:T(1,128)}, u32[]{:S(2)}) %copy-start.9) | copy-done | bytes 280
  21.1 0.0 copy-start.1
  21.1 2.5 %own_source.1 = (bf16[256,1024]{1,0:T(8,128)(2,1)S(1)}, bf16[256,256]{1,0:T(8,128)(2,1)S(1)}, f32[256,256]{1,0:T(8,128)S(1)}, bf16[256,256]{1,0:T(8,128)(2,1)S(1)}, s32[64]{0:T(128)S(1)}, /*index=5*/s32[8]{0:T(128)S(1)}) custom-call(s32[64]{0:T(128)S(1)} %bitcast.22, s32[64]{0:T(128)S(1)} %bitcast.24, s32[1]{0:T(128)} %bitcast.11.count, s32[12]{0:T(128)S(1)} %bitcast.19, ...), custom_call_target="tpu_custom_call" | custom-call | flops 1000000000 | bytes 4000000 | tf_op jit(solution)/shard_map/own_source/pallas_call | solution.py:239
  23.6 0.0 collective-permute-done.3.down
  23.6 0.0 collective-permute-done.2.up
  23.6 1.6 %collective-permute-done.1.right = bf16[1808,128]{1,0:T(8,128)(2,1)S(1)} collective-permute-done((bf16[1808,128]{1,0:T(8,128)(2,1)S(1)}, bf16[1808,128]{1,0:T(8,128)(2,1)S(1)}, u32[]{:S(2)}, u32[]{:S(2)}) %collective-permute-start.1) | collective-permute-done | bytes 462880 | tf_op jit(solution)/shard_map/ppermute | solution.py:208
  25.3 1.7 %collective-permute-done.left = bf16[1808,128]{1,0:T(8,128)(2,1)S(1)} collective-permute-done((bf16[1808,128]{1,0:T(8,128)(2,1)S(1)}, bf16[1808,128]{1,0:T(8,128)(2,1)S(1)}, u32[]{:S(2)}, u32[]{:S(2)}) %collective-permute-start) | collective-permute-done | bytes 462880 | tf_op jit(solution)/shard_map/ppermute | solution.py:208
  26.9 0.0 copy-done.1
  27.0 5.9 %near_sources.1 = (bf16[2,5,2,128,128]{4,3,2,1,0:T(8,128)(2,1)}, bf16[192,256]{1,0:T(8,128)(2,1)S(1)}, bf16[192,256]{1,0:T(8,128)(2,1)S(1)}, bf16[192,256]{1,0:T(8,128)(2,1)S(1)}, bf16[192,256]{1,0:T(8,128)(2,1)S(1)}) custom-call(s32[64]{0:T(128)S(1)} %bitcast.23, s32[64]{0:T(128)S(1)} %bitcast.25, s32[64]{0:T(128)S(1)} %get-tuple-element.13.order, ...), custom_call_target="tpu_custom_call" | custom-call | tf_op jit(solution)/shard_map/near_sources/pallas_call | solution.py:267
  32.9 4.6 %collective-permute-start.4 = (bf16[192,256]{1,0:T(8,128)(2,1)S(1)}, bf16[192,256]{1,0:T(8,128)(2,1)S(1)}, u32[]{:S(2)}, u32[]{:S(2)}) collective-permute-start(bf16[192,256]{1,0:T(8,128)(2,1)S(1)} %get-tuple-element.21), channel_id=1, source_target_pairs={{0,1},{1,2},{2,3},{3,0},{4,5},{5,6},{6,7},{7,4},{8,9},{9,10},{10,1... | collective-permute-start | bytes 294920 | tf_op jit(solution)/shard_map/ppermute | solution.py:208
  37.5 1.1 %collective-permute-start.5 = (bf16[192,256]{1,0:T(8,128)(2,1)S(1)}, bf16[192,256]{1,0:T(8,128)(2,1)S(1)}, u32[]{:S(2)}, u32[]{:S(2)}) collective-permute-start(bf16[192,256]{1,0:T(8,128)(2,1)S(1)} %get-tuple-element.22), channel_id=1, source_target_pairs={{0,2},{1,3},{2,0},{3,1},{4,6},{5,7},{6,4},{7,5},{8,10},{9,11},{10,... | collective-permute-start | bytes 294920 | tf_op jit(solution)/shard_map/ppermute | solution.py:208
  38.6 2.8 %collective-permute-start.6 = (bf16[192,256]{1,0:T(8,128)(2,1)S(1)}, bf16[192,256]{1,0:T(8,128)(2,1)S(1)}, u32[]{:S(2)}, u32[]{:S(2)}) collective-permute-start(bf16[192,256]{1,0:T(8,128)(2,1)S(1)} %get-tuple-element.23), channel_id=1, source_target_pairs={{0,3},{1,0},{2,1},{3,2},{4,7},{5,4},{6,5},{7,6},{8,11},{9,8},{10,9... | collective-permute-start | bytes 294920 | tf_op jit(solution)/shard_map/ppermute | solution.py:208
  41.5 0.0 collective-permute-done.4.refs_1_
  41.5 3.7 %collective-permute-done.5.refs_2_ = bf16[192,256]{1,0:T(8,128)(2,1)S(1)} collective-permute-done((bf16[192,256]{1,0:T(8,128)(2,1)S(1)}, bf16[192,256]{1,0:T(8,128)(2,1)S(1)}, u32[]{:S(2)}, u32[]{:S(2)}) %collective-permute-start.5) | collective-permute-done | bytes 98336 | tf_op jit(solution)/shard_map/ppermute | solution.py:208
  45.2 0.0 collective-permute-done.6.refs_3_
  45.2 0.1 total.1.refs_0_
  45.2 3.7 %collective-permute-start.9 = (bf16[192,256]{1,0:T(8,128)(2,1)S(1)}, bf16[192,256]{1,0:T(8,128)(2,1)S(1)}, u32[]{:S(2)}, u32[]{:S(2)}) collective-permute-start(bf16[192,256]{1,0:T(8,128)(2,1)S(1)} %total.1.refs_0_), channel_id=1, source_target_pairs={{0,3},{1,0},{2,1},{3,2},{4,7},{5,4},{6,5},{7,6},{8,11},{9,8},{10,9... | collective-permute-start | bytes 294920 | tf_op jit(solution)/shard_map/ppermute | solution.py:208
  49.0 0.0 collective-permute-start.8
  49.0 0.6 %collective-permute-start.7 = (bf16[192,256]{1,0:T(8,128)(2,1)S(1)}, bf16[192,256]{1,0:T(8,128)(2,1)S(1)}, u32[]{:S(2)}, u32[]{:S(2)}) collective-permute-start(bf16[192,256]{1,0:T(8,128)(2,1)S(1)} %total.1.refs_0_), channel_id=1, source_target_pairs={{0,1},{1,2},{2,3},{3,0},{4,5},{5,6},{6,7},{7,4},{8,9},{9,10},{10,1... | collective-permute-start | bytes 294920 | tf_op jit(solution)/shard_map/ppermute | solution.py:208
  49.6 1.6 %collective-permute-done.9.refs_3_ = bf16[192,256]{1,0:T(8,128)(2,1)S(1)} collective-permute-done((bf16[192,256]{1,0:T(8,128)(2,1)S(1)}, bf16[192,256]{1,0:T(8,128)(2,1)S(1)}, u32[]{:S(2)}, u32[]{:S(2)}) %collective-permute-start.9) | collective-permute-done | bytes 98336 | tf_op jit(solution)/shard_map/ppermute | solution.py:208
  51.2 5.7 %collective-permute-done.8.refs_2_ = bf16[192,256]{1,0:T(8,128)(2,1)S(1)} collective-permute-done((bf16[192,256]{1,0:T(8,128)(2,1)S(1)}, bf16[192,256]{1,0:T(8,128)(2,1)S(1)}, u32[]{:S(2)}, u32[]{:S(2)}) %collective-permute-start.8) | collective-permute-done | bytes 98336 | tf_op jit(solution)/shard_map/ppermute | solution.py:208
  56.9 0.0 collective-permute-done.7.refs_1_
  56.9 1.1 %spread.1 = f32[2,3,2,128,128]{4,3,2,1,0:T(8,128)} custom-call(bf16[192,256]{1,0:T(8,128)(2,1)S(1)} %total.1.refs_0_, bf16[192,256]{1,0:T(8,128)(2,1)S(1)} %collective-permute-done.7.refs_1_, bf16[192,256]{1,0:T(8,128)(2,1)S(1)} %collective-permute-done.8.refs_2_, bf16[192,256]{1,0:T(8,128)(2,1)S(1)} %collective-permute-done.9.refs_3_), custom_call_target="tpu_custom_call" | custom-call | tf_op jit(solution)/shard_map/spread/pallas_call | solution.py:292
Async XLA Ops:
  1.3 1.0 %copy-start.2 = (bf16[1,1,12,128,128]{4,3,2,1,0:T(8,128)(2,1)S(1)}, bf16[1,1,12,128,128]{4,3,2,1,0:T(8,128)(2,1)}, u32[]{:S(2)}) copy-start(bf16[1,1,12,128,128]{4,3,2,1,0:T(8,128)(2,1)} %param.13) | copy-start | bytes 1179652
  2.3 0.8 %copy-start.3 = (bf16[1,1,2,128,128]{4,3,2,1,0:T(8,128)(2,1)S(1)}, bf16[1,1,2,128,128]{4,3,2,1,0:T(8,128)(2,1)}, u32[]{:S(2)}) copy-start(bf16[1,1,2,128,128]{4,3,2,1,0:T(8,128)(2,1)} %param.16) | copy-start | bytes 196612
  3.1 0.7 %copy-start.4 = (s32[1,1,12]{2,1,0:T(1,128)S(1)}, s32[1,1,12]{2,1,0:T(1,128)}, u32[]{:S(2)}) copy-start(s32[1,1,12]{2,1,0:T(1,128)} %param.14) | copy-start | bytes 148
  3.8 0.7 %copy-start.6 = (s32[1,1,2]{2,1,0:T(1,128)S(1)}, s32[1,1,2]{2,1,0:T(1,128)}, u32[]{:S(2)}) copy-start(s32[1,1,2]{2,1,0:T(1,128)} %param.17) | copy-start | bytes 28
  5.0 18.6 %collective-permute-start.3 = (bf16[1808,128]{1,0:T(8,128)(2,1)S(1)}, bf16[1808,128]{1,0:T(8,128)(2,1)S(1)}, u32[]{:S(2)}, u32[]{:S(2)}) collective-permute-start(bf16[1808,128]{1,0:T(8,128)(2,1)S(1)} %pack.1.own), channel_id=1, source_target_pairs={{4,0},{8,4},{12,8},{16,12},{20,16},{24,20},{28,24},{5,1},{9,5},{13... | collective-permute-start | bytes 1388552 | tf_op jit(solution)/shard_map/ppermute | solution.py:208
  6.3 17.3 %collective-permute-start.2 = (bf16[1808,128]{1,0:T(8,128)(2,1)S(1)}, bf16[1808,128]{1,0:T(8,128)(2,1)S(1)}, u32[]{:S(2)}, u32[]{:S(2)}) collective-permute-start(bf16[1808,128]{1,0:T(8,128)(2,1)S(1)} %pack.1.own), channel_id=1, source_target_pairs={{0,4},{4,8},{8,12},{12,16},{16,20},{20,24},{24,28},{1,5},{5,9},{9,... | collective-permute-start | bytes 1388552 | tf_op jit(solution)/shard_map/ppermute | solution.py:208
  9.4 15.9 %collective-permute-start.1 = (bf16[1808,128]{1,0:T(8,128)(2,1)S(1)}, bf16[1808,128]{1,0:T(8,128)(2,1)S(1)}, u32[]{:S(2)}, u32[]{:S(2)}) collective-permute-start(bf16[1808,128]{1,0:T(8,128)(2,1)S(1)} %pack.1.own), channel_id=1, source_target_pairs={{1,0},{2,1},{3,2},{5,4},{6,5},{7,6},{9,8},{10,9},{11,10},{13,12},{... | collective-permute-start | bytes 1388552 | tf_op jit(solution)/shard_map/ppermute | solution.py:208
  10.7 16.3 %collective-permute-start = (bf16[1808,128]{1,0:T(8,128)(2,1)S(1)}, bf16[1808,128]{1,0:T(8,128)(2,1)S(1)}, u32[]{:S(2)}, u32[]{:S(2)}) collective-permute-start(bf16[1808,128]{1,0:T(8,128)(2,1)S(1)} %pack.1.own), channel_id=1, source_target_pairs={{0,1},{1,2},{2,3},{4,5},{5,6},{6,7},{8,9},{9,10},{10,11},{12,13},{... | collective-permute-start | bytes 1388552 | tf_op jit(solution)/shard_map/ppermute | solution.py:208
  16.9 1.6 %copy-start = (bf16[1,1,64,128,128]{4,3,2,1,0:T(8,128)(2,1)S(1)}, bf16[1,1,64,128,128]{4,3,2,1,0:T(8,128)(2,1)}, u32[]{:S(2)}) copy-start(bf16[1,1,64,128,128]{4,3,2,1,0:T(8,128)(2,1)} %param.9) | copy-start | bytes 6291460
  18.5 0.7 %copy-start.5 = (s32[1,1,12]{2,1,0:T(1,128)S(1)}, s32[1,1,12]{2,1,0:T(1,128)}, u32[]{:S(2)}) copy-start(s32[1,1,12]{2,1,0:T(1,128)} %param.14) | copy-start | bytes 148
  19.2 0.7 %copy-start.7 = (s32[1,1,2]{2,1,0:T(1,128)S(1)}, s32[1,1,2]{2,1,0:T(1,128)}, u32[]{:S(2)}) copy-start(s32[1,1,2]{2,1,0:T(1,128)} %param.17) | copy-start | bytes 28
  19.8 0.7 %copy-start.8 = (s32[1,1,64]{2,1,0:T(1,128)S(1)}, s32[1,1,64]{2,1,0:T(1,128)}, u32[]{:S(2)}) copy-start(s32[1,1,64]{2,1,0:T(1,128)} %param.10) | copy-start | bytes 772
  20.5 0.7 %copy-start.9 = (s32[1,1,64]{2,1,0:T(1,128)S(1)}, s32[1,1,64]{2,1,0:T(1,128)}, u32[]{:S(2)}) copy-start(s32[1,1,64]{2,1,0:T(1,128)} %param.11) | copy-start | bytes 772
  21.1 5.8 %copy-start.1 = (bf16[1,1,64,128,128]{4,3,2,1,0:T(8,128)(2,1)S(1)}, bf16[1,1,64,128,128]{4,3,2,1,0:T(8,128)(2,1)}, u32[]{:S(2)}) copy-start(bf16[1,1,64,128,128]{4,3,2,1,0:T(8,128)(2,1)} %param.9) | copy-start | bytes 6291460
  32.9 8.6 %collective-permute-start.4 = (bf16[192,256]{1,0:T(8,128)(2,1)S(1)}, bf16[192,256]{1,0:T(8,128)(2,1)S(1)}, u32[]{:S(2)}, u32[]{:S(2)}) collective-permute-start(bf16[192,256]{1,0:T(8,128)(2,1)S(1)} %get-tuple-element.21), channel_id=1, source_target_pairs={{0,1},{1,2},{2,3},{3,0},{4,5},{5,6},{6,7},{7,4},{8,9},{9,10},{10,1... | collective-permute-start | bytes 294920 | tf_op jit(solution)/shard_map/ppermute | solution.py:208
  37.5 7.7 %collective-permute-start.5 = (bf16[192,256]{1,0:T(8,128)(2,1)S(1)}, bf16[192,256]{1,0:T(8,128)(2,1)S(1)}, u32[]{:S(2)}, u32[]{:S(2)}) collective-permute-start(bf16[192,256]{1,0:T(8,128)(2,1)S(1)} %get-tuple-element.22), channel_id=1, source_target_pairs={{0,2},{1,3},{2,0},{3,1},{4,6},{5,7},{6,4},{7,5},{8,10},{9,11},{10,... | collective-permute-start | bytes 294920 | tf_op jit(solution)/shard_map/ppermute | solution.py:208
  38.6 6.6 %collective-permute-start.6 = (bf16[192,256]{1,0:T(8,128)(2,1)S(1)}, bf16[192,256]{1,0:T(8,128)(2,1)S(1)}, u32[]{:S(2)}, u32[]{:S(2)}) collective-permute-start(bf16[192,256]{1,0:T(8,128)(2,1)S(1)} %get-tuple-element.23), channel_id=1, source_target_pairs={{0,3},{1,0},{2,1},{3,2},{4,7},{5,4},{6,5},{7,6},{8,11},{9,8},{10,9... | collective-permute-start | bytes 294920 | tf_op jit(solution)/shard_map/ppermute | solution.py:208
  45.2 6.0 %collective-permute-start.9 = (bf16[192,256]{1,0:T(8,128)(2,1)S(1)}, bf16[192,256]{1,0:T(8,128)(2,1)S(1)}, u32[]{:S(2)}, u32[]{:S(2)}) collective-permute-start(bf16[192,256]{1,0:T(8,128)(2,1)S(1)} %total.1.refs_0_), channel_id=1, source_target_pairs={{0,3},{1,0},{2,1},{3,2},{4,7},{5,4},{6,5},{7,6},{8,11},{9,8},{10,9... | collective-permute-start | bytes 294920 | tf_op jit(solution)/shard_map/ppermute | solution.py:208
  49.0 7.9 %collective-permute-start.8 = (bf16[192,256]{1,0:T(8,128)(2,1)S(1)}, bf16[192,256]{1,0:T(8,128)(2,1)S(1)}, u32[]{:S(2)}, u32[]{:S(2)}) collective-permute-start(bf16[192,256]{1,0:T(8,128)(2,1)S(1)} %total.1.refs_0_), channel_id=1, source_target_pairs={{0,2},{1,3},{2,0},{3,1},{4,6},{5,7},{6,4},{7,5},{8,10},{9,11},{10,... | collective-permute-start | bytes 294920 | tf_op jit(solution)/shard_map/ppermute | solution.py:208
  49.0 7.9 %collective-permute-start.7 = (bf16[192,256]{1,0:T(8,128)(2,1)S(1)}, bf16[192,256]{1,0:T(8,128)(2,1)S(1)}, u32[]{:S(2)}, u32[]{:S(2)}) collective-permute-start(bf16[192,256]{1,0:T(8,128)(2,1)S(1)} %total.1.refs_0_), channel_id=1, source_target_pairs={{0,1},{1,2},{2,3},{3,0},{4,5},{5,6},{6,7},{7,4},{8,9},{9,10},{10,1... | collective-permute-start | bytes 294920 | tf_op jit(solution)/shard_map/ppermute | solution.py:208

commit v3 on v2

--- a/solution.py
+++ b/solution.py
@@ -20,22 +20,30 @@
 
 VMEM = pl.BlockSpec(memory_space=pltpu.VMEM)
 SMEM = pl.BlockSpec(memory_space=pltpu.SMEM)
+ANY = pl.BlockSpec(memory_space=pl.ANY)
 SMALL = pltpu.CompilerParams(vmem_limit_bytes=4 * 1024 * 1024)
 LARGE = pltpu.CompilerParams(vmem_limit_bytes=20 * 1024 * 1024)
 
 
-def pack_kernel(codes, count, aggs, blocks, second, out):
+def pack_kernel(codes, count, aggs, blocks, second, out, held, sems):
     n_p, n_s = blocks.shape[0], second.shape[0]
     slots = codes.shape[0]
-    out[0:n_p, :] = blocks[...]
-    out[n_p : n_p + n_s, :] = second[...]
+    first = pltpu.make_async_copy(blocks, held.at[0:n_p], sems.at[0])
+    after = pltpu.make_async_copy(second, held.at[n_p : n_p + n_s], sems.at[1])
+    first.start()
+    after.start()
     lane = lax.broadcasted_iota(jnp.int32, (META, out.shape[1]), 1)
     word = jnp.zeros(lane.shape, jnp.int32)
     for k in range(slots):
         word = jnp.where(lane == k, jnp.where(k < count[0], codes[k], PB), word)
     for j in range(CB):
         word = jnp.where(lane == slots + j, aggs[j], word)
-    out[n_p + n_s : n_p + n_s + META, :] = word.astype(F32).astype(BF16)
+    held[n_p + n_s : n_p + n_s + META, :] = word.astype(F32).astype(BF16)
+    first.wait()
+    after.wait()
+    whole = pltpu.make_async_copy(held, out, sems.at[2])
+    whole.start()
+    whole.wait()
 
 
 def slot_products(s, size, table, rows, cols, order, begin, end, fine, near, acc, base):
@@ -133,10 +141,8 @@
 
 def near_kernel(
     slots, size, cols_n, rows, cols, order, bounds, fine, turned, coarse0, half0, lift_t,
-    left, right, up, down, c_one, *rest,
+    left, right, up, down, c_one, sends, acc, terms, words, codes, table, sem,
 ):
-    sends = rest[:cols_n]
-    acc, terms, words, codes, table, sem = rest[cols_n:]
     near = (None, left, right, up, down)
     tail = (slots + CB) * size
     for s in range(1, NS):
@@ -169,36 +175,29 @@
             lift_t[...], halves[g].astype(BF16), preferred_element_type=F32
         )
     chunk = terms.shape[0] // cols_n
-    me = lax.axis_index("col")
-    for d in range(cols_n):
-        to = lax.rem(me + d, cols_n)
-        part = terms[pl.ds(pl.multiple_of(to * chunk, chunk), chunk), :]
-        sends[d][...] = part.astype(BF16)
-
-
-def sum_kernel(*refs):
-    total = refs[0][...].astype(F32)
-    for ref in refs[1:-1]:
-        total = total + ref[...].astype(F32)
-    refs[-1][...] = total.astype(BF16)
-
-
-def spread_kernel(size, cols_n, *refs):
-    out = refs[-1]
-    chunk = refs[0].shape[0]
+    for to in range(cols_n):
+        sends[to] = terms[to * chunk : (to + 1) * chunk, :].astype(BF16)
+
+
+def sum_kernel(parts, out):
+    total = parts[0].astype(F32)
+    for c in range(1, parts.shape[0]):
+        total = total + parts[c].astype(F32)
+    for c in range(parts.shape[0]):
+        out[c] = total.astype(BF16)
+
+
+def spread_kernel(size, parts, out):
+    chunk = parts.shape[1]
     unit = math.gcd(chunk, size)
     per = size // unit
-    me = lax.axis_index("col")
-    for d in range(cols_n):
-        owner = lax.rem(me - d + cols_n, cols_n)
+    for owner in range(parts.shape[0]):
         for t in range(chunk // unit):
             at = owner * (chunk // unit) + t
-            g = at // (G2 * per)
-            a = lax.rem(at // per, G2)
-            h = pl.multiple_of(lax.rem(at, per) * unit, unit)
+            g, a, h = at // (G2 * per), at // per % G2, at % per * unit
             for b in range(G2):
-                out[a, g, b, pl.ds(h, unit), :] = refs[d][
-                    t * unit : (t + 1) * unit, b * size : (b + 1) * size
+                out[a, g, b, h : h + unit, :] = parts[
+                    owner, t * unit : (t + 1) * unit, b * size : (b + 1) * size
                 ].astype(F32)
 
 
@@ -220,9 +219,10 @@
     packed = pl.pallas_call(
         pack_kernel,
         out_shape=jax.ShapeDtypeStruct((packed_rows, size), BF16),
-        in_specs=[SMEM] * 3 + [VMEM] * 2,
-        out_specs=VMEM,
-        compiler_params=SMALL,
+        in_specs=[SMEM] * 3 + [ANY] * 2,
+        out_specs=ANY,
+        scratch_shapes=[pltpu.VMEM((packed_rows, size), BF16), pltpu.SemaphoreType.DMA((3,))],
+        compiler_params=pltpu.CompilerParams(vmem_limit_bytes=60 * 1024 * 1024),
         name="pack",
     )(
         prolong_codes[0, 0],
@@ -263,12 +263,12 @@
     )
 
     chunk = 3 * G2 * size // cols_n
-    piece = jax.ShapeDtypeStruct((chunk, G2 * size), BF16)
-    c_one, *sends = pl.pallas_call(
+    pieces = jax.ShapeDtypeStruct((cols_n, chunk, G2 * size), BF16)
+    c_one, sends = pl.pallas_call(
         functools.partial(near_kernel, slots, size, cols_n),
-        out_shape=[jax.ShapeDtypeStruct((CB, NS, CB, size, size), BF16)] + [piece] * cols_n,
+        out_shape=[jax.ShapeDtypeStruct((CB, NS, CB, size, size), BF16), pieces],
         in_specs=[SMEM] * 4 + [VMEM] * 9,
-        out_specs=[VMEM] * (1 + cols_n),
+        out_specs=[VMEM] * 2,
         scratch_shapes=[
             pltpu.VMEM(((NS - 1) * FB + 1, size, wide), F32),
             pltpu.VMEM((3 * G2 * size, G2 * size), F32),
@@ -283,20 +283,20 @@
         fine_rows[0, 0], fine_cols[0, 0], order, bounds, fine_blocks[0, 0],
         turned, coarse0, half0, lift_t, left, right, up, down,
     )
-    parts = [sends[0]] + [shift(sends[d], "col", d, True) for d in range(1, cols_n)]
+    parts = lax.all_to_all(sends, "col", 0, 0)
     total = pl.pallas_call(
-        sum_kernel, out_shape=piece, in_specs=[VMEM] * cols_n, out_specs=VMEM,
-        compiler_params=SMALL, name="total"
-    )(*parts)
-    gathered = [total] + [shift(total, "col", d, True) for d in range(1, cols_n)]
+        sum_kernel, out_shape=pieces, in_specs=[VMEM], out_specs=VMEM,
+        compiler_params=SMALL, name="total",
+    )(parts)
+    gathered = lax.all_to_all(total, "col", 0, 0)
     c_two = pl.pallas_call(
-        functools.partial(spread_kernel, size, cols_n),
+        functools.partial(spread_kernel, size),
         out_shape=jax.ShapeDtypeStruct((G2, 3, G2, size, size), F32),
-        in_specs=[VMEM] * cols_n,
+        in_specs=[VMEM],
         out_specs=VMEM,
         compiler_params=SMALL,
         name="spread",
-    )(*gathered)
+    )(gathered)
     return (c_one[None, None], c_two[None])
 
 

time: 58.5 us -> 64.6 us (1.10)
  blocking collectives: 0 us -> 31.9 us
  starting transfers between devices: 24.2 us -> 11.2 us
  waiting for transfers between devices: 14.3 us -> 2.76 us
  local copies, waits for them, and re-layouts: 7.35 us -> 5.23 us
  Pallas kernels: 10.1 us -> 11.2 us
    all_to_all x0 -> x2, blocking collectives: none -> 31.9 us  [the longest x1 18.1 us: per_device(): parts = lax.all_to_all(sends, 'col', 0, 0)]
    ppermute x10 -> x4, starting transfers between devices: 24.2 us -> 11.2 us  [shift(): return lax.ppermute(x, axis, pairs)]
    ppermute x10 -> x4, waiting for transfers between devices: 14.3 us -> 2.76 us  [shift(): return lax.ppermute(x, axis, pairs)]
    unnamed x20 -> x14, local copies, waits for them, and re-layouts: 7.35 us -> 5.23 us
    pallas_call x1, Pallas kernels: 0.57 us -> 2.46 us  [per_device(): pl.pallas_call(pack_kernel, out_shape=jax.ShapeDtypeStruct((packed_rows,...]
  transfers between devices with their start and end apart: 10 -> 4, of which waited for: 5 -> 2; matrix products, arithmetic and copies ran while one was open for 0% -> 0% of each run, Pallas kernels for 4% -> 4%
where the time goes in v3:
time: 64.6 us; the launch traced here: 64.3 us
  blocking collectives  31.9 us (49%)
  Pallas kernels  11.2 us (17%)
  starting transfers between devices  11.2 us (17%)
  local copies, waits for them, and re-layouts  5.23 us (8%)
  waiting for transfers between devices  2.76 us (4%)
  between operations  2.01 us (3%)
    all_to_all x1, blocking collectives, per_device(): parts = lax.all_to_all(sends, 'col', 0, 0)  18.1 us
    all_to_all x1, blocking collectives, per_device(): gathered = lax.all_to_all(total, 'col', 0, 0)  13.8 us
    ppermute x4, starting transfers between devices, shift(): return lax.ppermute(x, axis, pairs)  11.2 us
    pallas_call x1, Pallas kernels, per_device(): pl.pallas_call(functools.partial(near_kernel, slots, size, cols_n), out_s...  5.41 us
    unnamed x14, local copies, waits for them, and re-layouts  5.23 us
    ppermute x4, waiting for transfers between devices, shift(): return lax.ppermute(x, axis, pairs)  2.76 us
    pallas_call x1, Pallas kernels, per_device(): pl.pallas_call(pack_kernel, out_shape=jax.ShapeDtypeStruct((packed_rows,...  2.46 us
    pallas_call x1, Pallas kernels, per_device(): pl.pallas_call(functools.partial(own_kernel, slots, size), out_shape=[jax...  2.33 us
  transfers between devices with their start and end apart: 4, of which 2 were waited for; matrix products, arithmetic and copies ran while one was open for 0% of the time, Pallas kernels for 4%

profile of v3, /device:TPU:0, one launch (start us, length us, event | category | flops | bytes accessed | tf_op | source)
XLA Modules:
  0.0 64.3 jit_solution(1954430476287618101)
XLA Ops:
  1.3 2.5 %pack.1.own = bf16[1808,128]{1,0:T(8,128)(2,1)} custom-call(s32[12]{0:T(128)} %bitcast.16, s32[1]{0:T(128)} %bitcast.12.count, s32[2]{0:T(128)} %bitcast.18, bf16[1536,128]{1,0:T(8,128)(2,1)} %bitcast.25, bf16[256,128]{1,0:T(8,128)(2,1)} %bitcast.26), custom_call_target="tpu_custom_call" | custom-call | tf_op jit(solution)/shard_map/pack/pallas_call | solution.py:219
  3.7 1.3 %collective-permute-start.3 = (bf16[1808,128]{1,0:T(8,128)(2,1)}, bf16[1808,128]{1,0:T(8,128)(2,1)S(1)}, u32[]{:S(2)}, u32[]{:S(2)}) collective-permute-start(bf16[1808,128]{1,0:T(8,128)(2,1)} %pack.1.own), channel_id=1, source_target_pairs={{4,0},{8,4},{12,8},{16,12},{20,16},{24,20},{28,24},{5,1},{9,5},{13... | collective-permute-start | bytes 1388552 | tf_op jit(solution)/shard_map/ppermute | solution.py:207
  5.0 3.1 %collective-permute-start.2 = (bf16[1808,128]{1,0:T(8,128)(2,1)}, bf16[1808,128]{1,0:T(8,128)(2,1)S(1)}, u32[]{:S(2)}, u32[]{:S(2)}) collective-permute-start(bf16[1808,128]{1,0:T(8,128)(2,1)} %pack.1.own), channel_id=1, source_target_pairs={{0,4},{4,8},{8,12},{12,16},{16,20},{20,24},{24,28},{1,5},{5,9},{9,... | collective-permute-start | bytes 1388552 | tf_op jit(solution)/shard_map/ppermute | solution.py:207
  8.1 1.3 %collective-permute-start.1 = (bf16[1808,128]{1,0:T(8,128)(2,1)}, bf16[1808,128]{1,0:T(8,128)(2,1)S(1)}, u32[]{:S(2)}, u32[]{:S(2)}) collective-permute-start(bf16[1808,128]{1,0:T(8,128)(2,1)} %pack.1.own), channel_id=1, source_target_pairs={{1,0},{2,1},{3,2},{5,4},{6,5},{7,6},{9,8},{10,9},{11,10},{13,12},{... | collective-permute-start | bytes 1388552 | tf_op jit(solution)/shard_map/ppermute | solution.py:207
  9.4 5.6 %collective-permute-start = (bf16[1808,128]{1,0:T(8,128)(2,1)}, bf16[1808,128]{1,0:T(8,128)(2,1)S(1)}, u32[]{:S(2)}, u32[]{:S(2)}) collective-permute-start(bf16[1808,128]{1,0:T(8,128)(2,1)} %pack.1.own), channel_id=1, source_target_pairs={{0,1},{1,2},{2,3},{4,5},{5,6},{6,7},{8,9},{9,10},{10,11},{12,13},{... | collective-permute-start | bytes 1388552 | tf_op jit(solution)/shard_map/ppermute | solution.py:207
  15.7 0.0 copy-start
  15.7 1.6 %copy-done = bf16[1,1,64,128,128]{4,3,2,1,0:T(8,128)(2,1)S(1)} copy-done((bf16[1,1,64,128,128]{4,3,2,1,0:T(8,128)(2,1)S(1)}, bf16[1,1,64,128,128]{4,3,2,1,0:T(8,128)(2,1)}, u32[]{:S(2)}) %copy-start) | copy-done | bytes 2097176
  17.2 0.0 copy-start.2
  17.3 1.0 %copy-done.2 = bf16[1808,128]{1,0:T(8,128)(2,1)S(1)} copy-done((bf16[1808,128]{1,0:T(8,128)(2,1)S(1)}, bf16[1808,128]{1,0:T(8,128)(2,1)}, u32[]{:S(2)}) %copy-start.2) | copy-done | bytes 462872
  18.3 0.0 copy-start.3
  18.3 0.7 %copy-done.3 = s32[1,1,12]{2,1,0:T(1,128)S(1)} copy-done((s32[1,1,12]{2,1,0:T(1,128)S(1)}, s32[1,1,12]{2,1,0:T(1,128)}, u32[]{:S(2)}) %copy-start.3) | copy-done | bytes 72
  18.9 0.0 copy-start.4
  18.9 0.7 %copy-done.4 = s32[1,1,2]{2,1,0:T(1,128)S(1)} copy-done((s32[1,1,2]{2,1,0:T(1,128)S(1)}, s32[1,1,2]{2,1,0:T(1,128)}, u32[]{:S(2)}) %copy-start.4) | copy-done | bytes 32
  19.6 0.0 copy-start.5
  19.6 0.7 %copy-done.5 = s32[1,1,64]{2,1,0:T(1,128)S(1)} copy-done((s32[1,1,64]{2,1,0:T(1,128)S(1)}, s32[1,1,64]{2,1,0:T(1,128)}, u32[]{:S(2)}) %copy-start.5) | copy-done | bytes 280
  20.2 0.0 copy-start.6
  20.2 0.7 %copy-done.6 = s32[1,1,64]{2,1,0:T(1,128)S(1)} copy-done((s32[1,1,64]{2,1,0:T(1,128)S(1)}, s32[1,1,64]{2,1,0:T(1,128)}, u32[]{:S(2)}) %copy-start.6) | copy-done | bytes 280
  20.9 0.0 copy-start.1
  20.9 2.3 %own_source.1 = (bf16[256,1024]{1,0:T(8,128)(2,1)S(1)}, bf16[256,256]{1,0:T(8,128)(2,1)S(1)}, f32[256,256]{1,0:T(8,128)S(1)}, bf16[256,256]{1,0:T(8,128)(2,1)S(1)}, s32[64]{0:T(128)S(1)}, /*index=5*/s32[8]{0:T(128)S(1)}) custom-call(s32[64]{0:T(128)S(1)} %bitcast.20, s32[64]{0:T(128)S(1)} %bitcast.22, s32[1]{0:T(128)} %bitcast.11.count, s32[12]{0:T(128)S(1)} %bitcast.17, ...), custom_call_target="tpu_custom_call" | custom-call | flops 1000000000 | bytes 4000000 | tf_op jit(solution)/shard_map/own_source/pallas_call | solution.py:239
  23.2 0.0 collective-permute-done.3.down
  23.2 0.0 collective-permute-done.2.up
  23.3 1.0 %collective-permute-done.1.right = bf16[1808,128]{1,0:T(8,128)(2,1)S(1)} collective-permute-done((bf16[1808,128]{1,0:T(8,128)(2,1)}, bf16[1808,128]{1,0:T(8,128)(2,1)S(1)}, u32[]{:S(2)}, u32[]{:S(2)}) %collective-permute-start.1) | collective-permute-done | bytes 462880 | tf_op jit(solution)/shard_map/ppermute | solution.py:207
  24.2 1.8 %collective-permute-done.left = bf16[1808,128]{1,0:T(8,128)(2,1)S(1)} collective-permute-done((bf16[1808,128]{1,0:T(8,128)(2,1)}, bf16[1808,128]{1,0:T(8,128)(2,1)S(1)}, u32[]{:S(2)}, u32[]{:S(2)}) %collective-permute-start) | collective-permute-done | bytes 462880 | tf_op jit(solution)/shard_map/ppermute | solution.py:207
  26.0 0.0 copy-done.1
  26.0 5.4 %near_sources.1 = (bf16[2,5,2,128,128]{4,3,2,1,0:T(8,128)(2,1)}, bf16[4,192,256]{2,1,0:T(8,128)(2,1)S(1)}) custom-call(s32[64]{0:T(128)S(1)} %bitcast.21, s32[64]{0:T(128)S(1)} %bitcast.23, s32[64]{0:T(128)S(1)} %get-tuple-element.10.order, s32[8]{0:T(128)S(1)} %get-tuple-element.11.bounds, bf16[64,128,128]{2,1,0:T(8,128)(2,1)S(1)} %bitcast.15, ...), custom_call_target="tpu_custom_call" | custom-call | tf_op jit(solution)/shard_map/near_sources/pallas_call | solution.py:267
  31.4 18.1 %all_to_all.10.parts = bf16[4,192,256]{2,1,0:T(8,128)(2,1)S(1)} all-to-all(bf16[4,192,256]{2,1,0:T(8,128)(2,1)S(1)} %get-tuple-element.17), channel_id=1, replica_groups=mesh['row'=8,'col'=4] {'col'}, dimensions={0} | all-to-all | bytes 786432 | tf_op jit(solution)/shard_map/all_to_all | solution.py:286
  49.5 0.1 total.1
  49.6 13.8 %all_to_all.11.parts = bf16[4,192,256]{2,1,0:T(8,128)(2,1)S(1)} all-to-all(bf16[4,192,256]{2,1,0:T(8,128)(2,1)S(1)} %total.1), channel_id=1, replica_groups=mesh['row'=8,'col'=4] {'col'}, dimensions={0} | all-to-all | bytes 786432 | tf_op jit(solution)/shard_map/all_to_all | solution.py:291
  63.4 0.9 %spread.1 = f32[2,3,2,128,128]{4,3,2,1,0:T(8,128)} custom-call(bf16[4,192,256]{2,1,0:T(8,128)(2,1)S(1)} %all_to_all.11.parts), custom_call_target="tpu_custom_call" | custom-call | tf_op jit(solution)/shard_map/spread/pallas_call | solution.py:292
Async XLA Ops:
  3.7 19.5 %collective-permute-start.3 = (bf16[1808,128]{1,0:T(8,128)(2,1)}, bf16[1808,128]{1,0:T(8,128)(2,1)S(1)}, u32[]{:S(2)}, u32[]{:S(2)}) collective-permute-start(bf16[1808,128]{1,0:T(8,128)(2,1)} %pack.1.own), channel_id=1, source_target_pairs={{4,0},{8,4},{12,8},{16,12},{20,16},{24,20},{28,24},{5,1},{9,5},{13... | collective-permute-start | bytes 1388552 | tf_op jit(solution)/shard_map/ppermute | solution.py:207
  5.0 18.2 %collective-permute-start.2 = (bf16[1808,128]{1,0:T(8,128)(2,1)}, bf16[1808,128]{1,0:T(8,128)(2,1)S(1)}, u32[]{:S(2)}, u32[]{:S(2)}) collective-permute-start(bf16[1808,128]{1,0:T(8,128)(2,1)} %pack.1.own), channel_id=1, source_target_pairs={{0,4},{4,8},{8,12},{12,16},{16,20},{20,24},{24,28},{1,5},{5,9},{9,... | collective-permute-start | bytes 1388552 | tf_op jit(solution)/shard_map/ppermute | solution.py:207
  8.1 16.1 %collective-permute-start.1 = (bf16[1808,128]{1,0:T(8,128)(2,1)}, bf16[1808,128]{1,0:T(8,128)(2,1)S(1)}, u32[]{:S(2)}, u32[]{:S(2)}) collective-permute-start(bf16[1808,128]{1,0:T(8,128)(2,1)} %pack.1.own), channel_id=1, source_target_pairs={{1,0},{2,1},{3,2},{5,4},{6,5},{7,6},{9,8},{10,9},{11,10},{13,12},{... | collective-permute-start | bytes 1388552 | tf_op jit(solution)/shard_map/ppermute | solution.py:207
  9.4 16.6 %collective-permute-start = (bf16[1808,128]{1,0:T(8,128)(2,1)}, bf16[1808,128]{1,0:T(8,128)(2,1)S(1)}, u32[]{:S(2)}, u32[]{:S(2)}) collective-permute-start(bf16[1808,128]{1,0:T(8,128)(2,1)} %pack.1.own), channel_id=1, source_target_pairs={{0,1},{1,2},{2,3},{4,5},{5,6},{6,7},{8,9},{9,10},{10,11},{12,13},{... | collective-permute-start | bytes 1388552 | tf_op jit(solution)/shard_map/ppermute | solution.py:207
  15.7 1.6 %copy-start = (bf16[1,1,64,128,128]{4,3,2,1,0:T(8,128)(2,1)S(1)}, bf16[1,1,64,128,128]{4,3,2,1,0:T(8,128)(2,1)}, u32[]{:S(2)}) copy-start(bf16[1,1,64,128,128]{4,3,2,1,0:T(8,128)(2,1)} %param.9) | copy-start | bytes 6291460
  17.2 1.0 %copy-start.2 = (bf16[1808,128]{1,0:T(8,128)(2,1)S(1)}, bf16[1808,128]{1,0:T(8,128)(2,1)}, u32[]{:S(2)}) copy-start(bf16[1808,128]{1,0:T(8,128)(2,1)} %pack.1.own) | copy-start | bytes 1388548
  18.3 0.7 %copy-start.3 = (s32[1,1,12]{2,1,0:T(1,128)S(1)}, s32[1,1,12]{2,1,0:T(1,128)}, u32[]{:S(2)}) copy-start(s32[1,1,12]{2,1,0:T(1,128)} %param.14) | copy-start | bytes 148
  18.9 0.7 %copy-start.4 = (s32[1,1,2]{2,1,0:T(1,128)S(1)}, s32[1,1,2]{2,1,0:T(1,128)}, u32[]{:S(2)}) copy-start(s32[1,1,2]{2,1,0:T(1,128)} %param.17) | copy-start | bytes 28
  19.6 0.7 %copy-start.5 = (s32[1,1,64]{2,1,0:T(1,128)S(1)}, s32[1,1,64]{2,1,0:T(1,128)}, u32[]{:S(2)}) copy-start(s32[1,1,64]{2,1,0:T(1,128)} %param.10) | copy-start | bytes 772
  20.2 0.7 %copy-start.6 = (s32[1,1,64]{2,1,0:T(1,128)S(1)}, s32[1,1,64]{2,1,0:T(1,128)}, u32[]{:S(2)}) copy-start(s32[1,1,64]{2,1,0:T(1,128)} %param.11) | copy-start | bytes 772
  20.9 5.1 %copy-start.1 = (bf16[1,1,64,128,128]{4,3,2,1,0:T(8,128)(2,1)S(1)}, bf16[1,1,64,128,128]{4,3,2,1,0:T(8,128)(2,1)}, u32[]{:S(2)}) copy-start(bf16[1,1,64,128,128]{4,3,2,1,0:T(8,128)(2,1)} %param.9) | copy-start | bytes 6291460

commit v4 on v2

v4 whole, which is shorter than its diff:
```python
import functools
import math

import jax
import jax.numpy as jnp
from jax import lax
from jax.experimental import pallas as pl
from jax.experimental.pallas import tpu as pltpu
from jax.sharding import PartitionSpec as P

FB = 8
CB = 2
G2 = 2
NS = 5
PB = FB * CB
UNROLL = 4
META = 16
F32 = jnp.float32
BF16 = jnp.bfloat16

VMEM = pl.BlockSpec(memory_space=pltpu.VMEM)
SMEM = pl.BlockSpec(memory_space=pltpu.SMEM)
ANY = pl.BlockSpec(memory_space=pl.ANY)
SMALL = pltpu.CompilerParams(vmem_limit_bytes=4 * 1024 * 1024)
LARGE = pltpu.CompilerParams(vmem_limit_bytes=20 * 1024 * 1024)


def pack_kernel(
    codes, count, aggs, rows, cols, f_count, blocks, second, out, ints, held, sems
):
    n_p, n_s = blocks.shape[0], second.shape[0]
    slots = codes.shape[0]
    first = pltpu.make_async_copy(blocks, held.at[0:n_p], sems.at[0])
    after = pltpu.make_async_copy(second, held.at[n_p : n_p + n_s], sems.at[1])
    first.start()
    after.start()
    lane = lax.broadcasted_iota(jnp.int32, (META, out.shape[1]), 1)
    word = jnp.zeros(lane.shape, jnp.int32)
    for k in range(slots):
        word = jnp.where(lane == k, jnp.where(k < count[0], codes[k], PB), word)
    for j in range(CB):
        word = jnp.where(lane == slots + j, aggs[j], word)
    held[n_p + n_s : n_p + n_s + META, :] = word.astype(F32).astype(BF16)
    first.wait()
    after.wait()
    whole = pltpu.make_async_copy(held, out, sems.at[2])
    whole.start()
    cap = cols.shape[0]
    for k in range(cap):
        ints[k] = cols[k]
        ints[cap + k] = rows[k]
    for k in range(slots):
        ints[2 * cap + k] = jnp.where(k < count[0], codes[k], PB)
    for j in range(CB):
        ints[2 * cap + slots + j] = aggs[j]
    ints[2 * cap + slots + CB] = f_count[0]
    whole.wait()


def slot_products(s, size, table, plan, cap, fine, near, acc, base):
    begin, end = plan[3 * cap + s], plan[3 * cap + s + 1]

    def step(t, carry):
        products, targets = [], []
        for u in range(UNROLL):
            at = begin + t * UNROLL + u
            live = at < end
            at = jnp.minimum(at, end - 1)
            m = plan[cap + at] - s * FB
            parts = []
            for j in range(CB):
                slot = table[s, m * CB + j]
                first = pl.multiple_of(jnp.maximum(slot, 0) * size, size)
                block = near[pl.ds(first, size), :]
                parts.append(jnp.where(slot >= 0, block, jnp.zeros_like(block)))
            wide = jnp.concatenate(parts, axis=1)
            products.append(jnp.dot(fine[plan[at]], wide, preferred_element_type=F32))
            targets.append(jnp.where(live, base + plan[2 * cap + at], acc.shape[0] - 1))
        for u in range(UNROLL):
            acc[targets[u]] += products[u]
        return carry

    lax.fori_loop(0, (end - begin + UNROLL - 1) // UNROLL, step, 0)


def fill_table(s, slots, table, code_of):
    for q in range(PB + 1):
        table[s, q] = -1
    for k in range(slots):
        table[s, code_of(k)] = k


def lift_of(near, slots, size, agg_of):
    lines = []
    for j in range(CB):
        block = near[(slots + j) * size : (slots + j + 1) * size, :]
        lines.append(
            jnp.concatenate(
                [jnp.where(agg_of(j) == a, block, jnp.zeros_like(block)) for a in range(G2)],
                axis=1,
            )
        )
    return jnp.concatenate(lines, axis=0)


def coarse_of(turned, acc, base, size, tile):
    product = acc[base : base + FB].reshape(FB * size, CB * size).astype(BF16)
    coarse = jnp.dot(turned, product, preferred_element_type=F32).astype(BF16)
    for i in range(CB):
        for j in range(CB):
            tile[i, j] = coarse[i * size : (i + 1) * size, j * size : (j + 1) * size]
    return coarse


def own_kernel(
    slots, size, ints, fine, own, turned, half, lift_t, plan, c_one, acc, tile, table, fill, sem
):
    cap = fine.shape[0]
    count = ints[2 * cap + slots + CB]
    for s in range(NS):
        fill[s] = 0

    def tally(k, carry):
        fill[ints[k] // FB] += 1
        return carry

    lax.fori_loop(0, count, tally, 0)
    at = jnp.int32(0)
    for s in range(NS):
        n = fill[s]
        plan[3 * cap + s] = at
        fill[s] = at
        at = at + n
    plan[3 * cap + NS] = at

    def place(k, carry):
        col = ints[k]
        s = col // FB
        to = fill[s]
        plan[to] = k
        plan[cap + to] = col
        plan[2 * cap + to] = ints[cap + k]
        fill[s] = to + 1
        return carry

    lax.fori_loop(0, count, place, 0)
    fill_table(0, slots, table, lambda k: ints[2 * cap + k])
    acc[...] = jnp.zeros_like(acc)
    for i in range(FB):
        for j in range(CB):
            slot = table[0, i * CB + j]
            block = own[pl.ds(pl.multiple_of(jnp.maximum(slot, 0) * size, size), size), :]
            block = jnp.where(slot >= 0, block, jnp.zeros_like(block))
            turned[j * size : (j + 1) * size, i * size : (i + 1) * size] = block.T
    slot_products(0, size, table, plan, cap, fine, own, acc, 0)
    coarse = coarse_of(turned[...], acc, 0, size, tile)
    store = pltpu.make_async_copy(tile, c_one.at[:, 0], sem)
    store.start()
    lift = lift_of(own, slots, size, lambda j: ints[2 * cap + slots + j])
    half[...] = jnp.dot(coarse, lift, preferred_element_type=F32)
    lift_t[...] = lift.T
    store.wait()


def near_coarse(sources, near, slots, size, plan, fine, turned, c_one, acc, tiles, words, codes, table, sems):
    cap = fine.shape[0]
    tail = (slots + CB) * size
    for s, ref in zip(sources, near):
        word = ref[tail : tail + META, :].astype(F32).astype(jnp.int32)
        words[s : s + 1, :] = word[0:1, :]
    fetch = pltpu.make_async_copy(words, codes, sems.at[0])
    fetch.start()
    acc[...] = jnp.zeros_like(acc)
    fetch.wait()
    parts, stores = [], []
    for n, (s, ref) in enumerate(zip(sources, near)):
        fill_table(s, slots, table, lambda k: codes[s, k])
        slot_products(s, size, table, plan, cap, fine, ref, acc, n * FB)
        coarse = coarse_of(turned[...], acc, n * FB, size, tiles.at[n])
        store = pltpu.make_async_copy(tiles.at[n], c_one.at[:, s], sems.at[1 + n])
        store.start()
        stores.append(store)
        lift = lift_of(ref, slots, size, lambda j: codes[s, slots + j])
        parts.append(jnp.dot(coarse, lift, preferred_element_type=F32))
    return parts, stores


def side_kernel(slots, size, plan, fine, turned, half, lift_t, left, right, c_in, c_one, term, *scratch):
    parts, stores = near_coarse((1, 2), (left, right), slots, size, plan, fine, turned, c_one, *scratch)
    whole = (half[...] + parts[0] + parts[1]).astype(BF16)
    term[...] = jnp.dot(lift_t[...], whole, preferred_element_type=F32)
    for store in stores:
        store.wait()


def row_kernel(slots, size, cols_n, plan, fine, turned, term, lift_t, up, down, c_in, c_one, *rest):
    sends, terms, scratch = rest[:cols_n], rest[cols_n], rest[cols_n + 1 :]
    parts, stores = near_coarse((3, 4), (up, down), slots, size, plan, fine, turned, c_one, *scratch)
    terms[0] = term[...]
    for g in range(2):
        terms[1 + g] = jnp.dot(lift_t[...], parts[g].astype(BF16), preferred_element_type=F32)
    chunk = terms.shape[1] // cols_n
    me = lax.axis_index("col")
    for d in range(cols_n):
        to = pl.multiple_of(lax.rem(me + d, cols_n) * chunk, chunk)
        for g in range(3):
            sends[d][g] = terms[g, pl.ds(to, chunk), :].astype(BF16)
    for store in stores:
        store.wait()


def sum_kernel(*refs):
    total = refs[0][...].astype(F32)
    for ref in refs[1:-1]:
        total = total + ref[...].astype(F32)
    refs[-1][...] = total.astype(BF16)


def spread_kernel(size, cols_n, *refs):
    out = refs[-1]
    chunk = refs[0].shape[1]
    unit = math.gcd(chunk, size)
    per = size // unit
    me = lax.axis_index("col")
    for d in range(cols_n):
        owner = lax.rem(me - d + cols_n, cols_n)
        for t in range(chunk // unit):
            at = owner * (chunk // unit) + t
            a = at // per
            h = pl.multiple_of(lax.rem(at, per) * unit, unit)
            for g in range(3):
                for b in range(G2):
                    out[a, g, b, pl.ds(h, unit), :] = refs[d][
                        g, t * unit : (t + 1) * unit, b * size : (b + 1) * size
                    ].astype(F32)


def shift(x, axis, step, wrap):
    n = lax.axis_size(axis)
    pairs = [(i, (i + step) % n) for i in range(n) if wrap or 0 <= i + step < n]
    return lax.ppermute(x, axis, pairs)


def per_device(
    fine_blocks, fine_rows, fine_cols, fine_counts, prolong_blocks, prolong_codes,
    prolong_counts, second_blocks, second_aggs,
):
    slots, size = prolong_blocks.shape[2], prolong_blocks.shape[3]
    cols_n = lax.axis_size("col")
    packed_rows = (slots + CB) * size + META
    grid_slots = fine_blocks.shape[2]
    wide = CB * size
    packed, ints = pl.pallas_call(
        pack_kernel,
        out_shape=[
            jax.ShapeDtypeStruct((packed_rows, size), BF16),
            jax.ShapeDtypeStruct((2 * grid_slots + slots + CB + 2,), jnp.int32),
        ],
        in_specs=[SMEM] * 6 + [ANY] * 2,
        out_specs=[ANY, SMEM],
        scratch_shapes=[pltpu.VMEM((packed_rows, size), BF16), pltpu.SemaphoreType.DMA((3,))],
        compiler_params=pltpu.CompilerParams(vmem_limit_bytes=60 * 1024 * 1024),
        name="pack",
    )(
        prolong_codes[0, 0],
        prolong_counts[0],
        second_aggs[0, 0],
        fine_rows[0, 0],
        fine_cols[0, 0],
        fine_counts[0],
        prolong_blocks.reshape(slots * size, size),
        second_blocks.reshape(CB * size, size),
    )
    up = shift(packed, "row", 1, False)
    down = shift(packed, "row", -1, False)
    left = shift(packed, "col", 1, False)
    right = shift(packed, "col", -1, False)

    c_shape = jax.ShapeDtypeStruct((CB, NS, CB, size, size), BF16)
    square = jax.ShapeDtypeStruct((wide, G2 * size), F32)
    table = pltpu.SMEM((NS, PB + 1), jnp.int32)
    turned, half, lift_t, plan, c_one = pl.pallas_call(
        functools.partial(own_kernel, slots, size),
        out_shape=[
            jax.ShapeDtypeStruct((wide, FB * size), BF16),
            square,
            jax.ShapeDtypeStruct((G2 * size, wide), BF16),
            jax.ShapeDtypeStruct((3 * grid_slots + 8,), jnp.int32),
            c_shape,
        ],
        in_specs=[SMEM] + [VMEM] * 2,
        out_specs=[VMEM] * 3 + [SMEM, ANY],
        scratch_shapes=[
            pltpu.VMEM((FB + 1, size, wide), F32),
            pltpu.VMEM((CB, CB, size, size), BF16),
            table,
            pltpu.SMEM((8,), jnp.int32),
            pltpu.SemaphoreType.DMA,
        ],
        compiler_params=LARGE,
        cost_estimate=pl.CostEstimate(flops=10**9, bytes_accessed=4 * 10**6, transcendentals=0),
        name="own_source",
    )(ints, fine_blocks[0, 0], packed)

    near_scratch = [
        pltpu.VMEM((2 * FB + 1, size, wide), F32),
        pltpu.VMEM((2, CB, CB, size, size), BF16),
        pltpu.VMEM((8, size), jnp.int32),
        pltpu.SMEM((8, size), jnp.int32),
        table,
        pltpu.SemaphoreType.DMA((3,)),
    ]
    c_one, term = pl.pallas_call(
        functools.partial(side_kernel, slots, size),
        out_shape=[c_shape, square],
        in_specs=[SMEM] + [VMEM] * 6 + [ANY],
        out_specs=[ANY, VMEM],
        input_output_aliases={7: 0},
        scratch_shapes=near_scratch,
        compiler_params=LARGE,
        name="col_sources",
    )(plan, fine_blocks[0, 0], turned, half, lift_t, left, right, c_one)

    chunk = G2 * size // cols_n
    piece = jax.ShapeDtypeStruct((3, chunk, G2 * size), BF16)
    c_one, *sends = pl.pallas_call(
        functools.partial(row_kernel, slots, size, cols_n),
        out_shape=[c_shape] + [piece] * cols_n,
        in_specs=[SMEM] + [VMEM] * 6 + [ANY],
        out_specs=[ANY] + [VMEM] * cols_n,
        input_output_aliases={7: 0},
        scratch_shapes=[pltpu.VMEM((3, G2 * size, G2 * size), F32)] + near_scratch,
        compiler_params=LARGE,
        name="row_sources",
    )(plan, fine_blocks[0, 0], turned, term, lift_t, up, down, c_one)

    parts = [sends[0]] + [shift(sends[d], "col", d, True) for d in range(1, cols_n)]
    total = pl.pallas_call(
        sum_kernel, out_shape=piece, in_specs=[VMEM] * cols_n, out_specs=VMEM,
        compiler_params=SMALL, name="total",
    )(*parts)
    gathered = [total] + [shift(total, "col", d, True) for d in range(1, cols_n)]
    c_two = pl.pallas_call(
        functools.partial(spread_kernel, size, cols_n),
        out_shape=jax.ShapeDtypeStruct((G2, 3, G2, size, size), F32),
        in_specs=[VMEM] * cols_n,
        out_specs=VMEM,
        compiler_params=SMALL,
        name="spread",
    )(*gathered)
    return (c_one[None, None], c_two[None])


def solution(mesh):
    in_specs = (
        P("row", "col", None, None, None),
        P("row", "col", None),
        P("row", "col", None),
        P("row", "col"),
        P("row", "col", None, None, None),
        P("row", "col", None),
        P("row", "col"),
        P("row", "col", None, None, None),
        P("row", "col", None),
    )
    out_specs = (
        P("row", "col", None, None, None, None, None),
        P("row", None, None, None, None, None),
    )
    return jax.shard_map(
        per_device, mesh=mesh, in_specs=in_specs, out_specs=out_specs, check_vma=False
    )
```

time: 58.5 us -> 56.5 us (0.966)
  the two profiles are of different devices: /device:TPU:0 before, /device:TPU:13 now
where the time goes in v4:
time: 56.5 us; the launch traced here: 55.7 us
  starting transfers between devices  18.8 us (33%)
  waiting for transfers between devices  16.5 us (29%)
  Pallas kernels  15 us (27%)
  local copies, waits for them, and re-layouts  3.29 us (6%)
  between operations  2.05 us (4%)
    ppermute x10, starting transfers between devices, shift(): return lax.ppermute(x, axis, pairs)  18.8 us
    ppermute x10, waiting for transfers between devices, shift(): return lax.ppermute(x, axis, pairs)  16.5 us
    pallas_call x1, Pallas kernels, per_device(): pl.pallas_call(functools.partial(side_kernel, slots, size), out_shape=[c_...  3.86 us
    pallas_call x1, Pallas kernels, per_device(): pl.pallas_call(functools.partial(row_kernel, slots, size, cols_n), out_sh...  3.65 us
    pallas_call x1, Pallas kernels, per_device(): pl.pallas_call(functools.partial(own_kernel, slots, size), out_shape=[jax...  3.46 us
    unnamed x8, local copies, waits for them, and re-layouts  3.29 us
    pallas_call x1, Pallas kernels, per_device(): pl.pallas_call(pack_kernel, out_shape=[jax.ShapeDtypeStruct((packed_rows,...  3.05 us
  transfers between devices with their start and end apart: 10, of which 6 were waited for; matrix products, arithmetic and copies ran while one was open for 0% of the time, Pallas kernels for 13%

profile of v4, /device:TPU:13, one launch (start us, length us, event | category | flops | bytes accessed | tf_op | source)
XLA Modules:
  0.0 55.7 jit_solution(8048365387424663178)
XLA Ops:
  1.9 3.0 %pack.1 = (bf16[1808,128]{1,0:T(8,128)(2,1)}, s32[144]{0:T(256)}) custom-call(s32[12]{0:T(128)} %bitcast.20, s32[1]{0:T(128)} %bitcast.12.count, s32[2]{0:T(128)} %bitcast.21, s32[64]{0:T(128)} %bitcast.22, s32[64]{0:T(128)} %bitcast.23, s32[1]{0:T(128)} %bitcast.11.f_count, bf16[1536,128]{1,0:T(8,128)(2,1)} %bitcast.18, bf16[256,128]{1,0:T(8,128)(2,1)} %bitcast.19), custom_call_target="tpu_custom_call" | custom-call | tf_op jit(solution)/shard_map/pack/pallas_call | solution.py:253
  5.0 3.2 %collective-permute-start = (bf16[1808,128]{1,0:T(8,128)(2,1)}, bf16[1808,128]{1,0:T(8,128)(2,1)S(1)}, u32[]{:S(2)}, u32[]{:S(2)}) collective-permute-start(bf16[1808,128]{1,0:T(8,128)(2,1)} %get-tuple-element.17.own), channel_id=1, source_target_pairs={{0,1},{1,2},{2,3},{4,5},{5,6},{6,7},{8,9},{9,10},{10,11},{12,13},{... | collective-permute-start | bytes 1388552 | tf_op jit(solution)/shard_map/ppermute | solution.py:241
  8.2 2.1 %collective-permute-start.1 = (bf16[1808,128]{1,0:T(8,128)(2,1)}, bf16[1808,128]{1,0:T(8,128)(2,1)S(1)}, u32[]{:S(2)}, u32[]{:S(2)}) collective-permute-start(bf16[1808,128]{1,0:T(8,128)(2,1)} %get-tuple-element.17.own), channel_id=1, source_target_pairs={{1,0},{2,1},{3,2},{5,4},{6,5},{7,6},{9,8},{10,9},{11,10},{13,12},{... | collective-permute-start | bytes 1388552 | tf_op jit(solution)/shard_map/ppermute | solution.py:241
  10.3 4.2 %collective-permute-start.2 = (bf16[1808,128]{1,0:T(8,128)(2,1)}, bf16[1808,128]{1,0:T(8,128)(2,1)S(1)}, u32[]{:S(2)}, u32[]{:S(2)}) collective-permute-start(bf16[1808,128]{1,0:T(8,128)(2,1)} %get-tuple-element.17.own), channel_id=1, source_target_pairs={{0,4},{4,8},{8,12},{12,16},{16,20},{20,24},{24,28},{1,5},{5,9},{9,... | collective-permute-start | bytes 1388552 | tf_op jit(solution)/shard_map/ppermute | solution.py:241
  14.5 1.9 %collective-permute-start.3 = (bf16[1808,128]{1,0:T(8,128)(2,1)}, bf16[1808,128]{1,0:T(8,128)(2,1)S(1)}, u32[]{:S(2)}, u32[]{:S(2)}) collective-permute-start(bf16[1808,128]{1,0:T(8,128)(2,1)} %get-tuple-element.17.own), channel_id=1, source_target_pairs={{4,0},{8,4},{12,8},{16,12},{20,16},{24,20},{28,24},{5,1},{9,5},{13... | collective-permute-start | bytes 1388552 | tf_op jit(solution)/shard_map/ppermute | solution.py:241
  16.5 0.0 copy-start
  16.5 1.6 %copy-done = bf16[1,1,64,128,128]{4,3,2,1,0:T(8,128)(2,1)S(1)} copy-done((bf16[1,1,64,128,128]{4,3,2,1,0:T(8,128)(2,1)S(1)}, bf16[1,1,64,128,128]{4,3,2,1,0:T(8,128)(2,1)}, u32[]{:S(2)}) %copy-start) | copy-done | bytes 2097176
  18.1 0.0 copy-start.2
  18.1 1.0 %copy-done.2 = bf16[1808,128]{1,0:T(8,128)(2,1)S(1)} copy-done((bf16[1808,128]{1,0:T(8,128)(2,1)S(1)}, bf16[1808,128]{1,0:T(8,128)(2,1)}, u32[]{:S(2)}) %copy-start.2) | copy-done | bytes 462872
  19.1 0.0 copy-start.3
  19.1 0.7 %copy-done.3 = s32[144]{0:T(256)S(1)} copy-done((s32[144]{0:T(256)S(1)}, s32[144]{0:T(256)}, u32[]{:S(2)}) %copy-start.3) | copy-done | bytes 600
  19.8 0.0 copy-start.1
  19.8 3.5 %own_source.1 = (bf16[256,1024]{1,0:T(8,128)(2,1)S(1)}, f32[256,256]{1,0:T(8,128)S(1)}, bf16[256,256]{1,0:T(8,128)(2,1)S(1)}, s32[200]{0:T(256)S(1)}, bf16[2,5,2,128,128]{4,3,2,1,0:T(8,128)(2,1)}) custom-call(s32[144]{0:T(256)S(1)} %copy-done.3, bf16[64,128,128]{2,1,0:T(8,128)(2,1)S(1)} %bitcast.13, bf16[1808,128]{1,0:T(8,128)(2,1)S(1)} %copy-done.2), custom_call_target="tpu_custom_call" | custom-call | flops 1000000000 | bytes 4000000 | tf_op jit(solution)/shard_map/own_source/pallas_call | solution.py:282
  23.2 0.0 collective-permute-done.left
  23.3 0.0 collective-permute-done.1.right
  23.3 0.0 copy-done.1
  23.3 3.9 %col_sources.1 = (bf16[2,5,2,128,128]{4,3,2,1,0:T(8,128)(2,1)}, f32[256,256]{1,0:T(8,128)S(1)}) custom-call(s32[200]{0:T(256)S(1)} %get-tuple-element.18.plan, bf16[64,128,128]{2,1,0:T(8,128)(2,1)S(1)} %bitcast.14, bf16[256,1024]{1,0:T(8,128)(2,1)S(1)} %get-tuple-element.19.turned, ...), custom_call_target="tpu_custom_call", output_to_operand_aliasing={{0}: (7, {})} | custom-call | tf_op jit(solution)/shard_map/col_sources/pallas_call | solution.py:313
  27.1 0.0 collective-permute-done.2.up
  27.2 0.0 collective-permute-done.3.down
  27.2 3.7 %row_sources.1 = (bf16[2,5,2,128,128]{4,3,2,1,0:T(8,128)(2,1)}, bf16[3,64,256]{2,1,0:T(8,128)(2,1)S(1)}, bf16[3,64,256]{2,1,0:T(8,128)(2,1)S(1)}, bf16[3,64,256]{2,1,0:T(8,128)(2,1)S(1)}, bf16[3,64,256]{2,1,0:T(8,128)(2,1)S(1)}) custom-call(s32[200]{0:T(256)S(1)} %get-tuple-element.18.plan, ...), custom_call_target="tpu_custom_call", output_to_operand_aliasing={{0}: (7, {})} | custom-call | tf_op jit(solution)/shard_map/row_sources/pallas_call | solution.py:326
  30.8 2.1 %collective-permute-start.4 = (bf16[3,64,256]{2,1,0:T(8,128)(2,1)S(1)}, bf16[3,64,256]{2,1,0:T(8,128)(2,1)S(1)}, u32[]{:S(2)}, u32[]{:S(2)}) collective-permute-start(bf16[3,64,256]{2,1,0:T(8,128)(2,1)S(1)} %get-tuple-element.27), channel_id=1, source_target_pairs={{0,1},{1,2},{2,3},{3,0},{4,5},{5,6},{6,7},{7,4},{8,9},{9,10},{10,1... | collective-permute-start | bytes 294920 | tf_op jit(solution)/shard_map/ppermute | solution.py:241
  32.9 2.7 %collective-permute-start.5 = (bf16[3,64,256]{2,1,0:T(8,128)(2,1)S(1)}, bf16[3,64,256]{2,1,0:T(8,128)(2,1)S(1)}, u32[]{:S(2)}, u32[]{:S(2)}) collective-permute-start(bf16[3,64,256]{2,1,0:T(8,128)(2,1)S(1)} %get-tuple-element.28), channel_id=1, source_target_pairs={{0,2},{1,3},{2,0},{3,1},{4,6},{5,7},{6,4},{7,5},{8,10},{9,11},{10,... | collective-permute-start | bytes 294920 | tf_op jit(solution)/shard_map/ppermute | solution.py:241
  35.6 0.0 collective-permute-start.6
  35.6 0.5 collective-permute-done.4.refs_1_
  36.2 5.8 %collective-permute-done.5.refs_2_ = bf16[3,64,256]{2,1,0:T(8,128)(2,1)S(1)} collective-permute-done((bf16[3,64,256]{2,1,0:T(8,128)(2,1)S(1)}, bf16[3,64,256]{2,1,0:T(8,128)(2,1)S(1)}, u32[]{:S(2)}, u32[]{:S(2)}) %collective-permute-start.5) | collective-permute-done | bytes 98336 | tf_op jit(solution)/shard_map/ppermute | solution.py:241
  41.9 1.9 %collective-permute-done.6.refs_3_ = bf16[3,64,256]{2,1,0:T(8,128)(2,1)S(1)} collective-permute-done((bf16[3,64,256]{2,1,0:T(8,128)(2,1)S(1)}, bf16[3,64,256]{2,1,0:T(8,128)(2,1)S(1)}, u32[]{:S(2)}, u32[]{:S(2)}) %collective-permute-start.6) | collective-permute-done | bytes 98336 | tf_op jit(solution)/shard_map/ppermute | solution.py:241
  43.9 0.1 total.1.refs_0_
  43.9 0.1 collective-permute-start.7
  44.0 1.1 %collective-permute-start.8 = (bf16[3,64,256]{2,1,0:T(8,128)(2,1)S(1)}, bf16[3,64,256]{2,1,0:T(8,128)(2,1)S(1)}, u32[]{:S(2)}, u32[]{:S(2)}) collective-permute-start(bf16[3,64,256]{2,1,0:T(8,128)(2,1)S(1)} %total.1.refs_0_), channel_id=1, source_target_pairs={{0,2},{1,3},{2,0},{3,1},{4,6},{5,7},{6,4},{7,5},{8,10},{9,11},{10,... | collective-permute-start | bytes 294920 | tf_op jit(solution)/shard_map/ppermute | solution.py:241
  45.1 1.3 %collective-permute-start.9 = (bf16[3,64,256]{2,1,0:T(8,128)(2,1)S(1)}, bf16[3,64,256]{2,1,0:T(8,128)(2,1)S(1)}, u32[]{:S(2)}, u32[]{:S(2)}) collective-permute-start(bf16[3,64,256]{2,1,0:T(8,128)(2,1)S(1)} %total.1.refs_0_), channel_id=1, source_target_pairs={{0,3},{1,0},{2,1},{3,2},{4,7},{5,4},{6,5},{7,6},{8,11},{9,8},{10,9... | collective-permute-start | bytes 294920 | tf_op jit(solution)/shard_map/ppermute | solution.py:241
  46.5 1.5 %collective-permute-done.7.refs_1_ = bf16[3,64,256]{2,1,0:T(8,128)(2,1)S(1)} collective-permute-done((bf16[3,64,256]{2,1,0:T(8,128)(2,1)S(1)}, bf16[3,64,256]{2,1,0:T(8,128)(2,1)S(1)}, u32[]{:S(2)}, u32[]{:S(2)}) %collective-permute-start.7) | collective-permute-done | bytes 98336 | tf_op jit(solution)/shard_map/ppermute | solution.py:241
  48.0 1.9 %collective-permute-done.8.refs_2_ = bf16[3,64,256]{2,1,0:T(8,128)(2,1)S(1)} collective-permute-done((bf16[3,64,256]{2,1,0:T(8,128)(2,1)S(1)}, bf16[3,64,256]{2,1,0:T(8,128)(2,1)S(1)}, u32[]{:S(2)}, u32[]{:S(2)}) %collective-permute-start.8) | collective-permute-done | bytes 98336 | tf_op jit(solution)/shard_map/ppermute | solution.py:241
  49.8 4.9 %collective-permute-done.9.refs_3_ = bf16[3,64,256]{2,1,0:T(8,128)(2,1)S(1)} collective-permute-done((bf16[3,64,256]{2,1,0:T(8,128)(2,1)S(1)}, bf16[3,64,256]{2,1,0:T(8,128)(2,1)S(1)}, u32[]{:S(2)}, u32[]{:S(2)}) %collective-permute-start.9) | collective-permute-done | bytes 98336 | tf_op jit(solution)/shard_map/ppermute | solution.py:241
  54.8 0.9 %spread.1 = f32[2,3,2,128,128]{4,3,2,1,0:T(8,128)} custom-call(bf16[3,64,256]{2,1,0:T(8,128)(2,1)S(1)} %total.1.refs_0_, bf16[3,64,256]{2,1,0:T(8,128)(2,1)S(1)} %collective-permute-done.7.refs_1_, bf16[3,64,256]{2,1,0:T(8,128)(2,1)S(1)} %collective-permute-done.8.refs_2_, bf16[3,64,256]{2,1,0:T(8,128)(2,1)S(1)} %collective-permute-done.9.refs_3_), custom_call_target="tpu_custom_call" | custom-call | tf_op jit(solution)/shard_map/spread/pallas_call | solution.py:343
Async XLA Ops:
  5.0 18.3 %collective-permute-start = (bf16[1808,128]{1,0:T(8,128)(2,1)}, bf16[1808,128]{1,0:T(8,128)(2,1)S(1)}, u32[]{:S(2)}, u32[]{:S(2)}) collective-permute-start(bf16[1808,128]{1,0:T(8,128)(2,1)} %get-tuple-element.17.own), channel_id=1, source_target_pairs={{0,1},{1,2},{2,3},{4,5},{5,6},{6,7},{8,9},{9,10},{10,11},{12,13},{... | collective-permute-start | bytes 1388552 | tf_op jit(solution)/shard_map/ppermute | solution.py:241
  8.2 15.1 %collective-permute-start.1 = (bf16[1808,128]{1,0:T(8,128)(2,1)}, bf16[1808,128]{1,0:T(8,128)(2,1)S(1)}, u32[]{:S(2)}, u32[]{:S(2)}) collective-permute-start(bf16[1808,128]{1,0:T(8,128)(2,1)} %get-tuple-element.17.own), channel_id=1, source_target_pairs={{1,0},{2,1},{3,2},{5,4},{6,5},{7,6},{9,8},{10,9},{11,10},{13,12},{... | collective-permute-start | bytes 1388552 | tf_op jit(solution)/shard_map/ppermute | solution.py:241
  10.3 16.8 %collective-permute-start.2 = (bf16[1808,128]{1,0:T(8,128)(2,1)}, bf16[1808,128]{1,0:T(8,128)(2,1)S(1)}, u32[]{:S(2)}, u32[]{:S(2)}) collective-permute-start(bf16[1808,128]{1,0:T(8,128)(2,1)} %get-tuple-element.17.own), channel_id=1, source_target_pairs={{0,4},{4,8},{8,12},{12,16},{16,20},{20,24},{24,28},{1,5},{5,9},{9,... | collective-permute-start | bytes 1388552 | tf_op jit(solution)/shard_map/ppermute | solution.py:241
  14.5 12.6 %collective-permute-start.3 = (bf16[1808,128]{1,0:T(8,128)(2,1)}, bf16[1808,128]{1,0:T(8,128)(2,1)S(1)}, u32[]{:S(2)}, u32[]{:S(2)}) collective-permute-start(bf16[1808,128]{1,0:T(8,128)(2,1)} %get-tuple-element.17.own), channel_id=1, source_target_pairs={{4,0},{8,4},{12,8},{16,12},{20,16},{24,20},{28,24},{5,1},{9,5},{13... | collective-permute-start | bytes 1388552 | tf_op jit(solution)/shard_map/ppermute | solution.py:241
  16.5 1.6 %copy-start = (bf16[1,1,64,128,128]{4,3,2,1,0:T(8,128)(2,1)S(1)}, bf16[1,1,64,128,128]{4,3,2,1,0:T(8,128)(2,1)}, u32[]{:S(2)}) copy-start(bf16[1,1,64,128,128]{4,3,2,1,0:T(8,128)(2,1)} %param.9) | copy-start | bytes 6291460
  18.1 1.0 %copy-start.2 = (bf16[1808,128]{1,0:T(8,128)(2,1)S(1)}, bf16[1808,128]{1,0:T(8,128)(2,1)}, u32[]{:S(2)}) copy-start(bf16[1808,128]{1,0:T(8,128)(2,1)} %get-tuple-element.17.own) | copy-start | bytes 1388548
  19.1 0.7 %copy-start.3 = (s32[144]{0:T(256)S(1)}, s32[144]{0:T(256)}, u32[]{:S(2)}) copy-start(s32[144]{0:T(256)} %get-tuple-element.16.ints) | copy-start | bytes 1732
  19.8 3.5 %copy-start.1 = (bf16[1,1,64,128,128]{4,3,2,1,0:T(8,128)(2,1)S(1)}, bf16[1,1,64,128,128]{4,3,2,1,0:T(8,128)(2,1)}, u32[]{:S(2)}) copy-start(bf16[1,1,64,128,128]{4,3,2,1,0:T(8,128)(2,1)} %param.9) | copy-start | bytes 6291460
  30.8 5.3 %collective-permute-start.4 = (bf16[3,64,256]{2,1,0:T(8,128)(2,1)S(1)}, bf16[3,64,256]{2,1,0:T(8,128)(2,1)S(1)}, u32[]{:S(2)}, u32[]{:S(2)}) collective-permute-start(bf16[3,64,256]{2,1,0:T(8,128)(2,1)S(1)} %get-tuple-element.27), channel_id=1, source_target_pairs={{0,1},{1,2},{2,3},{3,0},{4,5},{5,6},{6,7},{7,4},{8,9},{9,10},{10,1... | collective-permute-start | bytes 294920 | tf_op jit(solution)/shard_map/ppermute | solution.py:241
  32.9 9.0 %collective-permute-start.5 = (bf16[3,64,256]{2,1,0:T(8,128)(2,1)S(1)}, bf16[3,64,256]{2,1,0:T(8,128)(2,1)S(1)}, u32[]{:S(2)}, u32[]{:S(2)}) collective-permute-start(bf16[3,64,256]{2,1,0:T(8,128)(2,1)S(1)} %get-tuple-element.28), channel_id=1, source_target_pairs={{0,2},{1,3},{2,0},{3,1},{4,6},{5,7},{6,4},{7,5},{8,10},{9,11},{10,... | collective-permute-start | bytes 294920 | tf_op jit(solution)/shard_map/ppermute | solution.py:241
  35.6 8.2 %collective-permute-start.6 = (bf16[3,64,256]{2,1,0:T(8,128)(2,1)S(1)}, bf16[3,64,256]{2,1,0:T(8,128)(2,1)S(1)}, u32[]{:S(2)}, u32[]{:S(2)}) collective-permute-start(bf16[3,64,256]{2,1,0:T(8,128)(2,1)S(1)} %get-tuple-element.29), channel_id=1, source_target_pairs={{0,3},{1,0},{2,1},{3,2},{4,7},{5,4},{6,5},{7,6},{8,11},{9,8},{10,9... | collective-permute-start | bytes 294920 | tf_op jit(solution)/shard_map/ppermute | solution.py:241
  43.9 4.0 %collective-permute-start.7 = (bf16[3,64,256]{2,1,0:T(8,128)(2,1)S(1)}, bf16[3,64,256]{2,1,0:T(8,128)(2,1)S(1)}, u32[]{:S(2)}, u32[]{:S(2)}) collective-permute-start(bf16[3,64,256]{2,1,0:T(8,128)(2,1)S(1)} %total.1.refs_0_), channel_id=1, source_target_pairs={{0,1},{1,2},{2,3},{3,0},{4,5},{5,6},{6,7},{7,4},{8,9},{9,10},{10,1... | collective-permute-start | bytes 294920 | tf_op jit(solution)/shard_map/ppermute | solution.py:241
  44.0 5.8 %collective-permute-start.8 = (bf16[3,64,256]{2,1,0:T(8,128)(2,1)S(1)}, bf16[3,64,256]{2,1,0:T(8,128)(2,1)S(1)}, u32[]{:S(2)}, u32[]{:S(2)}) collective-permute-start(bf16[3,64,256]{2,1,0:T(8,128)(2,1)S(1)} %total.1.refs_0_), channel_id=1, source_target_pairs={{0,2},{1,3},{2,0},{3,1},{4,6},{5,7},{6,4},{7,5},{8,10},{9,11},{10,... | collective-permute-start | bytes 294920 | tf_op jit(solution)/shard_map/ppermute | solution.py:241
  45.1 9.6 %collective-permute-start.9 = (bf16[3,64,256]{2,1,0:T(8,128)(2,1)S(1)}, bf16[3,64,256]{2,1,0:T(8,128)(2,1)S(1)}, u32[]{:S(2)}, u32[]{:S(2)}) collective-permute-start(bf16[3,64,256]{2,1,0:T(8,128)(2,1)S(1)} %total.1.refs_0_), channel_id=1, source_target_pairs={{0,3},{1,0},{2,1},{3,2},{4,7},{5,4},{6,5},{7,6},{8,11},{9,8},{10,9... | collective-permute-start | bytes 294920 | tf_op jit(solution)/shard_map/ppermute | solution.py:241

commit v5 on v4

v5 whole, which is shorter than its diff:
```python
import functools
import math

import jax
import jax.numpy as jnp
from jax import lax
from jax.experimental import pallas as pl
from jax.experimental.pallas import tpu as pltpu
from jax.sharding import PartitionSpec as P

FB = 8
CB = 2
G2 = 2
NS = 5
PB = FB * CB
UNROLL = 4
META = 16
F32 = jnp.float32
BF16 = jnp.bfloat16

VMEM = pl.BlockSpec(memory_space=pltpu.VMEM)
HBM = pl.BlockSpec(memory_space=pltpu.HBM)
SMALL = pltpu.CompilerParams(vmem_limit_bytes=4 * 1024 * 1024)
SMEM = pl.BlockSpec(memory_space=pltpu.SMEM)
LARGE = pltpu.CompilerParams(vmem_limit_bytes=20 * 1024 * 1024)
WHOLE = pltpu.CompilerParams(vmem_limit_bytes=60 * 1024 * 1024)


def pack_kernel(
    codes, count, aggs, rows, cols, f_count, blocks, second, out, ints, held, sems
):
    n_p, n_s = blocks.shape[0], second.shape[0]
    slots, cap = codes.shape[0], cols.shape[0]
    copies = [
        pltpu.make_async_copy(blocks, held.at[0:n_p], sems.at[0]),
        pltpu.make_async_copy(second, held.at[n_p : n_p + n_s], sems.at[1]),
    ]
    for copy in copies:
        copy.start()
    lane = lax.broadcasted_iota(jnp.int32, (META, out.shape[1]), 1)
    word = jnp.zeros(lane.shape, jnp.int32)
    for k in range(slots):
        code = jnp.where(k < count[0], codes[k], PB)
        ints[cap + k] = code
        word = jnp.where(lane == k, code, word)
    for j in range(CB):
        ints[cap + slots + j] = aggs[j]
        word = jnp.where(lane == slots + j, aggs[j], word)
    ints[cap + slots + CB] = f_count[0]
    held[n_p + n_s : n_p + n_s + META, :] = word.astype(F32).astype(BF16)
    for copy in copies:
        copy.wait()
    whole = pltpu.make_async_copy(held, out, sems.at[2])
    whole.start()
    for k in range(cap):
        ints[k] = cols[k] * FB + rows[k]
    whole.wait()


def fill_table(s, slots, table, code_of):
    for q in range(PB + 1):
        table[s, q] = -1
    for k in range(slots):
        table[s, code_of(k)] = k


def block_at(s, q, size, table, near):
    slot = table[s, q]
    block = near[pl.ds(pl.multiple_of(jnp.maximum(slot, 0) * size, size), size), :]
    return jnp.where(slot >= 0, block, jnp.zeros_like(block))


def lift_of(near, slots, size, agg_of):
    lines = []
    for j in range(CB):
        block = near[(slots + j) * size : (slots + j + 1) * size, :]
        lines.append(
            jnp.concatenate(
                [jnp.where(agg_of(j) == a, block, jnp.zeros_like(block)) for a in range(G2)],
                axis=1,
            )
        )
    return jnp.concatenate(lines, axis=0)


def dense_of(s, size, table, near, dense):
    for i in range(FB):
        for j in range(CB):
            dense[i * size : (i + 1) * size, j * size : (j + 1) * size] = block_at(
                s, i * CB + j, size, table, near
            )


def coarse_of(size, weight, dense, tile):
    coarse = jnp.dot(weight, dense[...], preferred_element_type=F32).astype(BF16)
    for i in range(CB):
        for j in range(CB):
            tile[i, j] = coarse[i * size : (i + 1) * size, j * size : (j + 1) * size]
    return coarse


def own_kernel(
    slots, size, ints, fine, own, weights, half, lift_t, c_one, turned, acc, dense, tile, table, sem
):
    acc[...] = jnp.zeros_like(acc)
    cap = fine.shape[0]
    fill_table(0, slots, table, lambda k: ints[cap + k])
    for i in range(FB):
        for j in range(CB):
            block = block_at(0, i * CB + j, size, table, own)
            turned[i, j * size : (j + 1) * size, :] = block.T
    count = ints[cap + slots + CB]

    def step(t, carry):
        products, targets = [], []
        for u in range(UNROLL):
            k = t * UNROLL + u
            at = jnp.where(k < count, ints[k], NS * FB * FB)
            col = at // FB
            products.append(jnp.dot(turned[at - col * FB], fine[k], preferred_element_type=F32))
            targets.append(col)
        for u in range(UNROLL):
            acc[targets[u]] += products[u]
        return carry

    lax.fori_loop(0, (count + UNROLL - 1) // UNROLL, step, 0)
    own_weight = jnp.concatenate([acc[m].astype(BF16) for m in range(FB)], axis=1)
    dense_of(0, size, table, own, dense)
    coarse = coarse_of(size, own_weight, dense, tile)
    store = pltpu.make_async_copy(tile, c_one.at[:, 0], sem)
    store.start()
    for s in range(1, NS):
        for m in range(FB):
            weights[s - 1, :, m * size : (m + 1) * size] = acc[s * FB + m].astype(BF16)
    lift = lift_of(own, slots, size, lambda j: ints[cap + slots + j])
    half[...] = jnp.dot(coarse, lift, preferred_element_type=F32)
    lift_t[...] = lift.T
    store.wait()


def near_coarse(
    sources, near, slots, size, weights, c_one, dense, tiles, words, codes, table, sems
):
    tail = (slots + CB) * size
    for n, ref in enumerate(near):
        word = ref[tail : tail + META, :].astype(F32).astype(jnp.int32)
        words[n : n + 1, :] = word[0:1, :]
    fetch = pltpu.make_async_copy(words, codes, sems.at[0])
    fetch.start()
    fetch.wait()
    parts, stores = [], []
    for n, (s, ref) in enumerate(zip(sources, near)):
        fill_table(n, slots, table, lambda k: codes[n, k])
        dense_of(n, size, table, ref, dense.at[n])
        coarse = coarse_of(size, weights[s - 1], dense.at[n], tiles.at[n])
        store = pltpu.make_async_copy(tiles.at[n], c_one.at[:, s], sems.at[1 + n])
        store.start()
        stores.append(store)
        lift = lift_of(ref, slots, size, lambda j: codes[n, slots + j])
        parts.append(jnp.dot(coarse, lift, preferred_element_type=F32))
    return parts, stores


def side_kernel(slots, size, weights, half, lift_t, left, right, c_in, c_one, term, *scratch):
    parts, stores = near_coarse((1, 2), (left, right), slots, size, weights, c_one, *scratch)
    whole = (half[...] + parts[0] + parts[1]).astype(BF16)
    term[...] = jnp.dot(lift_t[...], whole, preferred_element_type=F32)
    for store in stores:
        store.wait()


def row_kernel(slots, size, cols_n, weights, term, lift_t, up, down, c_in, c_one, *rest):
    sends, terms, scratch = rest[:cols_n], rest[cols_n], rest[cols_n + 1 :]
    parts, stores = near_coarse((3, 4), (up, down), slots, size, weights, c_one, *scratch)
    terms[0] = term[...]
    for g in range(2):
        terms[1 + g] = jnp.dot(lift_t[...], parts[g].astype(BF16), preferred_element_type=F32)
    chunk = terms.shape[1] // cols_n
    me = lax.axis_index("col")
    for d in range(cols_n):
        to = pl.multiple_of(lax.rem(me + d, cols_n) * chunk, chunk)
        sends[d][...] = terms[:, pl.ds(to, chunk), :].astype(sends[d].dtype)
    for store in stores:
        store.wait()


def sum_kernel(*refs):
    total = refs[0][...]
    for ref in refs[1:-1]:
        total = total + ref[...].astype(F32)
    refs[-1][...] = total.astype(BF16)


def spread_kernel(size, cols_n, *refs):
    out = refs[-1]
    chunk = refs[0].shape[1]
    unit = math.gcd(chunk, size)
    per = size // unit
    me = lax.axis_index("col")
    for d in range(cols_n):
        owner = lax.rem(me - d + cols_n, cols_n)
        for t in range(chunk // unit):
            at = owner * (chunk // unit) + t
            a = at // per
            h = pl.multiple_of(lax.rem(at, per) * unit, unit)
            for g in range(3):
                for b in range(G2):
                    out[a, g, b, pl.ds(h, unit), :] = refs[d][
                        g, t * unit : (t + 1) * unit, b * size : (b + 1) * size
                    ].astype(F32)


def shift(x, axis, step, wrap):
    n = lax.axis_size(axis)
    pairs = [(i, (i + step) % n) for i in range(n) if wrap or 0 <= i + step < n]
    return lax.ppermute(x, axis, pairs)


def per_device(
    fine_blocks, fine_rows, fine_cols, fine_counts, prolong_blocks, prolong_codes,
    prolong_counts, second_blocks, second_aggs,
):
    slots, size = prolong_blocks.shape[2], prolong_blocks.shape[3]
    cap = fine_blocks.shape[2]
    cols_n = lax.axis_size("col")
    packed_rows = (slots + CB) * size + META
    wide = CB * size
    dma = pltpu.SemaphoreType.DMA
    packed, ints = pl.pallas_call(
        pack_kernel,
        out_shape=[
            jax.ShapeDtypeStruct((packed_rows, size), BF16),
            jax.ShapeDtypeStruct((cap + slots + CB + 2,), jnp.int32),
        ],
        in_specs=[SMEM] * 6 + [HBM] * 2,
        out_specs=[HBM, SMEM],
        scratch_shapes=[
            pltpu.VMEM((packed_rows, size), BF16),
            dma((3,)),
        ],
        compiler_params=WHOLE,
        name="pack",
    )(
        prolong_codes[0, 0], prolong_counts[0], second_aggs[0, 0],
        fine_rows[0, 0], fine_cols[0, 0], fine_counts[0],
        prolong_blocks.reshape(slots * size, size),
        second_blocks.reshape(CB * size, size),
    )
    up = shift(packed, "row", 1, False)
    down = shift(packed, "row", -1, False)
    left = shift(packed, "col", 1, False)
    right = shift(packed, "col", -1, False)

    c_shape = jax.ShapeDtypeStruct((CB, NS, CB, size, size), BF16)
    table = pltpu.SMEM((NS, PB + 1), jnp.int32)
    weights, half, lift_t, c_one = pl.pallas_call(
        functools.partial(own_kernel, slots, size),
        out_shape=[
            jax.ShapeDtypeStruct((NS - 1, wide, FB * size), BF16),
            jax.ShapeDtypeStruct((wide, G2 * size), F32),
            jax.ShapeDtypeStruct((G2 * size, wide), BF16),
            c_shape,
        ],
        in_specs=[SMEM, VMEM, VMEM],
        out_specs=[VMEM] * 3 + [HBM],
        scratch_shapes=[
            pltpu.VMEM((FB, wide, size), BF16),
            pltpu.VMEM((NS * FB + 1, wide, size), F32),
            pltpu.VMEM((FB * size, wide), BF16),
            pltpu.VMEM((CB, CB, size, size), BF16),
            table,
            dma,
        ],
        compiler_params=LARGE,
        cost_estimate=pl.CostEstimate(flops=10**9, bytes_accessed=4 * 10**6, transcendentals=0),
        name="own_source",
    )(ints, fine_blocks[0, 0], packed)

    near_scratch = [
        pltpu.VMEM((2, FB * size, wide), BF16),
        pltpu.VMEM((2, CB, CB, size, size), BF16),
        pltpu.VMEM((8, size), jnp.int32),
        pltpu.SMEM((8, size), jnp.int32),
        table,
        dma((3,)),
    ]
    square = jax.ShapeDtypeStruct((wide, G2 * size), F32)
    c_one, term = pl.pallas_call(
        functools.partial(side_kernel, slots, size),
        out_shape=[c_shape, square],
        in_specs=[VMEM] * 5 + [HBM],
        out_specs=[HBM, VMEM],
        input_output_aliases={5: 0},
        scratch_shapes=near_scratch,
        compiler_params=LARGE,
        name="col_sources",
    )(weights, half, lift_t, left, right, c_one)

    chunk = G2 * size // cols_n
    kept = jax.ShapeDtypeStruct((3, chunk, G2 * size), F32)
    piece = jax.ShapeDtypeStruct(kept.shape, BF16)
    c_one, *sends = pl.pallas_call(
        functools.partial(row_kernel, slots, size, cols_n),
        out_shape=[c_shape, kept] + [piece] * (cols_n - 1),
        in_specs=[VMEM] * 5 + [HBM],
        out_specs=[HBM] + [VMEM] * cols_n,
        input_output_aliases={5: 0},
        scratch_shapes=[pltpu.VMEM((3, G2 * size, G2 * size), F32)] + near_scratch,
        compiler_params=LARGE,
        name="row_sources",
    )(weights, term, lift_t, up, down, c_one)
    parts = [sends[0]] + [shift(sends[d], "col", d, True) for d in range(1, cols_n)]
    total = pl.pallas_call(
        sum_kernel, out_shape=piece, in_specs=[VMEM] * cols_n, out_specs=VMEM,
        compiler_params=SMALL, name="total",
    )(*parts)
    gathered = [total] + [shift(total, "col", d, True) for d in range(1, cols_n)]
    c_two = pl.pallas_call(
        functools.partial(spread_kernel, size, cols_n),
        out_shape=jax.ShapeDtypeStruct((G2, 3, G2, size, size), F32),
        in_specs=[VMEM] * cols_n,
        out_specs=VMEM,
        compiler_params=SMALL,
        name="spread",
    )(*gathered)
    return (c_one[None, None], c_two[None])


def solution(mesh):
    in_specs = (
        P("row", "col", None, None, None),
        P("row", "col", None),
        P("row", "col", None),
        P("row", "col"),
        P("row", "col", None, None, None),
        P("row", "col", None),
        P("row", "col"),
        P("row", "col", None, None, None),
        P("row", "col", None),
    )
    out_specs = (
        P("row", "col", None, None, None, None, None),
        P("row", None, None, None, None, None),
    )
    return jax.shard_map(
        per_device, mesh=mesh, in_specs=in_specs, out_specs=out_specs, check_vma=False
    )
```

time: 56.5 us -> 53.6 us (0.949); the launches traced: 55.7 us -> 54.1 us
  waiting for transfers between devices: 16.5 us -> 15.8 us
    pallas_call x1, Pallas kernels: 3.46 us -> 6.16 us  [per_device(): pl.pallas_call(functools.partial(own_kernel, slots, size), out_shape=[jax...]
    pallas_call x1, Pallas kernels: 3.86 us -> 2.17 us  [per_device(): pl.pallas_call(functools.partial(side_kernel, slots, size), out_shape=[c_...]
    pallas_call x1, Pallas kernels: 3.65 us -> 2.17 us  [per_device(): pl.pallas_call(functools.partial(row_kernel, slots, size, cols_n), out_sh...]
    ppermute x10, waiting for transfers between devices: 16.5 us -> 15.8 us  [shift(): return lax.ppermute(x, axis, pairs)]
    unnamed x8 -> x6, local copies, waits for them, and re-layouts: 3.29 us -> 3.18 us
  transfers between devices with their start and end apart: 10 -> 10, of which waited for: 6 -> 4; matrix products, arithmetic and copies ran while one was open for 0% -> 0% of each run, Pallas kernels for 13% -> 15%
where the time goes in v5:
time: 53.6 us; the launch traced here: 54.1 us
  starting transfers between devices  18.6 us (35%)
  waiting for transfers between devices  15.8 us (29%)
  Pallas kernels  14.5 us (27%)
  local copies, waits for them, and re-layouts  3.18 us (6%)
  between operations  2.05 us (4%)
    ppermute x10, starting transfers between devices, shift(): return lax.ppermute(x, axis, pairs)  18.6 us
    ppermute x10, waiting for transfers between devices, shift(): return lax.ppermute(x, axis, pairs)  15.8 us
    pallas_call x1, Pallas kernels, per_device(): pl.pallas_call(functools.partial(own_kernel, slots, size), out_shape=[jax...  6.16 us
    unnamed x6, local copies, waits for them, and re-layouts  3.18 us
    pallas_call x1, Pallas kernels, per_device(): pl.pallas_call(pack_kernel, out_shape=[jax.ShapeDtypeStruct((packed_rows,...  3 us
    pallas_call x1, Pallas kernels, per_device(): pl.pallas_call(functools.partial(side_kernel, slots, size), out_shape=[c_...  2.17 us
    pallas_call x1, Pallas kernels, per_device(): pl.pallas_call(functools.partial(row_kernel, slots, size, cols_n), out_sh...  2.17 us
  transfers between devices with their start and end apart: 10, of which 4 were waited for; matrix products, arithmetic and copies ran while one was open for 0% of the time, Pallas kernels for 15%

profile of v5, /device:TPU:13, one launch (start us, length us, event | category | flops | bytes accessed | tf_op | source)
XLA Modules:
  0.0 54.1 jit_solution(14027711204760687431)
XLA Ops:
  1.9 3.0 %pack.1 = (bf16[1808,128]{1,0:T(8,128)(2,1)}, s32[80]{0:T(128)}) custom-call(s32[12]{0:T(128)} %bitcast.18, s32[1]{0:T(128)} %bitcast.12.count, s32[2]{0:T(128)} %bitcast.19, s32[64]{0:T(128)} %bitcast.20, s32[64]{0:T(128)} %bitcast.21, s32[1]{0:T(128)} %bitcast.11.f_count, bf16[1536,128]{1,0:T(8,128)(2,1)} %bitcast.16, bf16[256,128]{1,0:T(8,128)(2,1)} %bitcast.17), custom_call_target="tpu_custom_call" | custom-call | tf_op jit(solution)/shard_map/pack/pallas_call | solution.py:229
  4.9 3.2 %collective-permute-start = (bf16[1808,128]{1,0:T(8,128)(2,1)}, bf16[1808,128]{1,0:T(8,128)(2,1)S(1)}, u32[]{:S(2)}, u32[]{:S(2)}) collective-permute-start(bf16[1808,128]{1,0:T(8,128)(2,1)} %get-tuple-element.16.own), channel_id=1, source_target_pairs={{0,1},{1,2},{2,3},{4,5},{5,6},{6,7},{8,9},{9,10},{10,11},{12,13},{... | collective-permute-start | bytes 1388552 | tf_op jit(solution)/shard_map/ppermute | solution.py:216
  8.1 2.1 %collective-permute-start.1 = (bf16[1808,128]{1,0:T(8,128)(2,1)}, bf16[1808,128]{1,0:T(8,128)(2,1)S(1)}, u32[]{:S(2)}, u32[]{:S(2)}) collective-permute-start(bf16[1808,128]{1,0:T(8,128)(2,1)} %get-tuple-element.16.own), channel_id=1, source_target_pairs={{1,0},{2,1},{3,2},{5,4},{6,5},{7,6},{9,8},{10,9},{11,10},{13,12},{... | collective-permute-start | bytes 1388552 | tf_op jit(solution)/shard_map/ppermute | solution.py:216
  10.2 4.2 %collective-permute-start.2 = (bf16[1808,128]{1,0:T(8,128)(2,1)}, bf16[1808,128]{1,0:T(8,128)(2,1)S(1)}, u32[]{:S(2)}, u32[]{:S(2)}) collective-permute-start(bf16[1808,128]{1,0:T(8,128)(2,1)} %get-tuple-element.16.own), channel_id=1, source_target_pairs={{0,4},{4,8},{8,12},{12,16},{16,20},{20,24},{24,28},{1,5},{5,9},{9,... | collective-permute-start | bytes 1388552 | tf_op jit(solution)/shard_map/ppermute | solution.py:216
  14.5 1.9 %collective-permute-start.3 = (bf16[1808,128]{1,0:T(8,128)(2,1)}, bf16[1808,128]{1,0:T(8,128)(2,1)S(1)}, u32[]{:S(2)}, u32[]{:S(2)}) collective-permute-start(bf16[1808,128]{1,0:T(8,128)(2,1)} %get-tuple-element.16.own), channel_id=1, source_target_pairs={{4,0},{8,4},{12,8},{16,12},{20,16},{24,20},{28,24},{5,1},{9,5},{13... | collective-permute-start | bytes 1388552 | tf_op jit(solution)/shard_map/ppermute | solution.py:216
  16.4 0.0 copy-start
  16.4 1.6 %copy-done = bf16[1,1,64,128,128]{4,3,2,1,0:T(8,128)(2,1)S(1)} copy-done((bf16[1,1,64,128,128]{4,3,2,1,0:T(8,128)(2,1)S(1)}, bf16[1,1,64,128,128]{4,3,2,1,0:T(8,128)(2,1)}, u32[]{:S(2)}) %copy-start) | copy-done | bytes 2097176
  18.0 0.0 copy-start.1
  18.0 1.0 %copy-done.1 = bf16[1808,128]{1,0:T(8,128)(2,1)S(1)} copy-done((bf16[1808,128]{1,0:T(8,128)(2,1)S(1)}, bf16[1808,128]{1,0:T(8,128)(2,1)}, u32[]{:S(2)}) %copy-start.1) | copy-done | bytes 462872
  19.0 0.0 copy-start.2
  19.0 0.6 %copy-done.2 = s32[80]{0:T(128)S(1)} copy-done((s32[80]{0:T(128)S(1)}, s32[80]{0:T(128)}, u32[]{:S(2)}) %copy-start.2) | copy-done | bytes 344
  19.6 6.2 %own_source.1 = (bf16[4,256,1024]{2,1,0:T(8,128)(2,1)S(1)}, f32[256,256]{1,0:T(8,128)S(1)}, bf16[256,256]{1,0:T(8,128)(2,1)S(1)}, bf16[2,5,2,128,128]{4,3,2,1,0:T(8,128)(2,1)}) custom-call(s32[80]{0:T(128)S(1)} %copy-done.2, bf16[64,128,128]{2,1,0:T(8,128)(2,1)S(1)} %bitcast.13, bf16[1808,128]{1,0:T(8,128)(2,1)S(1)} %copy-done.1), custom_call_target="tpu_custom_call" | custom-call | flops 1000000000 | bytes 4000000 | tf_op jit(solution)/shard_map/own_source/pallas_call | solution.py:256
  25.8 0.0 collective-permute-done.left
  25.8 0.0 collective-permute-done.1.right
  25.8 2.2 %col_sources.1 = (bf16[2,5,2,128,128]{4,3,2,1,0:T(8,128)(2,1)}, f32[256,256]{1,0:T(8,128)S(1)}) custom-call(bf16[4,256,1024]{2,1,0:T(8,128)(2,1)S(1)} %get-tuple-element.17.weights, f32[256,256]{1,0:T(8,128)S(1)} %get-tuple-element.18.half, bf16[256,256]{1,0:T(8,128)(2,1)S(1)} %get-tuple-element.19.lift_t, ...), custom_call_target="tpu_custom_call", output_to_operand_aliasing={{0}: (5, {})} | custom-call | tf_op jit(solution)/shard_map/col_sources/pallas_call | solution.py:288
  28.0 0.0 collective-permute-done.2.up
  28.0 0.0 collective-permute-done.3.down
  28.0 2.2 %row_sources.1 = (bf16[2,5,2,128,128]{4,3,2,1,0:T(8,128)(2,1)}, f32[3,64,256]{2,1,0:T(8,128)S(1)}, bf16[3,64,256]{2,1,0:T(8,128)(2,1)S(1)}, bf16[3,64,256]{2,1,0:T(8,128)(2,1)S(1)}, bf16[3,64,256]{2,1,0:T(8,128)(2,1)S(1)}) custom-call(bf16[4,256,1024]{2,1,0:T(8,128)(2,1)S(1)} %get-tuple-element.17.weights, ...), custom_call_target="tpu_custom_call", output_to_operand_aliasing={{0}: (5, {})} | custom-call | tf_op jit(solution)/shard_map/row_sources/pallas_call | solution.py:302
  30.2 1.3 %collective-permute-start.4 = (bf16[3,64,256]{2,1,0:T(8,128)(2,1)S(1)}, bf16[3,64,256]{2,1,0:T(8,128)(2,1)S(1)}, u32[]{:S(2)}, u32[]{:S(2)}) collective-permute-start(bf16[3,64,256]{2,1,0:T(8,128)(2,1)S(1)} %get-tuple-element.25), channel_id=1, source_target_pairs={{0,1},{1,2},{2,3},{3,0},{4,5},{5,6},{6,7},{7,4},{8,9},{9,10},{10,1... | collective-permute-start | bytes 294920 | tf_op jit(solution)/shard_map/ppermute | solution.py:216
  31.5 0.0 collective-permute-start.5
  31.5 1.3 %collective-permute-start.6 = (bf16[3,64,256]{2,1,0:T(8,128)(2,1)S(1)}, bf16[3,64,256]{2,1,0:T(8,128)(2,1)S(1)}, u32[]{:S(2)}, u32[]{:S(2)}) collective-permute-start(bf16[3,64,256]{2,1,0:T(8,128)(2,1)S(1)} %get-tuple-element.27), channel_id=1, source_target_pairs={{0,3},{1,0},{2,1},{3,2},{4,7},{5,4},{6,5},{7,6},{8,11},{9,8},{10,9... | collective-permute-start | bytes 294920 | tf_op jit(solution)/shard_map/ppermute | solution.py:216
  32.8 5.5 %collective-permute-done.4.refs_1_ = bf16[3,64,256]{2,1,0:T(8,128)(2,1)S(1)} collective-permute-done((bf16[3,64,256]{2,1,0:T(8,128)(2,1)S(1)}, bf16[3,64,256]{2,1,0:T(8,128)(2,1)S(1)}, u32[]{:S(2)}, u32[]{:S(2)}) %collective-permute-start.4) | collective-permute-done | bytes 98336 | tf_op jit(solution)/shard_map/ppermute | solution.py:216
  38.3 2.1 %collective-permute-done.5.refs_2_ = bf16[3,64,256]{2,1,0:T(8,128)(2,1)S(1)} collective-permute-done((bf16[3,64,256]{2,1,0:T(8,128)(2,1)S(1)}, bf16[3,64,256]{2,1,0:T(8,128)(2,1)S(1)}, u32[]{:S(2)}, u32[]{:S(2)}) %collective-permute-start.5) | collective-permute-done | bytes 98336 | tf_op jit(solution)/shard_map/ppermute | solution.py:216
  40.4 0.0 collective-permute-done.6.refs_3_
  40.4 0.1 total.1.refs_0_
  40.5 0.1 collective-permute-start.7
  40.6 3.1 %collective-permute-start.8 = (bf16[3,64,256]{2,1,0:T(8,128)(2,1)S(1)}, bf16[3,64,256]{2,1,0:T(8,128)(2,1)S(1)}, u32[]{:S(2)}, u32[]{:S(2)}) collective-permute-start(bf16[3,64,256]{2,1,0:T(8,128)(2,1)S(1)} %total.1.refs_0_), channel_id=1, source_target_pairs={{0,2},{1,3},{2,0},{3,1},{4,6},{5,7},{6,4},{7,5},{8,10},{9,11},{10,... | collective-permute-start | bytes 294920 | tf_op jit(solution)/shard_map/ppermute | solution.py:216
  43.6 1.4 %collective-permute-start.9 = (bf16[3,64,256]{2,1,0:T(8,128)(2,1)S(1)}, bf16[3,64,256]{2,1,0:T(8,128)(2,1)S(1)}, u32[]{:S(2)}, u32[]{:S(2)}) collective-permute-start(bf16[3,64,256]{2,1,0:T(8,128)(2,1)S(1)} %total.1.refs_0_), channel_id=1, source_target_pairs={{0,3},{1,0},{2,1},{3,2},{4,7},{5,4},{6,5},{7,6},{8,11},{9,8},{10,9... | collective-permute-start | bytes 294920 | tf_op jit(solution)/shard_map/ppermute | solution.py:216
  45.0 0.0 collective-permute-done.7.refs_1_
  45.0 3.5 %collective-permute-done.8.refs_2_ = bf16[3,64,256]{2,1,0:T(8,128)(2,1)S(1)} collective-permute-done((bf16[3,64,256]{2,1,0:T(8,128)(2,1)S(1)}, bf16[3,64,256]{2,1,0:T(8,128)(2,1)S(1)}, u32[]{:S(2)}, u32[]{:S(2)}) %collective-permute-start.8) | collective-permute-done | bytes 98336 | tf_op jit(solution)/shard_map/ppermute | solution.py:216
  48.5 4.6 %collective-permute-done.9.refs_3_ = bf16[3,64,256]{2,1,0:T(8,128)(2,1)S(1)} collective-permute-done((bf16[3,64,256]{2,1,0:T(8,128)(2,1)S(1)}, bf16[3,64,256]{2,1,0:T(8,128)(2,1)S(1)}, u32[]{:S(2)}, u32[]{:S(2)}) %collective-permute-start.9) | collective-permute-done | bytes 98336 | tf_op jit(solution)/shard_map/ppermute | solution.py:216
  53.1 0.9 %spread.1 = f32[2,3,2,128,128]{4,3,2,1,0:T(8,128)} custom-call(bf16[3,64,256]{2,1,0:T(8,128)(2,1)S(1)} %total.1.refs_0_, bf16[3,64,256]{2,1,0:T(8,128)(2,1)S(1)} %collective-permute-done.7.refs_1_, bf16[3,64,256]{2,1,0:T(8,128)(2,1)S(1)} %collective-permute-done.8.refs_2_, bf16[3,64,256]{2,1,0:T(8,128)(2,1)S(1)} %collective-permute-done.9.refs_3_), custom_call_target="tpu_custom_call" | custom-call | tf_op jit(solution)/shard_map/spread/pallas_call | solution.py:318
Async XLA Ops:
  4.9 20.9 %collective-permute-start = (bf16[1808,128]{1,0:T(8,128)(2,1)}, bf16[1808,128]{1,0:T(8,128)(2,1)S(1)}, u32[]{:S(2)}, u32[]{:S(2)}) collective-permute-start(bf16[1808,128]{1,0:T(8,128)(2,1)} %get-tuple-element.16.own), channel_id=1, source_target_pairs={{0,1},{1,2},{2,3},{4,5},{5,6},{6,7},{8,9},{9,10},{10,11},{12,13},{... | collective-permute-start | bytes 1388552 | tf_op jit(solution)/shard_map/ppermute | solution.py:216
  8.1 17.7 %collective-permute-start.1 = (bf16[1808,128]{1,0:T(8,128)(2,1)}, bf16[1808,128]{1,0:T(8,128)(2,1)S(1)}, u32[]{:S(2)}, u32[]{:S(2)}) collective-permute-start(bf16[1808,128]{1,0:T(8,128)(2,1)} %get-tuple-element.16.own), channel_id=1, source_target_pairs={{1,0},{2,1},{3,2},{5,4},{6,5},{7,6},{9,8},{10,9},{11,10},{13,12},{... | collective-permute-start | bytes 1388552 | tf_op jit(solution)/shard_map/ppermute | solution.py:216
  10.2 17.7 %collective-permute-start.2 = (bf16[1808,128]{1,0:T(8,128)(2,1)}, bf16[1808,128]{1,0:T(8,128)(2,1)S(1)}, u32[]{:S(2)}, u32[]{:S(2)}) collective-permute-start(bf16[1808,128]{1,0:T(8,128)(2,1)} %get-tuple-element.16.own), channel_id=1, source_target_pairs={{0,4},{4,8},{8,12},{12,16},{16,20},{20,24},{24,28},{1,5},{5,9},{9,... | collective-permute-start | bytes 1388552 | tf_op jit(solution)/shard_map/ppermute | solution.py:216
  14.5 13.5 %collective-permute-start.3 = (bf16[1808,128]{1,0:T(8,128)(2,1)}, bf16[1808,128]{1,0:T(8,128)(2,1)S(1)}, u32[]{:S(2)}, u32[]{:S(2)}) collective-permute-start(bf16[1808,128]{1,0:T(8,128)(2,1)} %get-tuple-element.16.own), channel_id=1, source_target_pairs={{4,0},{8,4},{12,8},{16,12},{20,16},{24,20},{28,24},{5,1},{9,5},{13... | collective-permute-start | bytes 1388552 | tf_op jit(solution)/shard_map/ppermute | solution.py:216
  16.4 1.6 %copy-start = (bf16[1,1,64,128,128]{4,3,2,1,0:T(8,128)(2,1)S(1)}, bf16[1,1,64,128,128]{4,3,2,1,0:T(8,128)(2,1)}, u32[]{:S(2)}) copy-start(bf16[1,1,64,128,128]{4,3,2,1,0:T(8,128)(2,1)} %param.9) | copy-start | bytes 6291460
  18.0 1.0 %copy-start.1 = (bf16[1808,128]{1,0:T(8,128)(2,1)S(1)}, bf16[1808,128]{1,0:T(8,128)(2,1)}, u32[]{:S(2)}) copy-start(bf16[1808,128]{1,0:T(8,128)(2,1)} %get-tuple-element.16.own) | copy-start | bytes 1388548
  19.0 0.6 %copy-start.2 = (s32[80]{0:T(128)S(1)}, s32[80]{0:T(128)}, u32[]{:S(2)}) copy-start(s32[80]{0:T(128)} %get-tuple-element.15.ints) | copy-start | bytes 964
  30.2 8.1 %collective-permute-start.4 = (bf16[3,64,256]{2,1,0:T(8,128)(2,1)S(1)}, bf16[3,64,256]{2,1,0:T(8,128)(2,1)S(1)}, u32[]{:S(2)}, u32[]{:S(2)}) collective-permute-start(bf16[3,64,256]{2,1,0:T(8,128)(2,1)S(1)} %get-tuple-element.25), channel_id=1, source_target_pairs={{0,1},{1,2},{2,3},{3,0},{4,5},{5,6},{6,7},{7,4},{8,9},{9,10},{10,1... | collective-permute-start | bytes 294920 | tf_op jit(solution)/shard_map/ppermute | solution.py:216
  31.5 8.9 %collective-permute-start.5 = (bf16[3,64,256]{2,1,0:T(8,128)(2,1)S(1)}, bf16[3,64,256]{2,1,0:T(8,128)(2,1)S(1)}, u32[]{:S(2)}, u32[]{:S(2)}) collective-permute-start(bf16[3,64,256]{2,1,0:T(8,128)(2,1)S(1)} %get-tuple-element.26), channel_id=1, source_target_pairs={{0,2},{1,3},{2,0},{3,1},{4,6},{5,7},{6,4},{7,5},{8,10},{9,11},{10,... | collective-permute-start | bytes 294920 | tf_op jit(solution)/shard_map/ppermute | solution.py:216
  31.5 8.9 %collective-permute-start.6 = (bf16[3,64,256]{2,1,0:T(8,128)(2,1)S(1)}, bf16[3,64,256]{2,1,0:T(8,128)(2,1)S(1)}, u32[]{:S(2)}, u32[]{:S(2)}) collective-permute-start(bf16[3,64,256]{2,1,0:T(8,128)(2,1)S(1)} %get-tuple-element.27), channel_id=1, source_target_pairs={{0,3},{1,0},{2,1},{3,2},{4,7},{5,4},{6,5},{7,6},{8,11},{9,8},{10,9... | collective-permute-start | bytes 294920 | tf_op jit(solution)/shard_map/ppermute | solution.py:216
  40.5 4.5 %collective-permute-start.7 = (bf16[3,64,256]{2,1,0:T(8,128)(2,1)S(1)}, bf16[3,64,256]{2,1,0:T(8,128)(2,1)S(1)}, u32[]{:S(2)}, u32[]{:S(2)}) collective-permute-start(bf16[3,64,256]{2,1,0:T(8,128)(2,1)S(1)} %total.1.refs_0_), channel_id=1, source_target_pairs={{0,1},{1,2},{2,3},{3,0},{4,5},{5,6},{6,7},{7,4},{8,9},{9,10},{10,1... | collective-permute-start | bytes 294920 | tf_op jit(solution)/shard_map/ppermute | solution.py:216
  40.6 8.0 %collective-permute-start.8 = (bf16[3,64,256]{2,1,0:T(8,128)(2,1)S(1)}, bf16[3,64,256]{2,1,0:T(8,128)(2,1)S(1)}, u32[]{:S(2)}, u32[]{:S(2)}) collective-permute-start(bf16[3,64,256]{2,1,0:T(8,128)(2,1)S(1)} %total.1.refs_0_), channel_id=1, source_target_pairs={{0,2},{1,3},{2,0},{3,1},{4,6},{5,7},{6,4},{7,5},{8,10},{9,11},{10,... | collective-permute-start | bytes 294920 | tf_op jit(solution)/shard_map/ppermute | solution.py:216
  43.6 9.5 %collective-permute-start.9 = (bf16[3,64,256]{2,1,0:T(8,128)(2,1)S(1)}, bf16[3,64,256]{2,1,0:T(8,128)(2,1)S(1)}, u32[]{:S(2)}, u32[]{:S(2)}) collective-permute-start(bf16[3,64,256]{2,1,0:T(8,128)(2,1)S(1)} %total.1.refs_0_), channel_id=1, source_target_pairs={{0,3},{1,0},{2,1},{3,2},{4,7},{5,4},{6,5},{7,6},{8,11},{9,8},{10,9... | collective-permute-start | bytes 294920 | tf_op jit(solution)/shard_map/ppermute | solution.py:216

commit v6 on v5

--- a/solution.py
+++ b/solution.py
@@ -26,11 +26,9 @@
 WHOLE = pltpu.CompilerParams(vmem_limit_bytes=60 * 1024 * 1024)
 
 
-def pack_kernel(
-    codes, count, aggs, rows, cols, f_count, blocks, second, out, ints, held, sems
-):
+def pack_kernel(codes, count, aggs, blocks, second, out, held, sems):
     n_p, n_s = blocks.shape[0], second.shape[0]
-    slots, cap = codes.shape[0], cols.shape[0]
+    slots = codes.shape[0]
     copies = [
         pltpu.make_async_copy(blocks, held.at[0:n_p], sems.at[0]),
         pltpu.make_async_copy(second, held.at[n_p : n_p + n_s], sems.at[1]),
@@ -40,20 +38,14 @@
     lane = lax.broadcasted_iota(jnp.int32, (META, out.shape[1]), 1)
     word = jnp.zeros(lane.shape, jnp.int32)
     for k in range(slots):
-        code = jnp.where(k < count[0], codes[k], PB)
-        ints[cap + k] = code
-        word = jnp.where(lane == k, code, word)
+        word = jnp.where(lane == k, jnp.where(k < count[0], codes[k], PB), word)
     for j in range(CB):
-        ints[cap + slots + j] = aggs[j]
         word = jnp.where(lane == slots + j, aggs[j], word)
-    ints[cap + slots + CB] = f_count[0]
     held[n_p + n_s : n_p + n_s + META, :] = word.astype(F32).astype(BF16)
     for copy in copies:
         copy.wait()
     whole = pltpu.make_async_copy(held, out, sems.at[2])
     whole.start()
-    for k in range(cap):
-        ints[k] = cols[k] * FB + rows[k]
     whole.wait()
 
 
@@ -100,46 +92,57 @@
 
 
 def own_kernel(
-    slots, size, ints, fine, own, weights, half, lift_t, c_one, turned, acc, dense, tile, table, sem
+    slots, size, rows, cols, count, codes, p_count, aggs, fine_at, own_at, stock_at, more_at, c_one,
+    fine, own, stock, more, turned, acc, dense, tile, table, sems,
 ):
+    fetch_own = pltpu.make_async_copy(own_at, own, sems.at[0])
+    fetch_own.start()
+    fetch_fine = pltpu.make_async_copy(fine_at, fine, sems.at[1])
+    fetch_fine.start()
     acc[...] = jnp.zeros_like(acc)
-    cap = fine.shape[0]
-    fill_table(0, slots, table, lambda k: ints[cap + k])
+    fill_table(0, slots, table, lambda k: jnp.where(k < p_count[0], codes[k], PB))
+    fetch_own.wait()
     for i in range(FB):
         for j in range(CB):
             block = block_at(0, i * CB + j, size, table, own)
             turned[i, j * size : (j + 1) * size, :] = block.T
-    count = ints[cap + slots + CB]
+    fetch_fine.wait()
 
     def step(t, carry):
         products, targets = [], []
         for u in range(UNROLL):
             k = t * UNROLL + u
-            at = jnp.where(k < count, ints[k], NS * FB * FB)
-            col = at // FB
-            products.append(jnp.dot(turned[at - col * FB], fine[k], preferred_element_type=F32))
-            targets.append(col)
+            products.append(jnp.dot(turned[rows[k]], fine[k], preferred_element_type=F32))
+            targets.append(jnp.where(k < count[0], cols[k], NS * FB))
         for u in range(UNROLL):
             acc[targets[u]] += products[u]
         return carry
 
-    lax.fori_loop(0, (count + UNROLL - 1) // UNROLL, step, 0)
+    lax.fori_loop(0, (count[0] + UNROLL - 1) // UNROLL, step, 0)
+    stores = []
+    for s in range(1, NS):
+        for m in range(FB):
+            stock[s - 1, :, m * size : (m + 1) * size] = acc[s * FB + m].astype(BF16)
+        stores.append(pltpu.make_async_copy(stock.at[s - 1], stock_at.at[s - 1], sems.at[1 + s]))
+        stores[-1].start()
     own_weight = jnp.concatenate([acc[m].astype(BF16) for m in range(FB)], axis=1)
     dense_of(0, size, table, own, dense)
     coarse = coarse_of(size, own_weight, dense, tile)
-    store = pltpu.make_async_copy(tile, c_one.at[:, 0], sem)
-    store.start()
-    for s in range(1, NS):
-        for m in range(FB):
-            weights[s - 1, :, m * size : (m + 1) * size] = acc[s * FB + m].astype(BF16)
-    lift = lift_of(own, slots, size, lambda j: ints[cap + slots + j])
-    half[...] = jnp.dot(coarse, lift, preferred_element_type=F32)
-    lift_t[...] = lift.T
-    store.wait()
+    lift = lift_of(own, slots, size, lambda j: aggs[j])
+    wide = CB * size
+    more[0] = lift.T
+    more[1] = coarse
+    more[2] = lift
+    stores.append(pltpu.make_async_copy(more, more_at, sems.at[0]))
+    stores[-1].start()
+    stores.append(pltpu.make_async_copy(tile, c_one.at[:, 0], sems.at[1]))
+    stores[-1].start()
+    for store in stores:
+        store.wait()
 
 
 def near_coarse(
-    sources, near, slots, size, weights, c_one, dense, tiles, words, codes, table, sems
+    sources, near, slots, size, stock, c_one, dense, tiles, words, codes, table, sems
 ):
     tail = (slots + CB) * size
     for n, ref in enumerate(near):
@@ -152,7 +155,7 @@
     for n, (s, ref) in enumerate(zip(sources, near)):
         fill_table(n, slots, table, lambda k: codes[n, k])
         dense_of(n, size, table, ref, dense.at[n])
-        coarse = coarse_of(size, weights[s - 1], dense.at[n], tiles.at[n])
+        coarse = coarse_of(size, stock[s - 1], dense.at[n], tiles.at[n])
         store = pltpu.make_async_copy(tiles.at[n], c_one.at[:, s], sems.at[1 + n])
         store.start()
         stores.append(store)
@@ -161,20 +164,27 @@
     return parts, stores
 
 
-def side_kernel(slots, size, weights, half, lift_t, left, right, c_in, c_one, term, *scratch):
-    parts, stores = near_coarse((1, 2), (left, right), slots, size, weights, c_one, *scratch)
+def half_kernel(more, lift_t, half):
+    lift_t[...] = more[0]
+    half[...] = jnp.dot(more[1], more[2], preferred_element_type=F32)
+
+
+def side_kernel(slots, size, stock, lift_t, half, left, right, c_in, c_one, term, *scratch):
+    parts, stores = near_coarse((1, 2), (left, right), slots, size, stock, c_one, *scratch)
     whole = (half[...] + parts[0] + parts[1]).astype(BF16)
     term[...] = jnp.dot(lift_t[...], whole, preferred_element_type=F32)
     for store in stores:
         store.wait()
 
 
-def row_kernel(slots, size, cols_n, weights, term, lift_t, up, down, c_in, c_one, *rest):
+def row_kernel(slots, size, cols_n, stock, lift_t, term, other, pair, c_in, c_one, *rest):
     sends, terms, scratch = rest[:cols_n], rest[cols_n], rest[cols_n + 1 :]
-    parts, stores = near_coarse((3, 4), (up, down), slots, size, weights, c_one, *scratch)
+    odd = lax.rem(lax.axis_index("row"), 2)
+    sources = (3 + odd, 4 - odd)
+    parts, stores = near_coarse(sources, (other, pair), slots, size, stock, c_one, *scratch)
     terms[0] = term[...]
-    for g in range(2):
-        terms[1 + g] = jnp.dot(lift_t[...], parts[g].astype(BF16), preferred_element_type=F32)
+    for n in range(2):
+        terms[sources[n] - 2] = jnp.dot(lift_t[...], parts[n].astype(BF16), preferred_element_type=F32)
     chunk = terms.shape[1] // cols_n
     me = lax.axis_index("col")
     for d in range(cols_n):
@@ -216,6 +226,10 @@
     return lax.ppermute(x, axis, pairs)
 
 
+def swap(x, axis, pairs):
+    return lax.ppermute(x, axis, pairs + [(j, i) for i, j in pairs])
+
+
 def per_device(
     fine_blocks, fine_rows, fine_cols, fine_counts, prolong_blocks, prolong_codes,
     prolong_counts, second_blocks, second_aggs,
@@ -226,55 +240,56 @@
     packed_rows = (slots + CB) * size + META
     wide = CB * size
     dma = pltpu.SemaphoreType.DMA
-    packed, ints = pl.pallas_call(
+    packed = pl.pallas_call(
         pack_kernel,
-        out_shape=[
-            jax.ShapeDtypeStruct((packed_rows, size), BF16),
-            jax.ShapeDtypeStruct((cap + slots + CB + 2,), jnp.int32),
-        ],
-        in_specs=[SMEM] * 6 + [HBM] * 2,
-        out_specs=[HBM, SMEM],
-        scratch_shapes=[
-            pltpu.VMEM((packed_rows, size), BF16),
-            dma((3,)),
-        ],
+        out_shape=jax.ShapeDtypeStruct((packed_rows, size), BF16),
+        in_specs=[SMEM] * 3 + [HBM] * 2,
+        out_specs=HBM,
+        scratch_shapes=[pltpu.VMEM((packed_rows, size), BF16), dma((3,))],
         compiler_params=WHOLE,
         name="pack",
     )(
         prolong_codes[0, 0], prolong_counts[0], second_aggs[0, 0],
-        fine_rows[0, 0], fine_cols[0, 0], fine_counts[0],
         prolong_blocks.reshape(slots * size, size),
         second_blocks.reshape(CB * size, size),
     )
-    up = shift(packed, "row", 1, False)
-    down = shift(packed, "row", -1, False)
+    rows_n = lax.axis_size("row")
+    pair = swap(packed, "row", [(i, i + 1) for i in range(0, rows_n - 1, 2)])
+    other = swap(packed, "row", [(i, i + 1) for i in range(1, rows_n - 1, 2)])
     left = shift(packed, "col", 1, False)
     right = shift(packed, "col", -1, False)
 
     c_shape = jax.ShapeDtypeStruct((CB, NS, CB, size, size), BF16)
     table = pltpu.SMEM((NS, PB + 1), jnp.int32)
-    weights, half, lift_t, c_one = pl.pallas_call(
+    stock, more, c_one = pl.pallas_call(
         functools.partial(own_kernel, slots, size),
         out_shape=[
             jax.ShapeDtypeStruct((NS - 1, wide, FB * size), BF16),
-            jax.ShapeDtypeStruct((wide, G2 * size), F32),
-            jax.ShapeDtypeStruct((G2 * size, wide), BF16),
+            jax.ShapeDtypeStruct((3, wide, G2 * size), BF16),
             c_shape,
         ],
-        in_specs=[SMEM, VMEM, VMEM],
-        out_specs=[VMEM] * 3 + [HBM],
+        in_specs=[SMEM] * 6 + [HBM] * 2,
+        out_specs=[HBM] * 3,
         scratch_shapes=[
+            pltpu.VMEM((cap, size, size), BF16),
+            pltpu.VMEM((packed_rows, size), BF16),
+            pltpu.VMEM((NS - 1, wide, FB * size), BF16),
+            pltpu.VMEM((3, wide, G2 * size), BF16),
             pltpu.VMEM((FB, wide, size), BF16),
             pltpu.VMEM((NS * FB + 1, wide, size), F32),
             pltpu.VMEM((FB * size, wide), BF16),
             pltpu.VMEM((CB, CB, size, size), BF16),
             table,
-            dma,
+            dma((6,)),
         ],
-        compiler_params=LARGE,
+        compiler_params=WHOLE,
         cost_estimate=pl.CostEstimate(flops=10**9, bytes_accessed=4 * 10**6, transcendentals=0),
         name="own_source",
-    )(ints, fine_blocks[0, 0], packed)
+    )(
+        fine_rows[0, 0], fine_cols[0, 0], fine_counts[0],
+        prolong_codes[0, 0], prolong_counts[0], second_aggs[0, 0],
+        fine_blocks[0, 0], packed,
+    )
 
     near_scratch = [
         pltpu.VMEM((2, FB * size, wide), BF16),
@@ -285,6 +300,15 @@
         dma((3,)),
     ]
     square = jax.ShapeDtypeStruct((wide, G2 * size), F32)
+    lift_t, half = pl.pallas_call(
+        half_kernel,
+        out_shape=[jax.ShapeDtypeStruct((G2 * size, wide), BF16), square],
+        in_specs=[VMEM],
+        out_specs=[VMEM] * 2,
+        compiler_params=SMALL,
+        cost_estimate=pl.CostEstimate(flops=10**9, bytes_accessed=4 * 10**6, transcendentals=0),
+        name="own_half",
+    )(more)
     c_one, term = pl.pallas_call(
         functools.partial(side_kernel, slots, size),
         out_shape=[c_shape, square],
@@ -294,7 +318,7 @@
         scratch_shapes=near_scratch,
         compiler_params=LARGE,
         name="col_sources",
-    )(weights, half, lift_t, left, right, c_one)
+    )(stock, lift_t, half, left, right, c_one)
 
     chunk = G2 * size // cols_n
     kept = jax.ShapeDtypeStruct((3, chunk, G2 * size), F32)
@@ -308,7 +332,7 @@
         scratch_shapes=[pltpu.VMEM((3, G2 * size, G2 * size), F32)] + near_scratch,
         compiler_params=LARGE,
         name="row_sources",
-    )(weights, term, lift_t, up, down, c_one)
+    )(stock, lift_t, term, other, pair, c_one)
     parts = [sends[0]] + [shift(sends[d], "col", d, True) for d in range(1, cols_n)]
     total = pl.pallas_call(
         sum_kernel, out_shape=piece, in_specs=[VMEM] * cols_n, out_specs=VMEM,

time: 53.6 us -> 51.6 us (0.963)
  the two profiles are of different devices: /device:TPU:13 before, /device:TPU:11 now
where the time goes in v6:
time: 51.6 us; the launch traced here: 51.1 us
  waiting for transfers between devices  17.5 us (34%)
  Pallas kernels  16 us (31%)
  starting transfers between devices  14.1 us (27%)
  between operations  2.07 us (4%)
  local copies, waits for them, and re-layouts  1.48 us (3%)
    ppermute x8, waiting for transfers between devices, shift(): return lax.ppermute(x, axis, pairs)  17.5 us
    ppermute x8, starting transfers between devices, shift(): return lax.ppermute(x, axis, pairs)  9.8 us
    pallas_call x1, Pallas kernels, per_device(): pl.pallas_call(functools.partial(own_kernel, slots, size), out_shape=[jax...  8.06 us
    ppermute x2, starting transfers between devices, swap(): return lax.ppermute(x, axis, pairs + [(j, i) for i, j in pairs])  4.31 us
    pallas_call x1, Pallas kernels, per_device(): pl.pallas_call(pack_kernel, out_shape=jax.ShapeDtypeStruct((packed_rows,...  2.46 us
    pallas_call x1, Pallas kernels, per_device(): pl.pallas_call(functools.partial(row_kernel, slots, size, cols_n), out_sh...  2.17 us
    pallas_call x1, Pallas kernels, per_device(): pl.pallas_call(functools.partial(side_kernel, slots, size), out_shape=[c_...  2.15 us
    unnamed x4, local copies, waits for them, and re-layouts  1.48 us
  transfers between devices with their start and end apart: 10, of which 6 were waited for; matrix products, arithmetic and copies ran while one was open for 0% of the time, Pallas kernels for 20%

profile of v6, /device:TPU:11, one launch (start us, length us, event | category | flops | bytes accessed | tf_op | source)
XLA Modules:
  0.0 51.1 jit_solution(7664215401838800253)
XLA Ops:
  1.3 2.5 %pack.1.own_at = bf16[1808,128]{1,0:T(8,128)(2,1)} custom-call(s32[12]{0:T(128)} %bitcast.18, s32[1]{0:T(128)} %bitcast.12.count, s32[2]{0:T(128)} %bitcast.20, bf16[1536,128]{1,0:T(8,128)(2,1)} %bitcast.16, bf16[256,128]{1,0:T(8,128)(2,1)} %bitcast.17), custom_call_target="tpu_custom_call" | custom-call | tf_op jit(solution)/shard_map/pack/pallas_call | solution.py:243
  3.7 3.2 %collective-permute-start = (bf16[1808,128]{1,0:T(8,128)(2,1)}, bf16[1808,128]{1,0:T(8,128)(2,1)S(1)}, u32[]{:S(2)}, u32[]{:S(2)}) collective-permute-start(bf16[1808,128]{1,0:T(8,128)(2,1)} %pack.1.own_at), channel_id=1, source_target_pairs={{0,1},{1,2},{2,3},{4,5},{5,6},{6,7},{8,9},{9,10},{10,11},{12,13},{... | collective-permute-start | bytes 1388552 | tf_op jit(solution)/shard_map/ppermute | solution.py:226
  7.0 2.1 %collective-permute-start.1 = (bf16[1808,128]{1,0:T(8,128)(2,1)}, bf16[1808,128]{1,0:T(8,128)(2,1)S(1)}, u32[]{:S(2)}, u32[]{:S(2)}) collective-permute-start(bf16[1808,128]{1,0:T(8,128)(2,1)} %pack.1.own_at), channel_id=1, source_target_pairs={{1,0},{2,1},{3,2},{5,4},{6,5},{7,6},{9,8},{10,9},{11,10},{13,12},{... | collective-permute-start | bytes 1388552 | tf_op jit(solution)/shard_map/ppermute | solution.py:226
  9.1 4.2 %collective-permute-start.2 = (bf16[1808,128]{1,0:T(8,128)(2,1)}, bf16[1808,128]{1,0:T(8,128)(2,1)S(1)}, u32[]{:S(2)}, u32[]{:S(2)}) collective-permute-start(bf16[1808,128]{1,0:T(8,128)(2,1)} %pack.1.own_at), channel_id=1, source_target_pairs={{4,8},{12,16},{20,24},{8,4},{16,12},{24,20},{5,9},{13,17},{21,25},... | collective-permute-start | bytes 1388552 | tf_op jit(solution)/shard_map/ppermute | solution.py:230
  13.3 0.1 collective-permute-start.3
  14.0 8.1 %own_source.1 = (bf16[4,256,1024]{2,1,0:T(8,128)(2,1)}, bf16[3,256,256]{2,1,0:T(8,128)(2,1)}, bf16[2,5,2,128,128]{4,3,2,1,0:T(8,128)(2,1)}) custom-call(s32[64]{0:T(128)} %bitcast.23, s32[64]{0:T(128)} %bitcast.24, s32[1]{0:T(128)} %bitcast.11.count, s32[12]{0:T(128)} %bitcast.19, s32[1]{0:T(128)} %bitcast.13.p_count, s32[2]{0:T(128)} %bitcast.21, ...), custom_call_target="tpu_custom_call" | custom-call | flops 1000000000 | bytes 4000000 | tf_op jit(solution)/shard_map/own_source/pallas_call | solution.py:264
  22.1 0.0 copy-start
  22.1 0.0 copy-start.1
  22.1 1.1 %copy-done.1 = bf16[3,256,256]{2,1,0:T(8,128)(2,1)S(1)} copy-done((bf16[3,256,256]{2,1,0:T(8,128)(2,1)S(1)}, bf16[3,256,256]{2,1,0:T(8,128)(2,1)}, u32[]{:S(2)}) %copy-start.1) | copy-done | bytes 393240
  23.3 0.2 own_half.1
  23.5 0.0 collective-permute-done.left
  23.5 0.0 collective-permute-done.1.right
  23.5 0.3 copy-done
  23.8 2.2 %col_sources.1 = (bf16[2,5,2,128,128]{4,3,2,1,0:T(8,128)(2,1)}, f32[256,256]{1,0:T(8,128)S(1)}) custom-call(bf16[4,256,1024]{2,1,0:T(8,128)(2,1)S(1)} %copy-done, bf16[256,256]{1,0:T(8,128)(2,1)S(1)} %get-tuple-element.16.lift_t, f32[256,256]{1,0:T(8,128)S(1)} %get-tuple-element.17.half, ...), custom_call_target="tpu_custom_call", output_to_operand_aliasing={{0}: (5, {})} | custom-call | tf_op jit(solution)/shard_map/col_sources/pallas_call | solution.py:312
  26.0 0.0 collective-permute-done.2.other
  26.0 0.0 collective-permute-done.3.pair
  26.0 2.2 %row_sources.1 = (bf16[2,5,2,128,128]{4,3,2,1,0:T(8,128)(2,1)}, f32[3,64,256]{2,1,0:T(8,128)S(1)}, bf16[3,64,256]{2,1,0:T(8,128)(2,1)S(1)}, bf16[3,64,256]{2,1,0:T(8,128)(2,1)S(1)}, bf16[3,64,256]{2,1,0:T(8,128)(2,1)S(1)}) custom-call(bf16[4,256,1024]{2,1,0:T(8,128)(2,1)S(1)} %copy-done, ...), custom_call_target="tpu_custom_call", output_to_operand_aliasing={{0}: (5, {})} | custom-call | tf_op jit(solution)/shard_map/row_sources/pallas_call | solution.py:326
  28.2 0.1 collective-permute-start.4
  28.3 0.8 %collective-permute-start.5 = (bf16[3,64,256]{2,1,0:T(8,128)(2,1)S(1)}, bf16[3,64,256]{2,1,0:T(8,128)(2,1)S(1)}, u32[]{:S(2)}, u32[]{:S(2)}) collective-permute-start(bf16[3,64,256]{2,1,0:T(8,128)(2,1)S(1)} %get-tuple-element.24), channel_id=1, source_target_pairs={{0,2},{1,3},{2,0},{3,1},{4,6},{5,7},{6,4},{7,5},{8,10},{9,11},{10,... | collective-permute-start | bytes 294920 | tf_op jit(solution)/shard_map/ppermute | solution.py:226
  29.1 1.4 %collective-permute-start.6 = (bf16[3,64,256]{2,1,0:T(8,128)(2,1)S(1)}, bf16[3,64,256]{2,1,0:T(8,128)(2,1)S(1)}, u32[]{:S(2)}, u32[]{:S(2)}) collective-permute-start(bf16[3,64,256]{2,1,0:T(8,128)(2,1)S(1)} %get-tuple-element.25), channel_id=1, source_target_pairs={{0,3},{1,0},{2,1},{3,2},{4,7},{5,4},{6,5},{7,6},{8,11},{9,8},{10,9... | collective-permute-start | bytes 294920 | tf_op jit(solution)/shard_map/ppermute | solution.py:226
  30.4 1.3 %collective-permute-done.4.refs_1_ = bf16[3,64,256]{2,1,0:T(8,128)(2,1)S(1)} collective-permute-done((bf16[3,64,256]{2,1,0:T(8,128)(2,1)S(1)}, bf16[3,64,256]{2,1,0:T(8,128)(2,1)S(1)}, u32[]{:S(2)}, u32[]{:S(2)}) %collective-permute-start.4) | collective-permute-done | bytes 98336 | tf_op jit(solution)/shard_map/ppermute | solution.py:226
  31.7 5.2 %collective-permute-done.5.refs_2_ = bf16[3,64,256]{2,1,0:T(8,128)(2,1)S(1)} collective-permute-done((bf16[3,64,256]{2,1,0:T(8,128)(2,1)S(1)}, bf16[3,64,256]{2,1,0:T(8,128)(2,1)S(1)}, u32[]{:S(2)}, u32[]{:S(2)}) %collective-permute-start.5) | collective-permute-done | bytes 98336 | tf_op jit(solution)/shard_map/ppermute | solution.py:226
  36.9 2.4 %collective-permute-done.6.refs_3_ = bf16[3,64,256]{2,1,0:T(8,128)(2,1)S(1)} collective-permute-done((bf16[3,64,256]{2,1,0:T(8,128)(2,1)S(1)}, bf16[3,64,256]{2,1,0:T(8,128)(2,1)S(1)}, u32[]{:S(2)}, u32[]{:S(2)}) %collective-permute-start.6) | collective-permute-done | bytes 98336 | tf_op jit(solution)/shard_map/ppermute | solution.py:226
  39.3 0.1 collective-permute-start.7
  39.4 1.1 %collective-permute-start.8 = (bf16[3,64,256]{2,1,0:T(8,128)(2,1)S(1)}, bf16[3,64,256]{2,1,0:T(8,128)(2,1)S(1)}, u32[]{:S(2)}, u32[]{:S(2)}) collective-permute-start(bf16[3,64,256]{2,1,0:T(8,128)(2,1)S(1)} %total.1.refs_0_), channel_id=1, source_target_pairs={{0,2},{1,3},{2,0},{3,1},{4,6},{5,7},{6,4},{7,5},{8,10},{9,11},{10,... | collective-permute-start | bytes 294920 | tf_op jit(solution)/shard_map/ppermute | solution.py:226
  40.5 1.1 %collective-permute-start.9 = (bf16[3,64,256]{2,1,0:T(8,128)(2,1)S(1)}, bf16[3,64,256]{2,1,0:T(8,128)(2,1)S(1)}, u32[]{:S(2)}, u32[]{:S(2)}) collective-permute-start(bf16[3,64,256]{2,1,0:T(8,128)(2,1)S(1)} %total.1.refs_0_), channel_id=1, source_target_pairs={{0,3},{1,0},{2,1},{3,2},{4,7},{5,4},{6,5},{7,6},{8,11},{9,8},{10,9... | collective-permute-start | bytes 294920 | tf_op jit(solution)/shard_map/ppermute | solution.py:226
  41.6 1.7 %collective-permute-done.7.refs_1_ = bf16[3,64,256]{2,1,0:T(8,128)(2,1)S(1)} collective-permute-done((bf16[3,64,256]{2,1,0:T(8,128)(2,1)S(1)}, bf16[3,64,256]{2,1,0:T(8,128)(2,1)S(1)}, u32[]{:S(2)}, u32[]{:S(2)}) %collective-permute-start.7) | collective-permute-done | bytes 98336 | tf_op jit(solution)/shard_map/ppermute | solution.py:226
  43.2 1.9 %collective-permute-done.8.refs_2_ = bf16[3,64,256]{2,1,0:T(8,128)(2,1)S(1)} collective-permute-done((bf16[3,64,256]{2,1,0:T(8,128)(2,1)S(1)}, bf16[3,64,256]{2,1,0:T(8,128)(2,1)S(1)}, u32[]{:S(2)}, u32[]{:S(2)}) %collective-permute-start.8) | collective-permute-done | bytes 98336 | tf_op jit(solution)/shard_map/ppermute | solution.py:226
  45.2 5.0 %collective-permute-done.9.refs_3_ = bf16[3,64,256]{2,1,0:T(8,128)(2,1)S(1)} collective-permute-done((bf16[3,64,256]{2,1,0:T(8,128)(2,1)S(1)}, bf16[3,64,256]{2,1,0:T(8,128)(2,1)S(1)}, u32[]{:S(2)}, u32[]{:S(2)}) %collective-permute-start.9) | collective-permute-done | bytes 98336 | tf_op jit(solution)/shard_map/ppermute | solution.py:226
  50.2 0.9 %spread.1 = f32[2,3,2,128,128]{4,3,2,1,0:T(8,128)} custom-call(bf16[3,64,256]{2,1,0:T(8,128)(2,1)S(1)} %total.1.refs_0_, bf16[3,64,256]{2,1,0:T(8,128)(2,1)S(1)} %collective-permute-done.7.refs_1_, bf16[3,64,256]{2,1,0:T(8,128)(2,1)S(1)} %collective-permute-done.8.refs_2_, bf16[3,64,256]{2,1,0:T(8,128)(2,1)S(1)} %collective-permute-done.9.refs_3_), custom_call_target="tpu_custom_call" | custom-call | tf_op jit(solution)/shard_map/spread/pallas_call | solution.py:342
  (1 shorter events, 0.0 us)
Async XLA Ops:
  3.7 19.7 %collective-permute-start = (bf16[1808,128]{1,0:T(8,128)(2,1)}, bf16[1808,128]{1,0:T(8,128)(2,1)S(1)}, u32[]{:S(2)}, u32[]{:S(2)}) collective-permute-start(bf16[1808,128]{1,0:T(8,128)(2,1)} %pack.1.own_at), channel_id=1, source_target_pairs={{0,1},{1,2},{2,3},{4,5},{5,6},{6,7},{8,9},{9,10},{10,11},{12,13},{... | collective-permute-start | bytes 1388552 | tf_op jit(solution)/shard_map/ppermute | solution.py:226
  7.0 16.5 %collective-permute-start.1 = (bf16[1808,128]{1,0:T(8,128)(2,1)}, bf16[1808,128]{1,0:T(8,128)(2,1)S(1)}, u32[]{:S(2)}, u32[]{:S(2)}) collective-permute-start(bf16[1808,128]{1,0:T(8,128)(2,1)} %pack.1.own_at), channel_id=1, source_target_pairs={{1,0},{2,1},{3,2},{5,4},{6,5},{7,6},{9,8},{10,9},{11,10},{13,12},{... | collective-permute-start | bytes 1388552 | tf_op jit(solution)/shard_map/ppermute | solution.py:226
  9.1 16.9 %collective-permute-start.2 = (bf16[1808,128]{1,0:T(8,128)(2,1)}, bf16[1808,128]{1,0:T(8,128)(2,1)S(1)}, u32[]{:S(2)}, u32[]{:S(2)}) collective-permute-start(bf16[1808,128]{1,0:T(8,128)(2,1)} %pack.1.own_at), channel_id=1, source_target_pairs={{4,8},{12,16},{20,24},{8,4},{16,12},{24,20},{5,9},{13,17},{21,25},... | collective-permute-start | bytes 1388552 | tf_op jit(solution)/shard_map/ppermute | solution.py:230
  13.3 12.7 %collective-permute-start.3 = (bf16[1808,128]{1,0:T(8,128)(2,1)}, bf16[1808,128]{1,0:T(8,128)(2,1)S(1)}, u32[]{:S(2)}, u32[]{:S(2)}) collective-permute-start(bf16[1808,128]{1,0:T(8,128)(2,1)} %pack.1.own_at), channel_id=1, source_target_pairs={{0,4},{8,12},{16,20},{24,28},{4,0},{12,8},{20,16},{28,24},{1,5},{9... | collective-permute-start | bytes 1388552 | tf_op jit(solution)/shard_map/ppermute | solution.py:230
  22.1 1.7 %copy-start = (bf16[4,256,1024]{2,1,0:T(8,128)(2,1)S(1)}, bf16[4,256,1024]{2,1,0:T(8,128)(2,1)}, u32[]{:S(2)}) copy-start(bf16[4,256,1024]{2,1,0:T(8,128)(2,1)} %get-tuple-element.14.stock) | copy-start | bytes 6291460
  22.1 1.1 %copy-start.1 = (bf16[3,256,256]{2,1,0:T(8,128)(2,1)S(1)}, bf16[3,256,256]{2,1,0:T(8,128)(2,1)}, u32[]{:S(2)}) copy-start(bf16[3,256,256]{2,1,0:T(8,128)(2,1)} %get-tuple-element.15.more) | copy-start | bytes 1179652
  28.2 3.5 %collective-permute-start.4 = (bf16[3,64,256]{2,1,0:T(8,128)(2,1)S(1)}, bf16[3,64,256]{2,1,0:T(8,128)(2,1)S(1)}, u32[]{:S(2)}, u32[]{:S(2)}) collective-permute-start(bf16[3,64,256]{2,1,0:T(8,128)(2,1)S(1)} %get-tuple-element.23), channel_id=1, source_target_pairs={{0,1},{1,2},{2,3},{3,0},{4,5},{5,6},{6,7},{7,4},{8,9},{9,10},{10,1... | collective-permute-start | bytes 294920 | tf_op jit(solution)/shard_map/ppermute | solution.py:226
  28.3 8.6 %collective-permute-start.5 = (bf16[3,64,256]{2,1,0:T(8,128)(2,1)S(1)}, bf16[3,64,256]{2,1,0:T(8,128)(2,1)S(1)}, u32[]{:S(2)}, u32[]{:S(2)}) collective-permute-start(bf16[3,64,256]{2,1,0:T(8,128)(2,1)S(1)} %get-tuple-element.24), channel_id=1, source_target_pairs={{0,2},{1,3},{2,0},{3,1},{4,6},{5,7},{6,4},{7,5},{8,10},{9,11},{10,... | collective-permute-start | bytes 294920 | tf_op jit(solution)/shard_map/ppermute | solution.py:226
  29.1 10.2 %collective-permute-start.6 = (bf16[3,64,256]{2,1,0:T(8,128)(2,1)S(1)}, bf16[3,64,256]{2,1,0:T(8,128)(2,1)S(1)}, u32[]{:S(2)}, u32[]{:S(2)}) collective-permute-start(bf16[3,64,256]{2,1,0:T(8,128)(2,1)S(1)} %get-tuple-element.25), channel_id=1, source_target_pairs={{0,3},{1,0},{2,1},{3,2},{4,7},{5,4},{6,5},{7,6},{8,11},{9,8},{10,9... | collective-permute-start | bytes 294920 | tf_op jit(solution)/shard_map/ppermute | solution.py:226
  39.3 3.9 %collective-permute-start.7 = (bf16[3,64,256]{2,1,0:T(8,128)(2,1)S(1)}, bf16[3,64,256]{2,1,0:T(8,128)(2,1)S(1)}, u32[]{:S(2)}, u32[]{:S(2)}) collective-permute-start(bf16[3,64,256]{2,1,0:T(8,128)(2,1)S(1)} %total.1.refs_0_), channel_id=1, source_target_pairs={{0,1},{1,2},{2,3},{3,0},{4,5},{5,6},{6,7},{7,4},{8,9},{9,10},{10,1... | collective-permute-start | bytes 294920 | tf_op jit(solution)/shard_map/ppermute | solution.py:226
  39.4 5.8 %collective-permute-start.8 = (bf16[3,64,256]{2,1,0:T(8,128)(2,1)S(1)}, bf16[3,64,256]{2,1,0:T(8,128)(2,1)S(1)}, u32[]{:S(2)}, u32[]{:S(2)}) collective-permute-start(bf16[3,64,256]{2,1,0:T(8,128)(2,1)S(1)} %total.1.refs_0_), channel_id=1, source_target_pairs={{0,2},{1,3},{2,0},{3,1},{4,6},{5,7},{6,4},{7,5},{8,10},{9,11},{10,... | collective-permute-start | bytes 294920 | tf_op jit(solution)/shard_map/ppermute | solution.py:226
  40.5 9.7 %collective-permute-start.9 = (bf16[3,64,256]{2,1,0:T(8,128)(2,1)S(1)}, bf16[3,64,256]{2,1,0:T(8,128)(2,1)S(1)}, u32[]{:S(2)}, u32[]{:S(2)}) collective-permute-start(bf16[3,64,256]{2,1,0:T(8,128)(2,1)S(1)} %total.1.refs_0_), channel_id=1, source_target_pairs={{0,3},{1,0},{2,1},{3,2},{4,7},{5,4},{6,5},{7,6},{8,11},{9,8},{10,9... | collective-permute-start | bytes 294920 | tf_op jit(solution)/shard_map/ppermute | solution.py:226

commit v7 on v6

--- a/solution.py
+++ b/solution.py
@@ -13,7 +13,7 @@
 G2 = 2
 NS = 5
 PB = FB * CB
-UNROLL = 4
+UNROLL = 8
 META = 16
 F32 = jnp.float32
 BF16 = jnp.bfloat16
@@ -92,20 +92,24 @@
 
 
 def own_kernel(
-    slots, size, rows, cols, count, codes, p_count, aggs, fine_at, own_at, stock_at, more_at, c_one,
-    fine, own, stock, more, turned, acc, dense, tile, table, sems,
+    slots, size, rows, cols, count, codes, p_count, aggs, fine_at, own_at,
+    stock_at, half_at, lift_at, token, c_one,
+    fine, own, stock, half, lift_t, turned, acc, dense, tile, table, sems,
 ):
     fetch_own = pltpu.make_async_copy(own_at, own, sems.at[0])
     fetch_own.start()
     fetch_fine = pltpu.make_async_copy(fine_at, fine, sems.at[1])
     fetch_fine.start()
     acc[...] = jnp.zeros_like(acc)
-    fill_table(0, slots, table, lambda k: jnp.where(k < p_count[0], codes[k], PB))
+    turned[...] = jnp.zeros_like(turned)
+    token[...] = jnp.zeros_like(token)
+    code_of = lambda k: jnp.where(k < p_count[0], codes[k], PB)
+    fill_table(0, slots, table, code_of)
     fetch_own.wait()
-    for i in range(FB):
-        for j in range(CB):
-            block = block_at(0, i * CB + j, size, table, own)
-            turned[i, j * size : (j + 1) * size, :] = block.T
+    for k in range(slots):
+        i = code_of(k) // CB
+        j = pl.multiple_of((code_of(k) - i * CB) * size, size)
+        turned[i, pl.ds(j, size), :] = own[k * size : (k + 1) * size, :].T
     fetch_fine.wait()
 
     def step(t, carry):
@@ -129,11 +133,11 @@
     dense_of(0, size, table, own, dense)
     coarse = coarse_of(size, own_weight, dense, tile)
     lift = lift_of(own, slots, size, lambda j: aggs[j])
-    wide = CB * size
-    more[0] = lift.T
-    more[1] = coarse
-    more[2] = lift
-    stores.append(pltpu.make_async_copy(more, more_at, sems.at[0]))
+    lift_t[...] = lift.T
+    half[...] = jnp.dot(coarse, lift, preferred_element_type=F32)
+    stores.append(pltpu.make_async_copy(lift_t, lift_at, sems.at[0]))
+    stores[-1].start()
+    stores.append(pltpu.make_async_copy(half, half_at, sems.at[6]))
     stores[-1].start()
     stores.append(pltpu.make_async_copy(tile, c_one.at[:, 0], sems.at[1]))
     stores[-1].start()
@@ -164,12 +168,11 @@
     return parts, stores
 
 
-def half_kernel(more, lift_t, half):
-    lift_t[...] = more[0]
-    half[...] = jnp.dot(more[1], more[2], preferred_element_type=F32)
-
-
-def side_kernel(slots, size, stock, lift_t, half, left, right, c_in, c_one, term, *scratch):
+def pass_kernel(token, out):
+    out[...] = token[...]
+
+
+def side_kernel(slots, size, stock, lift_t, half, left, right, token, c_in, c_one, term, *scratch):
     parts, stores = near_coarse((1, 2), (left, right), slots, size, stock, c_one, *scratch)
     whole = (half[...] + parts[0] + parts[1]).astype(BF16)
     term[...] = jnp.dot(lift_t[...], whole, preferred_element_type=F32)
@@ -201,21 +204,21 @@
     refs[-1][...] = total.astype(BF16)
 
 
-def spread_kernel(size, cols_n, *refs):
+def spread_kernel(size, steps, *refs):
     out = refs[-1]
     chunk = refs[0].shape[1]
     unit = math.gcd(chunk, size)
     per = size // unit
     me = lax.axis_index("col")
-    for d in range(cols_n):
-        owner = lax.rem(me - d + cols_n, cols_n)
+    for n, d in enumerate(steps):
+        owner = lax.rem(me - d + len(steps), len(steps))
         for t in range(chunk // unit):
             at = owner * (chunk // unit) + t
             a = at // per
             h = pl.multiple_of(lax.rem(at, per) * unit, unit)
             for g in range(3):
                 for b in range(G2):
-                    out[a, g, b, pl.ds(h, unit), :] = refs[d][
+                    out[a, g, b, pl.ds(h, unit), :] = refs[n][
                         g, t * unit : (t + 1) * unit, b * size : (b + 1) * size
                     ].astype(F32)
 
@@ -260,27 +263,32 @@
     right = shift(packed, "col", -1, False)
 
     c_shape = jax.ShapeDtypeStruct((CB, NS, CB, size, size), BF16)
+    square = jax.ShapeDtypeStruct((wide, G2 * size), F32)
+    mark = jax.ShapeDtypeStruct((8, size), F32)
     table = pltpu.SMEM((NS, PB + 1), jnp.int32)
-    stock, more, c_one = pl.pallas_call(
+    stock, half, lift_t, token, c_one = pl.pallas_call(
         functools.partial(own_kernel, slots, size),
         out_shape=[
             jax.ShapeDtypeStruct((NS - 1, wide, FB * size), BF16),
-            jax.ShapeDtypeStruct((3, wide, G2 * size), BF16),
+            square,
+            jax.ShapeDtypeStruct((G2 * size, wide), BF16),
+            mark,
             c_shape,
         ],
         in_specs=[SMEM] * 6 + [HBM] * 2,
-        out_specs=[HBM] * 3,
+        out_specs=[HBM] * 3 + [VMEM, HBM],
         scratch_shapes=[
             pltpu.VMEM((cap, size, size), BF16),
             pltpu.VMEM((packed_rows, size), BF16),
             pltpu.VMEM((NS - 1, wide, FB * size), BF16),
-            pltpu.VMEM((3, wide, G2 * size), BF16),
-            pltpu.VMEM((FB, wide, size), BF16),
+            pltpu.VMEM((wide, G2 * size), F32),
+            pltpu.VMEM((G2 * size, wide), BF16),
+            pltpu.VMEM((FB + 1, wide, size), BF16),
             pltpu.VMEM((NS * FB + 1, wide, size), F32),
             pltpu.VMEM((FB * size, wide), BF16),
             pltpu.VMEM((CB, CB, size, size), BF16),
             table,
-            dma((6,)),
+            dma((7,)),
         ],
         compiler_params=WHOLE,
         cost_estimate=pl.CostEstimate(flops=10**9, bytes_accessed=4 * 10**6, transcendentals=0),
@@ -299,26 +307,25 @@
         table,
         dma((3,)),
     ]
-    square = jax.ShapeDtypeStruct((wide, G2 * size), F32)
-    lift_t, half = pl.pallas_call(
-        half_kernel,
-        out_shape=[jax.ShapeDtypeStruct((G2 * size, wide), BF16), square],
+    token = pl.pallas_call(
+        pass_kernel,
+        out_shape=mark,
         in_specs=[VMEM],
-        out_specs=[VMEM] * 2,
+        out_specs=VMEM,
         compiler_params=SMALL,
         cost_estimate=pl.CostEstimate(flops=10**9, bytes_accessed=4 * 10**6, transcendentals=0),
-        name="own_half",
-    )(more)
+        name="pass_on",
+    )(token)
     c_one, term = pl.pallas_call(
         functools.partial(side_kernel, slots, size),
         out_shape=[c_shape, square],
-        in_specs=[VMEM] * 5 + [HBM],
+        in_specs=[VMEM] * 6 + [HBM],
         out_specs=[HBM, VMEM],
-        input_output_aliases={5: 0},
+        input_output_aliases={6: 0},
         scratch_shapes=near_scratch,
         compiler_params=LARGE,
         name="col_sources",
-    )(stock, lift_t, half, left, right, c_one)
+    )(stock, lift_t, half, left, right, token, c_one)
 
     chunk = G2 * size // cols_n
     kept = jax.ShapeDtypeStruct((3, chunk, G2 * size), F32)
@@ -333,14 +340,15 @@
         compiler_params=LARGE,
         name="row_sources",
     )(stock, lift_t, term, other, pair, c_one)
-    parts = [sends[0]] + [shift(sends[d], "col", d, True) for d in range(1, cols_n)]
+    steps = sorted(range(1, cols_n), key=lambda d: -min(d, cols_n - d))
+    parts = [sends[0]] + [shift(sends[d], "col", d, True) for d in steps]
     total = pl.pallas_call(
         sum_kernel, out_shape=piece, in_specs=[VMEM] * cols_n, out_specs=VMEM,
         compiler_params=SMALL, name="total",
     )(*parts)
-    gathered = [total] + [shift(total, "col", d, True) for d in range(1, cols_n)]
+    gathered = [total] + [shift(total, "col", d, True) for d in steps]
     c_two = pl.pallas_call(
-        functools.partial(spread_kernel, size, cols_n),
+        functools.partial(spread_kernel, size, [0] + steps),
         out_shape=jax.ShapeDtypeStruct((G2, 3, G2, size, size), F32),
         in_specs=[VMEM] * cols_n,
         out_specs=VMEM,

time: 51.6 us -> 51.6 us (level)
  the two profiles are of different devices: /device:TPU:11 before, /device:TPU:0 now
where the time goes in v7:
time: 51.6 us; the launch traced here: 51.3 us
  starting transfers between devices  23.3 us (45%)
  Pallas kernels  13.5 us (26%)
  waiting for transfers between devices  11.6 us (22%)
  between operations  2.05 us (4%)
  local copies, waits for them, and re-layouts  0.84 us (2%)
    ppermute x8, starting transfers between devices, shift(): return lax.ppermute(x, axis, pairs)  19.7 us
    ppermute x8, waiting for transfers between devices, shift(): return lax.ppermute(x, axis, pairs)  11.6 us
    pallas_call x1, Pallas kernels, per_device(): pl.pallas_call(functools.partial(own_kernel, slots, size), out_shape=[jax...  5.72 us
    ppermute x2, starting transfers between devices, swap(): return lax.ppermute(x, axis, pairs + [(j, i) for i, j in pairs])  3.58 us
    pallas_call x1, Pallas kernels, per_device(): pl.pallas_call(pack_kernel, out_shape=jax.ShapeDtypeStruct((packed_rows,...  2.46 us
    pallas_call x1, Pallas kernels, per_device(): pl.pallas_call(functools.partial(row_kernel, slots, size, cols_n), out_sh...  2.17 us
    pallas_call x1, Pallas kernels, per_device(): pl.pallas_call(functools.partial(side_kernel, slots, size), out_shape=[c_...  2.16 us
  transfers between devices with their start and end apart: 10, of which 5 were waited for; matrix products, arithmetic and copies ran while one was open for 0% of the time, Pallas kernels for 15%

profile of v7, /device:TPU:0, one launch (start us, length us, event | category | flops | bytes accessed | tf_op | source)
XLA Modules:
  0.0 51.3 jit_solution(11200776483973721760)
XLA Ops:
  1.3 2.5 %pack.1.own_at = bf16[1808,128]{1,0:T(8,128)(2,1)} custom-call(s32[12]{0:T(128)} %bitcast.18, s32[1]{0:T(128)} %bitcast.12.count, s32[2]{0:T(128)} %bitcast.20, bf16[1536,128]{1,0:T(8,128)(2,1)} %bitcast.16, bf16[256,128]{1,0:T(8,128)(2,1)} %bitcast.17), custom_call_target="tpu_custom_call" | custom-call | tf_op jit(solution)/shard_map/pack/pallas_call | solution.py:246
  3.7 5.0 %collective-permute-start = (bf16[1808,128]{1,0:T(8,128)(2,1)}, bf16[1808,128]{1,0:T(8,128)(2,1)S(1)}, u32[]{:S(2)}, u32[]{:S(2)}) collective-permute-start(bf16[1808,128]{1,0:T(8,128)(2,1)} %pack.1.own_at), channel_id=1, source_target_pairs={{0,1},{1,2},{2,3},{4,5},{5,6},{6,7},{8,9},{9,10},{10,11},{12,13},{... | collective-permute-start | bytes 1388552 | tf_op jit(solution)/shard_map/ppermute | solution.py:229
  8.7 1.3 %collective-permute-start.1 = (bf16[1808,128]{1,0:T(8,128)(2,1)}, bf16[1808,128]{1,0:T(8,128)(2,1)S(1)}, u32[]{:S(2)}, u32[]{:S(2)}) collective-permute-start(bf16[1808,128]{1,0:T(8,128)(2,1)} %pack.1.own_at), channel_id=1, source_target_pairs={{1,0},{2,1},{3,2},{5,4},{6,5},{7,6},{9,8},{10,9},{11,10},{13,12},{... | collective-permute-start | bytes 1388552 | tf_op jit(solution)/shard_map/ppermute | solution.py:229
  10.0 0.7 %collective-permute-start.2 = (bf16[1808,128]{1,0:T(8,128)(2,1)}, bf16[1808,128]{1,0:T(8,128)(2,1)S(1)}, u32[]{:S(2)}, u32[]{:S(2)}) collective-permute-start(bf16[1808,128]{1,0:T(8,128)(2,1)} %pack.1.own_at), channel_id=1, source_target_pairs={{4,8},{12,16},{20,24},{8,4},{16,12},{24,20},{5,9},{13,17},{21,25},... | collective-permute-start | bytes 1388552 | tf_op jit(solution)/shard_map/ppermute | solution.py:233
  10.7 2.9 %collective-permute-start.3 = (bf16[1808,128]{1,0:T(8,128)(2,1)}, bf16[1808,128]{1,0:T(8,128)(2,1)S(1)}, u32[]{:S(2)}, u32[]{:S(2)}) collective-permute-start(bf16[1808,128]{1,0:T(8,128)(2,1)} %pack.1.own_at), channel_id=1, source_target_pairs={{0,4},{8,12},{16,20},{24,28},{4,0},{12,8},{20,16},{28,24},{1,5},{9... | collective-permute-start | bytes 1388552 | tf_op jit(solution)/shard_map/ppermute | solution.py:233
  14.3 5.7 %own_source.1 = (bf16[4,256,1024]{2,1,0:T(8,128)(2,1)}, f32[256,256]{1,0:T(8,128)}, bf16[256,256]{1,0:T(8,128)(2,1)}, f32[8,128]{1,0:T(8,128)}, bf16[2,5,2,128,128]{4,3,2,1,0:T(8,128)(2,1)}) custom-call(s32[64]{0:T(128)} %bitcast.23, s32[64]{0:T(128)} %bitcast.24, s32[1]{0:T(128)} %bitcast.11.count, s32[12]{0:T(128)} %bitcast.19, s32[1]{0:T(128)} %bitcast.13.p_count, ...), custom_call_target="tpu_custom_call" | custom-call | flops 1000000000 | bytes 4000000 | tf_op jit(solution)/shard_map/own_source/pallas_call | solution.py:269
  20.0 0.0 copy-start
  20.0 0.0 copy-start.1
  20.0 0.0 copy-start.2
  20.0 0.0 copy-start.3
  20.0 0.8 %copy-done.3 = f32[8,128]{1,0:T(8,128)S(1)} copy-done((f32[8,128]{1,0:T(8,128)S(1)}, f32[8,128]{1,0:T(8,128)}, u32[]{:S(2)}) %copy-start.3) | copy-done | bytes 4120
  20.8 0.0 collective-permute-done.left
  20.8 2.0 %collective-permute-done.1.right = bf16[1808,128]{1,0:T(8,128)(2,1)S(1)} collective-permute-done((bf16[1808,128]{1,0:T(8,128)(2,1)}, bf16[1808,128]{1,0:T(8,128)(2,1)S(1)}, u32[]{:S(2)}, u32[]{:S(2)}) %collective-permute-start.1) | collective-permute-done | bytes 462880 | tf_op jit(solution)/shard_map/ppermute | solution.py:229
  22.9 0.0 copy-done
  22.9 0.0 copy-done.1
  22.9 0.0 copy-done.2
  22.9 2.2 %col_sources.1 = (bf16[2,5,2,128,128]{4,3,2,1,0:T(8,128)(2,1)}, f32[256,256]{1,0:T(8,128)S(1)}) custom-call(bf16[4,256,1024]{2,1,0:T(8,128)(2,1)S(1)} %copy-done, bf16[256,256]{1,0:T(8,128)(2,1)S(1)} %copy-done.1, f32[256,256]{1,0:T(8,128)S(1)} %copy-done.2, bf16[1808,128]{1,0:T(8,128)(2,1)S(1)} %collective-permute-done.left, ...), custom_call_target="tpu_custom_call", output_to_operand_aliasing={{0}: (6, {})} | custom-call | tf_op jit(solution)/shard_map/col_sources/pallas_call | solution.py:319
  25.1 0.0 collective-permute-done.2.other
  25.1 0.0 collective-permute-done.3.pair
  25.1 2.2 %row_sources.1 = (bf16[2,5,2,128,128]{4,3,2,1,0:T(8,128)(2,1)}, f32[3,64,256]{2,1,0:T(8,128)S(1)}, bf16[3,64,256]{2,1,0:T(8,128)(2,1)S(1)}, bf16[3,64,256]{2,1,0:T(8,128)(2,1)S(1)}, bf16[3,64,256]{2,1,0:T(8,128)(2,1)S(1)}) custom-call(bf16[4,256,1024]{2,1,0:T(8,128)(2,1)S(1)} %copy-done, ...), custom_call_target="tpu_custom_call", output_to_operand_aliasing={{0}: (5, {})} | custom-call | tf_op jit(solution)/shard_map/row_sources/pallas_call | solution.py:333
  27.3 2.6 %collective-permute-start.4 = (bf16[3,64,256]{2,1,0:T(8,128)(2,1)S(1)}, bf16[3,64,256]{2,1,0:T(8,128)(2,1)S(1)}, u32[]{:S(2)}, u32[]{:S(2)}) collective-permute-start(bf16[3,64,256]{2,1,0:T(8,128)(2,1)S(1)} %get-tuple-element.23), channel_id=1, source_target_pairs={{0,2},{1,3},{2,0},{3,1},{4,6},{5,7},{6,4},{7,5},{8,10},{9,11},{10,... | collective-permute-start | bytes 294920 | tf_op jit(solution)/shard_map/ppermute | solution.py:229
  29.9 1.7 %collective-permute-start.5 = (bf16[3,64,256]{2,1,0:T(8,128)(2,1)S(1)}, bf16[3,64,256]{2,1,0:T(8,128)(2,1)S(1)}, u32[]{:S(2)}, u32[]{:S(2)}) collective-permute-start(bf16[3,64,256]{2,1,0:T(8,128)(2,1)S(1)} %get-tuple-element.24), channel_id=1, source_target_pairs={{0,1},{1,2},{2,3},{3,0},{4,5},{5,6},{6,7},{7,4},{8,9},{9,10},{10,1... | collective-permute-start | bytes 294920 | tf_op jit(solution)/shard_map/ppermute | solution.py:229
  31.6 2.2 %collective-permute-start.6 = (bf16[3,64,256]{2,1,0:T(8,128)(2,1)S(1)}, bf16[3,64,256]{2,1,0:T(8,128)(2,1)S(1)}, u32[]{:S(2)}, u32[]{:S(2)}) collective-permute-start(bf16[3,64,256]{2,1,0:T(8,128)(2,1)S(1)} %get-tuple-element.25), channel_id=1, source_target_pairs={{0,3},{1,0},{2,1},{3,2},{4,7},{5,4},{6,5},{7,6},{8,11},{9,8},{10,9... | collective-permute-start | bytes 294920 | tf_op jit(solution)/shard_map/ppermute | solution.py:229
  33.7 3.9 %collective-permute-done.4.refs_1_ = bf16[3,64,256]{2,1,0:T(8,128)(2,1)S(1)} collective-permute-done((bf16[3,64,256]{2,1,0:T(8,128)(2,1)S(1)}, bf16[3,64,256]{2,1,0:T(8,128)(2,1)S(1)}, u32[]{:S(2)}, u32[]{:S(2)}) %collective-permute-start.4) | collective-permute-done | bytes 98336 | tf_op jit(solution)/shard_map/ppermute | solution.py:229
  37.6 0.0 collective-permute-done.5.refs_2_
  37.6 1.1 %collective-permute-done.6.refs_3_ = bf16[3,64,256]{2,1,0:T(8,128)(2,1)S(1)} collective-permute-done((bf16[3,64,256]{2,1,0:T(8,128)(2,1)S(1)}, bf16[3,64,256]{2,1,0:T(8,128)(2,1)S(1)}, u32[]{:S(2)}, u32[]{:S(2)}) %collective-permute-start.6) | collective-permute-done | bytes 98336 | tf_op jit(solution)/shard_map/ppermute | solution.py:229
  38.8 3.2 %collective-permute-start.7 = (bf16[3,64,256]{2,1,0:T(8,128)(2,1)S(1)}, bf16[3,64,256]{2,1,0:T(8,128)(2,1)S(1)}, u32[]{:S(2)}, u32[]{:S(2)}) collective-permute-start(bf16[3,64,256]{2,1,0:T(8,128)(2,1)S(1)} %total.1.refs_0_), channel_id=1, source_target_pairs={{0,2},{1,3},{2,0},{3,1},{4,6},{5,7},{6,4},{7,5},{8,10},{9,11},{10,... | collective-permute-start | bytes 294920 | tf_op jit(solution)/shard_map/ppermute | solution.py:229
  41.9 0.0 collective-permute-start.8
  41.9 3.8 %collective-permute-start.9 = (bf16[3,64,256]{2,1,0:T(8,128)(2,1)S(1)}, bf16[3,64,256]{2,1,0:T(8,128)(2,1)S(1)}, u32[]{:S(2)}, u32[]{:S(2)}) collective-permute-start(bf16[3,64,256]{2,1,0:T(8,128)(2,1)S(1)} %total.1.refs_0_), channel_id=1, source_target_pairs={{0,3},{1,0},{2,1},{3,2},{4,7},{5,4},{6,5},{7,6},{8,11},{9,8},{10,9... | collective-permute-start | bytes 294920 | tf_op jit(solution)/shard_map/ppermute | solution.py:229
  45.7 3.7 %collective-permute-done.7.refs_1_ = bf16[3,64,256]{2,1,0:T(8,128)(2,1)S(1)} collective-permute-done((bf16[3,64,256]{2,1,0:T(8,128)(2,1)S(1)}, bf16[3,64,256]{2,1,0:T(8,128)(2,1)S(1)}, u32[]{:S(2)}, u32[]{:S(2)}) %collective-permute-start.7) | collective-permute-done | bytes 98336 | tf_op jit(solution)/shard_map/ppermute | solution.py:229
  49.4 0.0 collective-permute-done.8.refs_2_
  49.4 0.9 %collective-permute-done.9.refs_3_ = bf16[3,64,256]{2,1,0:T(8,128)(2,1)S(1)} collective-permute-done((bf16[3,64,256]{2,1,0:T(8,128)(2,1)S(1)}, bf16[3,64,256]{2,1,0:T(8,128)(2,1)S(1)}, u32[]{:S(2)}, u32[]{:S(2)}) %collective-permute-start.9) | collective-permute-done | bytes 98336 | tf_op jit(solution)/shard_map/ppermute | solution.py:229
  50.3 0.9 %spread.1 = f32[2,3,2,128,128]{4,3,2,1,0:T(8,128)} custom-call(bf16[3,64,256]{2,1,0:T(8,128)(2,1)S(1)} %total.1.refs_0_, bf16[3,64,256]{2,1,0:T(8,128)(2,1)S(1)} %collective-permute-done.7.refs_1_, bf16[3,64,256]{2,1,0:T(8,128)(2,1)S(1)} %collective-permute-done.8.refs_2_, bf16[3,64,256]{2,1,0:T(8,128)(2,1)S(1)} %collective-permute-done.9.refs_3_), custom_call_target="tpu_custom_call" | custom-call | tf_op jit(solution)/shard_map/spread/pallas_call | solution.py:350
  (2 shorter events, 0.0 us)
Async XLA Ops:
  3.7 17.1 %collective-permute-start = (bf16[1808,128]{1,0:T(8,128)(2,1)}, bf16[1808,128]{1,0:T(8,128)(2,1)S(1)}, u32[]{:S(2)}, u32[]{:S(2)}) collective-permute-start(bf16[1808,128]{1,0:T(8,128)(2,1)} %pack.1.own_at), channel_id=1, source_target_pairs={{0,1},{1,2},{2,3},{4,5},{5,6},{6,7},{8,9},{9,10},{10,11},{12,13},{... | collective-permute-start | bytes 1388552 | tf_op jit(solution)/shard_map/ppermute | solution.py:229
  8.7 14.2 %collective-permute-start.1 = (bf16[1808,128]{1,0:T(8,128)(2,1)}, bf16[1808,128]{1,0:T(8,128)(2,1)S(1)}, u32[]{:S(2)}, u32[]{:S(2)}) collective-permute-start(bf16[1808,128]{1,0:T(8,128)(2,1)} %pack.1.own_at), channel_id=1, source_target_pairs={{1,0},{2,1},{3,2},{5,4},{6,5},{7,6},{9,8},{10,9},{11,10},{13,12},{... | collective-permute-start | bytes 1388552 | tf_op jit(solution)/shard_map/ppermute | solution.py:229
  10.0 15.1 %collective-permute-start.2 = (bf16[1808,128]{1,0:T(8,128)(2,1)}, bf16[1808,128]{1,0:T(8,128)(2,1)S(1)}, u32[]{:S(2)}, u32[]{:S(2)}) collective-permute-start(bf16[1808,128]{1,0:T(8,128)(2,1)} %pack.1.own_at), channel_id=1, source_target_pairs={{4,8},{12,16},{20,24},{8,4},{16,12},{24,20},{5,9},{13,17},{21,25},... | collective-permute-start | bytes 1388552 | tf_op jit(solution)/shard_map/ppermute | solution.py:233
  10.7 14.4 %collective-permute-start.3 = (bf16[1808,128]{1,0:T(8,128)(2,1)}, bf16[1808,128]{1,0:T(8,128)(2,1)S(1)}, u32[]{:S(2)}, u32[]{:S(2)}) collective-permute-start(bf16[1808,128]{1,0:T(8,128)(2,1)} %pack.1.own_at), channel_id=1, source_target_pairs={{0,4},{8,12},{16,20},{24,28},{4,0},{12,8},{20,16},{28,24},{1,5},{9... | collective-permute-start | bytes 1388552 | tf_op jit(solution)/shard_map/ppermute | solution.py:233
  20.0 2.9 %copy-start = (bf16[4,256,1024]{2,1,0:T(8,128)(2,1)S(1)}, bf16[4,256,1024]{2,1,0:T(8,128)(2,1)}, u32[]{:S(2)}) copy-start(bf16[4,256,1024]{2,1,0:T(8,128)(2,1)} %get-tuple-element.14.stock) | copy-start | bytes 6291460
  20.0 2.9 %copy-start.1 = (bf16[256,256]{1,0:T(8,128)(2,1)S(1)}, bf16[256,256]{1,0:T(8,128)(2,1)}, u32[]{:S(2)}) copy-start(bf16[256,256]{1,0:T(8,128)(2,1)} %get-tuple-element.15.lift_t) | copy-start | bytes 393220
  20.0 2.9 %copy-start.2 = (f32[256,256]{1,0:T(8,128)S(1)}, f32[256,256]{1,0:T(8,128)}, u32[]{:S(2)}) copy-start(f32[256,256]{1,0:T(8,128)} %get-tuple-element.16.half) | copy-start | bytes 786436
  20.0 0.8 %copy-start.3 = (f32[8,128]{1,0:T(8,128)S(1)}, f32[8,128]{1,0:T(8,128)}, u32[]{:S(2)}) copy-start(f32[8,128]{1,0:T(8,128)} %get-tuple-element.17.token) | copy-start | bytes 12292
  27.3 10.4 %collective-permute-start.4 = (bf16[3,64,256]{2,1,0:T(8,128)(2,1)S(1)}, bf16[3,64,256]{2,1,0:T(8,128)(2,1)S(1)}, u32[]{:S(2)}, u32[]{:S(2)}) collective-permute-start(bf16[3,64,256]{2,1,0:T(8,128)(2,1)S(1)} %get-tuple-element.23), channel_id=1, source_target_pairs={{0,2},{1,3},{2,0},{3,1},{4,6},{5,7},{6,4},{7,5},{8,10},{9,11},{10,... | collective-permute-start | bytes 294920 | tf_op jit(solution)/shard_map/ppermute | solution.py:229
  29.9 7.7 %collective-permute-start.5 = (bf16[3,64,256]{2,1,0:T(8,128)(2,1)S(1)}, bf16[3,64,256]{2,1,0:T(8,128)(2,1)S(1)}, u32[]{:S(2)}, u32[]{:S(2)}) collective-permute-start(bf16[3,64,256]{2,1,0:T(8,128)(2,1)S(1)} %get-tuple-element.24), channel_id=1, source_target_pairs={{0,1},{1,2},{2,3},{3,0},{4,5},{5,6},{6,7},{7,4},{8,9},{9,10},{10,1... | collective-permute-start | bytes 294920 | tf_op jit(solution)/shard_map/ppermute | solution.py:229
  31.6 7.1 %collective-permute-start.6 = (bf16[3,64,256]{2,1,0:T(8,128)(2,1)S(1)}, bf16[3,64,256]{2,1,0:T(8,128)(2,1)S(1)}, u32[]{:S(2)}, u32[]{:S(2)}) collective-permute-start(bf16[3,64,256]{2,1,0:T(8,128)(2,1)S(1)} %get-tuple-element.25), channel_id=1, source_target_pairs={{0,3},{1,0},{2,1},{3,2},{4,7},{5,4},{6,5},{7,6},{8,11},{9,8},{10,9... | collective-permute-start | bytes 294920 | tf_op jit(solution)/shard_map/ppermute | solution.py:229
  38.8 10.7 %collective-permute-start.7 = (bf16[3,64,256]{2,1,0:T(8,128)(2,1)S(1)}, bf16[3,64,256]{2,1,0:T(8,128)(2,1)S(1)}, u32[]{:S(2)}, u32[]{:S(2)}) collective-permute-start(bf16[3,64,256]{2,1,0:T(8,128)(2,1)S(1)} %total.1.refs_0_), channel_id=1, source_target_pairs={{0,2},{1,3},{2,0},{3,1},{4,6},{5,7},{6,4},{7,5},{8,10},{9,11},{10,... | collective-permute-start | bytes 294920 | tf_op jit(solution)/shard_map/ppermute | solution.py:229
  41.9 7.5 %collective-permute-start.8 = (bf16[3,64,256]{2,1,0:T(8,128)(2,1)S(1)}, bf16[3,64,256]{2,1,0:T(8,128)(2,1)S(1)}, u32[]{:S(2)}, u32[]{:S(2)}) collective-permute-start(bf16[3,64,256]{2,1,0:T(8,128)(2,1)S(1)} %total.1.refs_0_), channel_id=1, source_target_pairs={{0,1},{1,2},{2,3},{3,0},{4,5},{5,6},{6,7},{7,4},{8,9},{9,10},{10,1... | collective-permute-start | bytes 294920 | tf_op jit(solution)/shard_map/ppermute | solution.py:229
  41.9 8.4 %collective-permute-start.9 = (bf16[3,64,256]{2,1,0:T(8,128)(2,1)S(1)}, bf16[3,64,256]{2,1,0:T(8,128)(2,1)S(1)}, u32[]{:S(2)}, u32[]{:S(2)}) collective-permute-start(bf16[3,64,256]{2,1,0:T(8,128)(2,1)S(1)} %total.1.refs_0_), channel_id=1, source_target_pairs={{0,3},{1,0},{2,1},{3,2},{4,7},{5,4},{6,5},{7,6},{8,11},{9,8},{10,9... | collective-permute-start | bytes 294920 | tf_op jit(solution)/shard_map/ppermute | solution.py:229

commit v8 on v6

--- a/solution.py
+++ b/solution.py
@@ -13,7 +13,7 @@
 G2 = 2
 NS = 5
 PB = FB * CB
-UNROLL = 4
+UNROLL = 8
 META = 16
 F32 = jnp.float32
 BF16 = jnp.bfloat16
@@ -26,27 +26,42 @@
 WHOLE = pltpu.CompilerParams(vmem_limit_bytes=60 * 1024 * 1024)
 
 
-def pack_kernel(codes, count, aggs, blocks, second, out, held, sems):
+def pack_kernel(
+    codes_at, count_at, aggs_at, blocks, second, out, held, codes, count, aggs, table, sems
+):
     n_p, n_s = blocks.shape[0], second.shape[0]
-    slots = codes.shape[0]
-    copies = [
-        pltpu.make_async_copy(blocks, held.at[0:n_p], sems.at[0]),
-        pltpu.make_async_copy(second, held.at[n_p : n_p + n_s], sems.at[1]),
+    slots, cut = codes_at.shape[-1], n_p // 2
+    small = [
+        pltpu.make_async_copy(a, b, sems.at[n])
+        for n, (a, b) in enumerate([(codes_at, codes), (count_at, count), (aggs_at, aggs)])
     ]
-    for copy in copies:
+    large = [
+        pltpu.make_async_copy(blocks.at[0:cut], held.at[0:cut], sems.at[3]),
+        pltpu.make_async_copy(blocks.at[cut:n_p], held.at[cut:n_p], sems.at[4]),
+        pltpu.make_async_copy(second, held.at[n_p : n_p + n_s], sems.at[5]),
+    ]
+    for copy in small + large:
         copy.start()
+    for copy in small:
+        copy.wait()
+    fill_table(0, slots, table, lambda k: jnp.where(k < count[0, 0], codes[0, 0, k], PB))
     lane = lax.broadcasted_iota(jnp.int32, (META, out.shape[1]), 1)
     word = jnp.zeros(lane.shape, jnp.int32)
-    for k in range(slots):
-        word = jnp.where(lane == k, jnp.where(k < count[0], codes[k], PB), word)
+    for q in range(PB):
+        word = jnp.where(lane == q, table[0, q], word)
     for j in range(CB):
-        word = jnp.where(lane == slots + j, aggs[j], word)
+        word = jnp.where(lane == PB + j, aggs[0, 0, j], word)
     held[n_p + n_s : n_p + n_s + META, :] = word.astype(F32).astype(BF16)
-    for copy in copies:
-        copy.wait()
-    whole = pltpu.make_async_copy(held, out, sems.at[2])
-    whole.start()
-    whole.wait()
+    large[0].wait()
+    stores = [pltpu.make_async_copy(held.at[0:cut], out.at[0:cut], sems.at[6])]
+    stores[0].start()
+    large[1].wait()
+    large[2].wait()
+    rest = pl.ds(cut, out.shape[0] - cut)
+    stores.append(pltpu.make_async_copy(held.at[rest], out.at[rest], sems.at[7]))
+    stores[1].start()
+    for store in stores:
+        store.wait()
 
 
 def fill_table(s, slots, table, code_of):
@@ -100,12 +115,14 @@
     fetch_fine = pltpu.make_async_copy(fine_at, fine, sems.at[1])
     fetch_fine.start()
     acc[...] = jnp.zeros_like(acc)
-    fill_table(0, slots, table, lambda k: jnp.where(k < p_count[0], codes[k], PB))
+    turned[...] = jnp.zeros_like(turned)
+    code_of = lambda k: jnp.where(k < p_count[0], codes[k], PB)
+    fill_table(0, slots, table, code_of)
     fetch_own.wait()
-    for i in range(FB):
-        for j in range(CB):
-            block = block_at(0, i * CB + j, size, table, own)
-            turned[i, j * size : (j + 1) * size, :] = block.T
+    for k in range(slots):
+        i = code_of(k) // CB
+        j = pl.multiple_of((code_of(k) - i * CB) * size, size)
+        turned[i, pl.ds(j, size), :] = own[k * size : (k + 1) * size, :].T
     fetch_fine.wait()
 
     def step(t, carry):
@@ -142,7 +159,7 @@
 
 
 def near_coarse(
-    sources, near, slots, size, stock, c_one, dense, tiles, words, codes, table, sems
+    sources, near, slots, size, stock, c_one, dense, tiles, words, codes, sems
 ):
     tail = (slots + CB) * size
     for n, ref in enumerate(near):
@@ -153,13 +170,12 @@
     fetch.wait()
     parts, stores = [], []
     for n, (s, ref) in enumerate(zip(sources, near)):
-        fill_table(n, slots, table, lambda k: codes[n, k])
-        dense_of(n, size, table, ref, dense.at[n])
+        dense_of(n, size, codes, ref, dense.at[n])
         coarse = coarse_of(size, stock[s - 1], dense.at[n], tiles.at[n])
         store = pltpu.make_async_copy(tiles.at[n], c_one.at[:, s], sems.at[1 + n])
         store.start()
         stores.append(store)
-        lift = lift_of(ref, slots, size, lambda j: codes[n, slots + j])
+        lift = lift_of(ref, slots, size, lambda j: codes[n, PB + j])
         parts.append(jnp.dot(coarse, lift, preferred_element_type=F32))
     return parts, stores
 
@@ -243,13 +259,20 @@
     packed = pl.pallas_call(
         pack_kernel,
         out_shape=jax.ShapeDtypeStruct((packed_rows, size), BF16),
-        in_specs=[SMEM] * 3 + [HBM] * 2,
+        in_specs=[HBM] * 5,
         out_specs=HBM,
-        scratch_shapes=[pltpu.VMEM((packed_rows, size), BF16), dma((3,))],
+        scratch_shapes=[
+            pltpu.VMEM((packed_rows, size), BF16),
+            pltpu.SMEM(prolong_codes.shape, jnp.int32),
+            pltpu.SMEM(prolong_counts.shape, jnp.int32),
+            pltpu.SMEM(second_aggs.shape, jnp.int32),
+            pltpu.SMEM((1, PB + 1), jnp.int32),
+            dma((8,)),
+        ],
         compiler_params=WHOLE,
         name="pack",
     )(
-        prolong_codes[0, 0], prolong_counts[0], second_aggs[0, 0],
+        prolong_codes, prolong_counts, second_aggs,
         prolong_blocks.reshape(slots * size, size),
         second_blocks.reshape(CB * size, size),
     )
@@ -260,7 +283,7 @@
     right = shift(packed, "col", -1, False)
 
     c_shape = jax.ShapeDtypeStruct((CB, NS, CB, size, size), BF16)
-    table = pltpu.SMEM((NS, PB + 1), jnp.int32)
+    table = pltpu.SMEM((1, PB + 1), jnp.int32)
     stock, more, c_one = pl.pallas_call(
         functools.partial(own_kernel, slots, size),
         out_shape=[
@@ -275,7 +298,7 @@
             pltpu.VMEM((packed_rows, size), BF16),
             pltpu.VMEM((NS - 1, wide, FB * size), BF16),
             pltpu.VMEM((3, wide, G2 * size), BF16),
-            pltpu.VMEM((FB, wide, size), BF16),
+            pltpu.VMEM((FB + 1, wide, size), BF16),
             pltpu.VMEM((NS * FB + 1, wide, size), F32),
             pltpu.VMEM((FB * size, wide), BF16),
             pltpu.VMEM((CB, CB, size, size), BF16),
@@ -296,7 +319,6 @@
         pltpu.VMEM((2, CB, CB, size, size), BF16),
         pltpu.VMEM((8, size), jnp.int32),
         pltpu.SMEM((8, size), jnp.int32),
-        table,
         dma((3,)),
     ]
     square = jax.ShapeDtypeStruct((wide, G2 * size), F32)

time: 51.6 us -> 50.6 us (0.981)
  Pallas kernels: 16 us -> 12.6 us
  starting transfers between devices: 14.1 us -> 16.6 us
    pallas_call x1, Pallas kernels: 8.06 us -> 5.32 us  [per_device(): pl.pallas_call(functools.partial(own_kernel, slots, size), out_shape=[jax...]
    ppermute x8, starting transfers between devices: 9.8 us -> 12.3 us  [shift(): return lax.ppermute(x, axis, pairs)]
    ppermute x2, waiting for transfers between devices: 0.01 us -> 1.21 us  [swap(): return lax.ppermute(x, axis, pairs + [(j, i) for i, j in pairs])]
    ppermute x8, waiting for transfers between devices: 17.5 us -> 16.3 us  [shift(): return lax.ppermute(x, axis, pairs)]
    pallas_call x1, Pallas kernels: 2.46 us -> 1.81 us  [per_device(): pl.pallas_call(pack_kernel, out_shape=jax.ShapeDtypeStruct((packed_rows,...]
  transfers between devices with their start and end apart: 10 -> 10, of which waited for: 6 -> 7; matrix products, arithmetic and copies ran while one was open for 0% -> 0% of each run, Pallas kernels for 20% -> 15%
where the time goes in v8:
time: 50.6 us; the launch traced here: 50.2 us
  waiting for transfers between devices  17.5 us (35%)
  starting transfers between devices  16.6 us (33%)
  Pallas kernels  12.6 us (25%)
  between operations  2.05 us (4%)
  local copies, waits for them, and re-layouts  1.48 us (3%)
    ppermute x8, waiting for transfers between devices, shift(): return lax.ppermute(x, axis, pairs)  16.3 us
    ppermute x8, starting transfers between devices, shift(): return lax.ppermute(x, axis, pairs)  12.3 us
    pallas_call x1, Pallas kernels, per_device(): pl.pallas_call(functools.partial(own_kernel, slots, size), out_shape=[jax...  5.32 us
    ppermute x2, starting transfers between devices, swap(): return lax.ppermute(x, axis, pairs + [(j, i) for i, j in pairs])  4.31 us
    pallas_call x1, Pallas kernels, per_device(): pl.pallas_call(functools.partial(row_kernel, slots, size, cols_n), out_sh...  2.14 us
    pallas_call x1, Pallas kernels, per_device(): pl.pallas_call(functools.partial(side_kernel, slots, size), out_shape=[c_...  2.14 us
    pallas_call x1, Pallas kernels, per_device(): pl.pallas_call(pack_kernel, out_shape=jax.ShapeDtypeStruct((packed_rows,...  1.81 us
    unnamed x4, local copies, waits for them, and re-layouts  1.48 us
  transfers between devices with their start and end apart: 10, of which 7 were waited for; matrix products, arithmetic and copies ran while one was open for 0% of the time, Pallas kernels for 15%

profile of v8, /device:TPU:11, one launch (start us, length us, event | category | flops | bytes accessed | tf_op | source)
XLA Modules:
  0.0 50.2 jit_solution(15557327376624581851)
XLA Ops:
  1.3 1.8 %pack.1.own_at = bf16[1808,128]{1,0:T(8,128)(2,1)} custom-call(s32[1,1,12]{2,1,0:T(1,128)} %codes_at.1, s32[1,1]{1,0:T(1,128)} %copy.16.count_at, s32[1,1,2]{2,1,0:T(1,128)} %aggs_at.1, bf16[1536,128]{1,0:T(8,128)(2,1)} %bitcast.15, bf16[256,128]{1,0:T(8,128)(2,1)} %bitcast.16), custom_call_target="tpu_custom_call" | custom-call | tf_op jit(solution)/shard_map/pack/pallas_call | solution.py:259
  3.1 3.2 %collective-permute-start = (bf16[1808,128]{1,0:T(8,128)(2,1)}, bf16[1808,128]{1,0:T(8,128)(2,1)S(1)}, u32[]{:S(2)}, u32[]{:S(2)}) collective-permute-start(bf16[1808,128]{1,0:T(8,128)(2,1)} %pack.1.own_at), channel_id=1, source_target_pairs={{0,1},{1,2},{2,3},{4,5},{5,6},{6,7},{8,9},{9,10},{10,11},{12,13},{... | collective-permute-start | bytes 1388552 | tf_op jit(solution)/shard_map/ppermute | solution.py:242
  6.3 2.1 %collective-permute-start.1 = (bf16[1808,128]{1,0:T(8,128)(2,1)}, bf16[1808,128]{1,0:T(8,128)(2,1)S(1)}, u32[]{:S(2)}, u32[]{:S(2)}) collective-permute-start(bf16[1808,128]{1,0:T(8,128)(2,1)} %pack.1.own_at), channel_id=1, source_target_pairs={{1,0},{2,1},{3,2},{5,4},{6,5},{7,6},{9,8},{10,9},{11,10},{13,12},{... | collective-permute-start | bytes 1388552 | tf_op jit(solution)/shard_map/ppermute | solution.py:242
  8.4 4.2 %collective-permute-start.2 = (bf16[1808,128]{1,0:T(8,128)(2,1)}, bf16[1808,128]{1,0:T(8,128)(2,1)S(1)}, u32[]{:S(2)}, u32[]{:S(2)}) collective-permute-start(bf16[1808,128]{1,0:T(8,128)(2,1)} %pack.1.own_at), channel_id=1, source_target_pairs={{4,8},{12,16},{20,24},{8,4},{16,12},{24,20},{5,9},{13,17},{21,25},... | collective-permute-start | bytes 1388552 | tf_op jit(solution)/shard_map/ppermute | solution.py:246
  12.7 0.1 collective-permute-start.3
  13.4 5.3 %own_source.1 = (bf16[4,256,1024]{2,1,0:T(8,128)(2,1)}, bf16[3,256,256]{2,1,0:T(8,128)(2,1)}, bf16[2,5,2,128,128]{4,3,2,1,0:T(8,128)(2,1)}) custom-call(s32[64]{0:T(128)} %bitcast.20, s32[64]{0:T(128)} %bitcast.21, s32[1]{0:T(128)} %bitcast.11.count, s32[12]{0:T(128)} %bitcast.17, s32[1]{0:T(128)} %bitcast.12.p_count, s32[2]{0:T(128)} %bitcast.18, ...), custom_call_target="tpu_custom_call" | custom-call | flops 1000000000 | bytes 4000000 | tf_op jit(solution)/shard_map/own_source/pallas_call | solution.py:287
  18.7 0.0 copy-start
  18.7 0.0 copy-start.1
  18.7 1.1 %copy-done.1 = bf16[3,256,256]{2,1,0:T(8,128)(2,1)S(1)} copy-done((bf16[3,256,256]{2,1,0:T(8,128)(2,1)S(1)}, bf16[3,256,256]{2,1,0:T(8,128)(2,1)}, u32[]{:S(2)}) %copy-start.1) | copy-done | bytes 393240
  19.9 0.2 own_half.1
  20.1 0.0 collective-permute-done.left
  20.1 0.0 collective-permute-done.1.right
  20.1 0.3 copy-done
  20.4 2.1 %col_sources.1 = (bf16[2,5,2,128,128]{4,3,2,1,0:T(8,128)(2,1)}, f32[256,256]{1,0:T(8,128)S(1)}) custom-call(bf16[4,256,1024]{2,1,0:T(8,128)(2,1)S(1)} %copy-done, bf16[256,256]{1,0:T(8,128)(2,1)S(1)} %get-tuple-element.16.lift_t, f32[256,256]{1,0:T(8,128)S(1)} %get-tuple-element.17.half, ...), custom_call_target="tpu_custom_call", output_to_operand_aliasing={{0}: (5, {})} | custom-call | tf_op jit(solution)/shard_map/col_sources/pallas_call | solution.py:334
  22.6 1.2 %collective-permute-done.2.other = bf16[1808,128]{1,0:T(8,128)(2,1)S(1)} collective-permute-done((bf16[1808,128]{1,0:T(8,128)(2,1)}, bf16[1808,128]{1,0:T(8,128)(2,1)S(1)}, u32[]{:S(2)}, u32[]{:S(2)}) %collective-permute-start.2) | collective-permute-done | bytes 462880 | tf_op jit(solution)/shard_map/ppermute | solution.py:246
  23.8 0.0 collective-permute-done.3.pair
  23.8 2.1 %row_sources.1 = (bf16[2,5,2,128,128]{4,3,2,1,0:T(8,128)(2,1)}, f32[3,64,256]{2,1,0:T(8,128)S(1)}, bf16[3,64,256]{2,1,0:T(8,128)(2,1)S(1)}, bf16[3,64,256]{2,1,0:T(8,128)(2,1)S(1)}, bf16[3,64,256]{2,1,0:T(8,128)(2,1)S(1)}) custom-call(bf16[4,256,1024]{2,1,0:T(8,128)(2,1)S(1)} %copy-done, ...), custom_call_target="tpu_custom_call", output_to_operand_aliasing={{0}: (5, {})} | custom-call | tf_op jit(solution)/shard_map/row_sources/pallas_call | solution.py:348
  25.9 1.6 %collective-permute-start.4 = (bf16[3,64,256]{2,1,0:T(8,128)(2,1)S(1)}, bf16[3,64,256]{2,1,0:T(8,128)(2,1)S(1)}, u32[]{:S(2)}, u32[]{:S(2)}) collective-permute-start(bf16[3,64,256]{2,1,0:T(8,128)(2,1)S(1)} %get-tuple-element.23), channel_id=1, source_target_pairs={{0,1},{1,2},{2,3},{3,0},{4,5},{5,6},{6,7},{7,4},{8,9},{9,10},{10,1... | collective-permute-start | bytes 294920 | tf_op jit(solution)/shard_map/ppermute | solution.py:242
  27.6 0.8 %collective-permute-start.5 = (bf16[3,64,256]{2,1,0:T(8,128)(2,1)S(1)}, bf16[3,64,256]{2,1,0:T(8,128)(2,1)S(1)}, u32[]{:S(2)}, u32[]{:S(2)}) collective-permute-start(bf16[3,64,256]{2,1,0:T(8,128)(2,1)S(1)} %get-tuple-element.24), channel_id=1, source_target_pairs={{0,2},{1,3},{2,0},{3,1},{4,6},{5,7},{6,4},{7,5},{8,10},{9,11},{10,... | collective-permute-start | bytes 294920 | tf_op jit(solution)/shard_map/ppermute | solution.py:242
  28.4 1.4 %collective-permute-start.6 = (bf16[3,64,256]{2,1,0:T(8,128)(2,1)S(1)}, bf16[3,64,256]{2,1,0:T(8,128)(2,1)S(1)}, u32[]{:S(2)}, u32[]{:S(2)}) collective-permute-start(bf16[3,64,256]{2,1,0:T(8,128)(2,1)S(1)} %get-tuple-element.25), channel_id=1, source_target_pairs={{0,3},{1,0},{2,1},{3,2},{4,7},{5,4},{6,5},{7,6},{8,11},{9,8},{10,9... | collective-permute-start | bytes 294920 | tf_op jit(solution)/shard_map/ppermute | solution.py:242
  29.8 0.8 %collective-permute-done.4.refs_1_ = bf16[3,64,256]{2,1,0:T(8,128)(2,1)S(1)} collective-permute-done((bf16[3,64,256]{2,1,0:T(8,128)(2,1)S(1)}, bf16[3,64,256]{2,1,0:T(8,128)(2,1)S(1)}, u32[]{:S(2)}, u32[]{:S(2)}) %collective-permute-start.4) | collective-permute-done | bytes 98336 | tf_op jit(solution)/shard_map/ppermute | solution.py:242
  30.5 6.0 %collective-permute-done.5.refs_2_ = bf16[3,64,256]{2,1,0:T(8,128)(2,1)S(1)} collective-permute-done((bf16[3,64,256]{2,1,0:T(8,128)(2,1)S(1)}, bf16[3,64,256]{2,1,0:T(8,128)(2,1)S(1)}, u32[]{:S(2)}, u32[]{:S(2)}) %collective-permute-start.5) | collective-permute-done | bytes 98336 | tf_op jit(solution)/shard_map/ppermute | solution.py:242
  36.5 1.4 %collective-permute-done.6.refs_3_ = bf16[3,64,256]{2,1,0:T(8,128)(2,1)S(1)} collective-permute-done((bf16[3,64,256]{2,1,0:T(8,128)(2,1)S(1)}, bf16[3,64,256]{2,1,0:T(8,128)(2,1)S(1)}, u32[]{:S(2)}, u32[]{:S(2)}) %collective-permute-start.6) | collective-permute-done | bytes 98336 | tf_op jit(solution)/shard_map/ppermute | solution.py:242
  38.0 0.1 collective-permute-start.7
  38.0 1.7 %collective-permute-start.8 = (bf16[3,64,256]{2,1,0:T(8,128)(2,1)S(1)}, bf16[3,64,256]{2,1,0:T(8,128)(2,1)S(1)}, u32[]{:S(2)}, u32[]{:S(2)}) collective-permute-start(bf16[3,64,256]{2,1,0:T(8,128)(2,1)S(1)} %total.1.refs_0_), channel_id=1, source_target_pairs={{0,2},{1,3},{2,0},{3,1},{4,6},{5,7},{6,4},{7,5},{8,10},{9,11},{10,... | collective-permute-start | bytes 294920 | tf_op jit(solution)/shard_map/ppermute | solution.py:242
  39.8 1.4 %collective-permute-start.9 = (bf16[3,64,256]{2,1,0:T(8,128)(2,1)S(1)}, bf16[3,64,256]{2,1,0:T(8,128)(2,1)S(1)}, u32[]{:S(2)}, u32[]{:S(2)}) collective-permute-start(bf16[3,64,256]{2,1,0:T(8,128)(2,1)S(1)} %total.1.refs_0_), channel_id=1, source_target_pairs={{0,3},{1,0},{2,1},{3,2},{4,7},{5,4},{6,5},{7,6},{8,11},{9,8},{10,9... | collective-permute-start | bytes 294920 | tf_op jit(solution)/shard_map/ppermute | solution.py:242
  41.2 0.8 %collective-permute-done.7.refs_1_ = bf16[3,64,256]{2,1,0:T(8,128)(2,1)S(1)} collective-permute-done((bf16[3,64,256]{2,1,0:T(8,128)(2,1)S(1)}, bf16[3,64,256]{2,1,0:T(8,128)(2,1)S(1)}, u32[]{:S(2)}, u32[]{:S(2)}) %collective-permute-start.7) | collective-permute-done | bytes 98336 | tf_op jit(solution)/shard_map/ppermute | solution.py:242
  41.9 4.4 %collective-permute-done.8.refs_2_ = bf16[3,64,256]{2,1,0:T(8,128)(2,1)S(1)} collective-permute-done((bf16[3,64,256]{2,1,0:T(8,128)(2,1)S(1)}, bf16[3,64,256]{2,1,0:T(8,128)(2,1)S(1)}, u32[]{:S(2)}, u32[]{:S(2)}) %collective-permute-start.8) | collective-permute-done | bytes 98336 | tf_op jit(solution)/shard_map/ppermute | solution.py:242
  46.3 2.9 %collective-permute-done.9.refs_3_ = bf16[3,64,256]{2,1,0:T(8,128)(2,1)S(1)} collective-permute-done((bf16[3,64,256]{2,1,0:T(8,128)(2,1)S(1)}, bf16[3,64,256]{2,1,0:T(8,128)(2,1)S(1)}, u32[]{:S(2)}, u32[]{:S(2)}) %collective-permute-start.9) | collective-permute-done | bytes 98336 | tf_op jit(solution)/shard_map/ppermute | solution.py:242
  49.3 0.9 %spread.1 = f32[2,3,2,128,128]{4,3,2,1,0:T(8,128)} custom-call(bf16[3,64,256]{2,1,0:T(8,128)(2,1)S(1)} %total.1.refs_0_, bf16[3,64,256]{2,1,0:T(8,128)(2,1)S(1)} %collective-permute-done.7.refs_1_, bf16[3,64,256]{2,1,0:T(8,128)(2,1)S(1)} %collective-permute-done.8.refs_2_, bf16[3,64,256]{2,1,0:T(8,128)(2,1)S(1)} %collective-permute-done.9.refs_3_), custom_call_target="tpu_custom_call" | custom-call | tf_op jit(solution)/shard_map/spread/pallas_call | solution.py:364
  (1 shorter events, 0.0 us)
Async XLA Ops:
  3.1 17.0 %collective-permute-start = (bf16[1808,128]{1,0:T(8,128)(2,1)}, bf16[1808,128]{1,0:T(8,128)(2,1)S(1)}, u32[]{:S(2)}, u32[]{:S(2)}) collective-permute-start(bf16[1808,128]{1,0:T(8,128)(2,1)} %pack.1.own_at), channel_id=1, source_target_pairs={{0,1},{1,2},{2,3},{4,5},{5,6},{6,7},{8,9},{9,10},{10,11},{12,13},{... | collective-permute-start | bytes 1388552 | tf_op jit(solution)/shard_map/ppermute | solution.py:242
  6.3 13.8 %collective-permute-start.1 = (bf16[1808,128]{1,0:T(8,128)(2,1)}, bf16[1808,128]{1,0:T(8,128)(2,1)S(1)}, u32[]{:S(2)}, u32[]{:S(2)}) collective-permute-start(bf16[1808,128]{1,0:T(8,128)(2,1)} %pack.1.own_at), channel_id=1, source_target_pairs={{1,0},{2,1},{3,2},{5,4},{6,5},{7,6},{9,8},{10,9},{11,10},{13,12},{... | collective-permute-start | bytes 1388552 | tf_op jit(solution)/shard_map/ppermute | solution.py:242
  8.4 15.4 %collective-permute-start.2 = (bf16[1808,128]{1,0:T(8,128)(2,1)}, bf16[1808,128]{1,0:T(8,128)(2,1)S(1)}, u32[]{:S(2)}, u32[]{:S(2)}) collective-permute-start(bf16[1808,128]{1,0:T(8,128)(2,1)} %pack.1.own_at), channel_id=1, source_target_pairs={{4,8},{12,16},{20,24},{8,4},{16,12},{24,20},{5,9},{13,17},{21,25},... | collective-permute-start | bytes 1388552 | tf_op jit(solution)/shard_map/ppermute | solution.py:246
  12.7 11.1 %collective-permute-start.3 = (bf16[1808,128]{1,0:T(8,128)(2,1)}, bf16[1808,128]{1,0:T(8,128)(2,1)S(1)}, u32[]{:S(2)}, u32[]{:S(2)}) collective-permute-start(bf16[1808,128]{1,0:T(8,128)(2,1)} %pack.1.own_at), channel_id=1, source_target_pairs={{0,4},{8,12},{16,20},{24,28},{4,0},{12,8},{20,16},{28,24},{1,5},{9... | collective-permute-start | bytes 1388552 | tf_op jit(solution)/shard_map/ppermute | solution.py:246
  18.7 1.7 %copy-start = (bf16[4,256,1024]{2,1,0:T(8,128)(2,1)S(1)}, bf16[4,256,1024]{2,1,0:T(8,128)(2,1)}, u32[]{:S(2)}) copy-start(bf16[4,256,1024]{2,1,0:T(8,128)(2,1)} %get-tuple-element.14.stock) | copy-start | bytes 6291460
  18.7 1.1 %copy-start.1 = (bf16[3,256,256]{2,1,0:T(8,128)(2,1)S(1)}, bf16[3,256,256]{2,1,0:T(8,128)(2,1)}, u32[]{:S(2)}) copy-start(bf16[3,256,256]{2,1,0:T(8,128)(2,1)} %get-tuple-element.15.more) | copy-start | bytes 1179652
  25.9 4.6 %collective-permute-start.4 = (bf16[3,64,256]{2,1,0:T(8,128)(2,1)S(1)}, bf16[3,64,256]{2,1,0:T(8,128)(2,1)S(1)}, u32[]{:S(2)}, u32[]{:S(2)}) collective-permute-start(bf16[3,64,256]{2,1,0:T(8,128)(2,1)S(1)} %get-tuple-element.23), channel_id=1, source_target_pairs={{0,1},{1,2},{2,3},{3,0},{4,5},{5,6},{6,7},{7,4},{8,9},{9,10},{10,1... | collective-permute-start | bytes 294920 | tf_op jit(solution)/shard_map/ppermute | solution.py:242
  27.6 8.9 %collective-permute-start.5 = (bf16[3,64,256]{2,1,0:T(8,128)(2,1)S(1)}, bf16[3,64,256]{2,1,0:T(8,128)(2,1)S(1)}, u32[]{:S(2)}, u32[]{:S(2)}) collective-permute-start(bf16[3,64,256]{2,1,0:T(8,128)(2,1)S(1)} %get-tuple-element.24), channel_id=1, source_target_pairs={{0,2},{1,3},{2,0},{3,1},{4,6},{5,7},{6,4},{7,5},{8,10},{9,11},{10,... | collective-permute-start | bytes 294920 | tf_op jit(solution)/shard_map/ppermute | solution.py:242
  28.4 9.5 %collective-permute-start.6 = (bf16[3,64,256]{2,1,0:T(8,128)(2,1)S(1)}, bf16[3,64,256]{2,1,0:T(8,128)(2,1)S(1)}, u32[]{:S(2)}, u32[]{:S(2)}) collective-permute-start(bf16[3,64,256]{2,1,0:T(8,128)(2,1)S(1)} %get-tuple-element.25), channel_id=1, source_target_pairs={{0,3},{1,0},{2,1},{3,2},{4,7},{5,4},{6,5},{7,6},{8,11},{9,8},{10,9... | collective-permute-start | bytes 294920 | tf_op jit(solution)/shard_map/ppermute | solution.py:242
  38.0 4.0 %collective-permute-start.7 = (bf16[3,64,256]{2,1,0:T(8,128)(2,1)S(1)}, bf16[3,64,256]{2,1,0:T(8,128)(2,1)S(1)}, u32[]{:S(2)}, u32[]{:S(2)}) collective-permute-start(bf16[3,64,256]{2,1,0:T(8,128)(2,1)S(1)} %total.1.refs_0_), channel_id=1, source_target_pairs={{0,1},{1,2},{2,3},{3,0},{4,5},{5,6},{6,7},{7,4},{8,9},{9,10},{10,1... | collective-permute-start | bytes 294920 | tf_op jit(solution)/shard_map/ppermute | solution.py:242
  38.0 8.3 %collective-permute-start.8 = (bf16[3,64,256]{2,1,0:T(8,128)(2,1)S(1)}, bf16[3,64,256]{2,1,0:T(8,128)(2,1)S(1)}, u32[]{:S(2)}, u32[]{:S(2)}) collective-permute-start(bf16[3,64,256]{2,1,0:T(8,128)(2,1)S(1)} %total.1.refs_0_), channel_id=1, source_target_pairs={{0,2},{1,3},{2,0},{3,1},{4,6},{5,7},{6,4},{7,5},{8,10},{9,11},{10,... | collective-permute-start | bytes 294920 | tf_op jit(solution)/shard_map/ppermute | solution.py:242
  39.8 9.5 %collective-permute-start.9 = (bf16[3,64,256]{2,1,0:T(8,128)(2,1)S(1)}, bf16[3,64,256]{2,1,0:T(8,128)(2,1)S(1)}, u32[]{:S(2)}, u32[]{:S(2)}) collective-permute-start(bf16[3,64,256]{2,1,0:T(8,128)(2,1)S(1)} %total.1.refs_0_), channel_id=1, source_target_pairs={{0,3},{1,0},{2,1},{3,2},{4,7},{5,4},{6,5},{7,6},{8,11},{9,8},{10,9... | collective-permute-start | bytes 294920 | tf_op jit(solution)/shard_map/ppermute | solution.py:242

commit v9 on v8

--- a/solution.py
+++ b/solution.py
@@ -107,7 +107,8 @@
 
 
 def own_kernel(
-    slots, size, rows, cols, count, codes, p_count, aggs, fine_at, own_at, stock_at, more_at, c_one,
+    slots, size, rows, cols, count, codes, p_count, aggs, fine_at, own_at,
+    col_at, row_at, more_at, c_one,
     fine, own, stock, more, turned, acc, dense, tile, table, sems,
 ):
     fetch_own = pltpu.make_async_copy(own_at, own, sems.at[0])
@@ -140,7 +141,8 @@
     for s in range(1, NS):
         for m in range(FB):
             stock[s - 1, :, m * size : (m + 1) * size] = acc[s * FB + m].astype(BF16)
-        stores.append(pltpu.make_async_copy(stock.at[s - 1], stock_at.at[s - 1], sems.at[1 + s]))
+        stock_at, n = (col_at, s - 1) if s < 3 else (row_at, s - 3)
+        stores.append(pltpu.make_async_copy(stock.at[s - 1], stock_at.at[n], sems.at[1 + s]))
         stores[-1].start()
     own_weight = jnp.concatenate([acc[m].astype(BF16) for m in range(FB)], axis=1)
     dense_of(0, size, table, own, dense)
@@ -159,7 +161,7 @@
 
 
 def near_coarse(
-    sources, near, slots, size, stock, c_one, dense, tiles, words, codes, sems
+    base, sources, near, slots, size, stock, c_one, dense, tiles, words, codes, sems
 ):
     tail = (slots + CB) * size
     for n, ref in enumerate(near):
@@ -171,7 +173,7 @@
     parts, stores = [], []
     for n, (s, ref) in enumerate(zip(sources, near)):
         dense_of(n, size, codes, ref, dense.at[n])
-        coarse = coarse_of(size, stock[s - 1], dense.at[n], tiles.at[n])
+        coarse = coarse_of(size, stock[s - base], dense.at[n], tiles.at[n])
         store = pltpu.make_async_copy(tiles.at[n], c_one.at[:, s], sems.at[1 + n])
         store.start()
         stores.append(store)
@@ -185,8 +187,8 @@
     half[...] = jnp.dot(more[1], more[2], preferred_element_type=F32)
 
 
-def side_kernel(slots, size, stock, lift_t, half, left, right, c_in, c_one, term, *scratch):
-    parts, stores = near_coarse((1, 2), (left, right), slots, size, stock, c_one, *scratch)
+def side_kernel(slots, size, stock, lift_t, half, right, left, c_in, c_one, term, *scratch):
+    parts, stores = near_coarse(1, (2, 1), (right, left), slots, size, stock, c_one, *scratch)
     whole = (half[...] + parts[0] + parts[1]).astype(BF16)
     term[...] = jnp.dot(lift_t[...], whole, preferred_element_type=F32)
     for store in stores:
@@ -197,7 +199,7 @@
     sends, terms, scratch = rest[:cols_n], rest[cols_n], rest[cols_n + 1 :]
     odd = lax.rem(lax.axis_index("row"), 2)
     sources = (3 + odd, 4 - odd)
-    parts, stores = near_coarse(sources, (other, pair), slots, size, stock, c_one, *scratch)
+    parts, stores = near_coarse(3, sources, (other, pair), slots, size, stock, c_one, *scratch)
     terms[0] = term[...]
     for n in range(2):
         terms[sources[n] - 2] = jnp.dot(lift_t[...], parts[n].astype(BF16), preferred_element_type=F32)
@@ -218,22 +220,28 @@
 
 
 def spread_kernel(size, cols_n, *refs):
-    out = refs[-1]
-    chunk = refs[0].shape[1]
+    parts, out_at, out, sems = refs[:cols_n], refs[cols_n], refs[cols_n + 1], refs[cols_n + 2]
+    chunk = parts[0].shape[1]
     unit = math.gcd(chunk, size)
     per = size // unit
     me = lax.axis_index("col")
+    stores = []
     for d in range(cols_n):
         owner = lax.rem(me - d + cols_n, cols_n)
         for t in range(chunk // unit):
             at = owner * (chunk // unit) + t
             a = at // per
-            h = pl.multiple_of(lax.rem(at, per) * unit, unit)
+            rows = pl.ds(pl.multiple_of(lax.rem(at, per) * unit, unit), unit)
             for g in range(3):
                 for b in range(G2):
-                    out[a, g, b, pl.ds(h, unit), :] = refs[d][
+                    out[a, g, b, rows, :] = parts[d][
                         g, t * unit : (t + 1) * unit, b * size : (b + 1) * size
                     ].astype(F32)
+            spot = (a, slice(None), slice(None), rows)
+            stores.append(pltpu.make_async_copy(out.at[spot], out_at.at[spot], sems.at[len(stores)]))
+            stores[-1].start()
+    for store in stores:
+        store.wait()
 
 
 def shift(x, axis, step, wrap):
@@ -279,20 +287,21 @@
     rows_n = lax.axis_size("row")
     pair = swap(packed, "row", [(i, i + 1) for i in range(0, rows_n - 1, 2)])
     other = swap(packed, "row", [(i, i + 1) for i in range(1, rows_n - 1, 2)])
+    right = shift(packed, "col", -1, False)
     left = shift(packed, "col", 1, False)
-    right = shift(packed, "col", -1, False)
 
     c_shape = jax.ShapeDtypeStruct((CB, NS, CB, size, size), BF16)
     table = pltpu.SMEM((1, PB + 1), jnp.int32)
-    stock, more, c_one = pl.pallas_call(
+    col_stock, row_stock, more, c_one = pl.pallas_call(
         functools.partial(own_kernel, slots, size),
         out_shape=[
-            jax.ShapeDtypeStruct((NS - 1, wide, FB * size), BF16),
+            jax.ShapeDtypeStruct((2, wide, FB * size), BF16),
+            jax.ShapeDtypeStruct((2, wide, FB * size), BF16),
             jax.ShapeDtypeStruct((3, wide, G2 * size), BF16),
             c_shape,
         ],
         in_specs=[SMEM] * 6 + [HBM] * 2,
-        out_specs=[HBM] * 3,
+        out_specs=[HBM] * 4,
         scratch_shapes=[
             pltpu.VMEM((cap, size, size), BF16),
             pltpu.VMEM((packed_rows, size), BF16),
@@ -340,7 +349,7 @@
         scratch_shapes=near_scratch,
         compiler_params=LARGE,
         name="col_sources",
-    )(stock, lift_t, half, left, right, c_one)
+    )(col_stock, lift_t, half, right, left, c_one)
 
     chunk = G2 * size // cols_n
     kept = jax.ShapeDtypeStruct((3, chunk, G2 * size), F32)
@@ -354,7 +363,7 @@
         scratch_shapes=[pltpu.VMEM((3, G2 * size, G2 * size), F32)] + near_scratch,
         compiler_params=LARGE,
         name="row_sources",
-    )(stock, lift_t, term, other, pair, c_one)
+    )(row_stock, lift_t, term, other, pair, c_one)
     parts = [sends[0]] + [shift(sends[d], "col", d, True) for d in range(1, cols_n)]
     total = pl.pallas_call(
         sum_kernel, out_shape=piece, in_specs=[VMEM] * cols_n, out_specs=VMEM,
@@ -365,7 +374,11 @@
         functools.partial(spread_kernel, size, cols_n),
         out_shape=jax.ShapeDtypeStruct((G2, 3, G2, size, size), F32),
         in_specs=[VMEM] * cols_n,
-        out_specs=VMEM,
+        out_specs=HBM,
+        scratch_shapes=[
+            pltpu.VMEM((G2, 3, G2, size, size), F32),
+            dma((G2 * size // math.gcd(chunk, size),)),
+        ],
         compiler_params=SMALL,
         name="spread",
     )(*gathered)

time: 50.6 us -> 49.6 us (0.980)
  the two profiles are of different devices: /device:TPU:11 before, /device:TPU:0 now
where the time goes in v9:
time: 49.6 us; the launch traced here: 49.3 us
  starting transfers between devices  23.4 us (47%)
  Pallas kernels  12.3 us (25%)
  waiting for transfers between devices  10.5 us (21%)
  between operations  2.07 us (4%)
  local copies, waits for them, and re-layouts  1.11 us (2%)
    ppermute x8, starting transfers between devices, shift(): return lax.ppermute(x, axis, pairs)  19.3 us
    ppermute x8, waiting for transfers between devices, shift(): return lax.ppermute(x, axis, pairs)  10.5 us
    pallas_call x1, Pallas kernels, per_device(): pl.pallas_call(functools.partial(own_kernel, slots, size), out_shape=[jax...  5.02 us
    ppermute x2, starting transfers between devices, swap(): return lax.ppermute(x, axis, pairs + [(j, i) for i, j in pairs])  4.02 us
    pallas_call x1, Pallas kernels, per_device(): pl.pallas_call(functools.partial(row_kernel, slots, size, cols_n), out_sh...  2.15 us
    pallas_call x1, Pallas kernels, per_device(): pl.pallas_call(functools.partial(side_kernel, slots, size), out_shape=[c_...  2.14 us
    pallas_call x1, Pallas kernels, per_device(): pl.pallas_call(pack_kernel, out_shape=jax.ShapeDtypeStruct((packed_rows,...  1.81 us
    unnamed x6, local copies, waits for them, and re-layouts  1.11 us
  transfers between devices with their start and end apart: 10, of which 5 were waited for; matrix products, arithmetic and copies ran while one was open for 0% of the time, Pallas kernels for 15%

profile of v9, /device:TPU:0, one launch (start us, length us, event | category | flops | bytes accessed | tf_op | source)
XLA Modules:
  0.0 49.3 jit_solution(3242293450867423814)
XLA Ops:
  1.3 1.8 %pack.1.own_at = bf16[1808,128]{1,0:T(8,128)(2,1)} custom-call(s32[1,1,12]{2,1,0:T(1,128)} %codes_at.1, s32[1,1]{1,0:T(1,128)} %copy.16.count_at, s32[1,1,2]{2,1,0:T(1,128)} %aggs_at.1, bf16[1536,128]{1,0:T(8,128)(2,1)} %bitcast.15, bf16[256,128]{1,0:T(8,128)(2,1)} %bitcast.16), custom_call_target="tpu_custom_call" | custom-call | tf_op jit(solution)/shard_map/pack/pallas_call | solution.py:267
  3.1 1.3 %collective-permute-start = (bf16[1808,128]{1,0:T(8,128)(2,1)}, bf16[1808,128]{1,0:T(8,128)(2,1)S(1)}, u32[]{:S(2)}, u32[]{:S(2)}) collective-permute-start(bf16[1808,128]{1,0:T(8,128)(2,1)} %pack.1.own_at), channel_id=1, source_target_pairs={{1,0},{2,1},{3,2},{5,4},{6,5},{7,6},{9,8},{10,9},{11,10},{13,12},{... | collective-permute-start | bytes 1388552 | tf_op jit(solution)/shard_map/ppermute | solution.py:250
  4.4 5.6 %collective-permute-start.1 = (bf16[1808,128]{1,0:T(8,128)(2,1)}, bf16[1808,128]{1,0:T(8,128)(2,1)S(1)}, u32[]{:S(2)}, u32[]{:S(2)}) collective-permute-start(bf16[1808,128]{1,0:T(8,128)(2,1)} %pack.1.own_at), channel_id=1, source_target_pairs={{0,1},{1,2},{2,3},{4,5},{5,6},{6,7},{8,9},{9,10},{10,11},{12,13},{... | collective-permute-start | bytes 1388552 | tf_op jit(solution)/shard_map/ppermute | solution.py:250
  10.0 0.7 %collective-permute-start.2 = (bf16[1808,128]{1,0:T(8,128)(2,1)}, bf16[1808,128]{1,0:T(8,128)(2,1)S(1)}, u32[]{:S(2)}, u32[]{:S(2)}) collective-permute-start(bf16[1808,128]{1,0:T(8,128)(2,1)} %pack.1.own_at), channel_id=1, source_target_pairs={{4,8},{12,16},{20,24},{8,4},{16,12},{24,20},{5,9},{13,17},{21,25},... | collective-permute-start | bytes 1388552 | tf_op jit(solution)/shard_map/ppermute | solution.py:254
  10.7 3.3 %collective-permute-start.3 = (bf16[1808,128]{1,0:T(8,128)(2,1)}, bf16[1808,128]{1,0:T(8,128)(2,1)S(1)}, u32[]{:S(2)}, u32[]{:S(2)}) collective-permute-start(bf16[1808,128]{1,0:T(8,128)(2,1)} %pack.1.own_at), channel_id=1, source_target_pairs={{0,4},{8,12},{16,20},{24,28},{4,0},{12,8},{20,16},{28,24},{1,5},{9... | collective-permute-start | bytes 1388552 | tf_op jit(solution)/shard_map/ppermute | solution.py:254
  14.7 5.0 %own_source.1 = (bf16[2,256,1024]{2,1,0:T(8,128)(2,1)}, bf16[2,256,1024]{2,1,0:T(8,128)(2,1)}, bf16[3,256,256]{2,1,0:T(8,128)(2,1)}, bf16[2,5,2,128,128]{4,3,2,1,0:T(8,128)(2,1)}) custom-call(s32[64]{0:T(128)} %bitcast.20, s32[64]{0:T(128)} %bitcast.21, s32[1]{0:T(128)} %bitcast.11.count, s32[12]{0:T(128)} %bitcast.17, s32[1]{0:T(128)} %bitcast.12.p_count, ...), custom_call_target="tpu_custom_call" | custom-call | flops 1000000000 | bytes 4000000 | tf_op jit(solution)/shard_map/own_source/pallas_call | solution.py:295
  19.7 0.0 copy-start.1
  19.7 0.0 copy-start.2
  19.7 1.1 %copy-done.2 = bf16[3,256,256]{2,1,0:T(8,128)(2,1)S(1)} copy-done((bf16[3,256,256]{2,1,0:T(8,128)(2,1)S(1)}, bf16[3,256,256]{2,1,0:T(8,128)(2,1)}, u32[]{:S(2)}) %copy-start.2) | copy-done | bytes 393240
  20.8 0.2 own_half.1
  21.0 0.0 copy-start
  21.0 0.0 collective-permute-done.right
  21.0 0.0 collective-permute-done.1.left
  21.0 0.0 copy-done.1
  21.0 2.1 %col_sources.1 = (bf16[2,5,2,128,128]{4,3,2,1,0:T(8,128)(2,1)}, f32[256,256]{1,0:T(8,128)S(1)}) custom-call(bf16[2,256,1024]{2,1,0:T(8,128)(2,1)S(1)} %copy-done.1, bf16[256,256]{1,0:T(8,128)(2,1)S(1)} %get-tuple-element.17.lift_t, f32[256,256]{1,0:T(8,128)S(1)} %get-tuple-element.19.half, ...), custom_call_target="tpu_custom_call", output_to_operand_aliasing={{0}: (5, {})} | custom-call | tf_op jit(solution)/shard_map/col_sources/pallas_call | solution.py:343
  23.2 0.0 collective-permute-done.2.other
  23.2 0.0 collective-permute-done.3.pair
  23.2 0.0 copy-done
  23.2 2.1 %row_sources.1 = (bf16[2,5,2,128,128]{4,3,2,1,0:T(8,128)(2,1)}, f32[3,64,256]{2,1,0:T(8,128)S(1)}, bf16[3,64,256]{2,1,0:T(8,128)(2,1)S(1)}, bf16[3,64,256]{2,1,0:T(8,128)(2,1)S(1)}, bf16[3,64,256]{2,1,0:T(8,128)(2,1)S(1)}) custom-call(bf16[2,256,1024]{2,1,0:T(8,128)(2,1)S(1)} %copy-done, ...), custom_call_target="tpu_custom_call", output_to_operand_aliasing={{0}: (5, {})} | custom-call | tf_op jit(solution)/shard_map/row_sources/pallas_call | solution.py:357
  25.4 2.2 %collective-permute-start.4 = (bf16[3,64,256]{2,1,0:T(8,128)(2,1)S(1)}, bf16[3,64,256]{2,1,0:T(8,128)(2,1)S(1)}, u32[]{:S(2)}, u32[]{:S(2)}) collective-permute-start(bf16[3,64,256]{2,1,0:T(8,128)(2,1)S(1)} %get-tuple-element.25), channel_id=1, source_target_pairs={{0,1},{1,2},{2,3},{3,0},{4,5},{5,6},{6,7},{7,4},{8,9},{9,10},{10,1... | collective-permute-start | bytes 294920 | tf_op jit(solution)/shard_map/ppermute | solution.py:250
  27.6 2.3 %collective-permute-start.5 = (bf16[3,64,256]{2,1,0:T(8,128)(2,1)S(1)}, bf16[3,64,256]{2,1,0:T(8,128)(2,1)S(1)}, u32[]{:S(2)}, u32[]{:S(2)}) collective-permute-start(bf16[3,64,256]{2,1,0:T(8,128)(2,1)S(1)} %get-tuple-element.26), channel_id=1, source_target_pairs={{0,2},{1,3},{2,0},{3,1},{4,6},{5,7},{6,4},{7,5},{8,10},{9,11},{10,... | collective-permute-start | bytes 294920 | tf_op jit(solution)/shard_map/ppermute | solution.py:250
  29.9 2.8 %collective-permute-start.6 = (bf16[3,64,256]{2,1,0:T(8,128)(2,1)S(1)}, bf16[3,64,256]{2,1,0:T(8,128)(2,1)S(1)}, u32[]{:S(2)}, u32[]{:S(2)}) collective-permute-start(bf16[3,64,256]{2,1,0:T(8,128)(2,1)S(1)} %get-tuple-element.27), channel_id=1, source_target_pairs={{0,3},{1,0},{2,1},{3,2},{4,7},{5,4},{6,5},{7,6},{8,11},{9,8},{10,9... | collective-permute-start | bytes 294920 | tf_op jit(solution)/shard_map/ppermute | solution.py:250
  32.7 0.1 collective-permute-done.4.refs_1_
  32.8 4.3 %collective-permute-done.5.refs_2_ = bf16[3,64,256]{2,1,0:T(8,128)(2,1)S(1)} collective-permute-done((bf16[3,64,256]{2,1,0:T(8,128)(2,1)S(1)}, bf16[3,64,256]{2,1,0:T(8,128)(2,1)S(1)}, u32[]{:S(2)}, u32[]{:S(2)}) %collective-permute-start.5) | collective-permute-done | bytes 98336 | tf_op jit(solution)/shard_map/ppermute | solution.py:250
  37.1 0.0 collective-permute-done.6.refs_3_
  37.2 2.7 %collective-permute-start.7 = (bf16[3,64,256]{2,1,0:T(8,128)(2,1)S(1)}, bf16[3,64,256]{2,1,0:T(8,128)(2,1)S(1)}, u32[]{:S(2)}, u32[]{:S(2)}) collective-permute-start(bf16[3,64,256]{2,1,0:T(8,128)(2,1)S(1)} %total.1.refs_0_), channel_id=1, source_target_pairs={{0,1},{1,2},{2,3},{3,0},{4,5},{5,6},{6,7},{7,4},{8,9},{9,10},{10,1... | collective-permute-start | bytes 294920 | tf_op jit(solution)/shard_map/ppermute | solution.py:250
  39.9 1.9 %collective-permute-start.8 = (bf16[3,64,256]{2,1,0:T(8,128)(2,1)S(1)}, bf16[3,64,256]{2,1,0:T(8,128)(2,1)S(1)}, u32[]{:S(2)}, u32[]{:S(2)}) collective-permute-start(bf16[3,64,256]{2,1,0:T(8,128)(2,1)S(1)} %total.1.refs_0_), channel_id=1, source_target_pairs={{0,2},{1,3},{2,0},{3,1},{4,6},{5,7},{6,4},{7,5},{8,10},{9,11},{10,... | collective-permute-start | bytes 294920 | tf_op jit(solution)/shard_map/ppermute | solution.py:250
  41.8 0.5 %collective-permute-start.9 = (bf16[3,64,256]{2,1,0:T(8,128)(2,1)S(1)}, bf16[3,64,256]{2,1,0:T(8,128)(2,1)S(1)}, u32[]{:S(2)}, u32[]{:S(2)}) collective-permute-start(bf16[3,64,256]{2,1,0:T(8,128)(2,1)S(1)} %total.1.refs_0_), channel_id=1, source_target_pairs={{0,3},{1,0},{2,1},{3,2},{4,7},{5,4},{6,5},{7,6},{8,11},{9,8},{10,9... | collective-permute-start | bytes 294920 | tf_op jit(solution)/shard_map/ppermute | solution.py:250
  42.3 2.5 %collective-permute-done.7.refs_1_ = bf16[3,64,256]{2,1,0:T(8,128)(2,1)S(1)} collective-permute-done((bf16[3,64,256]{2,1,0:T(8,128)(2,1)S(1)}, bf16[3,64,256]{2,1,0:T(8,128)(2,1)S(1)}, u32[]{:S(2)}, u32[]{:S(2)}) %collective-permute-start.7) | collective-permute-done | bytes 98336 | tf_op jit(solution)/shard_map/ppermute | solution.py:250
  44.8 3.3 %collective-permute-done.8.refs_2_ = bf16[3,64,256]{2,1,0:T(8,128)(2,1)S(1)} collective-permute-done((bf16[3,64,256]{2,1,0:T(8,128)(2,1)S(1)}, bf16[3,64,256]{2,1,0:T(8,128)(2,1)S(1)}, u32[]{:S(2)}, u32[]{:S(2)}) %collective-permute-start.8) | collective-permute-done | bytes 98336 | tf_op jit(solution)/shard_map/ppermute | solution.py:250
  48.1 0.2 collective-permute-done.9.refs_3_
  48.3 0.9 %spread.1 = f32[2,3,2,128,128]{4,3,2,1,0:T(8,128)} custom-call(bf16[3,64,256]{2,1,0:T(8,128)(2,1)S(1)} %total.1.refs_0_, bf16[3,64,256]{2,1,0:T(8,128)(2,1)S(1)} %collective-permute-done.7.refs_1_, bf16[3,64,256]{2,1,0:T(8,128)(2,1)S(1)} %collective-permute-done.8.refs_2_, bf16[3,64,256]{2,1,0:T(8,128)(2,1)S(1)} %collective-permute-done.9.refs_3_), custom_call_target="tpu_custom_call" | custom-call | tf_op jit(solution)/shard_map/spread/pallas_call | solution.py:373
  (1 shorter events, 0.0 us)
Async XLA Ops:
  3.1 17.9 %collective-permute-start = (bf16[1808,128]{1,0:T(8,128)(2,1)}, bf16[1808,128]{1,0:T(8,128)(2,1)S(1)}, u32[]{:S(2)}, u32[]{:S(2)}) collective-permute-start(bf16[1808,128]{1,0:T(8,128)(2,1)} %pack.1.own_at), channel_id=1, source_target_pairs={{1,0},{2,1},{3,2},{5,4},{6,5},{7,6},{9,8},{10,9},{11,10},{13,12},{... | collective-permute-start | bytes 1388552 | tf_op jit(solution)/shard_map/ppermute | solution.py:250
  4.4 16.6 %collective-permute-start.1 = (bf16[1808,128]{1,0:T(8,128)(2,1)}, bf16[1808,128]{1,0:T(8,128)(2,1)S(1)}, u32[]{:S(2)}, u32[]{:S(2)}) collective-permute-start(bf16[1808,128]{1,0:T(8,128)(2,1)} %pack.1.own_at), channel_id=1, source_target_pairs={{0,1},{1,2},{2,3},{4,5},{5,6},{6,7},{8,9},{9,10},{10,11},{12,13},{... | collective-permute-start | bytes 1388552 | tf_op jit(solution)/shard_map/ppermute | solution.py:250
  10.0 13.2 %collective-permute-start.2 = (bf16[1808,128]{1,0:T(8,128)(2,1)}, bf16[1808,128]{1,0:T(8,128)(2,1)S(1)}, u32[]{:S(2)}, u32[]{:S(2)}) collective-permute-start(bf16[1808,128]{1,0:T(8,128)(2,1)} %pack.1.own_at), channel_id=1, source_target_pairs={{4,8},{12,16},{20,24},{8,4},{16,12},{24,20},{5,9},{13,17},{21,25},... | collective-permute-start | bytes 1388552 | tf_op jit(solution)/shard_map/ppermute | solution.py:254
  10.7 12.5 %collective-permute-start.3 = (bf16[1808,128]{1,0:T(8,128)(2,1)}, bf16[1808,128]{1,0:T(8,128)(2,1)S(1)}, u32[]{:S(2)}, u32[]{:S(2)}) collective-permute-start(bf16[1808,128]{1,0:T(8,128)(2,1)} %pack.1.own_at), channel_id=1, source_target_pairs={{0,4},{8,12},{16,20},{24,28},{4,0},{12,8},{20,16},{28,24},{1,5},{9... | collective-permute-start | bytes 1388552 | tf_op jit(solution)/shard_map/ppermute | solution.py:254
  19.7 1.3 %copy-start.1 = (bf16[2,256,1024]{2,1,0:T(8,128)(2,1)S(1)}, bf16[2,256,1024]{2,1,0:T(8,128)(2,1)}, u32[]{:S(2)}) copy-start(bf16[2,256,1024]{2,1,0:T(8,128)(2,1)} %get-tuple-element.18.stock) | copy-start | bytes 3145732
  19.7 1.1 %copy-start.2 = (bf16[3,256,256]{2,1,0:T(8,128)(2,1)S(1)}, bf16[3,256,256]{2,1,0:T(8,128)(2,1)}, u32[]{:S(2)}) copy-start(bf16[3,256,256]{2,1,0:T(8,128)(2,1)} %get-tuple-element.16.more) | copy-start | bytes 1179652
  21.0 2.2 %copy-start = (bf16[2,256,1024]{2,1,0:T(8,128)(2,1)S(1)}, bf16[2,256,1024]{2,1,0:T(8,128)(2,1)}, u32[]{:S(2)}) copy-start(bf16[2,256,1024]{2,1,0:T(8,128)(2,1)} %get-tuple-element.15.stock) | copy-start | bytes 3145732
  25.4 7.5 %collective-permute-start.4 = (bf16[3,64,256]{2,1,0:T(8,128)(2,1)S(1)}, bf16[3,64,256]{2,1,0:T(8,128)(2,1)S(1)}, u32[]{:S(2)}, u32[]{:S(2)}) collective-permute-start(bf16[3,64,256]{2,1,0:T(8,128)(2,1)S(1)} %get-tuple-element.25), channel_id=1, source_target_pairs={{0,1},{1,2},{2,3},{3,0},{4,5},{5,6},{6,7},{7,4},{8,9},{9,10},{10,1... | collective-permute-start | bytes 294920 | tf_op jit(solution)/shard_map/ppermute | solution.py:250
  27.6 9.6 %collective-permute-start.5 = (bf16[3,64,256]{2,1,0:T(8,128)(2,1)S(1)}, bf16[3,64,256]{2,1,0:T(8,128)(2,1)S(1)}, u32[]{:S(2)}, u32[]{:S(2)}) collective-permute-start(bf16[3,64,256]{2,1,0:T(8,128)(2,1)S(1)} %get-tuple-element.26), channel_id=1, source_target_pairs={{0,2},{1,3},{2,0},{3,1},{4,6},{5,7},{6,4},{7,5},{8,10},{9,11},{10,... | collective-permute-start | bytes 294920 | tf_op jit(solution)/shard_map/ppermute | solution.py:250
  29.9 7.3 %collective-permute-start.6 = (bf16[3,64,256]{2,1,0:T(8,128)(2,1)S(1)}, bf16[3,64,256]{2,1,0:T(8,128)(2,1)S(1)}, u32[]{:S(2)}, u32[]{:S(2)}) collective-permute-start(bf16[3,64,256]{2,1,0:T(8,128)(2,1)S(1)} %get-tuple-element.27), channel_id=1, source_target_pairs={{0,3},{1,0},{2,1},{3,2},{4,7},{5,4},{6,5},{7,6},{8,11},{9,8},{10,9... | collective-permute-start | bytes 294920 | tf_op jit(solution)/shard_map/ppermute | solution.py:250
  37.2 7.6 %collective-permute-start.7 = (bf16[3,64,256]{2,1,0:T(8,128)(2,1)S(1)}, bf16[3,64,256]{2,1,0:T(8,128)(2,1)S(1)}, u32[]{:S(2)}, u32[]{:S(2)}) collective-permute-start(bf16[3,64,256]{2,1,0:T(8,128)(2,1)S(1)} %total.1.refs_0_), channel_id=1, source_target_pairs={{0,1},{1,2},{2,3},{3,0},{4,5},{5,6},{6,7},{7,4},{8,9},{9,10},{10,1... | collective-permute-start | bytes 294920 | tf_op jit(solution)/shard_map/ppermute | solution.py:250
  39.9 8.3 %collective-permute-start.8 = (bf16[3,64,256]{2,1,0:T(8,128)(2,1)S(1)}, bf16[3,64,256]{2,1,0:T(8,128)(2,1)S(1)}, u32[]{:S(2)}, u32[]{:S(2)}) collective-permute-start(bf16[3,64,256]{2,1,0:T(8,128)(2,1)S(1)} %total.1.refs_0_), channel_id=1, source_target_pairs={{0,2},{1,3},{2,0},{3,1},{4,6},{5,7},{6,4},{7,5},{8,10},{9,11},{10,... | collective-permute-start | bytes 294920 | tf_op jit(solution)/shard_map/ppermute | solution.py:250
  41.8 6.5 %collective-permute-start.9 = (bf16[3,64,256]{2,1,0:T(8,128)(2,1)S(1)}, bf16[3,64,256]{2,1,0:T(8,128)(2,1)S(1)}, u32[]{:S(2)}, u32[]{:S(2)}) collective-permute-start(bf16[3,64,256]{2,1,0:T(8,128)(2,1)S(1)} %total.1.refs_0_), channel_id=1, source_target_pairs={{0,3},{1,0},{2,1},{3,2},{4,7},{5,4},{6,5},{7,6},{8,11},{9,8},{10,9... | collective-permute-start | bytes 294920 | tf_op jit(solution)/shard_map/ppermute | solution.py:250

commit v10 on v9

--- a/solution.py
+++ b/solution.py
@@ -108,8 +108,8 @@
 
 def own_kernel(
     slots, size, rows, cols, count, codes, p_count, aggs, fine_at, own_at,
-    col_at, row_at, more_at, c_one,
-    fine, own, stock, more, turned, acc, dense, tile, table, sems,
+    col_at, row_at, half_at, lift_at, c_one,
+    fine, own, stock, half, lift_t, turned, acc, dense, tile, table, sems,
 ):
     fetch_own = pltpu.make_async_copy(own_at, own, sems.at[0])
     fetch_own.start()
@@ -124,7 +124,10 @@
         i = code_of(k) // CB
         j = pl.multiple_of((code_of(k) - i * CB) * size, size)
         turned[i, pl.ds(j, size), :] = own[k * size : (k + 1) * size, :].T
+    lift_t[...] = lift_of(own, slots, size, lambda j: aggs[j]).T
     fetch_fine.wait()
+    stores = [pltpu.make_async_copy(lift_t, lift_at, sems.at[0])]
+    stores[0].start()
 
     def step(t, carry):
         products, targets = [], []
@@ -137,7 +140,6 @@
         return carry
 
     lax.fori_loop(0, (count[0] + UNROLL - 1) // UNROLL, step, 0)
-    stores = []
     for s in range(1, NS):
         for m in range(FB):
             stock[s - 1, :, m * size : (m + 1) * size] = acc[s * FB + m].astype(BF16)
@@ -148,11 +150,8 @@
     dense_of(0, size, table, own, dense)
     coarse = coarse_of(size, own_weight, dense, tile)
     lift = lift_of(own, slots, size, lambda j: aggs[j])
-    wide = CB * size
-    more[0] = lift.T
-    more[1] = coarse
-    more[2] = lift
-    stores.append(pltpu.make_async_copy(more, more_at, sems.at[0]))
+    half[...] = jnp.dot(coarse, lift, preferred_element_type=F32)
+    stores.append(pltpu.make_async_copy(half, half_at, sems.at[6]))
     stores[-1].start()
     stores.append(pltpu.make_async_copy(tile, c_one.at[:, 0], sems.at[1]))
     stores[-1].start()
@@ -182,9 +181,8 @@
     return parts, stores
 
 
-def half_kernel(more, lift_t, half):
-    lift_t[...] = more[0]
-    half[...] = jnp.dot(more[1], more[2], preferred_element_type=F32)
+def pass_kernel(lift_in, lift_t):
+    lift_t[...] = lift_in[...]
 
 
 def side_kernel(slots, size, stock, lift_t, half, right, left, c_in, c_one, term, *scratch):
@@ -206,7 +204,7 @@
     chunk = terms.shape[1] // cols_n
     me = lax.axis_index("col")
     for d in range(cols_n):
-        to = pl.multiple_of(lax.rem(me + d, cols_n) * chunk, chunk)
+        to = pl.multiple_of(partner(me, d, cols_n) * chunk, chunk)
         sends[d][...] = terms[:, pl.ds(to, chunk), :].astype(sends[d].dtype)
     for store in stores:
         store.wait()
@@ -219,22 +217,23 @@
     refs[-1][...] = total.astype(BF16)
 
 
-def spread_kernel(size, cols_n, *refs):
+def spread_kernel(size, steps, *refs):
+    cols_n = len(steps)
     parts, out_at, out, sems = refs[:cols_n], refs[cols_n], refs[cols_n + 1], refs[cols_n + 2]
     chunk = parts[0].shape[1]
     unit = math.gcd(chunk, size)
     per = size // unit
     me = lax.axis_index("col")
     stores = []
-    for d in range(cols_n):
-        owner = lax.rem(me - d + cols_n, cols_n)
+    for n, d in enumerate(steps):
+        owner = partner(me, -d, cols_n)
         for t in range(chunk // unit):
             at = owner * (chunk // unit) + t
             a = at // per
             rows = pl.ds(pl.multiple_of(lax.rem(at, per) * unit, unit), unit)
             for g in range(3):
                 for b in range(G2):
-                    out[a, g, b, rows, :] = parts[d][
+                    out[a, g, b, rows, :] = parts[n][
                         g, t * unit : (t + 1) * unit, b * size : (b + 1) * size
                     ].astype(F32)
             spot = (a, slice(None), slice(None), rows)
@@ -244,10 +243,18 @@
         store.wait()
 
 
-def shift(x, axis, step, wrap):
+def shift(x, axis, step):
     n = lax.axis_size(axis)
-    pairs = [(i, (i + step) % n) for i in range(n) if wrap or 0 <= i + step < n]
-    return lax.ppermute(x, axis, pairs)
+    return lax.ppermute(x, axis, [(i, i + step) for i in range(n) if 0 <= i + step < n])
+
+
+def partner(c, d, n):
+    return c ^ abs(d) if n & (n - 1) == 0 else (c + d + n) % n
+
+
+def exchange(x, d):
+    n = lax.axis_size("col")
+    return lax.ppermute(x, "col", [(i, partner(i, d, n)) for i in range(n)])
 
 
 def swap(x, axis, pairs):
@@ -287,32 +294,35 @@
     rows_n = lax.axis_size("row")
     pair = swap(packed, "row", [(i, i + 1) for i in range(0, rows_n - 1, 2)])
     other = swap(packed, "row", [(i, i + 1) for i in range(1, rows_n - 1, 2)])
-    right = shift(packed, "col", -1, False)
-    left = shift(packed, "col", 1, False)
+    right = shift(packed, "col", -1)
+    left = shift(packed, "col", 1)
 
     c_shape = jax.ShapeDtypeStruct((CB, NS, CB, size, size), BF16)
+    square = jax.ShapeDtypeStruct((wide, G2 * size), F32)
     table = pltpu.SMEM((1, PB + 1), jnp.int32)
-    col_stock, row_stock, more, c_one = pl.pallas_call(
+    col_stock, row_stock, half, lift_t, c_one = pl.pallas_call(
         functools.partial(own_kernel, slots, size),
         out_shape=[
             jax.ShapeDtypeStruct((2, wide, FB * size), BF16),
             jax.ShapeDtypeStruct((2, wide, FB * size), BF16),
-            jax.ShapeDtypeStruct((3, wide, G2 * size), BF16),
+            square,
+            jax.ShapeDtypeStruct((G2 * size, wide), BF16),
             c_shape,
         ],
         in_specs=[SMEM] * 6 + [HBM] * 2,
-        out_specs=[HBM] * 4,
+        out_specs=[HBM] * 5,
         scratch_shapes=[
             pltpu.VMEM((cap, size, size), BF16),
             pltpu.VMEM((packed_rows, size), BF16),
             pltpu.VMEM((NS - 1, wide, FB * size), BF16),
-            pltpu.VMEM((3, wide, G2 * size), BF16),
+            pltpu.VMEM((wide, G2 * size), F32),
+            pltpu.VMEM((G2 * size, wide), BF16),
             pltpu.VMEM((FB + 1, wide, size), BF16),
             pltpu.VMEM((NS * FB + 1, wide, size), F32),
             pltpu.VMEM((FB * size, wide), BF16),
             pltpu.VMEM((CB, CB, size, size), BF16),
             table,
-            dma((6,)),
+            dma((7,)),
         ],
         compiler_params=WHOLE,
         cost_estimate=pl.CostEstimate(flops=10**9, bytes_accessed=4 * 10**6, transcendentals=0),
@@ -330,16 +340,15 @@
         pltpu.SMEM((8, size), jnp.int32),
         dma((3,)),
     ]
-    square = jax.ShapeDtypeStruct((wide, G2 * size), F32)
-    lift_t, half = pl.pallas_call(
-        half_kernel,
-        out_shape=[jax.ShapeDtypeStruct((G2 * size, wide), BF16), square],
+    lift_t = pl.pallas_call(
+        pass_kernel,
+        out_shape=jax.ShapeDtypeStruct((G2 * size, wide), BF16),
         in_specs=[VMEM],
-        out_specs=[VMEM] * 2,
+        out_specs=VMEM,
         compiler_params=SMALL,
         cost_estimate=pl.CostEstimate(flops=10**9, bytes_accessed=4 * 10**6, transcendentals=0),
-        name="own_half",
-    )(more)
+        name="pass_on",
+    )(lift_t)
     c_one, term = pl.pallas_call(
         functools.partial(side_kernel, slots, size),
         out_shape=[c_shape, square],
@@ -364,14 +373,15 @@
         compiler_params=LARGE,
         name="row_sources",
     )(row_stock, lift_t, term, other, pair, c_one)
-    parts = [sends[0]] + [shift(sends[d], "col", d, True) for d in range(1, cols_n)]
+    steps = list(range(cols_n - 1, 0, -1))
+    parts = [sends[0]] + [exchange(sends[d], d) for d in steps]
     total = pl.pallas_call(
         sum_kernel, out_shape=piece, in_specs=[VMEM] * cols_n, out_specs=VMEM,
         compiler_params=SMALL, name="total",
     )(*parts)
-    gathered = [total] + [shift(total, "col", d, True) for d in range(1, cols_n)]
+    gathered = [total] + [exchange(total, d) for d in steps]
     c_two = pl.pallas_call(
-        functools.partial(spread_kernel, size, cols_n),
+        functools.partial(spread_kernel, size, [0] + steps),
         out_shape=jax.ShapeDtypeStruct((G2, 3, G2, size, size), F32),
         in_specs=[VMEM] * cols_n,
         out_specs=HBM,

time: 49.6 us -> 50.7 us (1.022)
  starting transfers between devices: 23.4 us -> 19.8 us
  waiting for transfers between devices: 10.5 us -> 13.6 us
  Pallas kernels: 12.3 us -> 13.9 us
    ppermute x8, starting transfers between devices: 19.3 us -> 15.8 us  [the longest x6 8.91 us: exchange(): return lax.ppermute(x, 'col', [(i, partner(i, d, n)) for i in range(n)])]
    ppermute x8, waiting for transfers between devices: 10.5 us -> 13.6 us  [the longest x6 13.6 us: exchange(): return lax.ppermute(x, 'col', [(i, partner(i, d, n)) for i in range(n)])]
    pallas_call x1, Pallas kernels: 5.02 us -> 6.86 us  [per_device(): pl.pallas_call(functools.partial(own_kernel, slots, size), out_shape=[jax...]
    unnamed x6 -> x8, local copies, waits for them, and re-layouts: 1.11 us -> 1.26 us
  transfers between devices with their start and end apart: 10 -> 10, of which waited for: 5 -> 4; matrix products, arithmetic and copies ran while one was open for 0% -> 0% of each run, Pallas kernels for 15% -> 18%
where the time goes in v10:
time: 50.7 us
  starting transfers between devices  19.8 us (39%)
  Pallas kernels  13.9 us (27%)
  waiting for transfers between devices  13.6 us (27%)
  between operations  2.07 us (4%)
  local copies, waits for them, and re-layouts  1.26 us (2%)
    ppermute x6, waiting for transfers between devices, exchange(): return lax.ppermute(x, 'col', [(i, partner(i, d, n)) for i in range(n)])  13.6 us
    ppermute x6, starting transfers between devices, exchange(): return lax.ppermute(x, 'col', [(i, partner(i, d, n)) for i in range(n)])  8.91 us
    ppermute x2, starting transfers between devices, shift(): lax.ppermute(x, axis, [(i, i + step) for i in range(n) if 0 <= i + step <...  6.88 us
    pallas_call x1, Pallas kernels, per_device(): pl.pallas_call(functools.partial(own_kernel, slots, size), out_shape=[jax...  6.86 us
    ppermute x2, starting transfers between devices, swap(): return lax.ppermute(x, axis, pairs + [(j, i) for i, j in pairs])  4.02 us
    pallas_call x1, Pallas kernels, per_device(): pl.pallas_call(functools.partial(row_kernel, slots, size, cols_n), out_sh...  2.14 us
    pallas_call x1, Pallas kernels, per_device(): pl.pallas_call(functools.partial(side_kernel, slots, size), out_shape=[c_...  2.14 us
    pallas_call x1, Pallas kernels, per_device(): pl.pallas_call(pack_kernel, out_shape=jax.ShapeDtypeStruct((packed_rows,...  1.81 us
  transfers between devices with their start and end apart: 10, of which 4 were waited for; matrix products, arithmetic and copies ran while one was open for 0% of the time, Pallas kernels for 18%

profile of v10, /device:TPU:0, one launch (start us, length us, event | category | flops | bytes accessed | tf_op | source)
XLA Modules:
  0.0 50.7 jit_solution(2156427703781045216)
XLA Ops:
  1.3 1.8 %pack.1.own_at = bf16[1808,128]{1,0:T(8,128)(2,1)} custom-call(s32[1,1,12]{2,1,0:T(1,128)} %codes_at.1, s32[1,1]{1,0:T(1,128)} %copy.16.count_at, s32[1,1,2]{2,1,0:T(1,128)} %aggs_at.1, bf16[1536,128]{1,0:T(8,128)(2,1)} %bitcast.15, bf16[256,128]{1,0:T(8,128)(2,1)} %bitcast.16), custom_call_target="tpu_custom_call" | custom-call | tf_op jit(solution)/shard_map/pack/pallas_call | solution.py:274
  3.1 1.3 %collective-permute-start = (bf16[1808,128]{1,0:T(8,128)(2,1)}, bf16[1808,128]{1,0:T(8,128)(2,1)S(1)}, u32[]{:S(2)}, u32[]{:S(2)}) collective-permute-start(bf16[1808,128]{1,0:T(8,128)(2,1)} %pack.1.own_at), channel_id=1, source_target_pairs={{1,0},{2,1},{3,2},{5,4},{6,5},{7,6},{9,8},{10,9},{11,10},{13,12},{... | collective-permute-start | bytes 1388552 | tf_op jit(solution)/shard_map/ppermute | solution.py:248
  4.4 5.6 %collective-permute-start.1 = (bf16[1808,128]{1,0:T(8,128)(2,1)}, bf16[1808,128]{1,0:T(8,128)(2,1)S(1)}, u32[]{:S(2)}, u32[]{:S(2)}) collective-permute-start(bf16[1808,128]{1,0:T(8,128)(2,1)} %pack.1.own_at), channel_id=1, source_target_pairs={{0,1},{1,2},{2,3},{4,5},{5,6},{6,7},{8,9},{9,10},{10,11},{12,13},{... | collective-permute-start | bytes 1388552 | tf_op jit(solution)/shard_map/ppermute | solution.py:248
  10.0 0.7 %collective-permute-start.2 = (bf16[1808,128]{1,0:T(8,128)(2,1)}, bf16[1808,128]{1,0:T(8,128)(2,1)S(1)}, u32[]{:S(2)}, u32[]{:S(2)}) collective-permute-start(bf16[1808,128]{1,0:T(8,128)(2,1)} %pack.1.own_at), channel_id=1, source_target_pairs={{4,8},{12,16},{20,24},{8,4},{16,12},{24,20},{5,9},{13,17},{21,25},... | collective-permute-start | bytes 1388552 | tf_op jit(solution)/shard_map/ppermute | solution.py:261
  10.7 3.3 %collective-permute-start.3 = (bf16[1808,128]{1,0:T(8,128)(2,1)}, bf16[1808,128]{1,0:T(8,128)(2,1)S(1)}, u32[]{:S(2)}, u32[]{:S(2)}) collective-permute-start(bf16[1808,128]{1,0:T(8,128)(2,1)} %pack.1.own_at), channel_id=1, source_target_pairs={{0,4},{8,12},{16,20},{24,28},{4,0},{12,8},{20,16},{28,24},{1,5},{9... | collective-permute-start | bytes 1388552 | tf_op jit(solution)/shard_map/ppermute | solution.py:261
  14.7 6.9 %own_source.1 = (bf16[2,256,1024]{2,1,0:T(8,128)(2,1)}, bf16[2,256,1024]{2,1,0:T(8,128)(2,1)}, f32[256,256]{1,0:T(8,128)}, bf16[256,256]{1,0:T(8,128)(2,1)}, bf16[2,5,2,128,128]{4,3,2,1,0:T(8,128)(2,1)}) custom-call(s32[64]{0:T(128)} %bitcast.20, s32[64]{0:T(128)} %bitcast.21, s32[1]{0:T(128)} %bitcast.11.count, s32[12]{0:T(128)} %bitcast.17, ...), custom_call_target="tpu_custom_call" | custom-call | flops 1000000000 | bytes 4000000 | tf_op jit(solution)/shard_map/own_source/pallas_call | solution.py:303
  21.5 0.0 copy-start.1
  21.5 0.0 copy-start.2
  21.5 0.0 copy-start.3
  21.6 1.0 %copy-done.3 = bf16[256,256]{1,0:T(8,128)(2,1)S(1)} copy-done((bf16[256,256]{1,0:T(8,128)(2,1)S(1)}, bf16[256,256]{1,0:T(8,128)(2,1)}, u32[]{:S(2)}) %copy-start.3) | copy-done | bytes 131096
  22.6 0.0 copy-start
  22.6 0.0 collective-permute-done.right
  22.6 0.0 collective-permute-done.1.left
  22.6 0.2 copy-done.1
  22.8 0.0 copy-done.2
  22.9 2.1 %col_sources.1 = (bf16[2,5,2,128,128]{4,3,2,1,0:T(8,128)(2,1)}, f32[256,256]{1,0:T(8,128)S(1)}) custom-call(bf16[2,256,1024]{2,1,0:T(8,128)(2,1)S(1)} %copy-done.1, bf16[256,256]{1,0:T(8,128)(2,1)S(1)} %pass_on.1.lift_t, f32[256,256]{1,0:T(8,128)S(1)} %copy-done.2, ...), custom_call_target="tpu_custom_call", output_to_operand_aliasing={{0}: (5, {})} | custom-call | tf_op jit(solution)/shard_map/col_sources/pallas_call | solution.py:352
  25.0 0.0 collective-permute-done.2.other
  25.0 0.0 collective-permute-done.3.pair
  25.0 0.0 copy-done
  25.0 2.1 %row_sources.1 = (bf16[2,5,2,128,128]{4,3,2,1,0:T(8,128)(2,1)}, f32[3,64,256]{2,1,0:T(8,128)S(1)}, bf16[3,64,256]{2,1,0:T(8,128)(2,1)S(1)}, bf16[3,64,256]{2,1,0:T(8,128)(2,1)S(1)}, bf16[3,64,256]{2,1,0:T(8,128)(2,1)S(1)}) custom-call(bf16[2,256,1024]{2,1,0:T(8,128)(2,1)S(1)} %copy-done, ...), custom_call_target="tpu_custom_call", output_to_operand_aliasing={{0}: (5, {})} | custom-call | tf_op jit(solution)/shard_map/row_sources/pallas_call | solution.py:366
  27.2 1.9 %collective-permute-start.4 = (bf16[3,64,256]{2,1,0:T(8,128)(2,1)S(1)}, bf16[3,64,256]{2,1,0:T(8,128)(2,1)S(1)}, u32[]{:S(2)}, u32[]{:S(2)}) collective-permute-start(bf16[3,64,256]{2,1,0:T(8,128)(2,1)S(1)} %get-tuple-element.23), channel_id=1, source_target_pairs={{0,3},{1,2},{2,1},{3,0},{4,7},{5,6},{6,5},{7,4},{8,11},{9,10},{10,... | collective-permute-start | bytes 294920 | tf_op jit(solution)/shard_map/ppermute | solution.py:257
  29.1 0.0 collective-permute-start.5
  29.1 2.5 %collective-permute-start.6 = (bf16[3,64,256]{2,1,0:T(8,128)(2,1)S(1)}, bf16[3,64,256]{2,1,0:T(8,128)(2,1)S(1)}, u32[]{:S(2)}, u32[]{:S(2)}) collective-permute-start(bf16[3,64,256]{2,1,0:T(8,128)(2,1)S(1)} %get-tuple-element.25), channel_id=1, source_target_pairs={{0,1},{1,0},{2,3},{3,2},{4,5},{5,4},{6,7},{7,6},{8,9},{9,8},{10,11... | collective-permute-start | bytes 294920 | tf_op jit(solution)/shard_map/ppermute | solution.py:257
  31.6 3.1 %collective-permute-done.4.refs_1_ = bf16[3,64,256]{2,1,0:T(8,128)(2,1)S(1)} collective-permute-done((bf16[3,64,256]{2,1,0:T(8,128)(2,1)S(1)}, bf16[3,64,256]{2,1,0:T(8,128)(2,1)S(1)}, u32[]{:S(2)}, u32[]{:S(2)}) %collective-permute-start.4) | collective-permute-done | bytes 98336 | tf_op jit(solution)/shard_map/ppermute | solution.py:257
  34.7 4.1 %collective-permute-done.5.refs_2_ = bf16[3,64,256]{2,1,0:T(8,128)(2,1)S(1)} collective-permute-done((bf16[3,64,256]{2,1,0:T(8,128)(2,1)S(1)}, bf16[3,64,256]{2,1,0:T(8,128)(2,1)S(1)}, u32[]{:S(2)}, u32[]{:S(2)}) %collective-permute-start.5) | collective-permute-done | bytes 98336 | tf_op jit(solution)/shard_map/ppermute | solution.py:257
  38.8 0.0 collective-permute-done.6.refs_3_
  38.8 2.1 %collective-permute-start.7 = (bf16[3,64,256]{2,1,0:T(8,128)(2,1)S(1)}, bf16[3,64,256]{2,1,0:T(8,128)(2,1)S(1)}, u32[]{:S(2)}, u32[]{:S(2)}) collective-permute-start(bf16[3,64,256]{2,1,0:T(8,128)(2,1)S(1)} %total.1.refs_0_), channel_id=1, source_target_pairs={{0,3},{1,2},{2,1},{3,0},{4,7},{5,6},{6,5},{7,4},{8,11},{9,10},{10,... | collective-permute-start | bytes 294920 | tf_op jit(solution)/shard_map/ppermute | solution.py:257
  41.0 0.0 collective-permute-start.8
  41.0 2.3 %collective-permute-start.9 = (bf16[3,64,256]{2,1,0:T(8,128)(2,1)S(1)}, bf16[3,64,256]{2,1,0:T(8,128)(2,1)S(1)}, u32[]{:S(2)}, u32[]{:S(2)}) collective-permute-start(bf16[3,64,256]{2,1,0:T(8,128)(2,1)S(1)} %total.1.refs_0_), channel_id=1, source_target_pairs={{0,1},{1,0},{2,3},{3,2},{4,5},{5,4},{6,7},{7,6},{8,9},{9,8},{10,11... | collective-permute-start | bytes 294920 | tf_op jit(solution)/shard_map/ppermute | solution.py:257
  43.3 3.2 %collective-permute-done.7.refs_1_ = bf16[3,64,256]{2,1,0:T(8,128)(2,1)S(1)} collective-permute-done((bf16[3,64,256]{2,1,0:T(8,128)(2,1)S(1)}, bf16[3,64,256]{2,1,0:T(8,128)(2,1)S(1)}, u32[]{:S(2)}, u32[]{:S(2)}) %collective-permute-start.7) | collective-permute-done | bytes 98336 | tf_op jit(solution)/shard_map/ppermute | solution.py:257
  46.4 3.3 %collective-permute-done.8.refs_2_ = bf16[3,64,256]{2,1,0:T(8,128)(2,1)S(1)} collective-permute-done((bf16[3,64,256]{2,1,0:T(8,128)(2,1)S(1)}, bf16[3,64,256]{2,1,0:T(8,128)(2,1)S(1)}, u32[]{:S(2)}, u32[]{:S(2)}) %collective-permute-start.8) | collective-permute-done | bytes 98336 | tf_op jit(solution)/shard_map/ppermute | solution.py:257
  49.7 0.0 collective-permute-done.9.refs_3_
  49.7 0.9 %spread.1 = f32[2,3,2,128,128]{4,3,2,1,0:T(8,128)} custom-call(bf16[3,64,256]{2,1,0:T(8,128)(2,1)S(1)} %total.1.refs_0_, bf16[3,64,256]{2,1,0:T(8,128)(2,1)S(1)} %collective-permute-done.7.refs_1_, bf16[3,64,256]{2,1,0:T(8,128)(2,1)S(1)} %collective-permute-done.8.refs_2_, bf16[3,64,256]{2,1,0:T(8,128)(2,1)S(1)} %collective-permute-done.9.refs_3_), custom_call_target="tpu_custom_call" | custom-call | tf_op jit(solution)/shard_map/spread/pallas_call | solution.py:383
  (2 shorter events, 0.1 us)
Async XLA Ops:
  3.1 19.5 %collective-permute-start = (bf16[1808,128]{1,0:T(8,128)(2,1)}, bf16[1808,128]{1,0:T(8,128)(2,1)S(1)}, u32[]{:S(2)}, u32[]{:S(2)}) collective-permute-start(bf16[1808,128]{1,0:T(8,128)(2,1)} %pack.1.own_at), channel_id=1, source_target_pairs={{1,0},{2,1},{3,2},{5,4},{6,5},{7,6},{9,8},{10,9},{11,10},{13,12},{... | collective-permute-start | bytes 1388552 | tf_op jit(solution)/shard_map/ppermute | solution.py:248
  4.4 18.2 %collective-permute-start.1 = (bf16[1808,128]{1,0:T(8,128)(2,1)}, bf16[1808,128]{1,0:T(8,128)(2,1)S(1)}, u32[]{:S(2)}, u32[]{:S(2)}) collective-permute-start(bf16[1808,128]{1,0:T(8,128)(2,1)} %pack.1.own_at), channel_id=1, source_target_pairs={{0,1},{1,2},{2,3},{4,5},{5,6},{6,7},{8,9},{9,10},{10,11},{12,13},{... | collective-permute-start | bytes 1388552 | tf_op jit(solution)/shard_map/ppermute | solution.py:248
  10.0 15.0 %collective-permute-start.2 = (bf16[1808,128]{1,0:T(8,128)(2,1)}, bf16[1808,128]{1,0:T(8,128)(2,1)S(1)}, u32[]{:S(2)}, u32[]{:S(2)}) collective-permute-start(bf16[1808,128]{1,0:T(8,128)(2,1)} %pack.1.own_at), channel_id=1, source_target_pairs={{4,8},{12,16},{20,24},{8,4},{16,12},{24,20},{5,9},{13,17},{21,25},... | collective-permute-start | bytes 1388552 | tf_op jit(solution)/shard_map/ppermute | solution.py:261
  10.7 14.3 %collective-permute-start.3 = (bf16[1808,128]{1,0:T(8,128)(2,1)}, bf16[1808,128]{1,0:T(8,128)(2,1)S(1)}, u32[]{:S(2)}, u32[]{:S(2)}) collective-permute-start(bf16[1808,128]{1,0:T(8,128)(2,1)} %pack.1.own_at), channel_id=1, source_target_pairs={{0,4},{8,12},{16,20},{24,28},{4,0},{12,8},{20,16},{28,24},{1,5},{9... | collective-permute-start | bytes 1388552 | tf_op jit(solution)/shard_map/ppermute | solution.py:261
  21.5 1.3 %copy-start.1 = (bf16[2,256,1024]{2,1,0:T(8,128)(2,1)S(1)}, bf16[2,256,1024]{2,1,0:T(8,128)(2,1)}, u32[]{:S(2)}) copy-start(bf16[2,256,1024]{2,1,0:T(8,128)(2,1)} %get-tuple-element.16.stock) | copy-start | bytes 3145732
  21.5 1.3 %copy-start.2 = (f32[256,256]{1,0:T(8,128)S(1)}, f32[256,256]{1,0:T(8,128)}, u32[]{:S(2)}) copy-start(f32[256,256]{1,0:T(8,128)} %get-tuple-element.17.half) | copy-start | bytes 786436
  21.5 1.0 %copy-start.3 = (bf16[256,256]{1,0:T(8,128)(2,1)S(1)}, bf16[256,256]{1,0:T(8,128)(2,1)}, u32[]{:S(2)}) copy-start(bf16[256,256]{1,0:T(8,128)(2,1)} %get-tuple-element.15.lift_in) | copy-start | bytes 393220
  22.6 2.5 %copy-start = (bf16[2,256,1024]{2,1,0:T(8,128)(2,1)S(1)}, bf16[2,256,1024]{2,1,0:T(8,128)(2,1)}, u32[]{:S(2)}) copy-start(bf16[2,256,1024]{2,1,0:T(8,128)(2,1)} %get-tuple-element.14.stock) | copy-start | bytes 3145732
  27.2 7.5 %collective-permute-start.4 = (bf16[3,64,256]{2,1,0:T(8,128)(2,1)S(1)}, bf16[3,64,256]{2,1,0:T(8,128)(2,1)S(1)}, u32[]{:S(2)}, u32[]{:S(2)}) collective-permute-start(bf16[3,64,256]{2,1,0:T(8,128)(2,1)S(1)} %get-tuple-element.23), channel_id=1, source_target_pairs={{0,3},{1,2},{2,1},{3,0},{4,7},{5,6},{6,5},{7,4},{8,11},{9,10},{10,... | collective-permute-start | bytes 294920 | tf_op jit(solution)/shard_map/ppermute | solution.py:257
  29.1 9.7 %collective-permute-start.5 = (bf16[3,64,256]{2,1,0:T(8,128)(2,1)S(1)}, bf16[3,64,256]{2,1,0:T(8,128)(2,1)S(1)}, u32[]{:S(2)}, u32[]{:S(2)}) collective-permute-start(bf16[3,64,256]{2,1,0:T(8,128)(2,1)S(1)} %get-tuple-element.24), channel_id=1, source_target_pairs={{0,2},{1,3},{2,0},{3,1},{4,6},{5,7},{6,4},{7,5},{8,10},{9,11},{10,... | collective-permute-start | bytes 294920 | tf_op jit(solution)/shard_map/ppermute | solution.py:257
  29.1 9.7 %collective-permute-start.6 = (bf16[3,64,256]{2,1,0:T(8,128)(2,1)S(1)}, bf16[3,64,256]{2,1,0:T(8,128)(2,1)S(1)}, u32[]{:S(2)}, u32[]{:S(2)}) collective-permute-start(bf16[3,64,256]{2,1,0:T(8,128)(2,1)S(1)} %get-tuple-element.25), channel_id=1, source_target_pairs={{0,1},{1,0},{2,3},{3,2},{4,5},{5,4},{6,7},{7,6},{8,9},{9,8},{10,11... | collective-permute-start | bytes 294920 | tf_op jit(solution)/shard_map/ppermute | solution.py:257
  38.8 7.6 %collective-permute-start.7 = (bf16[3,64,256]{2,1,0:T(8,128)(2,1)S(1)}, bf16[3,64,256]{2,1,0:T(8,128)(2,1)S(1)}, u32[]{:S(2)}, u32[]{:S(2)}) collective-permute-start(bf16[3,64,256]{2,1,0:T(8,128)(2,1)S(1)} %total.1.refs_0_), channel_id=1, source_target_pairs={{0,3},{1,2},{2,1},{3,0},{4,7},{5,6},{6,5},{7,4},{8,11},{9,10},{10,... | collective-permute-start | bytes 294920 | tf_op jit(solution)/shard_map/ppermute | solution.py:257
  41.0 8.8 %collective-permute-start.8 = (bf16[3,64,256]{2,1,0:T(8,128)(2,1)S(1)}, bf16[3,64,256]{2,1,0:T(8,128)(2,1)S(1)}, u32[]{:S(2)}, u32[]{:S(2)}) collective-permute-start(bf16[3,64,256]{2,1,0:T(8,128)(2,1)S(1)} %total.1.refs_0_), channel_id=1, source_target_pairs={{0,2},{1,3},{2,0},{3,1},{4,6},{5,7},{6,4},{7,5},{8,10},{9,11},{10,... | collective-permute-start | bytes 294920 | tf_op jit(solution)/shard_map/ppermute | solution.py:257
  41.0 8.8 %collective-permute-start.9 = (bf16[3,64,256]{2,1,0:T(8,128)(2,1)S(1)}, bf16[3,64,256]{2,1,0:T(8,128)(2,1)S(1)}, u32[]{:S(2)}, u32[]{:S(2)}) collective-permute-start(bf16[3,64,256]{2,1,0:T(8,128)(2,1)S(1)} %total.1.refs_0_), channel_id=1, source_target_pairs={{0,1},{1,0},{2,3},{3,2},{4,5},{5,4},{6,7},{7,6},{8,9},{9,8},{10,11... | collective-permute-start | bytes 294920 | tf_op jit(solution)/shard_map/ppermute | solution.py:257

commit v11 on v9

--- a/solution.py
+++ b/solution.py
@@ -21,7 +21,6 @@
 VMEM = pl.BlockSpec(memory_space=pltpu.VMEM)
 HBM = pl.BlockSpec(memory_space=pltpu.HBM)
 SMALL = pltpu.CompilerParams(vmem_limit_bytes=4 * 1024 * 1024)
-SMEM = pl.BlockSpec(memory_space=pltpu.SMEM)
 LARGE = pltpu.CompilerParams(vmem_limit_bytes=20 * 1024 * 1024)
 WHOLE = pltpu.CompilerParams(vmem_limit_bytes=60 * 1024 * 1024)
 
@@ -107,17 +106,26 @@
 
 
 def own_kernel(
-    slots, size, rows, cols, count, codes, p_count, aggs, fine_at, own_at,
+    slots, size, rows_at, cols_at, count_at, codes_at, p_count_at, aggs_at, fine_at, own_at,
     col_at, row_at, more_at, c_one,
-    fine, own, stock, more, turned, acc, dense, tile, table, sems,
+    fine, own, stock, more, turned, acc, dense, tile, rows, cols, count, codes, p_count, aggs, table, sems,
 ):
+    pairs = [
+        (rows_at, rows), (cols_at, cols), (count_at, count), (codes_at, codes),
+        (p_count_at, p_count), (aggs_at, aggs),
+    ]
+    small = [pltpu.make_async_copy(a, b, sems.at[2 + n]) for n, (a, b) in enumerate(pairs)]
+    for copy in small:
+        copy.start()
     fetch_own = pltpu.make_async_copy(own_at, own, sems.at[0])
     fetch_own.start()
     fetch_fine = pltpu.make_async_copy(fine_at, fine, sems.at[1])
     fetch_fine.start()
     acc[...] = jnp.zeros_like(acc)
     turned[...] = jnp.zeros_like(turned)
-    code_of = lambda k: jnp.where(k < p_count[0], codes[k], PB)
+    for copy in small:
+        copy.wait()
+    code_of = lambda k: jnp.where(k < p_count[0, 0], codes[0, 0, k], PB)
     fill_table(0, slots, table, code_of)
     fetch_own.wait()
     for k in range(slots):
@@ -130,13 +138,13 @@
         products, targets = [], []
         for u in range(UNROLL):
             k = t * UNROLL + u
-            products.append(jnp.dot(turned[rows[k]], fine[k], preferred_element_type=F32))
-            targets.append(jnp.where(k < count[0], cols[k], NS * FB))
+            products.append(jnp.dot(turned[rows[0, 0, k]], fine[k], preferred_element_type=F32))
+            targets.append(jnp.where(k < count[0, 0], cols[0, 0, k], NS * FB))
         for u in range(UNROLL):
             acc[targets[u]] += products[u]
         return carry
 
-    lax.fori_loop(0, (count[0] + UNROLL - 1) // UNROLL, step, 0)
+    lax.fori_loop(0, (count[0, 0] + UNROLL - 1) // UNROLL, step, 0)
     stores = []
     for s in range(1, NS):
         for m in range(FB):
@@ -147,7 +155,7 @@
     own_weight = jnp.concatenate([acc[m].astype(BF16) for m in range(FB)], axis=1)
     dense_of(0, size, table, own, dense)
     coarse = coarse_of(size, own_weight, dense, tile)
-    lift = lift_of(own, slots, size, lambda j: aggs[j])
+    lift = lift_of(own, slots, size, lambda j: aggs[0, 0, j])
     wide = CB * size
     more[0] = lift.T
     more[1] = coarse
@@ -292,6 +300,9 @@
 
     c_shape = jax.ShapeDtypeStruct((CB, NS, CB, size, size), BF16)
     table = pltpu.SMEM((1, PB + 1), jnp.int32)
+    integers = (
+        fine_rows, fine_cols, fine_counts, prolong_codes, prolong_counts, second_aggs
+    )
     col_stock, row_stock, more, c_one = pl.pallas_call(
         functools.partial(own_kernel, slots, size),
         out_shape=[
@@ -300,7 +311,7 @@
             jax.ShapeDtypeStruct((3, wide, G2 * size), BF16),
             c_shape,
         ],
-        in_specs=[SMEM] * 6 + [HBM] * 2,
+        in_specs=[HBM] * 8,
         out_specs=[HBM] * 4,
         scratch_shapes=[
             pltpu.VMEM((cap, size, size), BF16),
@@ -311,16 +322,15 @@
             pltpu.VMEM((NS * FB + 1, wide, size), F32),
             pltpu.VMEM((FB * size, wide), BF16),
             pltpu.VMEM((CB, CB, size, size), BF16),
+            *[pltpu.SMEM(x.shape, jnp.int32) for x in integers],
             table,
-            dma((6,)),
+            dma((8,)),
         ],
         compiler_params=WHOLE,
         cost_estimate=pl.CostEstimate(flops=10**9, bytes_accessed=4 * 10**6, transcendentals=0),
         name="own_source",
     )(
-        fine_rows[0, 0], fine_cols[0, 0], fine_counts[0],
-        prolong_codes[0, 0], prolong_counts[0], second_aggs[0, 0],
-        fine_blocks[0, 0], packed,
+        *integers, fine_blocks[0, 0], packed,
     )
 
     near_scratch = [

time: 49.6 us -> 49.7 us (level)
  starting transfers between devices: 23.4 us -> 21.3 us
  waiting for transfers between devices: 10.5 us -> 12.3 us
    ppermute x8, starting transfers between devices: 19.3 us -> 17.3 us  [shift(): return lax.ppermute(x, axis, pairs)]
    ppermute x8, waiting for transfers between devices: 10.5 us -> 12.3 us  [shift(): return lax.ppermute(x, axis, pairs)]
  transfers between devices with their start and end apart: 10 -> 10, of which waited for: 5 -> 4; matrix products, arithmetic and copies ran while one was open for 0% -> 0% of each run, Pallas kernels for 15% -> 16%
where the time goes in v11:
time: 49.7 us; the launch traced here: 49.3 us
  starting transfers between devices  21.3 us (43%)
  Pallas kernels  12.6 us (25%)
  waiting for transfers between devices  12.3 us (25%)
  between operations  2.07 us (4%)
  local copies, waits for them, and re-layouts  1.1 us (2%)
    ppermute x8, starting transfers between devices, shift(): return lax.ppermute(x, axis, pairs)  17.3 us
    ppermute x8, waiting for transfers between devices, shift(): return lax.ppermute(x, axis, pairs)  12.3 us
    pallas_call x1, Pallas kernels, per_device(): pl.pallas_call(functools.partial(own_kernel, slots, size), out_shape=[jax...  5.37 us
    ppermute x2, starting transfers between devices, swap(): return lax.ppermute(x, axis, pairs + [(j, i) for i, j in pairs])  4.02 us
    pallas_call x1, Pallas kernels, per_device(): pl.pallas_call(functools.partial(row_kernel, slots, size, cols_n), out_sh...  2.15 us
    pallas_call x1, Pallas kernels, per_device(): pl.pallas_call(functools.partial(side_kernel, slots, size), out_shape=[c_...  2.14 us
    pallas_call x1, Pallas kernels, per_device(): pl.pallas_call(pack_kernel, out_shape=jax.ShapeDtypeStruct((packed_rows,...  1.81 us
    unnamed x6, local copies, waits for them, and re-layouts  1.1 us
  transfers between devices with their start and end apart: 10, of which 4 were waited for; matrix products, arithmetic and copies ran while one was open for 0% of the time, Pallas kernels for 16%

profile of v11, /device:TPU:0, one launch (start us, length us, event | category | flops | bytes accessed | tf_op | source)
XLA Modules:
  0.0 49.3 jit_solution(1449420664784550157)
XLA Ops:
  1.3 1.8 %pack.1.own_at = bf16[1808,128]{1,0:T(8,128)(2,1)} custom-call(s32[1,1,12]{2,1,0:T(1,128)} %codes_at.3, s32[1,1]{1,0:T(1,128)S(6)} %copy.16.count_at.p_count_at, s32[1,1,2]{2,1,0:T(1,128)} %aggs_at.3, bf16[1536,128]{1,0:T(8,128)(2,1)} %bitcast.7, bf16[256,128]{1,0:T(8,128)(2,1)} %bitcast.8), custom_call_target="tpu_custom_call" | custom-call | tf_op jit(solution)/shard_map/pack/pallas_call | solution.py:275
  3.1 1.3 %collective-permute-start = (bf16[1808,128]{1,0:T(8,128)(2,1)}, bf16[1808,128]{1,0:T(8,128)(2,1)S(1)}, u32[]{:S(2)}, u32[]{:S(2)}) collective-permute-start(bf16[1808,128]{1,0:T(8,128)(2,1)} %pack.1.own_at), channel_id=1, source_target_pairs={{1,0},{2,1},{3,2},{5,4},{6,5},{7,6},{9,8},{10,9},{11,10},{13,12},{... | collective-permute-start | bytes 1388552 | tf_op jit(solution)/shard_map/ppermute | solution.py:258
  4.4 5.6 %collective-permute-start.1 = (bf16[1808,128]{1,0:T(8,128)(2,1)}, bf16[1808,128]{1,0:T(8,128)(2,1)S(1)}, u32[]{:S(2)}, u32[]{:S(2)}) collective-permute-start(bf16[1808,128]{1,0:T(8,128)(2,1)} %pack.1.own_at), channel_id=1, source_target_pairs={{0,1},{1,2},{2,3},{4,5},{5,6},{6,7},{8,9},{9,10},{10,11},{12,13},{... | collective-permute-start | bytes 1388552 | tf_op jit(solution)/shard_map/ppermute | solution.py:258
  10.0 0.7 %collective-permute-start.2 = (bf16[1808,128]{1,0:T(8,128)(2,1)}, bf16[1808,128]{1,0:T(8,128)(2,1)S(1)}, u32[]{:S(2)}, u32[]{:S(2)}) collective-permute-start(bf16[1808,128]{1,0:T(8,128)(2,1)} %pack.1.own_at), channel_id=1, source_target_pairs={{4,8},{12,16},{20,24},{8,4},{16,12},{24,20},{5,9},{13,17},{21,25},... | collective-permute-start | bytes 1388552 | tf_op jit(solution)/shard_map/ppermute | solution.py:262
  10.7 3.3 %collective-permute-start.3 = (bf16[1808,128]{1,0:T(8,128)(2,1)}, bf16[1808,128]{1,0:T(8,128)(2,1)S(1)}, u32[]{:S(2)}, u32[]{:S(2)}) collective-permute-start(bf16[1808,128]{1,0:T(8,128)(2,1)} %pack.1.own_at), channel_id=1, source_target_pairs={{0,4},{8,12},{16,20},{24,28},{4,0},{12,8},{20,16},{28,24},{1,5},{9... | collective-permute-start | bytes 1388552 | tf_op jit(solution)/shard_map/ppermute | solution.py:262
  14.7 5.4 %own_source.1 = (bf16[2,256,1024]{2,1,0:T(8,128)(2,1)}, bf16[2,256,1024]{2,1,0:T(8,128)(2,1)}, bf16[3,256,256]{2,1,0:T(8,128)(2,1)}, bf16[2,5,2,128,128]{4,3,2,1,0:T(8,128)(2,1)}) custom-call(s32[1,1,64]{2,1,0:T(1,128)} %rows_at.1, s32[1,1,64]{2,1,0:T(1,128)} %cols_at.1, s32[1,1]{1,0:T(1,128)S(6)} %copy.15.count_at, s32[1,1,12]{2,1,0:T(1,128)} %codes_at.3, ...), custom_call_target="tpu_custom_call" | custom-call | flops 1000000000 | bytes 4000000 | tf_op jit(solution)/shard_map/own_source/pallas_call | solution.py:306
  20.0 0.0 copy-start.1
  20.0 0.0 copy-start.2
  20.1 1.1 %copy-done.2 = bf16[3,256,256]{2,1,0:T(8,128)(2,1)S(1)} copy-done((bf16[3,256,256]{2,1,0:T(8,128)(2,1)S(1)}, bf16[3,256,256]{2,1,0:T(8,128)(2,1)}, u32[]{:S(2)}) %copy-start.2) | copy-done | bytes 393240
  21.1 0.2 own_half.1
  21.3 0.0 copy-start
  21.3 0.0 collective-permute-done.right
  21.4 0.0 collective-permute-done.1.left
  21.4 0.0 copy-done.1
  21.4 2.1 %col_sources.1 = (bf16[2,5,2,128,128]{4,3,2,1,0:T(8,128)(2,1)}, f32[256,256]{1,0:T(8,128)S(1)}) custom-call(bf16[2,256,1024]{2,1,0:T(8,128)(2,1)S(1)} %copy-done.1, bf16[256,256]{1,0:T(8,128)(2,1)S(1)} %get-tuple-element.17.lift_t, f32[256,256]{1,0:T(8,128)S(1)} %get-tuple-element.19.half, ...), custom_call_target="tpu_custom_call", output_to_operand_aliasing={{0}: (5, {})} | custom-call | tf_op jit(solution)/shard_map/col_sources/pallas_call | solution.py:353
  23.5 0.0 collective-permute-done.2.other
  23.5 0.0 collective-permute-done.3.pair
  23.5 0.0 copy-done
  23.6 2.1 %row_sources.1 = (bf16[2,5,2,128,128]{4,3,2,1,0:T(8,128)(2,1)}, f32[3,64,256]{2,1,0:T(8,128)S(1)}, bf16[3,64,256]{2,1,0:T(8,128)(2,1)S(1)}, bf16[3,64,256]{2,1,0:T(8,128)(2,1)S(1)}, bf16[3,64,256]{2,1,0:T(8,128)(2,1)S(1)}) custom-call(bf16[2,256,1024]{2,1,0:T(8,128)(2,1)S(1)} %copy-done, ...), custom_call_target="tpu_custom_call", output_to_operand_aliasing={{0}: (5, {})} | custom-call | tf_op jit(solution)/shard_map/row_sources/pallas_call | solution.py:367
  25.7 1.6 %collective-permute-start.4 = (bf16[3,64,256]{2,1,0:T(8,128)(2,1)S(1)}, bf16[3,64,256]{2,1,0:T(8,128)(2,1)S(1)}, u32[]{:S(2)}, u32[]{:S(2)}) collective-permute-start(bf16[3,64,256]{2,1,0:T(8,128)(2,1)S(1)} %get-tuple-element.25), channel_id=1, source_target_pairs={{0,1},{1,2},{2,3},{3,0},{4,5},{5,6},{6,7},{7,4},{8,9},{9,10},{10,1... | collective-permute-start | bytes 294920 | tf_op jit(solution)/shard_map/ppermute | solution.py:258
  27.3 2.3 %collective-permute-start.5 = (bf16[3,64,256]{2,1,0:T(8,128)(2,1)S(1)}, bf16[3,64,256]{2,1,0:T(8,128)(2,1)S(1)}, u32[]{:S(2)}, u32[]{:S(2)}) collective-permute-start(bf16[3,64,256]{2,1,0:T(8,128)(2,1)S(1)} %get-tuple-element.26), channel_id=1, source_target_pairs={{0,2},{1,3},{2,0},{3,1},{4,6},{5,7},{6,4},{7,5},{8,10},{9,11},{10,... | collective-permute-start | bytes 294920 | tf_op jit(solution)/shard_map/ppermute | solution.py:258
  29.6 1.3 %collective-permute-start.6 = (bf16[3,64,256]{2,1,0:T(8,128)(2,1)S(1)}, bf16[3,64,256]{2,1,0:T(8,128)(2,1)S(1)}, u32[]{:S(2)}, u32[]{:S(2)}) collective-permute-start(bf16[3,64,256]{2,1,0:T(8,128)(2,1)S(1)} %get-tuple-element.27), channel_id=1, source_target_pairs={{0,3},{1,0},{2,1},{3,2},{4,7},{5,4},{6,5},{7,6},{8,11},{9,8},{10,9... | collective-permute-start | bytes 294920 | tf_op jit(solution)/shard_map/ppermute | solution.py:258
  31.0 2.3 %collective-permute-done.4.refs_1_ = bf16[3,64,256]{2,1,0:T(8,128)(2,1)S(1)} collective-permute-done((bf16[3,64,256]{2,1,0:T(8,128)(2,1)S(1)}, bf16[3,64,256]{2,1,0:T(8,128)(2,1)S(1)}, u32[]{:S(2)}, u32[]{:S(2)}) %collective-permute-start.4) | collective-permute-done | bytes 98336 | tf_op jit(solution)/shard_map/ppermute | solution.py:258
  33.3 4.0 %collective-permute-done.5.refs_2_ = bf16[3,64,256]{2,1,0:T(8,128)(2,1)S(1)} collective-permute-done((bf16[3,64,256]{2,1,0:T(8,128)(2,1)S(1)}, bf16[3,64,256]{2,1,0:T(8,128)(2,1)S(1)}, u32[]{:S(2)}, u32[]{:S(2)}) %collective-permute-start.5) | collective-permute-done | bytes 98336 | tf_op jit(solution)/shard_map/ppermute | solution.py:258
  37.4 0.0 collective-permute-done.6.refs_3_
  37.4 2.7 %collective-permute-start.7 = (bf16[3,64,256]{2,1,0:T(8,128)(2,1)S(1)}, bf16[3,64,256]{2,1,0:T(8,128)(2,1)S(1)}, u32[]{:S(2)}, u32[]{:S(2)}) collective-permute-start(bf16[3,64,256]{2,1,0:T(8,128)(2,1)S(1)} %total.1.refs_0_), channel_id=1, source_target_pairs={{0,1},{1,2},{2,3},{3,0},{4,5},{5,6},{6,7},{7,4},{8,9},{9,10},{10,1... | collective-permute-start | bytes 294920 | tf_op jit(solution)/shard_map/ppermute | solution.py:258
  40.1 1.3 %collective-permute-start.8 = (bf16[3,64,256]{2,1,0:T(8,128)(2,1)S(1)}, bf16[3,64,256]{2,1,0:T(8,128)(2,1)S(1)}, u32[]{:S(2)}, u32[]{:S(2)}) collective-permute-start(bf16[3,64,256]{2,1,0:T(8,128)(2,1)S(1)} %total.1.refs_0_), channel_id=1, source_target_pairs={{0,2},{1,3},{2,0},{3,1},{4,6},{5,7},{6,4},{7,5},{8,10},{9,11},{10,... | collective-permute-start | bytes 294920 | tf_op jit(solution)/shard_map/ppermute | solution.py:258
  41.4 1.1 %collective-permute-start.9 = (bf16[3,64,256]{2,1,0:T(8,128)(2,1)S(1)}, bf16[3,64,256]{2,1,0:T(8,128)(2,1)S(1)}, u32[]{:S(2)}, u32[]{:S(2)}) collective-permute-start(bf16[3,64,256]{2,1,0:T(8,128)(2,1)S(1)} %total.1.refs_0_), channel_id=1, source_target_pairs={{0,3},{1,0},{2,1},{3,2},{4,7},{5,4},{6,5},{7,6},{8,11},{9,8},{10,9... | collective-permute-start | bytes 294920 | tf_op jit(solution)/shard_map/ppermute | solution.py:258
  42.5 2.4 %collective-permute-done.7.refs_1_ = bf16[3,64,256]{2,1,0:T(8,128)(2,1)S(1)} collective-permute-done((bf16[3,64,256]{2,1,0:T(8,128)(2,1)S(1)}, bf16[3,64,256]{2,1,0:T(8,128)(2,1)S(1)}, u32[]{:S(2)}, u32[]{:S(2)}) %collective-permute-start.7) | collective-permute-done | bytes 98336 | tf_op jit(solution)/shard_map/ppermute | solution.py:258
  44.9 3.4 %collective-permute-done.8.refs_2_ = bf16[3,64,256]{2,1,0:T(8,128)(2,1)S(1)} collective-permute-done((bf16[3,64,256]{2,1,0:T(8,128)(2,1)S(1)}, bf16[3,64,256]{2,1,0:T(8,128)(2,1)S(1)}, u32[]{:S(2)}, u32[]{:S(2)}) %collective-permute-start.8) | collective-permute-done | bytes 98336 | tf_op jit(solution)/shard_map/ppermute | solution.py:258
  48.4 0.0 collective-permute-done.9.refs_3_
  48.4 0.9 %spread.1 = f32[2,3,2,128,128]{4,3,2,1,0:T(8,128)} custom-call(bf16[3,64,256]{2,1,0:T(8,128)(2,1)S(1)} %total.1.refs_0_, bf16[3,64,256]{2,1,0:T(8,128)(2,1)S(1)} %collective-permute-done.7.refs_1_, bf16[3,64,256]{2,1,0:T(8,128)(2,1)S(1)} %collective-permute-done.8.refs_2_, bf16[3,64,256]{2,1,0:T(8,128)(2,1)S(1)} %collective-permute-done.9.refs_3_), custom_call_target="tpu_custom_call" | custom-call | tf_op jit(solution)/shard_map/spread/pallas_call | solution.py:383
  (1 shorter events, 0.0 us)
Async XLA Ops:
  3.1 18.3 %collective-permute-start = (bf16[1808,128]{1,0:T(8,128)(2,1)}, bf16[1808,128]{1,0:T(8,128)(2,1)S(1)}, u32[]{:S(2)}, u32[]{:S(2)}) collective-permute-start(bf16[1808,128]{1,0:T(8,128)(2,1)} %pack.1.own_at), channel_id=1, source_target_pairs={{1,0},{2,1},{3,2},{5,4},{6,5},{7,6},{9,8},{10,9},{11,10},{13,12},{... | collective-permute-start | bytes 1388552 | tf_op jit(solution)/shard_map/ppermute | solution.py:258
  4.4 17.0 %collective-permute-start.1 = (bf16[1808,128]{1,0:T(8,128)(2,1)}, bf16[1808,128]{1,0:T(8,128)(2,1)S(1)}, u32[]{:S(2)}, u32[]{:S(2)}) collective-permute-start(bf16[1808,128]{1,0:T(8,128)(2,1)} %pack.1.own_at), channel_id=1, source_target_pairs={{0,1},{1,2},{2,3},{4,5},{5,6},{6,7},{8,9},{9,10},{10,11},{12,13},{... | collective-permute-start | bytes 1388552 | tf_op jit(solution)/shard_map/ppermute | solution.py:258
  10.0 13.5 %collective-permute-start.2 = (bf16[1808,128]{1,0:T(8,128)(2,1)}, bf16[1808,128]{1,0:T(8,128)(2,1)S(1)}, u32[]{:S(2)}, u32[]{:S(2)}) collective-permute-start(bf16[1808,128]{1,0:T(8,128)(2,1)} %pack.1.own_at), channel_id=1, source_target_pairs={{4,8},{12,16},{20,24},{8,4},{16,12},{24,20},{5,9},{13,17},{21,25},... | collective-permute-start | bytes 1388552 | tf_op jit(solution)/shard_map/ppermute | solution.py:262
  10.7 12.9 %collective-permute-start.3 = (bf16[1808,128]{1,0:T(8,128)(2,1)}, bf16[1808,128]{1,0:T(8,128)(2,1)S(1)}, u32[]{:S(2)}, u32[]{:S(2)}) collective-permute-start(bf16[1808,128]{1,0:T(8,128)(2,1)} %pack.1.own_at), channel_id=1, source_target_pairs={{0,4},{8,12},{16,20},{24,28},{4,0},{12,8},{20,16},{28,24},{1,5},{9... | collective-permute-start | bytes 1388552 | tf_op jit(solution)/shard_map/ppermute | solution.py:262
  20.0 1.3 %copy-start.1 = (bf16[2,256,1024]{2,1,0:T(8,128)(2,1)S(1)}, bf16[2,256,1024]{2,1,0:T(8,128)(2,1)}, u32[]{:S(2)}) copy-start(bf16[2,256,1024]{2,1,0:T(8,128)(2,1)} %get-tuple-element.18.stock) | copy-start | bytes 3145732
  20.0 1.1 %copy-start.2 = (bf16[3,256,256]{2,1,0:T(8,128)(2,1)S(1)}, bf16[3,256,256]{2,1,0:T(8,128)(2,1)}, u32[]{:S(2)}) copy-start(bf16[3,256,256]{2,1,0:T(8,128)(2,1)} %get-tuple-element.16.more) | copy-start | bytes 1179652
  21.3 2.2 %copy-start = (bf16[2,256,1024]{2,1,0:T(8,128)(2,1)S(1)}, bf16[2,256,1024]{2,1,0:T(8,128)(2,1)}, u32[]{:S(2)}) copy-start(bf16[2,256,1024]{2,1,0:T(8,128)(2,1)} %get-tuple-element.15.stock) | copy-start | bytes 3145732
  25.7 7.6 %collective-permute-start.4 = (bf16[3,64,256]{2,1,0:T(8,128)(2,1)S(1)}, bf16[3,64,256]{2,1,0:T(8,128)(2,1)S(1)}, u32[]{:S(2)}, u32[]{:S(2)}) collective-permute-start(bf16[3,64,256]{2,1,0:T(8,128)(2,1)S(1)} %get-tuple-element.25), channel_id=1, source_target_pairs={{0,1},{1,2},{2,3},{3,0},{4,5},{5,6},{6,7},{7,4},{8,9},{9,10},{10,1... | collective-permute-start | bytes 294920 | tf_op jit(solution)/shard_map/ppermute | solution.py:258
  27.3 10.1 %collective-permute-start.5 = (bf16[3,64,256]{2,1,0:T(8,128)(2,1)S(1)}, bf16[3,64,256]{2,1,0:T(8,128)(2,1)S(1)}, u32[]{:S(2)}, u32[]{:S(2)}) collective-permute-start(bf16[3,64,256]{2,1,0:T(8,128)(2,1)S(1)} %get-tuple-element.26), channel_id=1, source_target_pairs={{0,2},{1,3},{2,0},{3,1},{4,6},{5,7},{6,4},{7,5},{8,10},{9,11},{10,... | collective-permute-start | bytes 294920 | tf_op jit(solution)/shard_map/ppermute | solution.py:258
  29.6 7.7 %collective-permute-start.6 = (bf16[3,64,256]{2,1,0:T(8,128)(2,1)S(1)}, bf16[3,64,256]{2,1,0:T(8,128)(2,1)S(1)}, u32[]{:S(2)}, u32[]{:S(2)}) collective-permute-start(bf16[3,64,256]{2,1,0:T(8,128)(2,1)S(1)} %get-tuple-element.27), channel_id=1, source_target_pairs={{0,3},{1,0},{2,1},{3,2},{4,7},{5,4},{6,5},{7,6},{8,11},{9,8},{10,9... | collective-permute-start | bytes 294920 | tf_op jit(solution)/shard_map/ppermute | solution.py:258
  37.4 7.5 %collective-permute-start.7 = (bf16[3,64,256]{2,1,0:T(8,128)(2,1)S(1)}, bf16[3,64,256]{2,1,0:T(8,128)(2,1)S(1)}, u32[]{:S(2)}, u32[]{:S(2)}) collective-permute-start(bf16[3,64,256]{2,1,0:T(8,128)(2,1)S(1)} %total.1.refs_0_), channel_id=1, source_target_pairs={{0,1},{1,2},{2,3},{3,0},{4,5},{5,6},{6,7},{7,4},{8,9},{9,10},{10,1... | collective-permute-start | bytes 294920 | tf_op jit(solution)/shard_map/ppermute | solution.py:258
  40.1 8.3 %collective-permute-start.8 = (bf16[3,64,256]{2,1,0:T(8,128)(2,1)S(1)}, bf16[3,64,256]{2,1,0:T(8,128)(2,1)S(1)}, u32[]{:S(2)}, u32[]{:S(2)}) collective-permute-start(bf16[3,64,256]{2,1,0:T(8,128)(2,1)S(1)} %total.1.refs_0_), channel_id=1, source_target_pairs={{0,2},{1,3},{2,0},{3,1},{4,6},{5,7},{6,4},{7,5},{8,10},{9,11},{10,... | collective-permute-start | bytes 294920 | tf_op jit(solution)/shard_map/ppermute | solution.py:258
  41.4 7.0 %collective-permute-start.9 = (bf16[3,64,256]{2,1,0:T(8,128)(2,1)S(1)}, bf16[3,64,256]{2,1,0:T(8,128)(2,1)S(1)}, u32[]{:S(2)}, u32[]{:S(2)}) collective-permute-start(bf16[3,64,256]{2,1,0:T(8,128)(2,1)S(1)} %total.1.refs_0_), channel_id=1, source_target_pairs={{0,3},{1,0},{2,1},{3,2},{4,7},{5,4},{6,5},{7,6},{8,11},{9,8},{10,9... | collective-permute-start | bytes 294920 | tf_op jit(solution)/shard_map/ppermute | solution.py:258

commit v12 on v11

--- a/solution.py
+++ b/solution.py
@@ -135,13 +135,10 @@
     fetch_fine.wait()
 
     def step(t, carry):
-        products, targets = [], []
         for u in range(UNROLL):
             k = t * UNROLL + u
-            products.append(jnp.dot(turned[rows[0, 0, k]], fine[k], preferred_element_type=F32))
-            targets.append(jnp.where(k < count[0, 0], cols[0, 0, k], NS * FB))
-        for u in range(UNROLL):
-            acc[targets[u]] += products[u]
+            target = jnp.where(k < count[0, 0], cols[0, 0, k], NS * FB)
+            acc[target] += jnp.dot(turned[rows[0, 0, k]], fine[k], preferred_element_type=F32)
         return carry
 
     lax.fori_loop(0, (count[0, 0] + UNROLL - 1) // UNROLL, step, 0)

time: 49.7 us -> 49.7 us (level)
  transfers between devices with their start and end apart: 10 -> 10, of which waited for: 4 -> 4; matrix products, arithmetic and copies ran while one was open for 0% -> 0% of each run, Pallas kernels for 16% -> 15%
where the time goes in v12:
time: 49.7 us; the launch traced here: 49.3 us
  starting transfers between devices  21.6 us (43%)
  Pallas kernels  12.3 us (25%)
  waiting for transfers between devices  12.1 us (24%)
  between operations  2.07 us (4%)
  local copies, waits for them, and re-layouts  1.1 us (2%)
    ppermute x8, starting transfers between devices, shift(): return lax.ppermute(x, axis, pairs)  17.6 us
    ppermute x8, waiting for transfers between devices, shift(): return lax.ppermute(x, axis, pairs)  12.1 us
    pallas_call x1, Pallas kernels, per_device(): pl.pallas_call(functools.partial(own_kernel, slots, size), out_shape=[jax...  5.07 us
    ppermute x2, starting transfers between devices, swap(): return lax.ppermute(x, axis, pairs + [(j, i) for i, j in pairs])  4.02 us
    pallas_call x1, Pallas kernels, per_device(): pl.pallas_call(functools.partial(row_kernel, slots, size, cols_n), out_sh...  2.15 us
    pallas_call x1, Pallas kernels, per_device(): pl.pallas_call(functools.partial(side_kernel, slots, size), out_shape=[c_...  2.13 us
    pallas_call x1, Pallas kernels, per_device(): pl.pallas_call(pack_kernel, out_shape=jax.ShapeDtypeStruct((packed_rows,...  1.81 us
    unnamed x6, local copies, waits for them, and re-layouts  1.1 us
  transfers between devices with their start and end apart: 10, of which 4 were waited for; matrix products, arithmetic and copies ran while one was open for 0% of the time, Pallas kernels for 15%

profile of v12, /device:TPU:0, one launch (start us, length us, event | category | flops | bytes accessed | tf_op | source)
XLA Modules:
  0.0 49.3 jit_solution(12303595112006145904)
XLA Ops:
  1.3 1.8 %pack.1.own_at = bf16[1808,128]{1,0:T(8,128)(2,1)} custom-call(s32[1,1,12]{2,1,0:T(1,128)} %codes_at.3, s32[1,1]{1,0:T(1,128)S(6)} %copy.16.count_at.p_count_at, s32[1,1,2]{2,1,0:T(1,128)} %aggs_at.3, bf16[1536,128]{1,0:T(8,128)(2,1)} %bitcast.7, bf16[256,128]{1,0:T(8,128)(2,1)} %bitcast.8), custom_call_target="tpu_custom_call" | custom-call | tf_op jit(solution)/shard_map/pack/pallas_call | solution.py:272
  3.1 1.3 %collective-permute-start = (bf16[1808,128]{1,0:T(8,128)(2,1)}, bf16[1808,128]{1,0:T(8,128)(2,1)S(1)}, u32[]{:S(2)}, u32[]{:S(2)}) collective-permute-start(bf16[1808,128]{1,0:T(8,128)(2,1)} %pack.1.own_at), channel_id=1, source_target_pairs={{1,0},{2,1},{3,2},{5,4},{6,5},{7,6},{9,8},{10,9},{11,10},{13,12},{... | collective-permute-start | bytes 1388552 | tf_op jit(solution)/shard_map/ppermute | solution.py:255
  4.4 5.6 %collective-permute-start.1 = (bf16[1808,128]{1,0:T(8,128)(2,1)}, bf16[1808,128]{1,0:T(8,128)(2,1)S(1)}, u32[]{:S(2)}, u32[]{:S(2)}) collective-permute-start(bf16[1808,128]{1,0:T(8,128)(2,1)} %pack.1.own_at), channel_id=1, source_target_pairs={{0,1},{1,2},{2,3},{4,5},{5,6},{6,7},{8,9},{9,10},{10,11},{12,13},{... | collective-permute-start | bytes 1388552 | tf_op jit(solution)/shard_map/ppermute | solution.py:255
  10.0 0.7 %collective-permute-start.2 = (bf16[1808,128]{1,0:T(8,128)(2,1)}, bf16[1808,128]{1,0:T(8,128)(2,1)S(1)}, u32[]{:S(2)}, u32[]{:S(2)}) collective-permute-start(bf16[1808,128]{1,0:T(8,128)(2,1)} %pack.1.own_at), channel_id=1, source_target_pairs={{4,8},{12,16},{20,24},{8,4},{16,12},{24,20},{5,9},{13,17},{21,25},... | collective-permute-start | bytes 1388552 | tf_op jit(solution)/shard_map/ppermute | solution.py:259
  10.7 3.3 %collective-permute-start.3 = (bf16[1808,128]{1,0:T(8,128)(2,1)}, bf16[1808,128]{1,0:T(8,128)(2,1)S(1)}, u32[]{:S(2)}, u32[]{:S(2)}) collective-permute-start(bf16[1808,128]{1,0:T(8,128)(2,1)} %pack.1.own_at), channel_id=1, source_target_pairs={{0,4},{8,12},{16,20},{24,28},{4,0},{12,8},{20,16},{28,24},{1,5},{9... | collective-permute-start | bytes 1388552 | tf_op jit(solution)/shard_map/ppermute | solution.py:259
  14.7 5.1 %own_source.1 = (bf16[2,256,1024]{2,1,0:T(8,128)(2,1)}, bf16[2,256,1024]{2,1,0:T(8,128)(2,1)}, bf16[3,256,256]{2,1,0:T(8,128)(2,1)}, bf16[2,5,2,128,128]{4,3,2,1,0:T(8,128)(2,1)}) custom-call(s32[1,1,64]{2,1,0:T(1,128)} %rows_at.1, s32[1,1,64]{2,1,0:T(1,128)} %cols_at.1, s32[1,1]{1,0:T(1,128)S(6)} %copy.15.count_at, s32[1,1,12]{2,1,0:T(1,128)} %codes_at.3, ...), custom_call_target="tpu_custom_call" | custom-call | flops 1000000000 | bytes 4000000 | tf_op jit(solution)/shard_map/own_source/pallas_call | solution.py:303
  19.7 0.0 copy-start.1
  19.8 0.0 copy-start.2
  19.8 1.1 %copy-done.2 = bf16[3,256,256]{2,1,0:T(8,128)(2,1)S(1)} copy-done((bf16[3,256,256]{2,1,0:T(8,128)(2,1)S(1)}, bf16[3,256,256]{2,1,0:T(8,128)(2,1)}, u32[]{:S(2)}) %copy-start.2) | copy-done | bytes 393240
  20.8 0.2 own_half.1
  21.0 0.0 copy-start
  21.0 0.0 collective-permute-done.right
  21.1 0.0 collective-permute-done.1.left
  21.1 0.0 copy-done.1
  21.1 2.1 %col_sources.1 = (bf16[2,5,2,128,128]{4,3,2,1,0:T(8,128)(2,1)}, f32[256,256]{1,0:T(8,128)S(1)}) custom-call(bf16[2,256,1024]{2,1,0:T(8,128)(2,1)S(1)} %copy-done.1, bf16[256,256]{1,0:T(8,128)(2,1)S(1)} %get-tuple-element.17.lift_t, f32[256,256]{1,0:T(8,128)S(1)} %get-tuple-element.19.half, ...), custom_call_target="tpu_custom_call", output_to_operand_aliasing={{0}: (5, {})} | custom-call | tf_op jit(solution)/shard_map/col_sources/pallas_call | solution.py:350
  23.2 0.0 collective-permute-done.2.other
  23.2 0.0 collective-permute-done.3.pair
  23.2 0.0 copy-done
  23.3 2.1 %row_sources.1 = (bf16[2,5,2,128,128]{4,3,2,1,0:T(8,128)(2,1)}, f32[3,64,256]{2,1,0:T(8,128)S(1)}, bf16[3,64,256]{2,1,0:T(8,128)(2,1)S(1)}, bf16[3,64,256]{2,1,0:T(8,128)(2,1)S(1)}, bf16[3,64,256]{2,1,0:T(8,128)(2,1)S(1)}) custom-call(bf16[2,256,1024]{2,1,0:T(8,128)(2,1)S(1)} %copy-done, ...), custom_call_target="tpu_custom_call", output_to_operand_aliasing={{0}: (5, {})} | custom-call | tf_op jit(solution)/shard_map/row_sources/pallas_call | solution.py:364
  25.4 1.6 %collective-permute-start.4 = (bf16[3,64,256]{2,1,0:T(8,128)(2,1)S(1)}, bf16[3,64,256]{2,1,0:T(8,128)(2,1)S(1)}, u32[]{:S(2)}, u32[]{:S(2)}) collective-permute-start(bf16[3,64,256]{2,1,0:T(8,128)(2,1)S(1)} %get-tuple-element.25), channel_id=1, source_target_pairs={{0,1},{1,2},{2,3},{3,0},{4,5},{5,6},{6,7},{7,4},{8,9},{9,10},{10,1... | collective-permute-start | bytes 294920 | tf_op jit(solution)/shard_map/ppermute | solution.py:255
  27.0 2.6 %collective-permute-start.5 = (bf16[3,64,256]{2,1,0:T(8,128)(2,1)S(1)}, bf16[3,64,256]{2,1,0:T(8,128)(2,1)S(1)}, u32[]{:S(2)}, u32[]{:S(2)}) collective-permute-start(bf16[3,64,256]{2,1,0:T(8,128)(2,1)S(1)} %get-tuple-element.26), channel_id=1, source_target_pairs={{0,2},{1,3},{2,0},{3,1},{4,6},{5,7},{6,4},{7,5},{8,10},{9,11},{10,... | collective-permute-start | bytes 294920 | tf_op jit(solution)/shard_map/ppermute | solution.py:255
  29.6 1.3 %collective-permute-start.6 = (bf16[3,64,256]{2,1,0:T(8,128)(2,1)S(1)}, bf16[3,64,256]{2,1,0:T(8,128)(2,1)S(1)}, u32[]{:S(2)}, u32[]{:S(2)}) collective-permute-start(bf16[3,64,256]{2,1,0:T(8,128)(2,1)S(1)} %get-tuple-element.27), channel_id=1, source_target_pairs={{0,3},{1,0},{2,1},{3,2},{4,7},{5,4},{6,5},{7,6},{8,11},{9,8},{10,9... | collective-permute-start | bytes 294920 | tf_op jit(solution)/shard_map/ppermute | solution.py:255
  31.0 2.0 %collective-permute-done.4.refs_1_ = bf16[3,64,256]{2,1,0:T(8,128)(2,1)S(1)} collective-permute-done((bf16[3,64,256]{2,1,0:T(8,128)(2,1)S(1)}, bf16[3,64,256]{2,1,0:T(8,128)(2,1)S(1)}, u32[]{:S(2)}, u32[]{:S(2)}) %collective-permute-start.4) | collective-permute-done | bytes 98336 | tf_op jit(solution)/shard_map/ppermute | solution.py:255
  32.9 4.2 %collective-permute-done.5.refs_2_ = bf16[3,64,256]{2,1,0:T(8,128)(2,1)S(1)} collective-permute-done((bf16[3,64,256]{2,1,0:T(8,128)(2,1)S(1)}, bf16[3,64,256]{2,1,0:T(8,128)(2,1)S(1)}, u32[]{:S(2)}, u32[]{:S(2)}) %collective-permute-start.5) | collective-permute-done | bytes 98336 | tf_op jit(solution)/shard_map/ppermute | solution.py:255
  37.1 0.0 collective-permute-done.6.refs_3_
  37.2 2.7 %collective-permute-start.7 = (bf16[3,64,256]{2,1,0:T(8,128)(2,1)S(1)}, bf16[3,64,256]{2,1,0:T(8,128)(2,1)S(1)}, u32[]{:S(2)}, u32[]{:S(2)}) collective-permute-start(bf16[3,64,256]{2,1,0:T(8,128)(2,1)S(1)} %total.1.refs_0_), channel_id=1, source_target_pairs={{0,1},{1,2},{2,3},{3,0},{4,5},{5,6},{6,7},{7,4},{8,9},{9,10},{10,1... | collective-permute-start | bytes 294920 | tf_op jit(solution)/shard_map/ppermute | solution.py:255
  39.9 1.5 %collective-permute-start.8 = (bf16[3,64,256]{2,1,0:T(8,128)(2,1)S(1)}, bf16[3,64,256]{2,1,0:T(8,128)(2,1)S(1)}, u32[]{:S(2)}, u32[]{:S(2)}) collective-permute-start(bf16[3,64,256]{2,1,0:T(8,128)(2,1)S(1)} %total.1.refs_0_), channel_id=1, source_target_pairs={{0,2},{1,3},{2,0},{3,1},{4,6},{5,7},{6,4},{7,5},{8,10},{9,11},{10,... | collective-permute-start | bytes 294920 | tf_op jit(solution)/shard_map/ppermute | solution.py:255
  41.4 0.9 %collective-permute-start.9 = (bf16[3,64,256]{2,1,0:T(8,128)(2,1)S(1)}, bf16[3,64,256]{2,1,0:T(8,128)(2,1)S(1)}, u32[]{:S(2)}, u32[]{:S(2)}) collective-permute-start(bf16[3,64,256]{2,1,0:T(8,128)(2,1)S(1)} %total.1.refs_0_), channel_id=1, source_target_pairs={{0,3},{1,0},{2,1},{3,2},{4,7},{5,4},{6,5},{7,6},{8,11},{9,8},{10,9... | collective-permute-start | bytes 294920 | tf_op jit(solution)/shard_map/ppermute | solution.py:255
  42.4 2.4 %collective-permute-done.7.refs_1_ = bf16[3,64,256]{2,1,0:T(8,128)(2,1)S(1)} collective-permute-done((bf16[3,64,256]{2,1,0:T(8,128)(2,1)S(1)}, bf16[3,64,256]{2,1,0:T(8,128)(2,1)S(1)}, u32[]{:S(2)}, u32[]{:S(2)}) %collective-permute-start.7) | collective-permute-done | bytes 98336 | tf_op jit(solution)/shard_map/ppermute | solution.py:255
  44.8 3.5 %collective-permute-done.8.refs_2_ = bf16[3,64,256]{2,1,0:T(8,128)(2,1)S(1)} collective-permute-done((bf16[3,64,256]{2,1,0:T(8,128)(2,1)S(1)}, bf16[3,64,256]{2,1,0:T(8,128)(2,1)S(1)}, u32[]{:S(2)}, u32[]{:S(2)}) %collective-permute-start.8) | collective-permute-done | bytes 98336 | tf_op jit(solution)/shard_map/ppermute | solution.py:255
  48.3 0.0 collective-permute-done.9.refs_3_
  48.3 0.9 %spread.1 = f32[2,3,2,128,128]{4,3,2,1,0:T(8,128)} custom-call(bf16[3,64,256]{2,1,0:T(8,128)(2,1)S(1)} %total.1.refs_0_, bf16[3,64,256]{2,1,0:T(8,128)(2,1)S(1)} %collective-permute-done.7.refs_1_, bf16[3,64,256]{2,1,0:T(8,128)(2,1)S(1)} %collective-permute-done.8.refs_2_, bf16[3,64,256]{2,1,0:T(8,128)(2,1)S(1)} %collective-permute-done.9.refs_3_), custom_call_target="tpu_custom_call" | custom-call | tf_op jit(solution)/shard_map/spread/pallas_call | solution.py:380
  (1 shorter events, 0.0 us)
Async XLA Ops:
  3.1 18.0 %collective-permute-start = (bf16[1808,128]{1,0:T(8,128)(2,1)}, bf16[1808,128]{1,0:T(8,128)(2,1)S(1)}, u32[]{:S(2)}, u32[]{:S(2)}) collective-permute-start(bf16[1808,128]{1,0:T(8,128)(2,1)} %pack.1.own_at), channel_id=1, source_target_pairs={{1,0},{2,1},{3,2},{5,4},{6,5},{7,6},{9,8},{10,9},{11,10},{13,12},{... | collective-permute-start | bytes 1388552 | tf_op jit(solution)/shard_map/ppermute | solution.py:255
  4.4 16.7 %collective-permute-start.1 = (bf16[1808,128]{1,0:T(8,128)(2,1)}, bf16[1808,128]{1,0:T(8,128)(2,1)S(1)}, u32[]{:S(2)}, u32[]{:S(2)}) collective-permute-start(bf16[1808,128]{1,0:T(8,128)(2,1)} %pack.1.own_at), channel_id=1, source_target_pairs={{0,1},{1,2},{2,3},{4,5},{5,6},{6,7},{8,9},{9,10},{10,11},{12,13},{... | collective-permute-start | bytes 1388552 | tf_op jit(solution)/shard_map/ppermute | solution.py:255
  10.0 13.2 %collective-permute-start.2 = (bf16[1808,128]{1,0:T(8,128)(2,1)}, bf16[1808,128]{1,0:T(8,128)(2,1)S(1)}, u32[]{:S(2)}, u32[]{:S(2)}) collective-permute-start(bf16[1808,128]{1,0:T(8,128)(2,1)} %pack.1.own_at), channel_id=1, source_target_pairs={{4,8},{12,16},{20,24},{8,4},{16,12},{24,20},{5,9},{13,17},{21,25},... | collective-permute-start | bytes 1388552 | tf_op jit(solution)/shard_map/ppermute | solution.py:259
  10.7 12.6 %collective-permute-start.3 = (bf16[1808,128]{1,0:T(8,128)(2,1)}, bf16[1808,128]{1,0:T(8,128)(2,1)S(1)}, u32[]{:S(2)}, u32[]{:S(2)}) collective-permute-start(bf16[1808,128]{1,0:T(8,128)(2,1)} %pack.1.own_at), channel_id=1, source_target_pairs={{0,4},{8,12},{16,20},{24,28},{4,0},{12,8},{20,16},{28,24},{1,5},{9... | collective-permute-start | bytes 1388552 | tf_op jit(solution)/shard_map/ppermute | solution.py:259
  19.7 1.3 %copy-start.1 = (bf16[2,256,1024]{2,1,0:T(8,128)(2,1)S(1)}, bf16[2,256,1024]{2,1,0:T(8,128)(2,1)}, u32[]{:S(2)}) copy-start(bf16[2,256,1024]{2,1,0:T(8,128)(2,1)} %get-tuple-element.18.stock) | copy-start | bytes 3145732
  19.8 1.1 %copy-start.2 = (bf16[3,256,256]{2,1,0:T(8,128)(2,1)S(1)}, bf16[3,256,256]{2,1,0:T(8,128)(2,1)}, u32[]{:S(2)}) copy-start(bf16[3,256,256]{2,1,0:T(8,128)(2,1)} %get-tuple-element.16.more) | copy-start | bytes 1179652
  21.0 2.2 %copy-start = (bf16[2,256,1024]{2,1,0:T(8,128)(2,1)S(1)}, bf16[2,256,1024]{2,1,0:T(8,128)(2,1)}, u32[]{:S(2)}) copy-start(bf16[2,256,1024]{2,1,0:T(8,128)(2,1)} %get-tuple-element.15.stock) | copy-start | bytes 3145732
  25.4 7.5 %collective-permute-start.4 = (bf16[3,64,256]{2,1,0:T(8,128)(2,1)S(1)}, bf16[3,64,256]{2,1,0:T(8,128)(2,1)S(1)}, u32[]{:S(2)}, u32[]{:S(2)}) collective-permute-start(bf16[3,64,256]{2,1,0:T(8,128)(2,1)S(1)} %get-tuple-element.25), channel_id=1, source_target_pairs={{0,1},{1,2},{2,3},{3,0},{4,5},{5,6},{6,7},{7,4},{8,9},{9,10},{10,1... | collective-permute-start | bytes 294920 | tf_op jit(solution)/shard_map/ppermute | solution.py:255
  27.0 10.1 %collective-permute-start.5 = (bf16[3,64,256]{2,1,0:T(8,128)(2,1)S(1)}, bf16[3,64,256]{2,1,0:T(8,128)(2,1)S(1)}, u32[]{:S(2)}, u32[]{:S(2)}) collective-permute-start(bf16[3,64,256]{2,1,0:T(8,128)(2,1)S(1)} %get-tuple-element.26), channel_id=1, source_target_pairs={{0,2},{1,3},{2,0},{3,1},{4,6},{5,7},{6,4},{7,5},{8,10},{9,11},{10,... | collective-permute-start | bytes 294920 | tf_op jit(solution)/shard_map/ppermute | solution.py:255
  29.6 7.5 %collective-permute-start.6 = (bf16[3,64,256]{2,1,0:T(8,128)(2,1)S(1)}, bf16[3,64,256]{2,1,0:T(8,128)(2,1)S(1)}, u32[]{:S(2)}, u32[]{:S(2)}) collective-permute-start(bf16[3,64,256]{2,1,0:T(8,128)(2,1)S(1)} %get-tuple-element.27), channel_id=1, source_target_pairs={{0,3},{1,0},{2,1},{3,2},{4,7},{5,4},{6,5},{7,6},{8,11},{9,8},{10,9... | collective-permute-start | bytes 294920 | tf_op jit(solution)/shard_map/ppermute | solution.py:255
  37.2 7.6 %collective-permute-start.7 = (bf16[3,64,256]{2,1,0:T(8,128)(2,1)S(1)}, bf16[3,64,256]{2,1,0:T(8,128)(2,1)S(1)}, u32[]{:S(2)}, u32[]{:S(2)}) collective-permute-start(bf16[3,64,256]{2,1,0:T(8,128)(2,1)S(1)} %total.1.refs_0_), channel_id=1, source_target_pairs={{0,1},{1,2},{2,3},{3,0},{4,5},{5,6},{6,7},{7,4},{8,9},{9,10},{10,1... | collective-permute-start | bytes 294920 | tf_op jit(solution)/shard_map/ppermute | solution.py:255
  39.9 8.4 %collective-permute-start.8 = (bf16[3,64,256]{2,1,0:T(8,128)(2,1)S(1)}, bf16[3,64,256]{2,1,0:T(8,128)(2,1)S(1)}, u32[]{:S(2)}, u32[]{:S(2)}) collective-permute-start(bf16[3,64,256]{2,1,0:T(8,128)(2,1)S(1)} %total.1.refs_0_), channel_id=1, source_target_pairs={{0,2},{1,3},{2,0},{3,1},{4,6},{5,7},{6,4},{7,5},{8,10},{9,11},{10,... | collective-permute-start | bytes 294920 | tf_op jit(solution)/shard_map/ppermute | solution.py:255
  41.4 6.9 %collective-permute-start.9 = (bf16[3,64,256]{2,1,0:T(8,128)(2,1)S(1)}, bf16[3,64,256]{2,1,0:T(8,128)(2,1)S(1)}, u32[]{:S(2)}, u32[]{:S(2)}) collective-permute-start(bf16[3,64,256]{2,1,0:T(8,128)(2,1)S(1)} %total.1.refs_0_), channel_id=1, source_target_pairs={{0,3},{1,0},{2,1},{3,2},{4,7},{5,4},{6,5},{7,6},{8,11},{9,8},{10,9... | collective-permute-start | bytes 294920 | tf_op jit(solution)/shard_map/ppermute | solution.py:255

commit v13 on v12

--- a/solution.py
+++ b/solution.py
@@ -105,9 +105,14 @@
     return coarse
 
 
+def other_sources():
+    odd = lax.rem(lax.axis_index("row"), 2)
+    return 2, 3 + odd, 1, 4 - odd
+
+
 def own_kernel(
     slots, size, rows_at, cols_at, count_at, codes_at, p_count_at, aggs_at, fine_at, own_at,
-    col_at, row_at, more_at, c_one,
+    early_at, late_at, more_at, c_one,
     fine, own, stock, more, turned, acc, dense, tile, rows, cols, count, codes, p_count, aggs, table, sems,
 ):
     pairs = [
@@ -143,11 +148,11 @@
 
     lax.fori_loop(0, (count[0, 0] + UNROLL - 1) // UNROLL, step, 0)
     stores = []
-    for s in range(1, NS):
+    for n, s in enumerate(other_sources()):
         for m in range(FB):
-            stock[s - 1, :, m * size : (m + 1) * size] = acc[s * FB + m].astype(BF16)
-        stock_at, n = (col_at, s - 1) if s < 3 else (row_at, s - 3)
-        stores.append(pltpu.make_async_copy(stock.at[s - 1], stock_at.at[n], sems.at[1 + s]))
+            stock[n, :, m * size : (m + 1) * size] = acc[s * FB + m].astype(BF16)
+        to = early_at.at[n] if n < 2 else late_at.at[n - 2]
+        stores.append(pltpu.make_async_copy(stock.at[n], to, sems.at[2 + n]))
         stores[-1].start()
     own_weight = jnp.concatenate([acc[m].astype(BF16) for m in range(FB)], axis=1)
     dense_of(0, size, table, own, dense)
@@ -166,7 +171,7 @@
 
 
 def near_coarse(
-    base, sources, near, slots, size, stock, c_one, dense, tiles, words, codes, sems
+    sources, near, slots, size, stock, c_one, dense, tiles, words, codes, sems
 ):
     tail = (slots + CB) * size
     for n, ref in enumerate(near):
@@ -178,7 +183,7 @@
     parts, stores = [], []
     for n, (s, ref) in enumerate(zip(sources, near)):
         dense_of(n, size, codes, ref, dense.at[n])
-        coarse = coarse_of(size, stock[s - base], dense.at[n], tiles.at[n])
+        coarse = coarse_of(size, stock[n], dense.at[n], tiles.at[n])
         store = pltpu.make_async_copy(tiles.at[n], c_one.at[:, s], sems.at[1 + n])
         store.start()
         stores.append(store)
@@ -192,22 +197,24 @@
     half[...] = jnp.dot(more[1], more[2], preferred_element_type=F32)
 
 
-def side_kernel(slots, size, stock, lift_t, half, right, left, c_in, c_one, term, *scratch):
-    parts, stores = near_coarse(1, (2, 1), (right, left), slots, size, stock, c_one, *scratch)
-    whole = (half[...] + parts[0] + parts[1]).astype(BF16)
-    term[...] = jnp.dot(lift_t[...], whole, preferred_element_type=F32)
+def early_kernel(
+    slots, size, stock, lift_t, half, right, other, c_in, c_one, part, term, *scratch
+):
+    sources = other_sources()[:2]
+    parts, stores = near_coarse(sources, (right, other), slots, size, stock, c_one, *scratch)
+    part[...] = half[...] + parts[0]
+    term[...] = jnp.dot(lift_t[...], parts[1].astype(BF16), preferred_element_type=F32)
     for store in stores:
         store.wait()
 
 
-def row_kernel(slots, size, cols_n, stock, lift_t, term, other, pair, c_in, c_one, *rest):
+def late_kernel(slots, size, cols_n, stock, lift_t, part, term, left, pair, c_in, c_one, *rest):
     sends, terms, scratch = rest[:cols_n], rest[cols_n], rest[cols_n + 1 :]
-    odd = lax.rem(lax.axis_index("row"), 2)
-    sources = (3 + odd, 4 - odd)
-    parts, stores = near_coarse(3, sources, (other, pair), slots, size, stock, c_one, *scratch)
-    terms[0] = term[...]
-    for n in range(2):
-        terms[sources[n] - 2] = jnp.dot(lift_t[...], parts[n].astype(BF16), preferred_element_type=F32)
+    sources = other_sources()
+    terms[sources[1] - 2] = term[...]
+    parts, stores = near_coarse(sources[2:], (left, pair), slots, size, stock, c_one, *scratch)
+    for g, half in ((0, part[...] + parts[0]), (sources[3] - 2, parts[1])):
+        terms[g] = jnp.dot(lift_t[...], half.astype(BF16), preferred_element_type=F32)
     chunk = terms.shape[1] // cols_n
     me = lax.axis_index("col")
     for d in range(cols_n):
@@ -300,7 +307,7 @@
     integers = (
         fine_rows, fine_cols, fine_counts, prolong_codes, prolong_counts, second_aggs
     )
-    col_stock, row_stock, more, c_one = pl.pallas_call(
+    early_stock, late_stock, more, c_one = pl.pallas_call(
         functools.partial(own_kernel, slots, size),
         out_shape=[
             jax.ShapeDtypeStruct((2, wide, FB * size), BF16),
@@ -347,30 +354,30 @@
         cost_estimate=pl.CostEstimate(flops=10**9, bytes_accessed=4 * 10**6, transcendentals=0),
         name="own_half",
     )(more)
-    c_one, term = pl.pallas_call(
-        functools.partial(side_kernel, slots, size),
-        out_shape=[c_shape, square],
+    c_one, part, term = pl.pallas_call(
+        functools.partial(early_kernel, slots, size),
+        out_shape=[c_shape, square, square],
         in_specs=[VMEM] * 5 + [HBM],
-        out_specs=[HBM, VMEM],
+        out_specs=[HBM, VMEM, VMEM],
         input_output_aliases={5: 0},
         scratch_shapes=near_scratch,
         compiler_params=LARGE,
-        name="col_sources",
-    )(col_stock, lift_t, half, right, left, c_one)
+        name="early_sources",
+    )(early_stock, lift_t, half, right, other, c_one)
 
     chunk = G2 * size // cols_n
     kept = jax.ShapeDtypeStruct((3, chunk, G2 * size), F32)
     piece = jax.ShapeDtypeStruct(kept.shape, BF16)
     c_one, *sends = pl.pallas_call(
-        functools.partial(row_kernel, slots, size, cols_n),
+        functools.partial(late_kernel, slots, size, cols_n),
         out_shape=[c_shape, kept] + [piece] * (cols_n - 1),
-        in_specs=[VMEM] * 5 + [HBM],
+        in_specs=[VMEM] * 6 + [HBM],
         out_specs=[HBM] + [VMEM] * cols_n,
-        input_output_aliases={5: 0},
+        input_output_aliases={6: 0},
         scratch_shapes=[pltpu.VMEM((3, G2 * size, G2 * size), F32)] + near_scratch,
         compiler_params=LARGE,
-        name="row_sources",
-    )(row_stock, lift_t, term, other, pair, c_one)
+        name="late_sources",
+    )(late_stock, lift_t, part, term, left, pair, c_one)
     parts = [sends[0]] + [shift(sends[d], "col", d, True) for d in range(1, cols_n)]
     total = pl.pallas_call(
         sum_kernel, out_shape=piece, in_specs=[VMEM] * cols_n, out_specs=VMEM,

time: 49.7 us -> 50 us (level)
  the two profiles are of different devices: /device:TPU:0 before, /device:TPU:13 now
where the time goes in v13:
time: 50 us; the launch traced here: 49.7 us
  waiting for transfers between devices  19 us (38%)
  starting transfers between devices  15.3 us (31%)
  Pallas kernels  12.3 us (25%)
  between operations  2.05 us (4%)
  local copies, waits for them, and re-layouts  1.08 us (2%)
    ppermute x8, waiting for transfers between devices, shift(): return lax.ppermute(x, axis, pairs)  19 us
    ppermute x8, starting transfers between devices, shift(): return lax.ppermute(x, axis, pairs)  11.2 us
    pallas_call x1, Pallas kernels, per_device(): pl.pallas_call(functools.partial(own_kernel, slots, size), out_shape=[jax...  5.08 us
    ppermute x2, starting transfers between devices, swap(): return lax.ppermute(x, axis, pairs + [(j, i) for i, j in pairs])  4.03 us
    pallas_call x1, Pallas kernels, per_device(): pl.pallas_call(functools.partial(late_kernel, slots, size, cols_n), out_s...  2.14 us
    pallas_call x1, Pallas kernels, per_device(): pl.pallas_call(functools.partial(early_kernel, slots, size), out_shape=[c...  2.12 us
    pallas_call x1, Pallas kernels, per_device(): pl.pallas_call(pack_kernel, out_shape=jax.ShapeDtypeStruct((packed_rows,...  1.81 us
    unnamed x6, local copies, waits for them, and re-layouts  1.08 us
  transfers between devices with their start and end apart: 10, of which 8 were waited for; matrix products, arithmetic and copies ran while one was open for 0% of the time, Pallas kernels for 15%

profile of v13, /device:TPU:13, one launch (start us, length us, event | category | flops | bytes accessed | tf_op | source)
XLA Modules:
  0.0 49.7 jit_solution(16999156998992694661)
XLA Ops:
  1.3 1.8 %pack.1.own_at = bf16[1808,128]{1,0:T(8,128)(2,1)} custom-call(s32[1,1,12]{2,1,0:T(1,128)} %codes_at.3, s32[1,1]{1,0:T(1,128)S(6)} %copy.16.count_at.p_count_at, s32[1,1,2]{2,1,0:T(1,128)} %aggs_at.3, bf16[1536,128]{1,0:T(8,128)(2,1)} %bitcast.7, bf16[256,128]{1,0:T(8,128)(2,1)} %bitcast.8), custom_call_target="tpu_custom_call" | custom-call | tf_op jit(solution)/shard_map/pack/pallas_call | solution.py:279
  3.1 2.1 %collective-permute-start = (bf16[1808,128]{1,0:T(8,128)(2,1)}, bf16[1808,128]{1,0:T(8,128)(2,1)S(1)}, u32[]{:S(2)}, u32[]{:S(2)}) collective-permute-start(bf16[1808,128]{1,0:T(8,128)(2,1)} %pack.1.own_at), channel_id=1, source_target_pairs={{1,0},{2,1},{3,2},{5,4},{6,5},{7,6},{9,8},{10,9},{11,10},{13,12},{... | collective-permute-start | bytes 1388552 | tf_op jit(solution)/shard_map/ppermute | solution.py:262
  5.2 4.0 %collective-permute-start.1 = (bf16[1808,128]{1,0:T(8,128)(2,1)}, bf16[1808,128]{1,0:T(8,128)(2,1)S(1)}, u32[]{:S(2)}, u32[]{:S(2)}) collective-permute-start(bf16[1808,128]{1,0:T(8,128)(2,1)} %pack.1.own_at), channel_id=1, source_target_pairs={{4,8},{12,16},{20,24},{8,4},{16,12},{24,20},{5,9},{13,17},{21,25},... | collective-permute-start | bytes 1388552 | tf_op jit(solution)/shard_map/ppermute | solution.py:266
  9.1 3.2 %collective-permute-start.2 = (bf16[1808,128]{1,0:T(8,128)(2,1)}, bf16[1808,128]{1,0:T(8,128)(2,1)S(1)}, u32[]{:S(2)}, u32[]{:S(2)}) collective-permute-start(bf16[1808,128]{1,0:T(8,128)(2,1)} %pack.1.own_at), channel_id=1, source_target_pairs={{0,1},{1,2},{2,3},{4,5},{5,6},{6,7},{8,9},{9,10},{10,11},{12,13},{... | collective-permute-start | bytes 1388552 | tf_op jit(solution)/shard_map/ppermute | solution.py:262
  12.4 0.1 collective-permute-start.3
  13.1 5.1 %own_source.1 = (bf16[2,256,1024]{2,1,0:T(8,128)(2,1)}, bf16[2,256,1024]{2,1,0:T(8,128)(2,1)}, bf16[3,256,256]{2,1,0:T(8,128)(2,1)}, bf16[2,5,2,128,128]{4,3,2,1,0:T(8,128)(2,1)}) custom-call(s32[1,1,64]{2,1,0:T(1,128)} %rows_at.1, s32[1,1,64]{2,1,0:T(1,128)} %cols_at.1, s32[1,1]{1,0:T(1,128)S(6)} %copy.15.count_at, s32[1,1,12]{2,1,0:T(1,128)} %codes_at.3, ...), custom_call_target="tpu_custom_call" | custom-call | flops 1000000000 | bytes 4000000 | tf_op jit(solution)/shard_map/own_source/pallas_call | solution.py:310
  18.2 0.0 copy-start.1
  18.2 0.0 copy-start.2
  18.2 1.1 %copy-done.2 = bf16[3,256,256]{2,1,0:T(8,128)(2,1)S(1)} copy-done((bf16[3,256,256]{2,1,0:T(8,128)(2,1)S(1)}, bf16[3,256,256]{2,1,0:T(8,128)(2,1)}, u32[]{:S(2)}) %copy-start.2) | copy-done | bytes 393240
  19.3 0.2 own_half.1
  19.5 0.0 copy-start
  19.5 0.0 collective-permute-done.right
  19.5 0.1 collective-permute-done.1.other
  19.5 0.0 copy-done.1
  19.5 2.1 %early_sources.1 = (bf16[2,5,2,128,128]{4,3,2,1,0:T(8,128)(2,1)}, f32[256,256]{1,0:T(8,128)S(1)}, f32[256,256]{1,0:T(8,128)S(1)}) custom-call(bf16[2,256,1024]{2,1,0:T(8,128)(2,1)S(1)} %copy-done.1, bf16[256,256]{1,0:T(8,128)(2,1)S(1)} %get-tuple-element.18.lift_t, f32[256,256]{1,0:T(8,128)S(1)} %get-tuple-element.20.half, ...), custom_call_target="tpu_custom_call", output_to_operand_aliasing={{0}: (5, {})} | custom-call | tf_op jit(solution)/shard_map/early_sources/pallas_call | solution.py:357
  21.7 2.1 %collective-permute-done.2.left = bf16[1808,128]{1,0:T(8,128)(2,1)S(1)} collective-permute-done((bf16[1808,128]{1,0:T(8,128)(2,1)}, bf16[1808,128]{1,0:T(8,128)(2,1)S(1)}, u32[]{:S(2)}, u32[]{:S(2)}) %collective-permute-start.2) | collective-permute-done | bytes 462880 | tf_op jit(solution)/shard_map/ppermute | solution.py:262
  23.8 0.0 collective-permute-done.3.pair
  23.8 0.0 copy-done
  23.8 2.1 %late_sources.1 = (bf16[2,5,2,128,128]{4,3,2,1,0:T(8,128)(2,1)}, f32[3,64,256]{2,1,0:T(8,128)S(1)}, bf16[3,64,256]{2,1,0:T(8,128)(2,1)S(1)}, bf16[3,64,256]{2,1,0:T(8,128)(2,1)S(1)}, bf16[3,64,256]{2,1,0:T(8,128)(2,1)S(1)}) custom-call(bf16[2,256,1024]{2,1,0:T(8,128)(2,1)S(1)} %copy-done, ...), custom_call_target="tpu_custom_call", output_to_operand_aliasing={{0}: (6, {})} | custom-call | tf_op jit(solution)/shard_map/late_sources/pallas_call | solution.py:371
  25.9 1.3 %collective-permute-start.4 = (bf16[3,64,256]{2,1,0:T(8,128)(2,1)S(1)}, bf16[3,64,256]{2,1,0:T(8,128)(2,1)S(1)}, u32[]{:S(2)}, u32[]{:S(2)}) collective-permute-start(bf16[3,64,256]{2,1,0:T(8,128)(2,1)S(1)} %get-tuple-element.27), channel_id=1, source_target_pairs={{0,1},{1,2},{2,3},{3,0},{4,5},{5,6},{6,7},{7,4},{8,9},{9,10},{10,1... | collective-permute-start | bytes 294920 | tf_op jit(solution)/shard_map/ppermute | solution.py:262
  27.3 1.1 %collective-permute-start.5 = (bf16[3,64,256]{2,1,0:T(8,128)(2,1)S(1)}, bf16[3,64,256]{2,1,0:T(8,128)(2,1)S(1)}, u32[]{:S(2)}, u32[]{:S(2)}) collective-permute-start(bf16[3,64,256]{2,1,0:T(8,128)(2,1)S(1)} %get-tuple-element.28), channel_id=1, source_target_pairs={{0,2},{1,3},{2,0},{3,1},{4,6},{5,7},{6,4},{7,5},{8,10},{9,11},{10,... | collective-permute-start | bytes 294920 | tf_op jit(solution)/shard_map/ppermute | solution.py:262
  28.4 1.4 %collective-permute-start.6 = (bf16[3,64,256]{2,1,0:T(8,128)(2,1)S(1)}, bf16[3,64,256]{2,1,0:T(8,128)(2,1)S(1)}, u32[]{:S(2)}, u32[]{:S(2)}) collective-permute-start(bf16[3,64,256]{2,1,0:T(8,128)(2,1)S(1)} %get-tuple-element.29), channel_id=1, source_target_pairs={{0,3},{1,0},{2,1},{3,2},{4,7},{5,4},{6,5},{7,6},{8,11},{9,8},{10,9... | collective-permute-start | bytes 294920 | tf_op jit(solution)/shard_map/ppermute | solution.py:262
  29.8 0.2 collective-permute-done.4.refs_1_
  30.0 5.4 %collective-permute-done.5.refs_2_ = bf16[3,64,256]{2,1,0:T(8,128)(2,1)S(1)} collective-permute-done((bf16[3,64,256]{2,1,0:T(8,128)(2,1)S(1)}, bf16[3,64,256]{2,1,0:T(8,128)(2,1)S(1)}, u32[]{:S(2)}, u32[]{:S(2)}) %collective-permute-start.5) | collective-permute-done | bytes 98336 | tf_op jit(solution)/shard_map/ppermute | solution.py:262
  35.4 2.5 %collective-permute-done.6.refs_3_ = bf16[3,64,256]{2,1,0:T(8,128)(2,1)S(1)} collective-permute-done((bf16[3,64,256]{2,1,0:T(8,128)(2,1)S(1)}, bf16[3,64,256]{2,1,0:T(8,128)(2,1)S(1)}, u32[]{:S(2)}, u32[]{:S(2)}) %collective-permute-start.6) | collective-permute-done | bytes 98336 | tf_op jit(solution)/shard_map/ppermute | solution.py:262
  38.0 0.1 collective-permute-start.7
  38.0 1.1 %collective-permute-start.8 = (bf16[3,64,256]{2,1,0:T(8,128)(2,1)S(1)}, bf16[3,64,256]{2,1,0:T(8,128)(2,1)S(1)}, u32[]{:S(2)}, u32[]{:S(2)}) collective-permute-start(bf16[3,64,256]{2,1,0:T(8,128)(2,1)S(1)} %total.1.refs_0_), channel_id=1, source_target_pairs={{0,2},{1,3},{2,0},{3,1},{4,6},{5,7},{6,4},{7,5},{8,10},{9,11},{10,... | collective-permute-start | bytes 294920 | tf_op jit(solution)/shard_map/ppermute | solution.py:262
  39.2 0.9 %collective-permute-start.9 = (bf16[3,64,256]{2,1,0:T(8,128)(2,1)S(1)}, bf16[3,64,256]{2,1,0:T(8,128)(2,1)S(1)}, u32[]{:S(2)}, u32[]{:S(2)}) collective-permute-start(bf16[3,64,256]{2,1,0:T(8,128)(2,1)S(1)} %total.1.refs_0_), channel_id=1, source_target_pairs={{0,3},{1,0},{2,1},{3,2},{4,7},{5,4},{6,5},{7,6},{8,11},{9,8},{10,9... | collective-permute-start | bytes 294920 | tf_op jit(solution)/shard_map/ppermute | solution.py:262
  40.1 1.8 %collective-permute-done.7.refs_1_ = bf16[3,64,256]{2,1,0:T(8,128)(2,1)S(1)} collective-permute-done((bf16[3,64,256]{2,1,0:T(8,128)(2,1)S(1)}, bf16[3,64,256]{2,1,0:T(8,128)(2,1)S(1)}, u32[]{:S(2)}, u32[]{:S(2)}) %collective-permute-start.7) | collective-permute-done | bytes 98336 | tf_op jit(solution)/shard_map/ppermute | solution.py:262
  41.9 2.0 %collective-permute-done.8.refs_2_ = bf16[3,64,256]{2,1,0:T(8,128)(2,1)S(1)} collective-permute-done((bf16[3,64,256]{2,1,0:T(8,128)(2,1)S(1)}, bf16[3,64,256]{2,1,0:T(8,128)(2,1)S(1)}, u32[]{:S(2)}, u32[]{:S(2)}) %collective-permute-start.8) | collective-permute-done | bytes 98336 | tf_op jit(solution)/shard_map/ppermute | solution.py:262
  43.8 4.9 %collective-permute-done.9.refs_3_ = bf16[3,64,256]{2,1,0:T(8,128)(2,1)S(1)} collective-permute-done((bf16[3,64,256]{2,1,0:T(8,128)(2,1)S(1)}, bf16[3,64,256]{2,1,0:T(8,128)(2,1)S(1)}, u32[]{:S(2)}, u32[]{:S(2)}) %collective-permute-start.9) | collective-permute-done | bytes 98336 | tf_op jit(solution)/shard_map/ppermute | solution.py:262
  48.8 0.9 %spread.1 = f32[2,3,2,128,128]{4,3,2,1,0:T(8,128)} custom-call(bf16[3,64,256]{2,1,0:T(8,128)(2,1)S(1)} %total.1.refs_0_, bf16[3,64,256]{2,1,0:T(8,128)(2,1)S(1)} %collective-permute-done.7.refs_1_, bf16[3,64,256]{2,1,0:T(8,128)(2,1)S(1)} %collective-permute-done.8.refs_2_, bf16[3,64,256]{2,1,0:T(8,128)(2,1)S(1)} %collective-permute-done.9.refs_3_), custom_call_target="tpu_custom_call" | custom-call | tf_op jit(solution)/shard_map/spread/pallas_call | solution.py:387
  (1 shorter events, 0.0 us)
Async XLA Ops:
  3.1 16.4 %collective-permute-start = (bf16[1808,128]{1,0:T(8,128)(2,1)}, bf16[1808,128]{1,0:T(8,128)(2,1)S(1)}, u32[]{:S(2)}, u32[]{:S(2)}) collective-permute-start(bf16[1808,128]{1,0:T(8,128)(2,1)} %pack.1.own_at), channel_id=1, source_target_pairs={{1,0},{2,1},{3,2},{5,4},{6,5},{7,6},{9,8},{10,9},{11,10},{13,12},{... | collective-permute-start | bytes 1388552 | tf_op jit(solution)/shard_map/ppermute | solution.py:262
  5.2 14.4 %collective-permute-start.1 = (bf16[1808,128]{1,0:T(8,128)(2,1)}, bf16[1808,128]{1,0:T(8,128)(2,1)S(1)}, u32[]{:S(2)}, u32[]{:S(2)}) collective-permute-start(bf16[1808,128]{1,0:T(8,128)(2,1)} %pack.1.own_at), channel_id=1, source_target_pairs={{4,8},{12,16},{20,24},{8,4},{16,12},{24,20},{5,9},{13,17},{21,25},... | collective-permute-start | bytes 1388552 | tf_op jit(solution)/shard_map/ppermute | solution.py:266
  9.1 14.6 %collective-permute-start.2 = (bf16[1808,128]{1,0:T(8,128)(2,1)}, bf16[1808,128]{1,0:T(8,128)(2,1)S(1)}, u32[]{:S(2)}, u32[]{:S(2)}) collective-permute-start(bf16[1808,128]{1,0:T(8,128)(2,1)} %pack.1.own_at), channel_id=1, source_target_pairs={{0,1},{1,2},{2,3},{4,5},{5,6},{6,7},{8,9},{9,10},{10,11},{12,13},{... | collective-permute-start | bytes 1388552 | tf_op jit(solution)/shard_map/ppermute | solution.py:262
  12.4 11.4 %collective-permute-start.3 = (bf16[1808,128]{1,0:T(8,128)(2,1)}, bf16[1808,128]{1,0:T(8,128)(2,1)S(1)}, u32[]{:S(2)}, u32[]{:S(2)}) collective-permute-start(bf16[1808,128]{1,0:T(8,128)(2,1)} %pack.1.own_at), channel_id=1, source_target_pairs={{0,4},{8,12},{16,20},{24,28},{4,0},{12,8},{20,16},{28,24},{1,5},{9... | collective-permute-start | bytes 1388552 | tf_op jit(solution)/shard_map/ppermute | solution.py:266
  18.2 1.4 %copy-start.1 = (bf16[2,256,1024]{2,1,0:T(8,128)(2,1)S(1)}, bf16[2,256,1024]{2,1,0:T(8,128)(2,1)}, u32[]{:S(2)}) copy-start(bf16[2,256,1024]{2,1,0:T(8,128)(2,1)} %get-tuple-element.19.stock) | copy-start | bytes 3145732
  18.2 1.1 %copy-start.2 = (bf16[3,256,256]{2,1,0:T(8,128)(2,1)S(1)}, bf16[3,256,256]{2,1,0:T(8,128)(2,1)}, u32[]{:S(2)}) copy-start(bf16[3,256,256]{2,1,0:T(8,128)(2,1)} %get-tuple-element.17.more) | copy-start | bytes 1179652
  19.5 4.3 %copy-start = (bf16[2,256,1024]{2,1,0:T(8,128)(2,1)S(1)}, bf16[2,256,1024]{2,1,0:T(8,128)(2,1)}, u32[]{:S(2)}) copy-start(bf16[2,256,1024]{2,1,0:T(8,128)(2,1)} %get-tuple-element.16.stock) | copy-start | bytes 3145732
  25.9 4.0 %collective-permute-start.4 = (bf16[3,64,256]{2,1,0:T(8,128)(2,1)S(1)}, bf16[3,64,256]{2,1,0:T(8,128)(2,1)S(1)}, u32[]{:S(2)}, u32[]{:S(2)}) collective-permute-start(bf16[3,64,256]{2,1,0:T(8,128)(2,1)S(1)} %get-tuple-element.27), channel_id=1, source_target_pairs={{0,1},{1,2},{2,3},{3,0},{4,5},{5,6},{6,7},{7,4},{8,9},{9,10},{10,1... | collective-permute-start | bytes 294920 | tf_op jit(solution)/shard_map/ppermute | solution.py:262
  27.3 8.1 %collective-permute-start.5 = (bf16[3,64,256]{2,1,0:T(8,128)(2,1)S(1)}, bf16[3,64,256]{2,1,0:T(8,128)(2,1)S(1)}, u32[]{:S(2)}, u32[]{:S(2)}) collective-permute-start(bf16[3,64,256]{2,1,0:T(8,128)(2,1)S(1)} %get-tuple-element.28), channel_id=1, source_target_pairs={{0,2},{1,3},{2,0},{3,1},{4,6},{5,7},{6,4},{7,5},{8,10},{9,11},{10,... | collective-permute-start | bytes 294920 | tf_op jit(solution)/shard_map/ppermute | solution.py:262
  28.4 9.5 %collective-permute-start.6 = (bf16[3,64,256]{2,1,0:T(8,128)(2,1)S(1)}, bf16[3,64,256]{2,1,0:T(8,128)(2,1)S(1)}, u32[]{:S(2)}, u32[]{:S(2)}) collective-permute-start(bf16[3,64,256]{2,1,0:T(8,128)(2,1)S(1)} %get-tuple-element.29), channel_id=1, source_target_pairs={{0,3},{1,0},{2,1},{3,2},{4,7},{5,4},{6,5},{7,6},{8,11},{9,8},{10,9... | collective-permute-start | bytes 294920 | tf_op jit(solution)/shard_map/ppermute | solution.py:262
  38.0 3.9 %collective-permute-start.7 = (bf16[3,64,256]{2,1,0:T(8,128)(2,1)S(1)}, bf16[3,64,256]{2,1,0:T(8,128)(2,1)S(1)}, u32[]{:S(2)}, u32[]{:S(2)}) collective-permute-start(bf16[3,64,256]{2,1,0:T(8,128)(2,1)S(1)} %total.1.refs_0_), channel_id=1, source_target_pairs={{0,1},{1,2},{2,3},{3,0},{4,5},{5,6},{6,7},{7,4},{8,9},{9,10},{10,1... | collective-permute-start | bytes 294920 | tf_op jit(solution)/shard_map/ppermute | solution.py:262
  38.0 5.8 %collective-permute-start.8 = (bf16[3,64,256]{2,1,0:T(8,128)(2,1)S(1)}, bf16[3,64,256]{2,1,0:T(8,128)(2,1)S(1)}, u32[]{:S(2)}, u32[]{:S(2)}) collective-permute-start(bf16[3,64,256]{2,1,0:T(8,128)(2,1)S(1)} %total.1.refs_0_), channel_id=1, source_target_pairs={{0,2},{1,3},{2,0},{3,1},{4,6},{5,7},{6,4},{7,5},{8,10},{9,11},{10,... | collective-permute-start | bytes 294920 | tf_op jit(solution)/shard_map/ppermute | solution.py:262
  39.2 9.6 %collective-permute-start.9 = (bf16[3,64,256]{2,1,0:T(8,128)(2,1)S(1)}, bf16[3,64,256]{2,1,0:T(8,128)(2,1)S(1)}, u32[]{:S(2)}, u32[]{:S(2)}) collective-permute-start(bf16[3,64,256]{2,1,0:T(8,128)(2,1)S(1)} %total.1.refs_0_), channel_id=1, source_target_pairs={{0,3},{1,0},{2,1},{3,2},{4,7},{5,4},{6,5},{7,6},{8,11},{9,8},{10,9... | collective-permute-start | bytes 294920 | tf_op jit(solution)/shard_map/ppermute | solution.py:262

commit v14 on v11

--- a/solution.py
+++ b/solution.py
@@ -227,14 +227,14 @@
     refs[-1][...] = total.astype(BF16)
 
 
-def spread_kernel(size, cols_n, *refs):
-    parts, out_at, out, sems = refs[:cols_n], refs[cols_n], refs[cols_n + 1], refs[cols_n + 2]
+def spread_kernel(size, cols_n, steps, *refs):
+    parts, (out_at, out, sems) = refs[: len(steps)], refs[-3:]
     chunk = parts[0].shape[1]
     unit = math.gcd(chunk, size)
     per = size // unit
     me = lax.axis_index("col")
     stores = []
-    for d in range(cols_n):
+    for n, d in enumerate(steps):
         owner = lax.rem(me - d + cols_n, cols_n)
         for t in range(chunk // unit):
             at = owner * (chunk // unit) + t
@@ -242,7 +242,7 @@
             rows = pl.ds(pl.multiple_of(lax.rem(at, per) * unit, unit), unit)
             for g in range(3):
                 for b in range(G2):
-                    out[a, g, b, rows, :] = parts[d][
+                    out[a, g, b, rows, :] = parts[n][
                         g, t * unit : (t + 1) * unit, b * size : (b + 1) * size
                     ].astype(F32)
             spot = (a, slice(None), slice(None), rows)
@@ -380,18 +380,25 @@
         compiler_params=SMALL, name="total",
     )(*parts)
     gathered = [total] + [shift(total, "col", d, True) for d in range(1, cols_n)]
-    c_two = pl.pallas_call(
-        functools.partial(spread_kernel, size, cols_n),
-        out_shape=jax.ShapeDtypeStruct((G2, 3, G2, size, size), F32),
-        in_specs=[VMEM] * cols_n,
-        out_specs=HBM,
-        scratch_shapes=[
-            pltpu.VMEM((G2, 3, G2, size, size), F32),
-            dma((G2 * size // math.gcd(chunk, size),)),
-        ],
-        compiler_params=SMALL,
-        name="spread",
-    )(*gathered)
+    c_two = None
+    cut = max(1, cols_n - 1)
+    for steps in (list(range(cut)), list(range(cut, cols_n))):
+        if not steps:
+            continue
+        before = [] if c_two is None else [c_two]
+        c_two = pl.pallas_call(
+            functools.partial(spread_kernel, size, cols_n, steps),
+            out_shape=jax.ShapeDtypeStruct((G2, 3, G2, size, size), F32),
+            in_specs=[VMEM] * len(steps) + [HBM] * len(before),
+            out_specs=HBM,
+            input_output_aliases={len(steps): 0} if before else {},
+            scratch_shapes=[
+                pltpu.VMEM((G2, 3, G2, size, size), F32),
+                dma((len(steps) * (chunk // math.gcd(chunk, size)),)),
+            ],
+            compiler_params=SMALL,
+            name="spread",
+        )(*[gathered[d] for d in steps], *before)
     return (c_one[None, None], c_two[None])
 
 

time: 49.7 us -> 50.4 us (1.014)
  Pallas kernels: 12.6 us -> 14.5 us
  starting transfers between devices: 21.3 us -> 20.4 us
    pallas_call x1, Pallas kernels: 5.37 us -> 6.57 us  [per_device(): pl.pallas_call(functools.partial(own_kernel, slots, size), out_shape=[jax...]
    ppermute x8, starting transfers between devices: 17.3 us -> 16.4 us  [shift(): return lax.ppermute(x, axis, pairs)]
    pallas_call x1 -> x2, Pallas kernels: 0.93 us -> 1.57 us  [per_device(): pl.pallas_call(functools.partial(spread_kernel, size, cols_n, steps), out...]
  transfers between devices with their start and end apart: 10 -> 10, of which waited for: 4 -> 4; matrix products, arithmetic and copies ran while one was open for 0% -> 0% of each run, Pallas kernels for 16% -> 19%
where the time goes in v14:
time: 50.4 us; the launch traced here: 50.1 us
  starting transfers between devices  20.4 us (40%)
  Pallas kernels  14.5 us (29%)
  waiting for transfers between devices  12.1 us (24%)
  between operations  2.08 us (4%)
  local copies, waits for them, and re-layouts  1.1 us (2%)
    ppermute x8, starting transfers between devices, shift(): return lax.ppermute(x, axis, pairs)  16.4 us
    ppermute x8, waiting for transfers between devices, shift(): return lax.ppermute(x, axis, pairs)  12.1 us
    pallas_call x1, Pallas kernels, per_device(): pl.pallas_call(functools.partial(own_kernel, slots, size), out_shape=[jax...  6.57 us
    ppermute x2, starting transfers between devices, swap(): return lax.ppermute(x, axis, pairs + [(j, i) for i, j in pairs])  4.02 us
    pallas_call x1, Pallas kernels, per_device(): pl.pallas_call(functools.partial(row_kernel, slots, size, cols_n), out_sh...  2.15 us
    pallas_call x1, Pallas kernels, per_device(): pl.pallas_call(functools.partial(side_kernel, slots, size), out_shape=[c_...  2.14 us
    pallas_call x1, Pallas kernels, per_device(): pl.pallas_call(pack_kernel, out_shape=jax.ShapeDtypeStruct((packed_rows,...  1.81 us
    pallas_call x2, Pallas kernels, per_device(): pl.pallas_call(functools.partial(spread_kernel, size, cols_n, steps), out...  1.57 us
  transfers between devices with their start and end apart: 10, of which 4 were waited for; matrix products, arithmetic and copies ran while one was open for 0% of the time, Pallas kernels for 19%

profile of v14, /device:TPU:0, one launch (start us, length us, event | category | flops | bytes accessed | tf_op | source)
XLA Modules:
  0.0 50.1 jit_solution(17076047703242487680)
XLA Ops:
  1.3 1.8 %pack.1.own_at = bf16[1808,128]{1,0:T(8,128)(2,1)} custom-call(s32[1,1,12]{2,1,0:T(1,128)} %codes_at.3, s32[1,1]{1,0:T(1,128)S(6)} %copy.18.count_at.p_count_at, s32[1,1,2]{2,1,0:T(1,128)} %aggs_at.3, bf16[1536,128]{1,0:T(8,128)(2,1)} %bitcast.7, bf16[256,128]{1,0:T(8,128)(2,1)} %bitcast.8), custom_call_target="tpu_custom_call" | custom-call | tf_op jit(solution)/shard_map/pack/pallas_call | solution.py:275
  3.1 1.3 %collective-permute-start = (bf16[1808,128]{1,0:T(8,128)(2,1)}, bf16[1808,128]{1,0:T(8,128)(2,1)S(1)}, u32[]{:S(2)}, u32[]{:S(2)}) collective-permute-start(bf16[1808,128]{1,0:T(8,128)(2,1)} %pack.1.own_at), channel_id=1, source_target_pairs={{1,0},{2,1},{3,2},{5,4},{6,5},{7,6},{9,8},{10,9},{11,10},{13,12},{... | collective-permute-start | bytes 1388552 | tf_op jit(solution)/shard_map/ppermute | solution.py:258
  4.4 5.6 %collective-permute-start.1 = (bf16[1808,128]{1,0:T(8,128)(2,1)}, bf16[1808,128]{1,0:T(8,128)(2,1)S(1)}, u32[]{:S(2)}, u32[]{:S(2)}) collective-permute-start(bf16[1808,128]{1,0:T(8,128)(2,1)} %pack.1.own_at), channel_id=1, source_target_pairs={{0,1},{1,2},{2,3},{4,5},{5,6},{6,7},{8,9},{9,10},{10,11},{12,13},{... | collective-permute-start | bytes 1388552 | tf_op jit(solution)/shard_map/ppermute | solution.py:258
  10.0 0.7 %collective-permute-start.2 = (bf16[1808,128]{1,0:T(8,128)(2,1)}, bf16[1808,128]{1,0:T(8,128)(2,1)S(1)}, u32[]{:S(2)}, u32[]{:S(2)}) collective-permute-start(bf16[1808,128]{1,0:T(8,128)(2,1)} %pack.1.own_at), channel_id=1, source_target_pairs={{4,8},{12,16},{20,24},{8,4},{16,12},{24,20},{5,9},{13,17},{21,25},... | collective-permute-start | bytes 1388552 | tf_op jit(solution)/shard_map/ppermute | solution.py:262
  10.7 3.3 %collective-permute-start.3 = (bf16[1808,128]{1,0:T(8,128)(2,1)}, bf16[1808,128]{1,0:T(8,128)(2,1)S(1)}, u32[]{:S(2)}, u32[]{:S(2)}) collective-permute-start(bf16[1808,128]{1,0:T(8,128)(2,1)} %pack.1.own_at), channel_id=1, source_target_pairs={{0,4},{8,12},{16,20},{24,28},{4,0},{12,8},{20,16},{28,24},{1,5},{9... | collective-permute-start | bytes 1388552 | tf_op jit(solution)/shard_map/ppermute | solution.py:262
  14.7 6.6 %own_source.1 = (bf16[2,256,1024]{2,1,0:T(8,128)(2,1)}, bf16[2,256,1024]{2,1,0:T(8,128)(2,1)}, bf16[3,256,256]{2,1,0:T(8,128)(2,1)}, bf16[2,5,2,128,128]{4,3,2,1,0:T(8,128)(2,1)}) custom-call(s32[1,1,64]{2,1,0:T(1,128)} %rows_at.1, s32[1,1,64]{2,1,0:T(1,128)} %cols_at.1, s32[1,1]{1,0:T(1,128)S(6)} %copy.17.count_at, s32[1,1,12]{2,1,0:T(1,128)} %codes_at.3, ...), custom_call_target="tpu_custom_call" | custom-call | flops 1000000000 | bytes 4000000 | tf_op jit(solution)/shard_map/own_source/pallas_call | solution.py:306
  21.2 0.0 copy-start.1
  21.2 0.0 copy-start.2
  21.3 1.1 %copy-done.2 = bf16[3,256,256]{2,1,0:T(8,128)(2,1)S(1)} copy-done((bf16[3,256,256]{2,1,0:T(8,128)(2,1)S(1)}, bf16[3,256,256]{2,1,0:T(8,128)(2,1)}, u32[]{:S(2)}) %copy-start.2) | copy-done | bytes 393240
  22.3 0.2 own_half.1
  22.5 0.0 copy-start
  22.5 0.0 collective-permute-done.right
  22.5 0.0 collective-permute-done.1.left
  22.6 0.0 copy-done.1
  22.6 2.1 %col_sources.1 = (bf16[2,5,2,128,128]{4,3,2,1,0:T(8,128)(2,1)}, f32[256,256]{1,0:T(8,128)S(1)}) custom-call(bf16[2,256,1024]{2,1,0:T(8,128)(2,1)S(1)} %copy-done.1, bf16[256,256]{1,0:T(8,128)(2,1)S(1)} %get-tuple-element.17.lift_t, f32[256,256]{1,0:T(8,128)S(1)} %get-tuple-element.19.half, ...), custom_call_target="tpu_custom_call", output_to_operand_aliasing={{0}: (5, {})} | custom-call | tf_op jit(solution)/shard_map/col_sources/pallas_call | solution.py:353
  24.7 0.0 collective-permute-done.2.other
  24.7 0.0 collective-permute-done.3.pair
  24.7 0.0 copy-done
  24.8 2.1 %row_sources.1 = (bf16[2,5,2,128,128]{4,3,2,1,0:T(8,128)(2,1)}, f32[3,64,256]{2,1,0:T(8,128)S(1)}, bf16[3,64,256]{2,1,0:T(8,128)(2,1)S(1)}, bf16[3,64,256]{2,1,0:T(8,128)(2,1)S(1)}, bf16[3,64,256]{2,1,0:T(8,128)(2,1)S(1)}) custom-call(bf16[2,256,1024]{2,1,0:T(8,128)(2,1)S(1)} %copy-done, ...), custom_call_target="tpu_custom_call", output_to_operand_aliasing={{0}: (5, {})} | custom-call | tf_op jit(solution)/shard_map/row_sources/pallas_call | solution.py:367
  26.9 0.1 collective-permute-start.4
  27.0 2.6 %collective-permute-start.5 = (bf16[3,64,256]{2,1,0:T(8,128)(2,1)S(1)}, bf16[3,64,256]{2,1,0:T(8,128)(2,1)S(1)}, u32[]{:S(2)}, u32[]{:S(2)}) collective-permute-start(bf16[3,64,256]{2,1,0:T(8,128)(2,1)S(1)} %get-tuple-element.26), channel_id=1, source_target_pairs={{0,2},{1,3},{2,0},{3,1},{4,6},{5,7},{6,4},{7,5},{8,10},{9,11},{10,... | collective-permute-start | bytes 294920 | tf_op jit(solution)/shard_map/ppermute | solution.py:258
  29.6 1.6 %collective-permute-start.6 = (bf16[3,64,256]{2,1,0:T(8,128)(2,1)S(1)}, bf16[3,64,256]{2,1,0:T(8,128)(2,1)S(1)}, u32[]{:S(2)}, u32[]{:S(2)}) collective-permute-start(bf16[3,64,256]{2,1,0:T(8,128)(2,1)S(1)} %get-tuple-element.27), channel_id=1, source_target_pairs={{0,3},{1,0},{2,1},{3,2},{4,7},{5,4},{6,5},{7,6},{8,11},{9,8},{10,9... | collective-permute-start | bytes 294920 | tf_op jit(solution)/shard_map/ppermute | solution.py:258
  31.3 3.0 %collective-permute-done.4.refs_1_ = bf16[3,64,256]{2,1,0:T(8,128)(2,1)S(1)} collective-permute-done((bf16[3,64,256]{2,1,0:T(8,128)(2,1)S(1)}, bf16[3,64,256]{2,1,0:T(8,128)(2,1)S(1)}, u32[]{:S(2)}, u32[]{:S(2)}) %collective-permute-start.4) | collective-permute-done | bytes 98336 | tf_op jit(solution)/shard_map/ppermute | solution.py:258
  34.3 3.0 %collective-permute-done.5.refs_2_ = bf16[3,64,256]{2,1,0:T(8,128)(2,1)S(1)} collective-permute-done((bf16[3,64,256]{2,1,0:T(8,128)(2,1)S(1)}, bf16[3,64,256]{2,1,0:T(8,128)(2,1)S(1)}, u32[]{:S(2)}, u32[]{:S(2)}) %collective-permute-start.5) | collective-permute-done | bytes 98336 | tf_op jit(solution)/shard_map/ppermute | solution.py:258
  37.3 0.0 collective-permute-done.6.refs_3_
  37.4 2.7 %collective-permute-start.8 = (bf16[3,64,256]{2,1,0:T(8,128)(2,1)S(1)}, bf16[3,64,256]{2,1,0:T(8,128)(2,1)S(1)}, u32[]{:S(2)}, u32[]{:S(2)}) collective-permute-start(bf16[3,64,256]{2,1,0:T(8,128)(2,1)S(1)} %total.1.refs_0_), channel_id=1, source_target_pairs={{0,1},{1,2},{2,3},{3,0},{4,5},{5,6},{6,7},{7,4},{8,9},{9,10},{10,1... | collective-permute-start | bytes 294920 | tf_op jit(solution)/shard_map/ppermute | solution.py:258
  40.1 1.7 %collective-permute-start.9 = (bf16[3,64,256]{2,1,0:T(8,128)(2,1)S(1)}, bf16[3,64,256]{2,1,0:T(8,128)(2,1)S(1)}, u32[]{:S(2)}, u32[]{:S(2)}) collective-permute-start(bf16[3,64,256]{2,1,0:T(8,128)(2,1)S(1)} %total.1.refs_0_), channel_id=1, source_target_pairs={{0,2},{1,3},{2,0},{3,1},{4,6},{5,7},{6,4},{7,5},{8,10},{9,11},{10,... | collective-permute-start | bytes 294920 | tf_op jit(solution)/shard_map/ppermute | solution.py:258
  41.8 0.7 %collective-permute-start.7 = (bf16[3,64,256]{2,1,0:T(8,128)(2,1)S(1)}, bf16[3,64,256]{2,1,0:T(8,128)(2,1)S(1)}, u32[]{:S(2)}, u32[]{:S(2)}) collective-permute-start(bf16[3,64,256]{2,1,0:T(8,128)(2,1)S(1)} %total.1.refs_0_), channel_id=1, source_target_pairs={{0,3},{1,0},{2,1},{3,2},{4,7},{5,4},{6,5},{7,6},{8,11},{9,8},{10,9... | collective-permute-start | bytes 294920 | tf_op jit(solution)/shard_map/ppermute | solution.py:258
  42.5 2.4 %collective-permute-done.8.refs_1_ = bf16[3,64,256]{2,1,0:T(8,128)(2,1)S(1)} collective-permute-done((bf16[3,64,256]{2,1,0:T(8,128)(2,1)S(1)}, bf16[3,64,256]{2,1,0:T(8,128)(2,1)S(1)}, u32[]{:S(2)}, u32[]{:S(2)}) %collective-permute-start.8) | collective-permute-done | bytes 98336 | tf_op jit(solution)/shard_map/ppermute | solution.py:258
  45.0 3.6 %collective-permute-done.9.refs_2_ = bf16[3,64,256]{2,1,0:T(8,128)(2,1)S(1)} collective-permute-done((bf16[3,64,256]{2,1,0:T(8,128)(2,1)S(1)}, bf16[3,64,256]{2,1,0:T(8,128)(2,1)S(1)}, u32[]{:S(2)}, u32[]{:S(2)}) %collective-permute-start.9) | collective-permute-done | bytes 98336 | tf_op jit(solution)/shard_map/ppermute | solution.py:258
  48.5 0.8 %spread.2.refs_1_ = f32[2,3,2,128,128]{4,3,2,1,0:T(8,128)} custom-call(bf16[3,64,256]{2,1,0:T(8,128)(2,1)S(1)} %total.1.refs_0_, bf16[3,64,256]{2,1,0:T(8,128)(2,1)S(1)} %collective-permute-done.8.refs_1_, bf16[3,64,256]{2,1,0:T(8,128)(2,1)S(1)} %collective-permute-done.9.refs_2_), custom_call_target="tpu_custom_call" | custom-call | tf_op jit(solution)/shard_map/spread/pallas_call | solution.py:389
  49.4 0.0 collective-permute-done.7.refs_0_
  49.4 0.7 %spread.3 = f32[2,3,2,128,128]{4,3,2,1,0:T(8,128)} custom-call(bf16[3,64,256]{2,1,0:T(8,128)(2,1)S(1)} %collective-permute-done.7.refs_0_, f32[2,3,2,128,128]{4,3,2,1,0:T(8,128)} %spread.2.refs_1_), custom_call_target="tpu_custom_call", output_to_operand_aliasing={{}: (1, {})} | custom-call | tf_op jit(solution)/shard_map/spread/pallas_call | solution.py:389
  (1 shorter events, 0.0 us)
Async XLA Ops:
  3.1 19.4 %collective-permute-start = (bf16[1808,128]{1,0:T(8,128)(2,1)}, bf16[1808,128]{1,0:T(8,128)(2,1)S(1)}, u32[]{:S(2)}, u32[]{:S(2)}) collective-permute-start(bf16[1808,128]{1,0:T(8,128)(2,1)} %pack.1.own_at), channel_id=1, source_target_pairs={{1,0},{2,1},{3,2},{5,4},{6,5},{7,6},{9,8},{10,9},{11,10},{13,12},{... | collective-permute-start | bytes 1388552 | tf_op jit(solution)/shard_map/ppermute | solution.py:258
  4.4 18.2 %collective-permute-start.1 = (bf16[1808,128]{1,0:T(8,128)(2,1)}, bf16[1808,128]{1,0:T(8,128)(2,1)S(1)}, u32[]{:S(2)}, u32[]{:S(2)}) collective-permute-start(bf16[1808,128]{1,0:T(8,128)(2,1)} %pack.1.own_at), channel_id=1, source_target_pairs={{0,1},{1,2},{2,3},{4,5},{5,6},{6,7},{8,9},{9,10},{10,11},{12,13},{... | collective-permute-start | bytes 1388552 | tf_op jit(solution)/shard_map/ppermute | solution.py:258
  10.0 14.7 %collective-permute-start.2 = (bf16[1808,128]{1,0:T(8,128)(2,1)}, bf16[1808,128]{1,0:T(8,128)(2,1)S(1)}, u32[]{:S(2)}, u32[]{:S(2)}) collective-permute-start(bf16[1808,128]{1,0:T(8,128)(2,1)} %pack.1.own_at), channel_id=1, source_target_pairs={{4,8},{12,16},{20,24},{8,4},{16,12},{24,20},{5,9},{13,17},{21,25},... | collective-permute-start | bytes 1388552 | tf_op jit(solution)/shard_map/ppermute | solution.py:262
  10.7 14.1 %collective-permute-start.3 = (bf16[1808,128]{1,0:T(8,128)(2,1)}, bf16[1808,128]{1,0:T(8,128)(2,1)S(1)}, u32[]{:S(2)}, u32[]{:S(2)}) collective-permute-start(bf16[1808,128]{1,0:T(8,128)(2,1)} %pack.1.own_at), channel_id=1, source_target_pairs={{0,4},{8,12},{16,20},{24,28},{4,0},{12,8},{20,16},{28,24},{1,5},{9... | collective-permute-start | bytes 1388552 | tf_op jit(solution)/shard_map/ppermute | solution.py:262
  21.2 1.3 %copy-start.1 = (bf16[2,256,1024]{2,1,0:T(8,128)(2,1)S(1)}, bf16[2,256,1024]{2,1,0:T(8,128)(2,1)}, u32[]{:S(2)}) copy-start(bf16[2,256,1024]{2,1,0:T(8,128)(2,1)} %get-tuple-element.18.stock) | copy-start | bytes 3145732
  21.2 1.1 %copy-start.2 = (bf16[3,256,256]{2,1,0:T(8,128)(2,1)S(1)}, bf16[3,256,256]{2,1,0:T(8,128)(2,1)}, u32[]{:S(2)}) copy-start(bf16[3,256,256]{2,1,0:T(8,128)(2,1)} %get-tuple-element.16.more) | copy-start | bytes 1179652
  22.5 2.2 %copy-start = (bf16[2,256,1024]{2,1,0:T(8,128)(2,1)S(1)}, bf16[2,256,1024]{2,1,0:T(8,128)(2,1)}, u32[]{:S(2)}) copy-start(bf16[2,256,1024]{2,1,0:T(8,128)(2,1)} %get-tuple-element.15.stock) | copy-start | bytes 3145732
  26.9 7.4 %collective-permute-start.4 = (bf16[3,64,256]{2,1,0:T(8,128)(2,1)S(1)}, bf16[3,64,256]{2,1,0:T(8,128)(2,1)S(1)}, u32[]{:S(2)}, u32[]{:S(2)}) collective-permute-start(bf16[3,64,256]{2,1,0:T(8,128)(2,1)S(1)} %get-tuple-element.25), channel_id=1, source_target_pairs={{0,1},{1,2},{2,3},{3,0},{4,5},{5,6},{6,7},{7,4},{8,9},{9,10},{10,1... | collective-permute-start | bytes 294920 | tf_op jit(solution)/shard_map/ppermute | solution.py:258
  27.0 10.3 %collective-permute-start.5 = (bf16[3,64,256]{2,1,0:T(8,128)(2,1)S(1)}, bf16[3,64,256]{2,1,0:T(8,128)(2,1)S(1)}, u32[]{:S(2)}, u32[]{:S(2)}) collective-permute-start(bf16[3,64,256]{2,1,0:T(8,128)(2,1)S(1)} %get-tuple-element.26), channel_id=1, source_target_pairs={{0,2},{1,3},{2,0},{3,1},{4,6},{5,7},{6,4},{7,5},{8,10},{9,11},{10,... | collective-permute-start | bytes 294920 | tf_op jit(solution)/shard_map/ppermute | solution.py:258
  29.6 7.7 %collective-permute-start.6 = (bf16[3,64,256]{2,1,0:T(8,128)(2,1)S(1)}, bf16[3,64,256]{2,1,0:T(8,128)(2,1)S(1)}, u32[]{:S(2)}, u32[]{:S(2)}) collective-permute-start(bf16[3,64,256]{2,1,0:T(8,128)(2,1)S(1)} %get-tuple-element.27), channel_id=1, source_target_pairs={{0,3},{1,0},{2,1},{3,2},{4,7},{5,4},{6,5},{7,6},{8,11},{9,8},{10,9... | collective-permute-start | bytes 294920 | tf_op jit(solution)/shard_map/ppermute | solution.py:258
  37.4 7.6 %collective-permute-start.8 = (bf16[3,64,256]{2,1,0:T(8,128)(2,1)S(1)}, bf16[3,64,256]{2,1,0:T(8,128)(2,1)S(1)}, u32[]{:S(2)}, u32[]{:S(2)}) collective-permute-start(bf16[3,64,256]{2,1,0:T(8,128)(2,1)S(1)} %total.1.refs_0_), channel_id=1, source_target_pairs={{0,1},{1,2},{2,3},{3,0},{4,5},{5,6},{6,7},{7,4},{8,9},{9,10},{10,1... | collective-permute-start | bytes 294920 | tf_op jit(solution)/shard_map/ppermute | solution.py:258
  40.1 8.4 %collective-permute-start.9 = (bf16[3,64,256]{2,1,0:T(8,128)(2,1)S(1)}, bf16[3,64,256]{2,1,0:T(8,128)(2,1)S(1)}, u32[]{:S(2)}, u32[]{:S(2)}) collective-permute-start(bf16[3,64,256]{2,1,0:T(8,128)(2,1)S(1)} %total.1.refs_0_), channel_id=1, source_target_pairs={{0,2},{1,3},{2,0},{3,1},{4,6},{5,7},{6,4},{7,5},{8,10},{9,11},{10,... | collective-permute-start | bytes 294920 | tf_op jit(solution)/shard_map/ppermute | solution.py:258
  41.8 7.6 %collective-permute-start.7 = (bf16[3,64,256]{2,1,0:T(8,128)(2,1)S(1)}, bf16[3,64,256]{2,1,0:T(8,128)(2,1)S(1)}, u32[]{:S(2)}, u32[]{:S(2)}) collective-permute-start(bf16[3,64,256]{2,1,0:T(8,128)(2,1)S(1)} %total.1.refs_0_), channel_id=1, source_target_pairs={{0,3},{1,0},{2,1},{3,2},{4,7},{5,4},{6,5},{7,6},{8,11},{9,8},{10,9... | collective-permute-start | bytes 294920 | tf_op jit(solution)/shard_map/ppermute | solution.py:258

commit v15 on v11

--- a/solution.py
+++ b/solution.py
@@ -374,7 +374,8 @@
         compiler_params=LARGE,
         name="row_sources",
     )(row_stock, lift_t, term, other, pair, c_one)
-    parts = [sends[0]] + [shift(sends[d], "col", d, True) for d in range(1, cols_n)]
+    farthest = sorted(range(1, cols_n), key=lambda d: -min(d, cols_n - d))
+    parts = [sends[0]] + [shift(sends[d], "col", d, True) for d in farthest]
     total = pl.pallas_call(
         sum_kernel, out_shape=piece, in_specs=[VMEM] * cols_n, out_specs=VMEM,
         compiler_params=SMALL, name="total",

time: 49.7 us -> 49 us (0.986)
  waiting for transfers between devices: 12.3 us -> 9.46 us
  starting transfers between devices: 21.3 us -> 23.6 us
    ppermute x8, waiting for transfers between devices: 12.3 us -> 9.46 us  [shift(): return lax.ppermute(x, axis, pairs)]
    ppermute x8, starting transfers between devices: 17.3 us -> 19.6 us  [shift(): return lax.ppermute(x, axis, pairs)]
  transfers between devices with their start and end apart: 10 -> 10, of which waited for: 4 -> 4; matrix products, arithmetic and copies ran while one was open for 0% -> 0% of each run, Pallas kernels for 16% -> 15%
where the time goes in v15:
time: 49 us; the launch traced here: 48.6 us
  starting transfers between devices  23.6 us (48%)
  Pallas kernels  12.3 us (25%)
  waiting for transfers between devices  9.46 us (19%)
  between operations  2.07 us (4%)
  local copies, waits for them, and re-layouts  1.1 us (2%)
    ppermute x8, starting transfers between devices, shift(): return lax.ppermute(x, axis, pairs)  19.6 us
    ppermute x8, waiting for transfers between devices, shift(): return lax.ppermute(x, axis, pairs)  9.46 us
    pallas_call x1, Pallas kernels, per_device(): pl.pallas_call(functools.partial(own_kernel, slots, size), out_shape=[jax...  5.07 us
    ppermute x2, starting transfers between devices, swap(): return lax.ppermute(x, axis, pairs + [(j, i) for i, j in pairs])  4.02 us
    pallas_call x1, Pallas kernels, per_device(): pl.pallas_call(functools.partial(row_kernel, slots, size, cols_n), out_sh...  2.15 us
    pallas_call x1, Pallas kernels, per_device(): pl.pallas_call(functools.partial(side_kernel, slots, size), out_shape=[c_...  2.13 us
    pallas_call x1, Pallas kernels, per_device(): pl.pallas_call(pack_kernel, out_shape=jax.ShapeDtypeStruct((packed_rows,...  1.81 us
    unnamed x6, local copies, waits for them, and re-layouts  1.1 us
  transfers between devices with their start and end apart: 10, of which 4 were waited for; matrix products, arithmetic and copies ran while one was open for 0% of the time, Pallas kernels for 15%

profile of v15, /device:TPU:0, one launch (start us, length us, event | category | flops | bytes accessed | tf_op | source)
XLA Modules:
  0.0 48.6 jit_solution(14608228903702339738)
XLA Ops:
  1.3 1.8 %pack.1.own_at = bf16[1808,128]{1,0:T(8,128)(2,1)} custom-call(s32[1,1,12]{2,1,0:T(1,128)} %codes_at.3, s32[1,1]{1,0:T(1,128)S(6)} %copy.16.count_at.p_count_at, s32[1,1,2]{2,1,0:T(1,128)} %aggs_at.3, bf16[1536,128]{1,0:T(8,128)(2,1)} %bitcast.7, bf16[256,128]{1,0:T(8,128)(2,1)} %bitcast.8), custom_call_target="tpu_custom_call" | custom-call | tf_op jit(solution)/shard_map/pack/pallas_call | solution.py:275
  3.1 1.3 %collective-permute-start = (bf16[1808,128]{1,0:T(8,128)(2,1)}, bf16[1808,128]{1,0:T(8,128)(2,1)S(1)}, u32[]{:S(2)}, u32[]{:S(2)}) collective-permute-start(bf16[1808,128]{1,0:T(8,128)(2,1)} %pack.1.own_at), channel_id=1, source_target_pairs={{1,0},{2,1},{3,2},{5,4},{6,5},{7,6},{9,8},{10,9},{11,10},{13,12},{... | collective-permute-start | bytes 1388552 | tf_op jit(solution)/shard_map/ppermute | solution.py:258
  4.4 5.6 %collective-permute-start.1 = (bf16[1808,128]{1,0:T(8,128)(2,1)}, bf16[1808,128]{1,0:T(8,128)(2,1)S(1)}, u32[]{:S(2)}, u32[]{:S(2)}) collective-permute-start(bf16[1808,128]{1,0:T(8,128)(2,1)} %pack.1.own_at), channel_id=1, source_target_pairs={{0,1},{1,2},{2,3},{4,5},{5,6},{6,7},{8,9},{9,10},{10,11},{12,13},{... | collective-permute-start | bytes 1388552 | tf_op jit(solution)/shard_map/ppermute | solution.py:258
  10.0 0.7 %collective-permute-start.2 = (bf16[1808,128]{1,0:T(8,128)(2,1)}, bf16[1808,128]{1,0:T(8,128)(2,1)S(1)}, u32[]{:S(2)}, u32[]{:S(2)}) collective-permute-start(bf16[1808,128]{1,0:T(8,128)(2,1)} %pack.1.own_at), channel_id=1, source_target_pairs={{4,8},{12,16},{20,24},{8,4},{16,12},{24,20},{5,9},{13,17},{21,25},... | collective-permute-start | bytes 1388552 | tf_op jit(solution)/shard_map/ppermute | solution.py:262
  10.7 3.3 %collective-permute-start.3 = (bf16[1808,128]{1,0:T(8,128)(2,1)}, bf16[1808,128]{1,0:T(8,128)(2,1)S(1)}, u32[]{:S(2)}, u32[]{:S(2)}) collective-permute-start(bf16[1808,128]{1,0:T(8,128)(2,1)} %pack.1.own_at), channel_id=1, source_target_pairs={{0,4},{8,12},{16,20},{24,28},{4,0},{12,8},{20,16},{28,24},{1,5},{9... | collective-permute-start | bytes 1388552 | tf_op jit(solution)/shard_map/ppermute | solution.py:262
  14.7 5.1 %own_source.1 = (bf16[2,256,1024]{2,1,0:T(8,128)(2,1)}, bf16[2,256,1024]{2,1,0:T(8,128)(2,1)}, bf16[3,256,256]{2,1,0:T(8,128)(2,1)}, bf16[2,5,2,128,128]{4,3,2,1,0:T(8,128)(2,1)}) custom-call(s32[1,1,64]{2,1,0:T(1,128)} %rows_at.1, s32[1,1,64]{2,1,0:T(1,128)} %cols_at.1, s32[1,1]{1,0:T(1,128)S(6)} %copy.15.count_at, s32[1,1,12]{2,1,0:T(1,128)} %codes_at.3, ...), custom_call_target="tpu_custom_call" | custom-call | flops 1000000000 | bytes 4000000 | tf_op jit(solution)/shard_map/own_source/pallas_call | solution.py:306
  19.7 0.0 copy-start.1
  19.8 0.0 copy-start.2
  19.8 1.1 %copy-done.2 = bf16[3,256,256]{2,1,0:T(8,128)(2,1)S(1)} copy-done((bf16[3,256,256]{2,1,0:T(8,128)(2,1)S(1)}, bf16[3,256,256]{2,1,0:T(8,128)(2,1)}, u32[]{:S(2)}) %copy-start.2) | copy-done | bytes 393240
  20.8 0.2 own_half.1
  21.0 0.0 copy-start
  21.0 0.0 collective-permute-done.right
  21.1 0.0 collective-permute-done.1.left
  21.1 0.0 copy-done.1
  21.1 2.1 %col_sources.1 = (bf16[2,5,2,128,128]{4,3,2,1,0:T(8,128)(2,1)}, f32[256,256]{1,0:T(8,128)S(1)}) custom-call(bf16[2,256,1024]{2,1,0:T(8,128)(2,1)S(1)} %copy-done.1, bf16[256,256]{1,0:T(8,128)(2,1)S(1)} %get-tuple-element.17.lift_t, f32[256,256]{1,0:T(8,128)S(1)} %get-tuple-element.19.half, ...), custom_call_target="tpu_custom_call", output_to_operand_aliasing={{0}: (5, {})} | custom-call | tf_op jit(solution)/shard_map/col_sources/pallas_call | solution.py:353
  23.2 0.0 collective-permute-done.2.other
  23.2 0.0 collective-permute-done.3.pair
  23.2 0.0 copy-done
  23.3 2.1 %row_sources.1 = (bf16[2,5,2,128,128]{4,3,2,1,0:T(8,128)(2,1)}, f32[3,64,256]{2,1,0:T(8,128)S(1)}, bf16[3,64,256]{2,1,0:T(8,128)(2,1)S(1)}, bf16[3,64,256]{2,1,0:T(8,128)(2,1)S(1)}, bf16[3,64,256]{2,1,0:T(8,128)(2,1)S(1)}) custom-call(bf16[2,256,1024]{2,1,0:T(8,128)(2,1)S(1)} %copy-done, ...), custom_call_target="tpu_custom_call", output_to_operand_aliasing={{0}: (5, {})} | custom-call | tf_op jit(solution)/shard_map/row_sources/pallas_call | solution.py:367
  25.4 4.1 %collective-permute-start.4 = (bf16[3,64,256]{2,1,0:T(8,128)(2,1)S(1)}, bf16[3,64,256]{2,1,0:T(8,128)(2,1)S(1)}, u32[]{:S(2)}, u32[]{:S(2)}) collective-permute-start(bf16[3,64,256]{2,1,0:T(8,128)(2,1)S(1)} %get-tuple-element.25), channel_id=1, source_target_pairs={{0,2},{1,3},{2,0},{3,1},{4,6},{5,7},{6,4},{7,5},{8,10},{9,11},{10,... | collective-permute-start | bytes 294920 | tf_op jit(solution)/shard_map/ppermute | solution.py:258
  29.6 0.1 collective-permute-start.5
  29.7 3.7 %collective-permute-start.6 = (bf16[3,64,256]{2,1,0:T(8,128)(2,1)S(1)}, bf16[3,64,256]{2,1,0:T(8,128)(2,1)S(1)}, u32[]{:S(2)}, u32[]{:S(2)}) collective-permute-start(bf16[3,64,256]{2,1,0:T(8,128)(2,1)S(1)} %get-tuple-element.27), channel_id=1, source_target_pairs={{0,3},{1,0},{2,1},{3,2},{4,7},{5,4},{6,5},{7,6},{8,11},{9,8},{10,9... | collective-permute-start | bytes 294920 | tf_op jit(solution)/shard_map/ppermute | solution.py:258
  33.4 3.8 %collective-permute-done.4.refs_1_ = bf16[3,64,256]{2,1,0:T(8,128)(2,1)S(1)} collective-permute-done((bf16[3,64,256]{2,1,0:T(8,128)(2,1)S(1)}, bf16[3,64,256]{2,1,0:T(8,128)(2,1)S(1)}, u32[]{:S(2)}, u32[]{:S(2)}) %collective-permute-start.4) | collective-permute-done | bytes 98336 | tf_op jit(solution)/shard_map/ppermute | solution.py:258
  37.2 0.0 collective-permute-done.5.refs_2_
  37.2 0.3 collective-permute-done.6.refs_3_
  37.5 1.7 %collective-permute-start.7 = (bf16[3,64,256]{2,1,0:T(8,128)(2,1)S(1)}, bf16[3,64,256]{2,1,0:T(8,128)(2,1)S(1)}, u32[]{:S(2)}, u32[]{:S(2)}) collective-permute-start(bf16[3,64,256]{2,1,0:T(8,128)(2,1)S(1)} %total.1.refs_0_), channel_id=1, source_target_pairs={{0,1},{1,2},{2,3},{3,0},{4,5},{5,6},{6,7},{7,4},{8,9},{9,10},{10,1... | collective-permute-start | bytes 294920 | tf_op jit(solution)/shard_map/ppermute | solution.py:258
  39.2 1.5 %collective-permute-start.8 = (bf16[3,64,256]{2,1,0:T(8,128)(2,1)S(1)}, bf16[3,64,256]{2,1,0:T(8,128)(2,1)S(1)}, u32[]{:S(2)}, u32[]{:S(2)}) collective-permute-start(bf16[3,64,256]{2,1,0:T(8,128)(2,1)S(1)} %total.1.refs_0_), channel_id=1, source_target_pairs={{0,2},{1,3},{2,0},{3,1},{4,6},{5,7},{6,4},{7,5},{8,10},{9,11},{10,... | collective-permute-start | bytes 294920 | tf_op jit(solution)/shard_map/ppermute | solution.py:258
  40.7 1.6 %collective-permute-start.9 = (bf16[3,64,256]{2,1,0:T(8,128)(2,1)S(1)}, bf16[3,64,256]{2,1,0:T(8,128)(2,1)S(1)}, u32[]{:S(2)}, u32[]{:S(2)}) collective-permute-start(bf16[3,64,256]{2,1,0:T(8,128)(2,1)S(1)} %total.1.refs_0_), channel_id=1, source_target_pairs={{0,3},{1,0},{2,1},{3,2},{4,7},{5,4},{6,5},{7,6},{8,11},{9,8},{10,9... | collective-permute-start | bytes 294920 | tf_op jit(solution)/shard_map/ppermute | solution.py:258
  42.3 2.8 %collective-permute-done.7.refs_1_ = bf16[3,64,256]{2,1,0:T(8,128)(2,1)S(1)} collective-permute-done((bf16[3,64,256]{2,1,0:T(8,128)(2,1)S(1)}, bf16[3,64,256]{2,1,0:T(8,128)(2,1)S(1)}, u32[]{:S(2)}, u32[]{:S(2)}) %collective-permute-start.7) | collective-permute-done | bytes 98336 | tf_op jit(solution)/shard_map/ppermute | solution.py:258
  45.1 2.5 %collective-permute-done.8.refs_2_ = bf16[3,64,256]{2,1,0:T(8,128)(2,1)S(1)} collective-permute-done((bf16[3,64,256]{2,1,0:T(8,128)(2,1)S(1)}, bf16[3,64,256]{2,1,0:T(8,128)(2,1)S(1)}, u32[]{:S(2)}, u32[]{:S(2)}) %collective-permute-start.8) | collective-permute-done | bytes 98336 | tf_op jit(solution)/shard_map/ppermute | solution.py:258
  47.6 0.0 collective-permute-done.9.refs_3_
  47.6 0.9 %spread.1 = f32[2,3,2,128,128]{4,3,2,1,0:T(8,128)} custom-call(bf16[3,64,256]{2,1,0:T(8,128)(2,1)S(1)} %total.1.refs_0_, bf16[3,64,256]{2,1,0:T(8,128)(2,1)S(1)} %collective-permute-done.7.refs_1_, bf16[3,64,256]{2,1,0:T(8,128)(2,1)S(1)} %collective-permute-done.8.refs_2_, bf16[3,64,256]{2,1,0:T(8,128)(2,1)S(1)} %collective-permute-done.9.refs_3_), custom_call_target="tpu_custom_call" | custom-call | tf_op jit(solution)/shard_map/spread/pallas_call | solution.py:384
  (1 shorter events, 0.0 us)
Async XLA Ops:
  3.1 18.0 %collective-permute-start = (bf16[1808,128]{1,0:T(8,128)(2,1)}, bf16[1808,128]{1,0:T(8,128)(2,1)S(1)}, u32[]{:S(2)}, u32[]{:S(2)}) collective-permute-start(bf16[1808,128]{1,0:T(8,128)(2,1)} %pack.1.own_at), channel_id=1, source_target_pairs={{1,0},{2,1},{3,2},{5,4},{6,5},{7,6},{9,8},{10,9},{11,10},{13,12},{... | collective-permute-start | bytes 1388552 | tf_op jit(solution)/shard_map/ppermute | solution.py:258
  4.4 16.7 %collective-permute-start.1 = (bf16[1808,128]{1,0:T(8,128)(2,1)}, bf16[1808,128]{1,0:T(8,128)(2,1)S(1)}, u32[]{:S(2)}, u32[]{:S(2)}) collective-permute-start(bf16[1808,128]{1,0:T(8,128)(2,1)} %pack.1.own_at), channel_id=1, source_target_pairs={{0,1},{1,2},{2,3},{4,5},{5,6},{6,7},{8,9},{9,10},{10,11},{12,13},{... | collective-permute-start | bytes 1388552 | tf_op jit(solution)/shard_map/ppermute | solution.py:258
  10.0 13.2 %collective-permute-start.2 = (bf16[1808,128]{1,0:T(8,128)(2,1)}, bf16[1808,128]{1,0:T(8,128)(2,1)S(1)}, u32[]{:S(2)}, u32[]{:S(2)}) collective-permute-start(bf16[1808,128]{1,0:T(8,128)(2,1)} %pack.1.own_at), channel_id=1, source_target_pairs={{4,8},{12,16},{20,24},{8,4},{16,12},{24,20},{5,9},{13,17},{21,25},... | collective-permute-start | bytes 1388552 | tf_op jit(solution)/shard_map/ppermute | solution.py:262
  10.7 12.6 %collective-permute-start.3 = (bf16[1808,128]{1,0:T(8,128)(2,1)}, bf16[1808,128]{1,0:T(8,128)(2,1)S(1)}, u32[]{:S(2)}, u32[]{:S(2)}) collective-permute-start(bf16[1808,128]{1,0:T(8,128)(2,1)} %pack.1.own_at), channel_id=1, source_target_pairs={{0,4},{8,12},{16,20},{24,28},{4,0},{12,8},{20,16},{28,24},{1,5},{9... | collective-permute-start | bytes 1388552 | tf_op jit(solution)/shard_map/ppermute | solution.py:262
  19.7 1.3 %copy-start.1 = (bf16[2,256,1024]{2,1,0:T(8,128)(2,1)S(1)}, bf16[2,256,1024]{2,1,0:T(8,128)(2,1)}, u32[]{:S(2)}) copy-start(bf16[2,256,1024]{2,1,0:T(8,128)(2,1)} %get-tuple-element.18.stock) | copy-start | bytes 3145732
  19.8 1.1 %copy-start.2 = (bf16[3,256,256]{2,1,0:T(8,128)(2,1)S(1)}, bf16[3,256,256]{2,1,0:T(8,128)(2,1)}, u32[]{:S(2)}) copy-start(bf16[3,256,256]{2,1,0:T(8,128)(2,1)} %get-tuple-element.16.more) | copy-start | bytes 1179652
  21.0 2.2 %copy-start = (bf16[2,256,1024]{2,1,0:T(8,128)(2,1)S(1)}, bf16[2,256,1024]{2,1,0:T(8,128)(2,1)}, u32[]{:S(2)}) copy-start(bf16[2,256,1024]{2,1,0:T(8,128)(2,1)} %get-tuple-element.15.stock) | copy-start | bytes 3145732
  25.4 11.8 %collective-permute-start.4 = (bf16[3,64,256]{2,1,0:T(8,128)(2,1)S(1)}, bf16[3,64,256]{2,1,0:T(8,128)(2,1)S(1)}, u32[]{:S(2)}, u32[]{:S(2)}) collective-permute-start(bf16[3,64,256]{2,1,0:T(8,128)(2,1)S(1)} %get-tuple-element.25), channel_id=1, source_target_pairs={{0,2},{1,3},{2,0},{3,1},{4,6},{5,7},{6,4},{7,5},{8,10},{9,11},{10,... | collective-permute-start | bytes 294920 | tf_op jit(solution)/shard_map/ppermute | solution.py:258
  29.6 7.6 %collective-permute-start.5 = (bf16[3,64,256]{2,1,0:T(8,128)(2,1)S(1)}, bf16[3,64,256]{2,1,0:T(8,128)(2,1)S(1)}, u32[]{:S(2)}, u32[]{:S(2)}) collective-permute-start(bf16[3,64,256]{2,1,0:T(8,128)(2,1)S(1)} %get-tuple-element.26), channel_id=1, source_target_pairs={{0,1},{1,2},{2,3},{3,0},{4,5},{5,6},{6,7},{7,4},{8,9},{9,10},{10,1... | collective-permute-start | bytes 294920 | tf_op jit(solution)/shard_map/ppermute | solution.py:258
  29.7 7.8 %collective-permute-start.6 = (bf16[3,64,256]{2,1,0:T(8,128)(2,1)S(1)}, bf16[3,64,256]{2,1,0:T(8,128)(2,1)S(1)}, u32[]{:S(2)}, u32[]{:S(2)}) collective-permute-start(bf16[3,64,256]{2,1,0:T(8,128)(2,1)S(1)} %get-tuple-element.27), channel_id=1, source_target_pairs={{0,3},{1,0},{2,1},{3,2},{4,7},{5,4},{6,5},{7,6},{8,11},{9,8},{10,9... | collective-permute-start | bytes 294920 | tf_op jit(solution)/shard_map/ppermute | solution.py:258
  37.5 7.6 %collective-permute-start.7 = (bf16[3,64,256]{2,1,0:T(8,128)(2,1)S(1)}, bf16[3,64,256]{2,1,0:T(8,128)(2,1)S(1)}, u32[]{:S(2)}, u32[]{:S(2)}) collective-permute-start(bf16[3,64,256]{2,1,0:T(8,128)(2,1)S(1)} %total.1.refs_0_), channel_id=1, source_target_pairs={{0,1},{1,2},{2,3},{3,0},{4,5},{5,6},{6,7},{7,4},{8,9},{9,10},{10,1... | collective-permute-start | bytes 294920 | tf_op jit(solution)/shard_map/ppermute | solution.py:258
  39.2 8.4 %collective-permute-start.8 = (bf16[3,64,256]{2,1,0:T(8,128)(2,1)S(1)}, bf16[3,64,256]{2,1,0:T(8,128)(2,1)S(1)}, u32[]{:S(2)}, u32[]{:S(2)}) collective-permute-start(bf16[3,64,256]{2,1,0:T(8,128)(2,1)S(1)} %total.1.refs_0_), channel_id=1, source_target_pairs={{0,2},{1,3},{2,0},{3,1},{4,6},{5,7},{6,4},{7,5},{8,10},{9,11},{10,... | collective-permute-start | bytes 294920 | tf_op jit(solution)/shard_map/ppermute | solution.py:258
  40.7 6.9 %collective-permute-start.9 = (bf16[3,64,256]{2,1,0:T(8,128)(2,1)S(1)}, bf16[3,64,256]{2,1,0:T(8,128)(2,1)S(1)}, u32[]{:S(2)}, u32[]{:S(2)}) collective-permute-start(bf16[3,64,256]{2,1,0:T(8,128)(2,1)S(1)} %total.1.refs_0_), channel_id=1, source_target_pairs={{0,3},{1,0},{2,1},{3,2},{4,7},{5,4},{6,5},{7,6},{8,11},{9,8},{10,9... | collective-permute-start | bytes 294920 | tf_op jit(solution)/shard_map/ppermute | solution.py:258

commit v16 on v15

--- a/solution.py
+++ b/solution.py
@@ -227,14 +227,15 @@
     refs[-1][...] = total.astype(BF16)
 
 
-def spread_kernel(size, cols_n, *refs):
+def spread_kernel(size, steps, *refs):
+    cols_n = len(steps)
     parts, out_at, out, sems = refs[:cols_n], refs[cols_n], refs[cols_n + 1], refs[cols_n + 2]
     chunk = parts[0].shape[1]
     unit = math.gcd(chunk, size)
     per = size // unit
     me = lax.axis_index("col")
     stores = []
-    for d in range(cols_n):
+    for n, d in enumerate(steps):
         owner = lax.rem(me - d + cols_n, cols_n)
         for t in range(chunk // unit):
             at = owner * (chunk // unit) + t
@@ -242,7 +243,7 @@
             rows = pl.ds(pl.multiple_of(lax.rem(at, per) * unit, unit), unit)
             for g in range(3):
                 for b in range(G2):
-                    out[a, g, b, rows, :] = parts[d][
+                    out[a, g, b, rows, :] = parts[n][
                         g, t * unit : (t + 1) * unit, b * size : (b + 1) * size
                     ].astype(F32)
             spot = (a, slice(None), slice(None), rows)
@@ -380,9 +381,10 @@
         sum_kernel, out_shape=piece, in_specs=[VMEM] * cols_n, out_specs=VMEM,
         compiler_params=SMALL, name="total",
     )(*parts)
-    gathered = [total] + [shift(total, "col", d, True) for d in range(1, cols_n)]
+    nearest = farthest[::-1]
+    gathered = [total] + [shift(total, "col", d, True) for d in nearest]
     c_two = pl.pallas_call(
-        functools.partial(spread_kernel, size, cols_n),
+        functools.partial(spread_kernel, size, [0] + nearest),
         out_shape=jax.ShapeDtypeStruct((G2, 3, G2, size, size), F32),
         in_specs=[VMEM] * cols_n,
         out_specs=HBM,

time: 49 us -> 50.7 us (1.035)
  waiting for transfers between devices: 9.46 us -> 13.1 us
  starting transfers between devices: 23.6 us -> 22 us
    ppermute x8, waiting for transfers between devices: 9.46 us -> 13.1 us  [shift(): return lax.ppermute(x, axis, pairs)]
    ppermute x8, starting transfers between devices: 19.6 us -> 18 us  [shift(): return lax.ppermute(x, axis, pairs)]
  transfers between devices with their start and end apart: 10 -> 10, of which waited for: 4 -> 5; matrix products, arithmetic and copies ran while one was open for 0% -> 0% of each run, Pallas kernels for 15% -> 14%
where the time goes in v16:
time: 50.7 us; the launch traced here: 50.3 us
  starting transfers between devices  22 us (43%)
  waiting for transfers between devices  13.1 us (26%)
  Pallas kernels  12 us (24%)
  between operations  2.07 us (4%)
  local copies, waits for them, and re-layouts  1.1 us (2%)
    ppermute x8, starting transfers between devices, shift(): return lax.ppermute(x, axis, pairs)  18 us
    ppermute x8, waiting for transfers between devices, shift(): return lax.ppermute(x, axis, pairs)  13.1 us
    pallas_call x1, Pallas kernels, per_device(): pl.pallas_call(functools.partial(own_kernel, slots, size), out_shape=[jax...  4.77 us
    ppermute x2, starting transfers between devices, swap(): return lax.ppermute(x, axis, pairs + [(j, i) for i, j in pairs])  4.02 us
    pallas_call x1, Pallas kernels, per_device(): pl.pallas_call(functools.partial(row_kernel, slots, size, cols_n), out_sh...  2.15 us
    pallas_call x1, Pallas kernels, per_device(): pl.pallas_call(functools.partial(side_kernel, slots, size), out_shape=[c_...  2.14 us
    pallas_call x1, Pallas kernels, per_device(): pl.pallas_call(pack_kernel, out_shape=jax.ShapeDtypeStruct((packed_rows,...  1.81 us
    unnamed x6, local copies, waits for them, and re-layouts  1.1 us
  transfers between devices with their start and end apart: 10, of which 5 were waited for; matrix products, arithmetic and copies ran while one was open for 0% of the time, Pallas kernels for 14%

profile of v16, /device:TPU:0, one launch (start us, length us, event | category | flops | bytes accessed | tf_op | source)
XLA Modules:
  0.0 50.3 jit_solution(13874911580847130130)
XLA Ops:
  1.3 1.8 %pack.1.own_at = bf16[1808,128]{1,0:T(8,128)(2,1)} custom-call(s32[1,1,12]{2,1,0:T(1,128)} %codes_at.3, s32[1,1]{1,0:T(1,128)S(6)} %copy.16.count_at.p_count_at, s32[1,1,2]{2,1,0:T(1,128)} %aggs_at.3, bf16[1536,128]{1,0:T(8,128)(2,1)} %bitcast.7, bf16[256,128]{1,0:T(8,128)(2,1)} %bitcast.8), custom_call_target="tpu_custom_call" | custom-call | tf_op jit(solution)/shard_map/pack/pallas_call | solution.py:276
  3.1 1.3 %collective-permute-start = (bf16[1808,128]{1,0:T(8,128)(2,1)}, bf16[1808,128]{1,0:T(8,128)(2,1)S(1)}, u32[]{:S(2)}, u32[]{:S(2)}) collective-permute-start(bf16[1808,128]{1,0:T(8,128)(2,1)} %pack.1.own_at), channel_id=1, source_target_pairs={{1,0},{2,1},{3,2},{5,4},{6,5},{7,6},{9,8},{10,9},{11,10},{13,12},{... | collective-permute-start | bytes 1388552 | tf_op jit(solution)/shard_map/ppermute | solution.py:259
  4.4 5.6 %collective-permute-start.1 = (bf16[1808,128]{1,0:T(8,128)(2,1)}, bf16[1808,128]{1,0:T(8,128)(2,1)S(1)}, u32[]{:S(2)}, u32[]{:S(2)}) collective-permute-start(bf16[1808,128]{1,0:T(8,128)(2,1)} %pack.1.own_at), channel_id=1, source_target_pairs={{0,1},{1,2},{2,3},{4,5},{5,6},{6,7},{8,9},{9,10},{10,11},{12,13},{... | collective-permute-start | bytes 1388552 | tf_op jit(solution)/shard_map/ppermute | solution.py:259
  10.0 0.7 %collective-permute-start.2 = (bf16[1808,128]{1,0:T(8,128)(2,1)}, bf16[1808,128]{1,0:T(8,128)(2,1)S(1)}, u32[]{:S(2)}, u32[]{:S(2)}) collective-permute-start(bf16[1808,128]{1,0:T(8,128)(2,1)} %pack.1.own_at), channel_id=1, source_target_pairs={{4,8},{12,16},{20,24},{8,4},{16,12},{24,20},{5,9},{13,17},{21,25},... | collective-permute-start | bytes 1388552 | tf_op jit(solution)/shard_map/ppermute | solution.py:263
  10.7 3.3 %collective-permute-start.3 = (bf16[1808,128]{1,0:T(8,128)(2,1)}, bf16[1808,128]{1,0:T(8,128)(2,1)S(1)}, u32[]{:S(2)}, u32[]{:S(2)}) collective-permute-start(bf16[1808,128]{1,0:T(8,128)(2,1)} %pack.1.own_at), channel_id=1, source_target_pairs={{0,4},{8,12},{16,20},{24,28},{4,0},{12,8},{20,16},{28,24},{1,5},{9... | collective-permute-start | bytes 1388552 | tf_op jit(solution)/shard_map/ppermute | solution.py:263
  14.7 4.8 %own_source.1 = (bf16[2,256,1024]{2,1,0:T(8,128)(2,1)}, bf16[2,256,1024]{2,1,0:T(8,128)(2,1)}, bf16[3,256,256]{2,1,0:T(8,128)(2,1)}, bf16[2,5,2,128,128]{4,3,2,1,0:T(8,128)(2,1)}) custom-call(s32[1,1,64]{2,1,0:T(1,128)} %rows_at.1, s32[1,1,64]{2,1,0:T(1,128)} %cols_at.1, s32[1,1]{1,0:T(1,128)S(6)} %copy.15.count_at, s32[1,1,12]{2,1,0:T(1,128)} %codes_at.3, ...), custom_call_target="tpu_custom_call" | custom-call | flops 1000000000 | bytes 4000000 | tf_op jit(solution)/shard_map/own_source/pallas_call | solution.py:307
  19.4 0.0 copy-start.1
  19.5 0.0 copy-start.2
  19.5 1.1 %copy-done.2 = bf16[3,256,256]{2,1,0:T(8,128)(2,1)S(1)} copy-done((bf16[3,256,256]{2,1,0:T(8,128)(2,1)S(1)}, bf16[3,256,256]{2,1,0:T(8,128)(2,1)}, u32[]{:S(2)}) %copy-start.2) | copy-done | bytes 393240
  20.5 0.2 own_half.1
  20.7 0.0 copy-start
  20.7 0.0 collective-permute-done.right
  20.8 0.0 collective-permute-done.1.left
  20.8 0.0 copy-done.1
  20.8 2.1 %col_sources.1 = (bf16[2,5,2,128,128]{4,3,2,1,0:T(8,128)(2,1)}, f32[256,256]{1,0:T(8,128)S(1)}) custom-call(bf16[2,256,1024]{2,1,0:T(8,128)(2,1)S(1)} %copy-done.1, bf16[256,256]{1,0:T(8,128)(2,1)S(1)} %get-tuple-element.17.lift_t, f32[256,256]{1,0:T(8,128)S(1)} %get-tuple-element.19.half, ...), custom_call_target="tpu_custom_call", output_to_operand_aliasing={{0}: (5, {})} | custom-call | tf_op jit(solution)/shard_map/col_sources/pallas_call | solution.py:354
  22.9 0.0 collective-permute-done.2.other
  22.9 0.0 collective-permute-done.3.pair
  22.9 0.0 copy-done
  23.0 2.1 %row_sources.1 = (bf16[2,5,2,128,128]{4,3,2,1,0:T(8,128)(2,1)}, f32[3,64,256]{2,1,0:T(8,128)S(1)}, bf16[3,64,256]{2,1,0:T(8,128)(2,1)S(1)}, bf16[3,64,256]{2,1,0:T(8,128)(2,1)S(1)}, bf16[3,64,256]{2,1,0:T(8,128)(2,1)S(1)}) custom-call(bf16[2,256,1024]{2,1,0:T(8,128)(2,1)S(1)} %copy-done, ...), custom_call_target="tpu_custom_call", output_to_operand_aliasing={{0}: (5, {})} | custom-call | tf_op jit(solution)/shard_map/row_sources/pallas_call | solution.py:368
  25.1 3.0 %collective-permute-start.4 = (bf16[3,64,256]{2,1,0:T(8,128)(2,1)S(1)}, bf16[3,64,256]{2,1,0:T(8,128)(2,1)S(1)}, u32[]{:S(2)}, u32[]{:S(2)}) collective-permute-start(bf16[3,64,256]{2,1,0:T(8,128)(2,1)S(1)} %get-tuple-element.25), channel_id=1, source_target_pairs={{0,2},{1,3},{2,0},{3,1},{4,6},{5,7},{6,4},{7,5},{8,10},{9,11},{10,... | collective-permute-start | bytes 294920 | tf_op jit(solution)/shard_map/ppermute | solution.py:259
  28.1 1.6 %collective-permute-start.5 = (bf16[3,64,256]{2,1,0:T(8,128)(2,1)S(1)}, bf16[3,64,256]{2,1,0:T(8,128)(2,1)S(1)}, u32[]{:S(2)}, u32[]{:S(2)}) collective-permute-start(bf16[3,64,256]{2,1,0:T(8,128)(2,1)S(1)} %get-tuple-element.26), channel_id=1, source_target_pairs={{0,1},{1,2},{2,3},{3,0},{4,5},{5,6},{6,7},{7,4},{8,9},{9,10},{10,1... | collective-permute-start | bytes 294920 | tf_op jit(solution)/shard_map/ppermute | solution.py:259
  29.7 2.2 %collective-permute-start.6 = (bf16[3,64,256]{2,1,0:T(8,128)(2,1)S(1)}, bf16[3,64,256]{2,1,0:T(8,128)(2,1)S(1)}, u32[]{:S(2)}, u32[]{:S(2)}) collective-permute-start(bf16[3,64,256]{2,1,0:T(8,128)(2,1)S(1)} %get-tuple-element.27), channel_id=1, source_target_pairs={{0,3},{1,0},{2,1},{3,2},{4,7},{5,4},{6,5},{7,6},{8,11},{9,8},{10,9... | collective-permute-start | bytes 294920 | tf_op jit(solution)/shard_map/ppermute | solution.py:259
  31.9 3.8 %collective-permute-done.4.refs_1_ = bf16[3,64,256]{2,1,0:T(8,128)(2,1)S(1)} collective-permute-done((bf16[3,64,256]{2,1,0:T(8,128)(2,1)S(1)}, bf16[3,64,256]{2,1,0:T(8,128)(2,1)S(1)}, u32[]{:S(2)}, u32[]{:S(2)}) %collective-permute-start.4) | collective-permute-done | bytes 98336 | tf_op jit(solution)/shard_map/ppermute | solution.py:259
  35.6 0.0 collective-permute-done.5.refs_2_
  35.7 1.4 %collective-permute-done.6.refs_3_ = bf16[3,64,256]{2,1,0:T(8,128)(2,1)S(1)} collective-permute-done((bf16[3,64,256]{2,1,0:T(8,128)(2,1)S(1)}, bf16[3,64,256]{2,1,0:T(8,128)(2,1)S(1)}, u32[]{:S(2)}, u32[]{:S(2)}) %collective-permute-start.6) | collective-permute-done | bytes 98336 | tf_op jit(solution)/shard_map/ppermute | solution.py:259
  37.1 2.7 %collective-permute-start.7 = (bf16[3,64,256]{2,1,0:T(8,128)(2,1)S(1)}, bf16[3,64,256]{2,1,0:T(8,128)(2,1)S(1)}, u32[]{:S(2)}, u32[]{:S(2)}) collective-permute-start(bf16[3,64,256]{2,1,0:T(8,128)(2,1)S(1)} %total.1.refs_0_), channel_id=1, source_target_pairs={{0,3},{1,0},{2,1},{3,2},{4,7},{5,4},{6,5},{7,6},{8,11},{9,8},{10,9... | collective-permute-start | bytes 294920 | tf_op jit(solution)/shard_map/ppermute | solution.py:259
  39.8 0.0 collective-permute-start.8
  39.8 1.6 %collective-permute-start.9 = (bf16[3,64,256]{2,1,0:T(8,128)(2,1)S(1)}, bf16[3,64,256]{2,1,0:T(8,128)(2,1)S(1)}, u32[]{:S(2)}, u32[]{:S(2)}) collective-permute-start(bf16[3,64,256]{2,1,0:T(8,128)(2,1)S(1)} %total.1.refs_0_), channel_id=1, source_target_pairs={{0,2},{1,3},{2,0},{3,1},{4,6},{5,7},{6,4},{7,5},{8,10},{9,11},{10,... | collective-permute-start | bytes 294920 | tf_op jit(solution)/shard_map/ppermute | solution.py:259
  41.4 1.6 %collective-permute-done.7.refs_1_ = bf16[3,64,256]{2,1,0:T(8,128)(2,1)S(1)} collective-permute-done((bf16[3,64,256]{2,1,0:T(8,128)(2,1)S(1)}, bf16[3,64,256]{2,1,0:T(8,128)(2,1)S(1)}, u32[]{:S(2)}, u32[]{:S(2)}) %collective-permute-start.7) | collective-permute-done | bytes 98336 | tf_op jit(solution)/shard_map/ppermute | solution.py:259
  43.0 4.2 %collective-permute-done.8.refs_2_ = bf16[3,64,256]{2,1,0:T(8,128)(2,1)S(1)} collective-permute-done((bf16[3,64,256]{2,1,0:T(8,128)(2,1)S(1)}, bf16[3,64,256]{2,1,0:T(8,128)(2,1)S(1)}, u32[]{:S(2)}, u32[]{:S(2)}) %collective-permute-start.8) | collective-permute-done | bytes 98336 | tf_op jit(solution)/shard_map/ppermute | solution.py:259
  47.2 2.2 %collective-permute-done.9.refs_3_ = bf16[3,64,256]{2,1,0:T(8,128)(2,1)S(1)} collective-permute-done((bf16[3,64,256]{2,1,0:T(8,128)(2,1)S(1)}, bf16[3,64,256]{2,1,0:T(8,128)(2,1)S(1)}, u32[]{:S(2)}, u32[]{:S(2)}) %collective-permute-start.9) | collective-permute-done | bytes 98336 | tf_op jit(solution)/shard_map/ppermute | solution.py:259
  49.4 0.9 %spread.1 = f32[2,3,2,128,128]{4,3,2,1,0:T(8,128)} custom-call(bf16[3,64,256]{2,1,0:T(8,128)(2,1)S(1)} %total.1.refs_0_, bf16[3,64,256]{2,1,0:T(8,128)(2,1)S(1)} %collective-permute-done.7.refs_1_, bf16[3,64,256]{2,1,0:T(8,128)(2,1)S(1)} %collective-permute-done.8.refs_2_, bf16[3,64,256]{2,1,0:T(8,128)(2,1)S(1)} %collective-permute-done.9.refs_3_), custom_call_target="tpu_custom_call" | custom-call | tf_op jit(solution)/shard_map/spread/pallas_call | solution.py:386
  (1 shorter events, 0.0 us)
Async XLA Ops:
  3.1 17.7 %collective-permute-start = (bf16[1808,128]{1,0:T(8,128)(2,1)}, bf16[1808,128]{1,0:T(8,128)(2,1)S(1)}, u32[]{:S(2)}, u32[]{:S(2)}) collective-permute-start(bf16[1808,128]{1,0:T(8,128)(2,1)} %pack.1.own_at), channel_id=1, source_target_pairs={{1,0},{2,1},{3,2},{5,4},{6,5},{7,6},{9,8},{10,9},{11,10},{13,12},{... | collective-permute-start | bytes 1388552 | tf_op jit(solution)/shard_map/ppermute | solution.py:259
  4.4 16.4 %collective-permute-start.1 = (bf16[1808,128]{1,0:T(8,128)(2,1)}, bf16[1808,128]{1,0:T(8,128)(2,1)S(1)}, u32[]{:S(2)}, u32[]{:S(2)}) collective-permute-start(bf16[1808,128]{1,0:T(8,128)(2,1)} %pack.1.own_at), channel_id=1, source_target_pairs={{0,1},{1,2},{2,3},{4,5},{5,6},{6,7},{8,9},{9,10},{10,11},{12,13},{... | collective-permute-start | bytes 1388552 | tf_op jit(solution)/shard_map/ppermute | solution.py:259
  10.0 12.9 %collective-permute-start.2 = (bf16[1808,128]{1,0:T(8,128)(2,1)}, bf16[1808,128]{1,0:T(8,128)(2,1)S(1)}, u32[]{:S(2)}, u32[]{:S(2)}) collective-permute-start(bf16[1808,128]{1,0:T(8,128)(2,1)} %pack.1.own_at), channel_id=1, source_target_pairs={{4,8},{12,16},{20,24},{8,4},{16,12},{24,20},{5,9},{13,17},{21,25},... | collective-permute-start | bytes 1388552 | tf_op jit(solution)/shard_map/ppermute | solution.py:263
  10.7 12.3 %collective-permute-start.3 = (bf16[1808,128]{1,0:T(8,128)(2,1)}, bf16[1808,128]{1,0:T(8,128)(2,1)S(1)}, u32[]{:S(2)}, u32[]{:S(2)}) collective-permute-start(bf16[1808,128]{1,0:T(8,128)(2,1)} %pack.1.own_at), channel_id=1, source_target_pairs={{0,4},{8,12},{16,20},{24,28},{4,0},{12,8},{20,16},{28,24},{1,5},{9... | collective-permute-start | bytes 1388552 | tf_op jit(solution)/shard_map/ppermute | solution.py:263
  19.4 1.3 %copy-start.1 = (bf16[2,256,1024]{2,1,0:T(8,128)(2,1)S(1)}, bf16[2,256,1024]{2,1,0:T(8,128)(2,1)}, u32[]{:S(2)}) copy-start(bf16[2,256,1024]{2,1,0:T(8,128)(2,1)} %get-tuple-element.18.stock) | copy-start | bytes 3145732
  19.5 1.1 %copy-start.2 = (bf16[3,256,256]{2,1,0:T(8,128)(2,1)S(1)}, bf16[3,256,256]{2,1,0:T(8,128)(2,1)}, u32[]{:S(2)}) copy-start(bf16[3,256,256]{2,1,0:T(8,128)(2,1)} %get-tuple-element.16.more) | copy-start | bytes 1179652
  20.7 2.2 %copy-start = (bf16[2,256,1024]{2,1,0:T(8,128)(2,1)S(1)}, bf16[2,256,1024]{2,1,0:T(8,128)(2,1)}, u32[]{:S(2)}) copy-start(bf16[2,256,1024]{2,1,0:T(8,128)(2,1)} %get-tuple-element.15.stock) | copy-start | bytes 3145732
  25.1 10.5 %collective-permute-start.4 = (bf16[3,64,256]{2,1,0:T(8,128)(2,1)S(1)}, bf16[3,64,256]{2,1,0:T(8,128)(2,1)S(1)}, u32[]{:S(2)}, u32[]{:S(2)}) collective-permute-start(bf16[3,64,256]{2,1,0:T(8,128)(2,1)S(1)} %get-tuple-element.25), channel_id=1, source_target_pairs={{0,2},{1,3},{2,0},{3,1},{4,6},{5,7},{6,4},{7,5},{8,10},{9,11},{10,... | collective-permute-start | bytes 294920 | tf_op jit(solution)/shard_map/ppermute | solution.py:259
  28.1 7.6 %collective-permute-start.5 = (bf16[3,64,256]{2,1,0:T(8,128)(2,1)S(1)}, bf16[3,64,256]{2,1,0:T(8,128)(2,1)S(1)}, u32[]{:S(2)}, u32[]{:S(2)}) collective-permute-start(bf16[3,64,256]{2,1,0:T(8,128)(2,1)S(1)} %get-tuple-element.26), channel_id=1, source_target_pairs={{0,1},{1,2},{2,3},{3,0},{4,5},{5,6},{6,7},{7,4},{8,9},{9,10},{10,1... | collective-permute-start | bytes 294920 | tf_op jit(solution)/shard_map/ppermute | solution.py:259
  29.7 7.4 %collective-permute-start.6 = (bf16[3,64,256]{2,1,0:T(8,128)(2,1)S(1)}, bf16[3,64,256]{2,1,0:T(8,128)(2,1)S(1)}, u32[]{:S(2)}, u32[]{:S(2)}) collective-permute-start(bf16[3,64,256]{2,1,0:T(8,128)(2,1)S(1)} %get-tuple-element.27), channel_id=1, source_target_pairs={{0,3},{1,0},{2,1},{3,2},{4,7},{5,4},{6,5},{7,6},{8,11},{9,8},{10,9... | collective-permute-start | bytes 294920 | tf_op jit(solution)/shard_map/ppermute | solution.py:259
  37.1 6.0 %collective-permute-start.7 = (bf16[3,64,256]{2,1,0:T(8,128)(2,1)S(1)}, bf16[3,64,256]{2,1,0:T(8,128)(2,1)S(1)}, u32[]{:S(2)}, u32[]{:S(2)}) collective-permute-start(bf16[3,64,256]{2,1,0:T(8,128)(2,1)S(1)} %total.1.refs_0_), channel_id=1, source_target_pairs={{0,3},{1,0},{2,1},{3,2},{4,7},{5,4},{6,5},{7,6},{8,11},{9,8},{10,9... | collective-permute-start | bytes 294920 | tf_op jit(solution)/shard_map/ppermute | solution.py:259
  39.8 7.4 %collective-permute-start.8 = (bf16[3,64,256]{2,1,0:T(8,128)(2,1)S(1)}, bf16[3,64,256]{2,1,0:T(8,128)(2,1)S(1)}, u32[]{:S(2)}, u32[]{:S(2)}) collective-permute-start(bf16[3,64,256]{2,1,0:T(8,128)(2,1)S(1)} %total.1.refs_0_), channel_id=1, source_target_pairs={{0,1},{1,2},{2,3},{3,0},{4,5},{5,6},{6,7},{7,4},{8,9},{9,10},{10,1... | collective-permute-start | bytes 294920 | tf_op jit(solution)/shard_map/ppermute | solution.py:259
  39.8 9.6 %collective-permute-start.9 = (bf16[3,64,256]{2,1,0:T(8,128)(2,1)S(1)}, bf16[3,64,256]{2,1,0:T(8,128)(2,1)S(1)}, u32[]{:S(2)}, u32[]{:S(2)}) collective-permute-start(bf16[3,64,256]{2,1,0:T(8,128)(2,1)S(1)} %total.1.refs_0_), channel_id=1, source_target_pairs={{0,2},{1,3},{2,0},{3,1},{4,6},{5,7},{6,4},{7,5},{8,10},{9,11},{10,... | collective-permute-start | bytes 294920 | tf_op jit(solution)/shard_map/ppermute | solution.py:259
